TPU v7x, 32 devices: a whole 2x2x4 slice. The times are simulated.
32 devices in a mesh: dp: 16 (over z, y, core), mp: 2 (over x).
Axes of the slice: x: 2, y: 2, z: 4, core: 2. Of those that a mesh axis runs over, the one named last changes fastest.
Arguments:
- tokens: bfloat16 [32768, 1152], P(('dp', 'mp')), may hold values from -6 to 6
- conditioning: bfloat16 [128, 1152], P('dp'), may hold values from -6 to 6
- kept_ids: int32 [128, 179], P('dp'), may hold values from 0 to 255, as said below
- ada_weight: bfloat16 [1152, 6912], P(None, 'mp'), may hold values from -0.1875 to 0.1875
- ada_bias: float32 [6912], P('mp'), may hold values from -3 to 3
- attn_qkv: bfloat16 [1152, 3, 1152], P(None, None, 'mp'), may hold values from -0.1875 to 0.1875
- attn_out: bfloat16 [1152, 1152], P('mp'), may hold values from -0.75 to 0.75
- mlp_up: bfloat16 [1152, 4608], P(None, 'mp'), may hold values from -0.1875 to 0.1875
- mlp_down: bfloat16 [4608, 1152], P('mp'), may hold values from -0.09375 to 0.09375
- rel_table: float32 [16, 961], P('mp'), may hold values from -4 to 4
- grad_out_kept: bfloat16 [22912, 1152], P(('dp', 'mp')), may hold values from -6 to 6
- grad_out_full: bfloat16 [32768, 1152], P(('dp', 'mp')), may hold values from -6 to 6
Outputs:
- out_kept: bfloat16 [22912, 1152], P(('dp', 'mp'))
- out_full: bfloat16 [32768, 1152], P(('dp', 'mp'))
- grad_tokens: bfloat16 [32768, 1152], P(('dp', 'mp'))
- grad_cond: bfloat16 [128, 1152], P(('dp', 'mp'))
- grad_ada_weight: float32 [1152, 6912], P('dp', 'mp')
- grad_ada_bias: float32 [6912], P('mp')
- grad_attn_qkv: float32 [1152, 3, 1152], P('dp', None, 'mp')
- grad_attn_out: float32 [1152, 1152], P('mp', 'dp')
- grad_mlp_up: float32 [1152, 4608], P('dp', 'mp')
- grad_mlp_down: float32 [4608, 1152], P('mp', 'dp')
- grad_rel_table: float32 [16, 961], P('mp')
Inputs may be any that keep to these rules, and one draw needn't show every extreme that they name: `kept_ids`: each row holds 179 distinct patch indices of its image in ascending order.
All inputs are finite; a program needn't handle non-finite values.
Results may differ from a plain program's by a relative error of at most 0.02.
The roundings to bfloat16 on the way count: a program that leaves them out, or rounds other values in their place, can miss the bound.
Values may be sent and summed in bfloat16 or wider, within the bound.
A program may use at most 448 MiB of HBM per device.

v0:
```python
import math

import jax
import jax.numpy as jnp
from jax import lax
from jax.sharding import PartitionSpec as P

HEAD_DIM = 72
GRID = 16
PATCHES = 256
KEEP = 179
BUCKETS = 961


EPSILON = 1e-06
PRECISE = lax.Precision.HIGHEST


def normalize(rows):
    row_mean = jnp.mean(rows, axis=-1, keepdims=True)
    centered = rows - row_mean
    inverse = lax.rsqrt(jnp.mean(centered * centered, axis=-1, keepdims=True) + EPSILON)
    return (centered * inverse, inverse)


def norm_back(normed, inverse, upstream):
    return inverse * (
        upstream
        - jnp.mean(upstream, axis=-1, keepdims=True)
        - normed * jnp.mean(upstream * normed, axis=-1, keepdims=True)
    )


def gelu_tanh(values):
    return jax.nn.gelu(values, approximate=True)


def relative_index(query_pos, key_pos):
    bucket_span = 2 * GRID - 1
    row_gap = query_pos[..., :, None] // GRID - key_pos[..., None, :] // GRID + GRID - 1
    column_gap = query_pos[..., :, None] % GRID - key_pos[..., None, :] % GRID + GRID - 1
    return row_gap * bucket_span + column_gap


def rows_product(left_rows, right_rows):
    return lax.dot_general(
        left_rows, right_rows, (((0,), (0,)), ((), ())), preferred_element_type=jnp.float32
    )


def contract_last(left_rows, weight_mat):
    return lax.dot_general(
        left_rows, weight_mat, (((1,), (1,)), ((), ())), preferred_element_type=jnp.float32
    )


def spread_rows(rows):
    return lax.all_gather(rows, "mp", axis=0, tiled=True)


def spread_grads(rows):
    return lax.all_gather(rows, "mp", axis=0, tiled=True)


def summed_rows(left_rows, weight_mat):
    share_rows = left_rows.shape[0] // lax.axis_size("mp")

    def term_of(row_start, row_count):
        return jnp.dot(left_rows, weight_mat, preferred_element_type=jnp.float32)

    return lax.psum_scatter(
        term_of(jnp.int32(0), share_rows * lax.axis_size("mp")).astype(jnp.bfloat16),
        "mp",
        scatter_dimension=0,
        tiled=True,
    ).astype(jnp.float32)


def summed_grads(left_rows, weight_mat):
    share_rows = left_rows.shape[0] // lax.axis_size("mp")

    def term_of(row_start, row_count):
        term_rows = contract_last(left_rows, weight_mat)
        return term_rows

    return lax.psum_scatter(
        term_of(jnp.int32(0), share_rows * lax.axis_size("mp")).astype(jnp.bfloat16),
        "mp",
        scatter_dimension=0,
        tiled=True,
    ).astype(jnp.float32)


def kept_sums(left_rows, weight_mat):
    share_rows = left_rows.shape[0] // lax.axis_size("mp")

    def term_of(row_start, row_count):
        return contract_last(left_rows, weight_mat)

    return lax.psum_scatter(
        term_of(jnp.int32(0), share_rows * lax.axis_size("mp")).astype(jnp.bfloat16),
        "mp",
        scatter_dimension=0,
        tiled=True,
    ).astype(jnp.float32)


def split_blocks(stacked, blocks):
    return stacked.reshape((blocks, stacked.shape[0] // blocks) + stacked.shape[1:])


def merge_blocks(stacked):
    return stacked.reshape((-1,) + stacked.shape[2:])


def block_scores(query_blk, key_blk, bias_blk, score_scale):
    raw_scores = jnp.einsum(
        "nqhd,nkhd->nhqk", query_blk, key_blk, preferred_element_type=jnp.float32
    )
    return raw_scores * score_scale + bias_blk


def attend_forward(queries, key_rows, values, bias_blocks, score_scale):
    blocks = bias_blocks.shape[0]

    def one_block(items):
        scores = block_scores(items[0], items[1], items[3], score_scale)
        row_top = jnp.max(scores, axis=-1, keepdims=True)
        exp_scores = jnp.exp(scores - row_top)
        row_total = jnp.sum(exp_scores, axis=-1, keepdims=True)
        attn_probs = (exp_scores / row_total).astype(jnp.bfloat16)
        mixed = jnp.einsum(
            "nhqk,nkhd->nqhd", attn_probs, items[2], preferred_element_type=jnp.float32
        )
        return (mixed.astype(jnp.bfloat16), row_top[..., 0] + jnp.log(row_total[..., 0]))

    attended, log_total = lax.map(
        one_block,
        (
            split_blocks(queries, blocks),
            split_blocks(key_rows, blocks),
            split_blocks(values, blocks),
            bias_blocks,
        ),
    )
    return (merge_blocks(attended), merge_blocks(log_total))


def attend_backward(queries, key_rows, values, bias_blocks, log_total, grad_attended, score_scale):
    blocks = bias_blocks.shape[0]

    def one_block(items):
        query_blk, key_blk, value_blk, bias_blk, total_blk, upstream = items
        attn_probs = jnp.exp(
            block_scores(query_blk, key_blk, bias_blk, score_scale) - total_blk[..., None]
        )
        grad_value = jnp.einsum(
            "nhqk,nqhd->nkhd",
            attn_probs.astype(jnp.bfloat16),
            upstream,
            preferred_element_type=jnp.float32,
        )
        grad_probs = jnp.einsum(
            "nqhd,nkhd->nhqk", upstream, value_blk, preferred_element_type=jnp.float32
        )
        weighted = jnp.sum(attn_probs * grad_probs, axis=-1, keepdims=True)
        grad_scores = (attn_probs * (grad_probs - weighted)).astype(jnp.bfloat16)
        grad_query = (
            jnp.einsum("nhqk,nkhd->nqhd", grad_scores, key_blk, preferred_element_type=jnp.float32)
            * score_scale
        )
        grad_key = (
            jnp.einsum(
                "nhqk,nqhd->nkhd", grad_scores, query_blk, preferred_element_type=jnp.float32
            )
            * score_scale
        )
        return (
            jnp.stack([grad_query, grad_key, grad_value], axis=2).astype(jnp.bfloat16),
            grad_scores,
        )

    grad_qkv, grad_scores = lax.map(
        one_block,
        (
            split_blocks(queries, blocks),
            split_blocks(key_rows, blocks),
            split_blocks(values, blocks),
            bias_blocks,
            split_blocks(log_total, blocks),
            split_blocks(grad_attended, blocks),
        ),
    )
    return (merge_blocks(grad_qkv), merge_blocks(grad_scores))


def local(
    tokens,
    conditioning,
    kept_ids,
    ada_weight,
    ada_bias,
    attn_qkv,
    attn_out,
    mlp_up,
    mlp_down,
    rel_table,
    grad_out_kept,
    grad_out_full,
):
    model_ways = lax.axis_size("mp")
    images_group = conditioning.shape[0]
    images_here = images_group // model_ways
    model_place = lax.axis_index("mp")
    model_width = tokens.shape[1]
    score_scale = HEAD_DIM ** (-0.5)
    patch_ids = jnp.arange(PATCHES, dtype=jnp.int32)
    own_kept = lax.dynamic_slice_in_dim(kept_ids, model_place * images_here, images_here, 0)
    picker_own = (own_kept[:, :, None] == patch_ids[None, None, :]).astype(jnp.float32)
    qkv_whole, out_whole, up_whole, down_whole, table_whole = (
        attn_qkv,
        attn_out,
        mlp_up,
        mlp_down,
        rel_table,
    )
    heads_here = table_whole.shape[0]
    qkv_matrix = qkv_whole.reshape(model_width, -1)
    per_block = math.gcd(images_group, 8)
    blocks = images_group // per_block
    cond_values = conditioning.astype(jnp.float32)
    silu_cond = jax.nn.silu(cond_values).astype(jnp.bfloat16)
    mod_columns = (
        jnp.dot(silu_cond, ada_weight, preferred_element_type=jnp.float32) + ada_bias
    ).astype(jnp.bfloat16)
    modulation = lax.all_to_all(mod_columns, "mp", split_axis=0, concat_axis=1, tiled=True)
    modulation = modulation.astype(jnp.float32).reshape(images_here, 6, 1, model_width)
    shift_one, scale_one, gate_one, shift_two, scale_two, gate_two = [
        modulation[:, column] for column in range(6)
    ]
    token_rows = tokens.reshape(images_here, PATCHES, model_width)
    full_rows = token_rows.astype(jnp.float32)
    kept_rows = jnp.einsum(
        "nkp,npd->nkd",
        picker_own.astype(jnp.bfloat16),
        token_rows,
        preferred_element_type=jnp.float32,
    )
    full_index = relative_index(patch_ids, patch_ids)
    bias_full = jnp.take(table_whole, full_index, axis=1)
    full_blocks = bias_full[None, None]
    kept_index = relative_index(kept_ids, kept_ids)
    bias_kept = jnp.transpose(jnp.take(table_whole, kept_index, axis=1), (1, 0, 2, 3))
    kept_blocks = split_blocks(bias_kept, blocks)

    def one_pass(resid, gathered, bias_blocks, grad_output):
        row_count = resid.shape[1]
        projected = jnp.dot(gathered, qkv_matrix, preferred_element_type=jnp.float32).astype(
            jnp.bfloat16
        )
        projected = projected.reshape(images_group, row_count, 3, heads_here, HEAD_DIM)
        queries, key_rows, values = (projected[:, :, 0], projected[:, :, 1], projected[:, :, 2])
        attended, log_total = attend_forward(queries, key_rows, values, bias_blocks, score_scale)
        attended_flat = attended.reshape(images_group * row_count, heads_here * HEAD_DIM)
        branch_attn = summed_rows(attended_flat, out_whole).reshape(
            images_here, row_count, model_width
        )
        middle = resid + gate_one * branch_attn
        normed_mid, inverse_mid = normalize(middle)
        second = (normed_mid * (1.0 + scale_two) + shift_two).astype(jnp.bfloat16)
        gathered_mid = spread_rows(second.reshape(-1, model_width))
        hidden_pre = jnp.dot(gathered_mid, up_whole, preferred_element_type=jnp.float32)
        hidden_values, gelu_pull = jax.vjp(gelu_tanh, hidden_pre)
        hidden = hidden_values.astype(jnp.bfloat16)
        branch_mlp = summed_rows(hidden, down_whole).reshape(images_here, row_count, model_width)
        result = (middle + gate_two * branch_mlp).astype(jnp.bfloat16)
        grad_result = grad_output.astype(jnp.float32).reshape(images_here, row_count, model_width)
        grad_gate_two = jnp.sum(grad_result * branch_mlp, axis=1, keepdims=True)
        grad_mlp = spread_grads(
            (gate_two * grad_result).astype(jnp.bfloat16).reshape(-1, model_width)
        )
        grad_down = rows_product(hidden, grad_mlp)
        grad_hidden = contract_last(grad_mlp, down_whole)
        grad_pre = gelu_pull(grad_hidden)[0].astype(jnp.bfloat16)
        grad_up = rows_product(gathered_mid, grad_pre)
        grad_second = summed_grads(grad_pre, up_whole).reshape(images_here, row_count, model_width)
        grad_shift_two = jnp.sum(grad_second, axis=1, keepdims=True)
        grad_scale_two = jnp.sum(grad_second * normed_mid, axis=1, keepdims=True)
        grad_middle = grad_result + norm_back(
            normed_mid, inverse_mid, grad_second * (1.0 + scale_two)
        )
        grad_gate_one = jnp.sum(grad_middle * branch_attn, axis=1, keepdims=True)
        grad_attn = spread_grads(
            (gate_one * grad_middle).astype(jnp.bfloat16).reshape(-1, model_width)
        )
        grad_proj = rows_product(attended_flat, grad_attn)
        grad_attended = contract_last(grad_attn, out_whole).astype(jnp.bfloat16)
        grad_attended = grad_attended.reshape(images_group, row_count, heads_here, HEAD_DIM)
        grad_qkv, grad_scores = attend_backward(
            queries, key_rows, values, bias_blocks, log_total, grad_attended, score_scale
        )
        grad_qkv = grad_qkv.reshape(images_group * row_count, -1)
        grad_qkv_weight = rows_product(gathered, grad_qkv)
        mod_parts = [grad_gate_one, grad_shift_two, grad_scale_two, grad_gate_two]
        return (
            result,
            grad_middle,
            mod_parts,
            grad_qkv,
            grad_scores,
            (grad_qkv_weight, grad_proj, grad_up, grad_down),
        )

    normed_full, inverse_full = normalize(full_rows)
    normed_kept, inverse_kept = normalize(kept_rows)
    first_full = (normed_full * (1.0 + scale_one) + shift_one).astype(jnp.bfloat16)
    gathered_full = spread_rows(first_full.reshape(-1, model_width))
    first_kept = (normed_kept * (1.0 + scale_one) + shift_one).astype(jnp.bfloat16)
    gathered_kept = lax.all_gather(first_kept.reshape(-1, model_width), "mp", axis=0, tiled=True)
    kept_pass = one_pass(kept_rows, gathered_kept, kept_blocks, grad_out_kept)
    full_pass = one_pass(full_rows, gathered_full, full_blocks, grad_out_full)
    grad_first_full = summed_grads(full_pass[3], qkv_matrix).reshape(
        images_here, PATCHES, model_width
    )
    grad_first_kept = kept_sums(kept_pass[3], qkv_matrix).reshape(images_here, KEEP, model_width)
    grad_shift_one = jnp.sum(grad_first_full, axis=1, keepdims=True) + jnp.sum(
        grad_first_kept, axis=1, keepdims=True
    )
    grad_scale_one = jnp.sum(grad_first_full * normed_full, axis=1, keepdims=True) + jnp.sum(
        grad_first_kept * normed_kept, axis=1, keepdims=True
    )
    back_full = norm_back(normed_full, inverse_full, grad_first_full * (1.0 + scale_one))
    back_kept = norm_back(normed_kept, inverse_kept, grad_first_kept * (1.0 + scale_one))
    kept_spread = jnp.einsum(
        "nkp,nkd->npd", picker_own, kept_pass[1] + back_kept, precision=PRECISE
    )
    grad_token_rows = full_pass[1] + back_full + kept_spread
    grad_tokens = grad_token_rows.reshape(-1, model_width).astype(jnp.bfloat16)
    later_parts = [kept_pass[2][column] + full_pass[2][column] for column in range(4)]
    grad_mod = jnp.concatenate([grad_shift_one, grad_scale_one] + later_parts, axis=1).reshape(
        images_here, 6 * model_width
    )
    grad_mod_columns = lax.all_to_all(grad_mod, "mp", split_axis=1, concat_axis=0, tiled=True)
    grad_ada_weight = lax.dot_general(
        silu_cond.astype(jnp.float32), grad_mod_columns, (((0,), (0,)), ((), ())), precision=PRECISE
    )
    grad_ada_bias = jnp.sum(grad_mod_columns, axis=0)
    silu_part = lax.dot_general(
        grad_mod_columns,
        ada_weight.astype(jnp.float32),
        (((1,), (1,)), ((), ())),
        precision=PRECISE,
    )
    grad_silu = lax.psum_scatter(
        silu_part.astype(jnp.bfloat16), "mp", scatter_dimension=0, tiled=True
    ).astype(jnp.float32)
    own_cond = lax.dynamic_slice_in_dim(cond_values, model_place * images_here, images_here, 0)
    silu_pull = jax.vjp(jax.nn.silu, own_cond)[1]
    grad_cond = silu_pull(grad_silu)[0].astype(jnp.bfloat16)
    full_scores_sum = jnp.sum(full_pass[4].astype(jnp.float32), axis=0).reshape(heads_here, -1)
    table_full = jax.ops.segment_sum(
        full_scores_sum.T, full_index.reshape(-1), num_segments=BUCKETS
    )
    kept_scores = jnp.transpose(kept_pass[4].astype(jnp.float32), (0, 2, 3, 1)).reshape(
        -1, heads_here
    )
    table_kept = jax.ops.segment_sum(kept_scores, kept_index.reshape(-1), num_segments=BUCKETS)
    grad_table = (table_full + table_kept).T
    grad_qkv_weight = (kept_pass[5][0] + full_pass[5][0]).reshape(model_width, 3, -1)
    grad_proj = kept_pass[5][1] + full_pass[5][1]
    grad_up = kept_pass[5][2] + full_pass[5][2]
    grad_down = kept_pass[5][3] + full_pass[5][3]
    shares = (grad_qkv_weight, grad_proj, grad_up, grad_down, grad_table)
    summed = (
        lax.psum_scatter(
            shares[0].astype(jnp.bfloat16), "dp", scatter_dimension=0, tiled=True
        ).astype(jnp.float32),
        lax.psum_scatter(
            shares[1].astype(jnp.bfloat16), "dp", scatter_dimension=1, tiled=True
        ).astype(jnp.float32),
        lax.psum_scatter(
            shares[2].astype(jnp.bfloat16), "dp", scatter_dimension=0, tiled=True
        ).astype(jnp.float32),
        lax.psum_scatter(
            shares[3].astype(jnp.bfloat16), "dp", scatter_dimension=1, tiled=True
        ).astype(jnp.float32),
        lax.psum_scatter(
            grad_ada_weight.astype(jnp.bfloat16), "dp", scatter_dimension=0, tiled=True
        ).astype(jnp.float32),
    )
    small_totals = lax.psum((grad_ada_bias, shares[4]), "dp")
    out_kept = kept_pass[0].reshape(-1, model_width)
    out_full = full_pass[0].reshape(-1, model_width)
    return (
        out_kept,
        out_full,
        grad_tokens,
        grad_cond,
        summed[4],
        small_totals[0],
        summed[0],
        summed[1],
        summed[2],
        summed[3],
        small_totals[1],
    )


def solution(mesh):
    placed = (
        P(("dp", "mp"), None),
        P("dp", None),
        P("dp", None),
        P(None, "mp"),
        P("mp"),
        P(None, None, "mp"),
        P("mp", None),
        P(None, "mp"),
        P("mp", None),
        P("mp", None),
        P(("dp", "mp"), None),
        P(("dp", "mp"), None),
    )
    return jax.shard_map(
        local,
        mesh=mesh,
        in_specs=placed,
        out_specs=(
            P(("dp", "mp"), None),
            P(("dp", "mp"), None),
            P(("dp", "mp"), None),
            P(("dp", "mp"), None),
            P("dp", "mp"),
            P("mp"),
            P("dp", None, "mp"),
            P("mp", "dp"),
            P("dp", "mp"),
            P("mp", "dp"),
            P("mp", None),
        ),
        check_vma=False,
    )
```

profile of v0, /device:TPU:0, one launch (start us, length us, event | category | flops | bytes accessed | tf_op | source)
XLA Modules:
  0.0 3857.6 jit_solution(17887969565963629206)
XLA Ops:
  27.8 215.6 %gather_fusion.1 = f32[65536,8]{1,0:T(8,128)} fusion(f32[8,961]{0,1:T(8,128)S(1)} %copy.160, s32[65536]{0:T(1024)S(1)} %broadcast_clamp_fusion), kind=kCustom, calls=%fused_computation.1 | custom fusion | bytes 4456448 | tf_op jit(solution)/shard_map/jit(_take)/gather | solution.py:250
  243.4 19.5 copy.170
  266.5 14.2 convolution_convert_fusion.4
  288.8 7.8 fusion.132
  296.6 9.9 fusion.11
  306.5 9.8 convert_bitcast_fusion
  338.9 49.3 %reduce-scatter.24.cloned.1.call-done = bf16[1024,1152]{1,0:T(8,128)(2,1)} async-done(((bf16[2048,1152]{1,0:T(8,128)(2,1)}), bf16[1024,1152]{1,0:T(8,128)(2,1)}) %reduce-scatter.24.cloned.1.call-update) | async-done | bytes 2359312 | tf_op jit(solution)/shard_map/reduce_scatter | solution.py:71
  402.6 468.4 %gather_fusion = f32[256328,8]{1,0:T(8,128)} fusion(f32[8,961]{0,1:T(8,128)S(1)} %copy.160, s32[257024]{0:T(1024)S(1)} %pad_clamp_fusion), kind=kCustom, calls=%fused_computation | custom fusion | bytes 17430304 | tf_op jit(solution)/shard_map/jit(_take)/gather | solution.py:253
  871.0 65.9 %copy.161 = f32[256328,8]{0,1:T(8,128)} copy(f32[256328,8]{1,0:T(8,128)} %gather_fusion) | data formatting | bytes 16404992 | tf_op jit(solution)/shard_map/jit(_take)/gather | solution.py:253
  937.0 17.7 reshape.967
  954.6 12.9 copy.162
  981.5 11.7 convolution_convert_fusion.6
  993.2 15.0 reshape.1018
  1028.8 16.8 fusion.127
  1045.6 7.1 fusion.26
  1071.6 41.6 %fusion = bf16[720,1152]{1,0:T(8,128)(2,1)S(1)} fusion(bf16[1432,1152]{1,0:T(8,128)(2,1)} %convolution_convert_fusion.5), kind=kCustom, calls=%all-reduce-scatter | all-reduce-scatter fusion | flops 1658881 | bytes 4958720
  1118.2 8.4 concatenate.4
  1143.0 18.9 fusion.133
  1161.9 30.1 fusion.10
  1195.5 16.7 convolution_convert_fusion.8
  1212.3 22.5 convolution_convert_fusion.9
  1248.5 15.0 fusion.134
  1267.8 23.8 fusion.18
  1294.4 13.0 convolution_convert_fusion.7
  1311.9 24.6 reduce-scatter.26.cloned.1.call-done
  1336.4 7.4 fusion.52
  1343.9 73.0 %fusion.2 = bf16[720,1152]{1,0:T(8,128)(2,1)S(1)} fusion(bf16[1432,1152]{1,0:T(8,128)(2,1)} %convolution_convert_fusion.7), kind=kCustom, calls=%all-reduce-scatter.2 | all-reduce-scatter fusion | flops 1658881 | bytes 4958720
  1422.6 8.3 concatenate.6
  1460.6 12.5 multiply_reduce_fusion
  1473.1 10.0 fusion.86
  1483.2 14.1 convert_reduce_fusion
  1504.8 7.0 copy.178
  1511.7 6.3 copy.217
  1521.0 11.8 convolution_convert_fusion.2
  1533.7 11.9 fusion.136
  1545.6 15.0 fusion.24
  1560.7 16.9 fusion.124
  1577.6 15.6 convolution_convert_fusion.10
  1606.6 20.6 fusion.25
  1627.2 9.6 multiply_reduce_fusion.1
  1641.2 8.0 multiply_convert_fusion.3
  1665.8 7.1 copy.184
  1672.8 12.6 convert_element_type.337
  1690.9 8.8 convolution_convert_fusion.1
  1704.8 13.2 fusion.137
  1718.1 10.6 fusion.32
  1728.7 6.5 copy.206
  1735.3 74.0 %fusion.125 = (bf16[720,1152]{1,0:T(8,128)(2,1)}, bf16[720,1152]{1,0:T(8,128)(2,1)S(1)}) fusion(bf16[1432,1152]{1,0:T(8,128)(2,1)} %convolution_convert_fusion.10, bf16[1432,1152]{1,0:T(8,128)(2,1)} %convolution_convert_fusion.1), kind=kCustom, calls=%all-reduce-scatter.4 | all-reduce-scatter fusion | flops 3317761 | bytes 9916928
  1815.0 10.0 concatenate.5
  1832.7 8.4 concatenate.7
  1860.1 10.9 fusion.60
  1871.5 8.2 all_to_all.32
  1879.8 8.5 convolution_convert_fusion
  1903.5 21.6 fusion.35
  1925.1 13.2 copy.190
  1938.3 13.2 reshape.990
  1951.4 56.9 %copy.191 = f32[256328,8]{1,0:T(8,128)} copy(f32[256328,8]{0,1:T(8,128)} %reshape.990) | data formatting | bytes 16404992 | tf_op jit(solution)/shard_map/reshape | solution.py:364
  2008.3 1363.2 %scatter_custom_fusion.1 = f32[961,8]{1,0:T(8,128)} fusion(s32[256328]{0:T(1024)} %reshape.988, f32[256328,8]{1,0:T(8,128)} %copy.191, f32[]{:T(128)} %constant.261.clone.1), kind=kCustom, calls=%fused_computation.210 | custom fusion | flops 2050624 | bytes 31264 | tf_op jit(solution)/shard_map/scatter-add | solution.py:367
  3385.9 16.5 copy.188
  3402.4 347.5 %scatter_custom_fusion = f32[961,8]{1,0:T(8,128)S(1)} fusion(s32[65536]{0:T(1024)} %bitcast.345, f32[65536,8]{1,0:T(8,128)} %copy.188, f32[]{:T(128)} %constant.261.clone.1), kind=kCustom, calls=%fused_computation.212 | custom fusion | flops 524288 | bytes 31264 | tf_op jit(solution)/shard_map/scatter-add | solution.py:361
  3758.2 10.5 fusion.64
  3768.8 63.0 %all-reduce.11 = (f32[3456]{0:T(1024)}, f32[8,961]{0,1:T(8,128)S(1)}) all-reduce(f32[3456]{0:T(1024)S(1)} %reduce_sum.342, f32[8,961]{0,1:T(8,128)S(1)} %add_bitcast_fusion), channel_id=1, replica_groups=mesh['dp'=16,'mp'=2] {'dp'}, use_global_device_ids=true, to_apply=%region_45.46 | all-reduce | flops 11144 | bytes 89152 | tf_op jit(solution)/shard_map/psum | solution.py:391
  3832.6 8.8 convolution_convert_fusion.13
  3841.4 6.8 all-reduce.4
  (464 shorter events, 336.4 us)
Async XLA Ops:
  7.2 312.7 %copy-start = (bf16[576,1152]{1,0:T(8,128)(2,1)S(1)}, bf16[576,1152]{1,0:T(8,128)(2,1)}, u32[]{:S(2)}) copy-start(bf16[576,1152]{1,0:T(8,128)(2,1)} %param.18) | copy-start | bytes 3981316
  12.3 8.7 all-to-all-start
  16.6 249.9 %all-gather.13.cloned.1.call-start = ((), (), s32[]{:S(2)}) async-start(), calls=%async_computation.11 | async-start | bytes 7077888 | tf_op jit(solution)/shard_map/all_gather | solution.py:58
  21.8 371.4 %copy-start.34 = (f32[4,1152]{1,0:T(4,128)}, f32[4,1152]{1,0:T(4,128)S(1)}, u32[]{:S(2)}) copy-start(f32[4,1152]{1,0:T(4,128)S(1)} %get-tuple-element.207) | copy-start | bytes 55300
  26.7 361.5 %reduce-scatter.24.cloned.1.call-start = ((), (), s32[]{:S(2)}) async-start(), calls=%async_computation.12 | async-start | bytes 7077888 | tf_op jit(solution)/shard_map/reduce_scatter | solution.py:71
  27.5 235.5 %copy-start.91 = (s32[256]{0:T(256)}, s32[256]{0:T(256)S(1)}, u32[]{:S(2)}) copy-start(s32[256]{0:T(256)S(1)} %get-tuple-element.225) | copy-start | bytes 3076
  27.5 235.5 %copy-start.93 = (s32[256]{0:T(256)}, s32[256]{0:T(256)S(1)}, u32[]{:S(2)}) copy-start(s32[256]{0:T(256)S(1)} %get-tuple-element.226) | copy-start | bytes 3076
  296.6 9.9 copy-start.50
  306.5 9.8 copy-start.62
  325.7 651.5 %all-gather.21.cloned.1.call-start = ((), (), s32[]{:S(2)}) async-start(), calls=%async_computation.21 | async-start | bytes 4976640 | tf_op jit(solution)/shard_map/all_gather | solution.py:319
  334.9 808.0 %all-gather.17.cloned.1.call-start = ((), (), s32[]{:S(2)}) async-start(), calls=%async_computation.15 | async-start | bytes 7077888 | tf_op jit(solution)/shard_map/all_gather | solution.py:62
  338.5 823.3 %all-gather.15.cloned.1.call-start = ((), (), s32[]{:S(2)}) async-start(), calls=%async_computation.13 | async-start | bytes 7077888 | tf_op jit(solution)/shard_map/all_gather | solution.py:58
  338.6 59.8 %copy-start.57 = (s32[8,179]{1,0:T(8,128)}, s32[8,179]{1,0:T(8,128)S(1)}, u32[]{:S(2)}) copy-start(s32[8,179]{1,0:T(8,128)S(1)} %get-tuple-element.208) | copy-start | bytes 17188
  338.6 59.8 %copy-start.59 = (s32[8,179]{1,0:T(8,128)}, s32[8,179]{1,0:T(8,128)S(1)}, u32[]{:S(2)}) copy-start(s32[8,179]{1,0:T(8,128)S(1)} %get-tuple-element.209) | copy-start | bytes 17188
  338.7 57.2 %copy-start.47 = (s32[8,179]{0,1:T(8,128)}, s32[8,179]{0,1:T(8,128)S(1)}, u32[]{:S(2)}) copy-start(s32[8,179]{0,1:T(8,128)S(1)} %copy.157) | copy-start | bytes 17188
  338.9 57.1 %copy-start.49 = (s32[8,179]{0,1:T(8,128)}, s32[8,179]{0,1:T(8,128)S(1)}, u32[]{:S(2)}) copy-start(s32[8,179]{0,1:T(8,128)S(1)} %copy.158) | copy-start | bytes 17188
  395.9 848.4 %all-gather.25.cloned.1.call-start = ((), (), s32[]{:S(2)}) async-start(), calls=%async_computation.23 | async-start | bytes 4976640 | tf_op jit(solution)/shard_map/all_gather | solution.py:62
  954.6 12.9 copy-start.54
  976.9 286.6 %all-gather.23.cloned.1.call-start = ((), (), s32[]{:S(2)}) async-start(), calls=%async_computation.22 | async-start | bytes 4976640 | tf_op jit(solution)/shard_map/all_gather | solution.py:58
  1071.6 45.3 %copy-start.106 = (u32[32]{0:T(128)S(1)}, u32[32]{0:T(128)}, u32[]{:S(2)}) copy-start(u32[32]{0:T(128)} %constant.284) | copy-start | bytes 388
  1113.2 5.0 collective-permute-start
  1142.9 164.5 %reduce-scatter.28.cloned.1.call-start = ((), (), s32[]{:S(2)}) async-start(), calls=%async_computation.16 | async-start | bytes 7077888 | tf_op jit(solution)/shard_map/reduce_scatter | solution.py:86
  1212.2 124.2 %reduce-scatter.26.cloned.1.call-start = ((), (), s32[]{:S(2)}) async-start(), calls=%async_computation.14 | async-start | bytes 7077888 | tf_op jit(solution)/shard_map/reduce_scatter | solution.py:71
  1234.8 218.0 %all-gather.19.cloned.1.call-start = ((), (), s32[]{:S(2)}) async-start(), calls=%async_computation.17 | async-start | bytes 7077888 | tf_op jit(solution)/shard_map/all_gather | solution.py:62
  1294.4 13.0 copy-start.36
  1294.4 13.0 copy-start.70
  1294.4 13.0 copy-start.73
  1307.4 29.0 copy-start.55
  1311.8 32.0 copy-start.95
  1311.9 31.9 copy-start.97
  1343.8 77.5 %copy-start.51 = (f32[8,8,256]{2,1,0:T(8,128)S(1)}, f32[8,8,256]{2,1,0:T(8,128)}, u32[]{:S(2)}) copy-start(f32[8,8,256]{2,1,0:T(8,128)} %copy-done.50) | copy-start | bytes 196612
  1343.8 77.5 %copy-start.63 = (f32[8,8,256]{2,1,0:T(8,128)S(1)}, f32[8,8,256]{2,1,0:T(8,128)}, u32[]{:S(2)}) copy-start(f32[8,8,256]{2,1,0:T(8,128)} %copy-done.62) | copy-start | bytes 196612
  1343.8 249.3 %all-gather.27.cloned.1.call-start = ((), (), s32[]{:S(2)}) async-start(), calls=%async_computation.24 | async-start | bytes 4976640 | tf_op jit(solution)/shard_map/all_gather | solution.py:62
  1416.9 5.8 collective-permute-start.2
  1452.8 407.3 %reduce-scatter.30.cloned.1.call-start = ((), (), s32[]{:S(2)}) async-start(), calls=%async_computation.18 | async-start | bytes 7077888 | tf_op jit(solution)/shard_map/reduce_scatter | solution.py:86
  1483.2 14.1 copy-start.15
  1532.8 12.8 slice-start.5
  1532.8 1844.6 %reduce-scatter.32.cloned.1.call-start = ((), (), s32[]{:S(2)}) async-start(), calls=%async_computation.19 | async-start | bytes 5640192 | tf_op jit(solution)/shard_map/reduce_scatter | solution.py:381
  1533.6 11.9 slice-start.6
  1560.6 17.0 slice-start.3
  1560.6 1818.6 %reduce-scatter.34.cloned.1.call-start = ((), (), s32[]{:S(2)}) async-start(), calls=%async_computation.20 | async-start | bytes 5640192 | tf_op jit(solution)/shard_map/reduce_scatter | solution.py:384
  1560.6 16.9 slice-start.4
  1627.2 2123.9 %reduce-scatter.40.cloned.1.call-start = ((), (), s32[]{:S(2)}) async-start(), calls=%async_computation.27 | async-start | bytes 1566720
  1672.8 12.6 copy-start.33
  1685.5 14.2 slice-start.7
  1704.8 2047.9 %reduce-scatter.36.cloned.1.call-start = ((), (), s32[]{:S(2)}) async-start(), calls=%async_computation.25 | async-start | bytes 4386816
  1704.8 13.3 copy-start.29
  1735.2 78.4 %copy-start.90 = (f32[1024]{0:T(1024)S(1)}, f32[1024]{0:T(1024)}, u32[]{:S(2)}) copy-start(f32[1024]{0:T(1024)} %copy-done.89) | copy-start | bytes 12292
  1735.2 78.4 %copy-start.80 = (f32[1024]{0:T(1024)S(1)}, f32[1024]{0:T(1024)}, u32[]{:S(2)}) copy-start(f32[1024]{0:T(1024)} %copy-done.79) | copy-start | bytes 12292
  1735.2 2113.6 %reduce-scatter.38.cloned.1.call-start = ((), (), s32[]{:S(2)}) async-start(), calls=%async_computation.26 | async-start | bytes 8460288
  1809.3 23.5 copy-start.22
  1810.0 5.0 collective-permute-start.1
  1813.7 46.4 %copy-start.101 = (f32[4,256]{1,0:T(4,128)}, f32[4,256]{1,0:T(4,128)S(1)}, u32[]{:S(2)}) copy-start(f32[4,256]{1,0:T(4,128)S(1)} %div.154) | copy-start | bytes 12292
  1813.7 19.0 collective-permute-start.3
  1860.0 11.0 copy-start.83
  1860.0 11.1 copy-start.82
  1860.0 11.1 copy-start.84
  1860.0 19.7 copy-start.61
  2008.3 1369.0 %copy-start.105 = (f32[4,179]{1,0:T(4,128)S(1)}, f32[4,179]{1,0:T(4,128)}, u32[]{:S(2)}) copy-start(f32[4,179]{1,0:T(4,128)} %get-tuple-element.165) | copy-start | bytes 8596
  3402.4 355.7 %copy-start.100 = (s32[4,179]{1,0:T(4,128)S(1)}, s32[4,179]{1,0:T(4,128)}, u32[]{:S(2)}) copy-start(s32[4,179]{1,0:T(4,128)} %copy-done.99) | copy-start | bytes 8596
  3402.4 355.8 %copy-start.102 = (f32[4,256]{1,0:T(4,128)S(1)}, f32[4,256]{1,0:T(4,128)}, u32[]{:S(2)}) copy-start(f32[4,256]{1,0:T(4,128)} %copy-done.101) | copy-start | bytes 12292
  3758.2 10.6 copy-start.44
  3758.2 74.4 %copy-start.42 = (f32[8,3456]{1,0:T(8,128)S(1)}, f32[8,3456]{1,0:T(8,128)}, u32[]{:S(2)}) copy-start(f32[8,3456]{1,0:T(8,128)} %copy-done.41) | copy-start | bytes 331780
  3768.8 79.4 %copy-start.81 = (f32[8,1152]{1,0:T(8,128)S(1)}, f32[8,1152]{1,0:T(8,128)}, u32[]{:S(2)}) copy-start(f32[8,1152]{1,0:T(8,128)} %convert_element_type.284) | copy-start | bytes 110596
  (78 other events, 362.8 us)
Sparse Core Ops, SparseCore 0:
  26.8 64.9 all-gather.12
  325.8 62.2 reduce-scatter.23
  390.4 46.8 all-gather.20
  438.8 62.6 all-gather.16
  502.9 62.6 all-gather.14
  977.1 46.8 all-gather.24
  1143.0 48.5 all-gather.22
  1212.4 61.6 reduce-scatter.27
  1276.4 59.9 reduce-scatter.25
  1344.0 92.1 all-gather.18
  1452.9 48.4 all-gather.26
  1532.9 61.6 reduce-scatter.29
  1598.6 79.8 reduce-scatter.31
  1682.4 78.3 reduce-scatter.33
  1764.3 57.7 reduce-scatter.39
  1825.9 70.9 reduce-scatter.35
  1900.9 99.8 reduce-scatter.37
where the time goes:
time: 3870 us; the launch traced here: 3860 us
  other arithmetic  1890 us (49%)
  local copies, waits for them, and re-layouts  1140 us (29%)
  matrix products  445 us (11%)
  blocking collectives  266 us (7%)
  waiting for transfers between devices  75.6 us (2%)
    scatter-add x1, other arithmetic, local(): jax.ops.segment_sum(kept_scores, kept_index.reshape(-1), num_segments=BUC...  1360 us
    gather x4, local copies, waits for them, and re-layouts, local(): jnp.take(table_whole, kept_index, axis=1)  565 us
    scatter-add x1, other arithmetic, local(): jax.ops.segment_sum(full_scores_sum.T, full_index.reshape(-1), num_segmen...  347 us
    gather x2, local copies, waits for them, and re-layouts, local(): bias_full = jnp.take(table_whole, full_index, axis=1)  235 us
    unnamed x4, blocking collectives  195 us
    unnamed x270, local copies, waits for them, and re-layouts  128 us
    dot_general x8, matrix products, rows_product(): lax.dot_general(left_rows, right_rows, (((0,), (0,)), ((), ())), preferre...  98.5 us
    dot_general x8, matrix products, contract_last(): lax.dot_general(left_rows, weight_mat, (((1,), (1,)), ((), ())), preferre...  94.6 us
  transfers between devices with their start and end apart: 22, of which 3 were waited for; matrix products, arithmetic and copies ran while one was open for 92% of the time, Pallas kernels for 0%

commit v1 on v0

v1 whole, which is shorter than its diff:
```python
import functools
import math

import jax
import jax.numpy as jnp
from jax import lax
from jax.experimental import pallas as pl
from jax.experimental.pallas import tpu as pltpu
from jax.sharding import PartitionSpec as P

HEAD_DIM = 72
GRID = 16
PATCHES = 256
BUCKETS = 961
SPAN = 2 * GRID - 1
EPSILON = 1e-06
PRECISE = lax.Precision.HIGHEST
BF = jnp.bfloat16
F32 = jnp.float32
LOG2E = math.log2(math.e)
VMEM_LIMIT = 60 * 1024 * 1024


def dot(a, b, dims):
    return lax.dot_general(a, b, ((dims[0:1], dims[1:2]), ((), ())), preferred_element_type=F32)


def nn(a, b):
    return dot(a, b, (1, 0))


def nt(a, b):
    return dot(a, b, (1, 1))


def tn(a, b):
    return dot(a, b, (0, 0))


def normalize(rows):
    centered = rows - jnp.mean(rows, axis=-1, keepdims=True)
    inverse = lax.rsqrt(jnp.mean(centered * centered, axis=-1, keepdims=True) + EPSILON)
    return centered * inverse, inverse


def norm_back(normed, inverse, upstream):
    return inverse * (
        upstream
        - jnp.mean(upstream, axis=-1, keepdims=True)
        - normed * jnp.mean(upstream * normed, axis=-1, keepdims=True)
    )


def params(n_grid=1):
    return pltpu.CompilerParams(
        vmem_limit_bytes=VMEM_LIMIT, dimension_semantics=("arbitrary",) * n_grid
    )


def cost(flops, bytes_accessed, transcendentals=0):
    return pl.CostEstimate(
        flops=int(flops), bytes_accessed=int(bytes_accessed), transcendentals=int(transcendentals)
    )


def const_spec(shape):
    return pl.BlockSpec(shape, lambda *_: (0,) * len(shape), pipeline_mode=pl.Buffered(1))


def bias_kernel(strip_ref, bias_ref):
    strip = strip_ref[0]
    for key_row in range(GRID):
        start = (GRID - 1 - key_row) * GRID
        bias_ref[0, key_row * GRID : (key_row + 1) * GRID, :] = strip[:, start : start + PATCHES]


def bias_whole(table):
    heads = table.shape[0]
    grid_table = table.reshape(heads, SPAN, SPAN) * LOG2E
    strip = jnp.stack(
        [grid_table[:, :, GRID - 1 - c : 2 * GRID - 1 - c] for c in range(GRID)], axis=1
    ).reshape(heads, GRID, SPAN * GRID)
    strip = jnp.pad(strip, ((0, 0), (0, 0), (0, 512 - SPAN * GRID)))
    return pl.pallas_call(
        bias_kernel,
        grid=(heads,),
        in_specs=[pl.BlockSpec((1, GRID, 512), lambda h: (h, 0, 0))],
        out_specs=pl.BlockSpec((1, PATCHES, PATCHES), lambda h: (h, 0, 0)),
        out_shape=jax.ShapeDtypeStruct((heads, PATCHES, PATCHES), F32),
        compiler_params=params(),
        cost_estimate=cost(0, heads * PATCHES * PATCHES * 4),
    )(strip)


def table_of_strips(strips):
    heads = strips.shape[0]
    parts = strips[:, :, : SPAN * GRID].reshape(heads, GRID, SPAN, GRID)
    total = jnp.zeros((heads, SPAN, SPAN), F32)
    for c in range(GRID):
        total = total + jnp.pad(parts[:, c], ((0, 0), (0, 0), (GRID - 1 - c, c)))
    return total.reshape(heads, BUCKETS)


def head_rows(head, per_block):
    base = (head // per_block) * (3 * per_block * HEAD_DIM) + (head % per_block) * HEAD_DIM
    step = per_block * HEAD_DIM
    return [pl.ds(pl.multiple_of(base + c * step, 8), HEAD_DIM) for c in range(3)]


def key_mask(pick):
    ones = jnp.ones((pick.shape[0], PATCHES), BF)
    return (tn(pick, ones) - 1.0) * 1e30


def forward_kernel(
    per_block, tok_ref, mod_ref, pick_ref, weight_ref, out_w_ref, bias_ref,
    first_ref, qkv_ref, att_ref, lse_ref, middle_ref, second_ref, branch_ref,
    qkv_s, att_s, attk_s,
):
    heads = bias_ref.shape[0]
    tok = tok_ref[...].astype(F32)
    shift_one, scale_one, gate_one = mod_ref[0, 0:1], mod_ref[0, 1:2], mod_ref[0, 2:3]
    shift_two, scale_two = mod_ref[0, 3:4], mod_ref[0, 4:5]
    normed, _ = normalize(tok)
    first = (normed * (1.0 + scale_one) + shift_one).astype(BF)
    first_ref[...] = first
    step = weight_ref.shape[0] // 6
    for c in range(6):
        rows = slice(c * step, (c + 1) * step)
        part = nt(weight_ref[rows, :], first)
        qkv_s[rows, :] = part
        qkv_ref[rows, :] = part.astype(BF)
    pick = pick_ref[0]
    mask = key_mask(pick)
    scale = HEAD_DIM ** (-0.5) * LOG2E

    def one_head(head, carry):
        q_at, k_at, v_at = head_rows(head, per_block)
        queries = qkv_s[q_at, :].astype(BF)
        keys = qkv_s[k_at, :].astype(BF)
        values = qkv_s[v_at, :].astype(BF)
        scores = tn(keys, queries) * scale + bias_ref[head]
        here = pl.ds(pl.multiple_of(head * HEAD_DIM, 8), HEAD_DIM)

        def attend(scores):
            top = jnp.max(scores, axis=0, keepdims=True)
            weights = jnp.exp2(scores - top)
            total = jnp.sum(weights, axis=0, keepdims=True)
            probs = (weights * (1.0 / total)).astype(BF)
            return nn(values, probs), top + jnp.log2(total)

        att_s[here, :], lse_ref[0, pl.ds(head, 1), :] = attend(scores)
        attk_s[here, :], lse_ref[0, pl.ds(heads + head, 1), :] = attend(scores + mask)
        return carry

    lax.fori_loop(0, heads, one_head, 0, unroll=2)
    att = att_s[...].astype(BF)
    att_kept = attk_s[...].astype(BF)
    att_ref[:, :PATCHES] = att
    att_ref[:, PATCHES:] = att_kept
    out_w = out_w_ref[...]
    kept_att = nt(pick, att_kept).astype(BF)
    for rows, source, residual in (
        (slice(0, PATCHES), att.T, tok),
        (slice(PATCHES, PATCHES + pick.shape[0]), kept_att, nn(pick, tok_ref[...])),
    ):
        branch = nn(source, out_w)
        branch_ref[rows, :] = branch.astype(BF)
        middle = residual + gate_one * branch
        middle_ref[rows, :] = middle
        second_ref[rows, :] = (normalize(middle)[0] * (1.0 + scale_two) + shift_two).astype(BF)


def forward(tokens, mod, pick, weight_t, out_w, bias, per_block):
    images, padded = pick.shape[0], pick.shape[1]
    width = tokens.shape[1]
    rows = PATCHES + padded
    heads = bias.shape[0]
    proj = weight_t.shape[0]
    return pl.pallas_call(
        functools.partial(forward_kernel, per_block),
        grid=(images,),
        in_specs=[
            pl.BlockSpec((PATCHES, width), lambda i: (i, 0)),
            pl.BlockSpec((1, 8, width), lambda i: (i, 0, 0)),
            pl.BlockSpec((1, padded, PATCHES), lambda i: (i, 0, 0)),
            const_spec(weight_t.shape),
            const_spec(out_w.shape),
            const_spec(bias.shape),
        ],
        out_specs=[
            pl.BlockSpec((PATCHES, width), lambda i: (i, 0)),
            pl.BlockSpec((proj, PATCHES), lambda i: (0, i)),
            pl.BlockSpec((width, 2 * PATCHES), lambda i: (0, i)),
            pl.BlockSpec((1, 2 * heads, PATCHES), lambda i: (i, 0, 0)),
            pl.BlockSpec((rows, width), lambda i: (i, 0)),
            pl.BlockSpec((rows, width), lambda i: (i, 0)),
            pl.BlockSpec((rows, width), lambda i: (i, 0)),
        ],
        out_shape=[
            jax.ShapeDtypeStruct((images * PATCHES, width), BF),
            jax.ShapeDtypeStruct((proj, images * PATCHES), BF),
            jax.ShapeDtypeStruct((width, images * 2 * PATCHES), BF),
            jax.ShapeDtypeStruct((images, 2 * heads, PATCHES), F32),
            jax.ShapeDtypeStruct((images * rows, width), F32),
            jax.ShapeDtypeStruct((images * rows, width), BF),
            jax.ShapeDtypeStruct((images * rows, width), BF),
        ],
        scratch_shapes=[
            pltpu.VMEM((proj, PATCHES), F32),
            pltpu.VMEM((width, PATCHES), F32),
            pltpu.VMEM((width, PATCHES), F32),
        ],
        compiler_params=params(),
        cost_estimate=cost(images * 1.3e10, images * 8e6, images * heads * PATCHES * PATCHES * 2),
    )(tokens, mod, pick, weight_t, out_w, bias)


def gelu_pair(pre):
    root = math.sqrt(2.0 / math.pi)
    square = pre * pre
    bend = jnp.tanh(pre * (root + (root * 0.044715) * square))
    half = 0.5 + 0.5 * bend
    slope = half + (0.5 * pre) * (1.0 - bend * bend) * (root + (3.0 * root * 0.044715) * square)
    return pre * half, slope


def mlp_kernel(
    chunk, fresh, second_ref, dmlp_ref, up_ref, down_ref, *refs
):
    if fresh:
        branch_ref, dsecond_ref, grads_ref, second_t, dmlp_t, hidden_s, dpre_s, sem = refs
    else:
        branch_in, dsecond_in, branch_ref, dsecond_ref, grads_ref = refs[:5]
        second_t, dmlp_t, hidden_s, dpre_s, sem = refs[5:]
    rows = second_ref.shape[0]
    tile = up_ref.shape[1]
    width = second_ref.shape[1]

    @pl.when(pl.program_id(0) == 0)
    def _():
        if fresh:
            branch_ref[...] = jnp.zeros_like(branch_ref)
            dsecond_ref[...] = jnp.zeros_like(dsecond_ref)
        else:
            one = pltpu.make_async_copy(branch_in, branch_ref, sem.at[0])
            two = pltpu.make_async_copy(dsecond_in, dsecond_ref, sem.at[1])
            one.start()
            two.start()
        for at in range(0, rows, chunk):
            second_t[:, at : at + chunk] = second_ref[at : at + chunk, :].T
            dmlp_t[:, at : at + chunk] = dmlp_ref[at : at + chunk, :].T
        if not fresh:
            one.wait()
            two.wait()

    def one_chunk(index, carry):
        at = pl.ds(pl.multiple_of(index * chunk, chunk), chunk)
        pre = nn(second_ref[at, :], up_ref[...])
        dhidden = nt(dmlp_ref[at, :], down_ref[...])
        value, slope = gelu_pair(pre)
        hidden = value.astype(BF)
        dpre = (dhidden * slope).astype(BF)
        hidden_s[at, :] = hidden
        dpre_s[at, :] = dpre
        branch_ref[at, :] += nn(hidden, down_ref[...])
        dsecond_ref[at, :] += nt(dpre, up_ref[...])
        return carry

    lax.fori_loop(0, rows // chunk, one_chunk, 0)
    part = width // 3
    for c in range(3):
        at = slice(c * part, (c + 1) * part)
        grads_ref[at, :tile] = nn(second_t[at, :], dpre_s[...]).astype(BF)
        grads_ref[at, tile:] = nn(dmlp_t[at, :], hidden_s[...]).astype(BF)


def mlp_chunk(rows):
    for chunk in (896, 448, 64):
        if rows % chunk == 0:
            return chunk
    return rows


def mlp(second, dmlp, up, down, sums=None):
    rows, width = second.shape
    hidden = up.shape[1]
    tile = 768 if hidden % 768 == 0 else hidden
    fresh = sums is None
    chunk = mlp_chunk(rows)
    in_specs = [
        const_spec(second.shape),
        const_spec(second.shape),
        pl.BlockSpec((width, tile), lambda f: (0, f)),
        pl.BlockSpec((tile, width), lambda f: (f, 0)),
    ]
    operands = [second, dmlp, up, down]
    if not fresh:
        in_specs += [pl.BlockSpec(memory_space=pl.ANY)] * 2
        operands += list(sums)
    return pl.pallas_call(
        functools.partial(mlp_kernel, chunk, fresh),
        grid=(hidden // tile,),
        in_specs=in_specs,
        out_specs=[
            const_spec(second.shape),
            const_spec(second.shape),
            pl.BlockSpec((width, 2 * tile), lambda f: (0, f)),
        ],
        out_shape=[
            jax.ShapeDtypeStruct(second.shape, F32),
            jax.ShapeDtypeStruct(second.shape, F32),
            jax.ShapeDtypeStruct((width, 2 * hidden), BF),
        ],
        scratch_shapes=[
            pltpu.VMEM((width, rows), BF),
            pltpu.VMEM((width, rows), BF),
            pltpu.VMEM((rows, tile), BF),
            pltpu.VMEM((rows, tile), BF),
            pltpu.SemaphoreType.DMA((2,)),
        ],
        compiler_params=params(),
        cost_estimate=cost(12 * rows * width * hidden * 1.7, 30e6, rows * hidden),
    )(*operands), tile


def split_mlp_grads(grads, tile):
    parts = grads.reshape(grads.shape[0], -1, 2, tile)
    return (
        parts[:, :, 0].reshape(grads.shape[0], -1),
        parts[:, :, 1].reshape(grads.shape[0], -1),
    )


def backward_kernel(
    per_block, tok_ref, mod_ref, pick_ref, weight_ref, out_w_ref, bias_ref,
    qkv_ref, lse_ref, middle_ref, branch_ref, mlp_ref, dsecond_ref, grad_ref,
    out_ref, dtok_ref, dmod_ref, dattn_ref, dqkv_ref, strips_ref,
    qkv_s, datt_s, dattk_s, dscores_s,
):
    heads = bias_ref.shape[0]
    step = pl.program_id(0)
    shift_one, scale_one, gate_one = mod_ref[0, 0:1], mod_ref[0, 1:2], mod_ref[0, 2:3]
    scale_two, gate_two = mod_ref[0, 4:5], mod_ref[0, 5:6]
    pick = pick_ref[0]
    dmiddles = []
    sums = [0.0, 0.0, 0.0, 0.0]
    for rows in (slice(0, PATCHES), slice(PATCHES, PATCHES + pick.shape[0])):
        middle = middle_ref[rows, :]
        branch_mlp = mlp_ref[rows, :]
        dsecond = dsecond_ref[rows, :]
        grad = grad_ref[rows, :].astype(F32)
        out_ref[rows, :] = (middle + gate_two * branch_mlp).astype(BF)
        normed, inverse = normalize(middle)
        dmiddle = grad + norm_back(normed, inverse, dsecond * (1.0 + scale_two))
        branch = branch_ref[rows, :].astype(F32)
        for c, term in enumerate(
            (dmiddle * branch, dsecond, dsecond * normed, grad * branch_mlp)
        ):
            sums[c] = sums[c] + jnp.sum(term, axis=0, keepdims=True)
        dmiddles.append(dmiddle)
    for c in range(4):
        dmod_ref[0, 2 + c : 3 + c, :] = sums[c]
    dattn = (gate_one * dmiddles[0]).astype(BF)
    dattn_kept = tn(pick, (gate_one * dmiddles[1]).astype(BF)).astype(BF)
    dattn_ref[:PATCHES, :] = dattn
    dattn_ref[PATCHES:, :] = dattn_kept
    high = dmiddles[1].astype(BF)
    low = (dmiddles[1] - high.astype(F32)).astype(BF)
    dresid = dmiddles[0] + tn(pick, high) + tn(pick, low)
    datt_s[...] = nt(out_w_ref[...], dattn)
    dattk_s[...] = nt(out_w_ref[...], dattn_kept)
    qkv_s[...] = qkv_ref[...].astype(F32)
    mask = key_mask(pick)
    scale = HEAD_DIM ** (-0.5)

    @pl.when(step == 0)
    def _():
        dscores_s[...] = jnp.zeros_like(dscores_s)

    def one_head(head, carry):
        q_at, k_at, v_at = head_rows(head, per_block)
        queries = qkv_s[q_at, :].astype(BF)
        keys = qkv_s[k_at, :].astype(BF)
        values = qkv_s[v_at, :].astype(BF)
        here = pl.ds(pl.multiple_of(head * HEAD_DIM, 8), HEAD_DIM)
        scores = tn(keys, queries) * (scale * LOG2E) + bias_ref[head]

        def pull(scores, top, upstream):
            probs = jnp.exp2(scores - top)
            dprobs = tn(values, upstream)
            dvalues = nt(upstream, probs.astype(BF))
            weighted = jnp.sum(probs * dprobs, axis=0, keepdims=True)
            return probs * (dprobs - weighted), dvalues

        dscores, dvalues = pull(
            scores, lse_ref[0, pl.ds(head, 1), :], datt_s[here, :].astype(BF)
        )
        dscores_kept, dvalues_kept = pull(
            scores + mask, lse_ref[0, pl.ds(heads + head, 1), :], dattk_s[here, :].astype(BF)
        )
        dscores = dscores + dscores_kept
        dscores_s[head] += dscores
        rounded = dscores.astype(BF)
        qkv_s[q_at, :] = nn(keys, rounded) * scale
        qkv_s[k_at, :] = nt(queries, rounded) * scale
        qkv_s[v_at, :] = dvalues + dvalues_kept
        return carry

    lax.fori_loop(0, heads, one_head, 0, unroll=2)
    dqkv = qkv_s[...].astype(BF)
    dqkv_ref[...] = dqkv
    dfirst = tn(dqkv, weight_ref[...])
    normed, inverse = normalize(tok_ref[...].astype(F32))
    dmod_ref[0, 0:1, :] = jnp.sum(dfirst, axis=0, keepdims=True)
    dmod_ref[0, 1:2, :] = jnp.sum(dfirst * normed, axis=0, keepdims=True)
    dmod_ref[0, 6:8, :] = jnp.zeros((2, dfirst.shape[1]), F32)
    dtok_ref[...] = (dresid + norm_back(normed, inverse, dfirst * (1.0 + scale_one))).astype(BF)

    @pl.when(step == pl.num_programs(0) - 1)
    def _():
        def fold(head, carry):
            strip = jnp.zeros((GRID, 512), F32)
            for key_row in range(GRID):
                start = (GRID - 1 - key_row) * GRID
                block = dscores_s[head, key_row * GRID : (key_row + 1) * GRID, :]
                block = jnp.concatenate([block, jnp.zeros((GRID, 512 - PATCHES), F32)], axis=1)
                strip = strip + pltpu.roll(block, start, 1)
            strips_ref[head] = strip
            return carry

        lax.fori_loop(0, heads, fold, 0)


def backward(
    tokens, mod, pick, weight_t, out_w, bias, qkv, lse, middle, branch, branch_mlp, dsecond,
    grads, per_block,
):
    images, padded = pick.shape[0], pick.shape[1]
    width = tokens.shape[1]
    rows = PATCHES + padded
    heads = bias.shape[0]
    proj = weight_t.shape[0]
    by_row = pl.BlockSpec((rows, width), lambda i: (i, 0))
    one_row = pl.BlockSpec((rows, width), lambda i: (i, 0), pipeline_mode=pl.Buffered(1))
    return pl.pallas_call(
        functools.partial(backward_kernel, per_block),
        grid=(images,),
        in_specs=[
            pl.BlockSpec((PATCHES, width), lambda i: (i, 0)),
            pl.BlockSpec((1, 8, width), lambda i: (i, 0, 0)),
            pl.BlockSpec((1, padded, PATCHES), lambda i: (i, 0, 0)),
            const_spec(weight_t.shape),
            const_spec(out_w.shape),
            const_spec(bias.shape),
            pl.BlockSpec((proj, PATCHES), lambda i: (0, i)),
            pl.BlockSpec((1, 2 * heads, PATCHES), lambda i: (i, 0, 0)),
            by_row,
            by_row,
            by_row,
            by_row,
            by_row,
        ],
        out_specs=[
            by_row,
            pl.BlockSpec((PATCHES, width), lambda i: (i, 0)),
            pl.BlockSpec((1, 8, width), lambda i: (i, 0, 0)),
            pl.BlockSpec((2 * PATCHES, width), lambda i: (i, 0)),
            pl.BlockSpec((proj, PATCHES), lambda i: (0, i)),
            const_spec((heads, GRID, 512)),
        ],
        out_shape=[
            jax.ShapeDtypeStruct((images * rows, width), BF),
            jax.ShapeDtypeStruct((images * PATCHES, width), BF),
            jax.ShapeDtypeStruct((images, 8, width), F32),
            jax.ShapeDtypeStruct((images * 2 * PATCHES, width), BF),
            jax.ShapeDtypeStruct((proj, images * PATCHES), BF),
            jax.ShapeDtypeStruct((heads, GRID, 512), F32),
        ],
        scratch_shapes=[
            pltpu.VMEM((proj, PATCHES), F32),
            pltpu.VMEM((width, PATCHES), F32),
            pltpu.VMEM((width, PATCHES), F32),
            pltpu.VMEM((heads, PATCHES, PATCHES), F32),
        ],
        compiler_params=params(),
        cost_estimate=cost(images * 2.2e10, images * 1e7, images * heads * PATCHES * PATCHES * 2),
    )(
        tokens, mod, pick, weight_t, out_w, bias, qkv, lse, middle, branch, branch_mlp,
        dsecond, grads,
    )


def shift_mp(value, steps):
    ways = lax.axis_size("mp")
    return lax.ppermute(value, "mp", [(i, (i - steps) % ways) for i in range(ways)])


def from_others(block):
    ways, places = lax.axis_size("mp"), lax.axis_size("dp")
    half = block.shape[0] // 2
    core = lax.axis_index("dp") % 2
    mine = lax.dynamic_slice_in_dim(block, core * half, half, 0)
    got = []
    for steps in range(1, ways):
        near = shift_mp(mine, steps)
        far = lax.ppermute(near, "dp", [(i, i ^ 1) for i in range(places)])
        whole = jnp.zeros_like(block)
        whole = lax.dynamic_update_slice_in_dim(whole, near, core * half, 0)
        whole = lax.dynamic_update_slice_in_dim(whole, far, (1 - core) * half, 0)
        got.append(whole)
    return got


def home(parts):
    total = parts[0].astype(F32)
    for steps in range(1, len(parts)):
        total = total + shift_mp(parts[steps], -steps).astype(F32)
    return total


def scatter_dp(part):
    return lax.psum_scatter(part, "dp", scatter_dimension=0, tiled=True)


def local(
    tokens, conditioning, kept_ids, ada_weight, ada_bias, attn_qkv, attn_out, mlp_up, mlp_down,
    rel_table, grad_out_kept, grad_out_full,
):
    ways = lax.axis_size("mp")
    place = lax.axis_index("mp")
    images_group = conditioning.shape[0]
    images = images_group // ways
    width = tokens.shape[1]
    keep = kept_ids.shape[1]
    padded = -(-keep // 64) * 64
    per_block = rel_table.shape[0]
    cols = ada_bias.shape[0]

    silu_cond = jax.nn.silu(conditioning.astype(F32)).astype(BF)
    columns = (jnp.dot(silu_cond, ada_weight, preferred_element_type=F32) + ada_bias).astype(BF)
    mod = lax.all_to_all(columns, "mp", split_axis=0, concat_axis=1, tiled=True)
    mod = jnp.pad(mod.astype(F32).reshape(images, 6, width), ((0, 0), (0, 2), (0, 0)))

    weight_own = jnp.transpose(attn_qkv.reshape(width, -1))
    weight_t = jnp.concatenate([weight_own] + from_others(weight_own), axis=0)
    out_w = jnp.concatenate([attn_out] + from_others(attn_out), axis=0)
    table = jnp.concatenate(
        [rel_table] + [shift_mp(rel_table, s) for s in range(1, ways)], axis=0
    )
    bias = bias_whole(table)
    weight_t, out_w, late_up, late_down = lax.optimization_barrier(
        (weight_t, out_w, mlp_up, mlp_down)
    )
    up_others = from_others(late_up)
    down_others = from_others(late_down)

    own_kept = lax.dynamic_slice_in_dim(kept_ids, place * images, images, 0)
    own_kept = jnp.pad(own_kept, ((0, 0), (0, padded - keep)), constant_values=-1)
    pick = (own_kept[:, :, None] == jnp.arange(PATCHES, dtype=jnp.int32)).astype(BF)
    grads = jnp.concatenate(
        [
            grad_out_full.reshape(images, PATCHES, width),
            jnp.pad(
                grad_out_kept.reshape(images, keep, width), ((0, 0), (0, padded - keep), (0, 0))
            ),
        ],
        axis=1,
    )
    dmlp = (mod[:, 5:6] * grads.astype(F32)).astype(BF).reshape(-1, width)
    grads = grads.reshape(-1, width)

    first, qkv, att, lse, middle, second, branch = forward(
        tokens, mod, pick, weight_t, out_w, bias, per_block
    )
    (branch_mlp, dsecond, grads_own), tile_own = mlp(second, dmlp, mlp_up, mlp_down)
    reduced = [scatter_dp(grads_own)]
    for up, down in zip(up_others, down_others):
        (branch_mlp, dsecond, grads_next), _ = mlp(
            second, dmlp, up, down, (branch_mlp, dsecond)
        )
        reduced.append(scatter_dp(grads_next))
    out, dtok, dmod, dattn, dqkv, strips = backward(
        tokens, mod, pick, weight_t, out_w, bias, qkv, lse, middle, branch, branch_mlp, dsecond,
        grads, per_block,
    )
    dweight = dot(first, dqkv, (0, 1)).astype(BF)
    dout_t = dot(dattn, att, (0, 1)).astype(BF)
    proj_block, out_block = weight_own.shape[0], attn_out.shape[0]
    dweight, dout_t, *reduced = lax.optimization_barrier((dweight, dout_t, *reduced))
    attn_sums = scatter_dp(jnp.concatenate([dweight, dout_t], axis=1))
    split = ways * proj_block
    attn_parts = [
        jnp.concatenate(
            [
                attn_sums[:, j * proj_block : (j + 1) * proj_block],
                attn_sums[:, split + j * out_block : split + (j + 1) * out_block],
            ],
            axis=1,
        )
        for j in range(ways)
    ]
    mlp_grads = home(reduced)
    attn_grads = home(attn_parts)
    grad_up, grad_down_t = split_mlp_grads(mlp_grads, tile_own)
    grad_qkv = attn_grads[:, :proj_block].reshape(-1, 3, proj_block // 3)
    grad_out = jnp.transpose(attn_grads[:, proj_block:])

    dmod_rows = dmod[:, :6].reshape(images, 6 * width)
    dcolumns = lax.all_to_all(dmod_rows, "mp", split_axis=1, concat_axis=0, tiled=True)
    dtable = home(list(jnp.split(table_of_strips(strips), ways, axis=0)))
    flat = jnp.concatenate([dcolumns.reshape(-1), dtable.reshape(-1)])
    count = flat.shape[0]
    packed = jnp.pad(flat, (0, -count % 1024)).reshape(-1, 128)
    every = lax.all_gather(packed, "dp", axis=0, tiled=True)
    every = every.reshape(lax.axis_size("dp"), -1)[:, :count]
    all_columns = every[:, : images_group * cols].reshape(-1, cols)
    dtable = jnp.sum(every[:, images_group * cols :], axis=0).reshape(rel_table.shape)
    all_cond = lax.all_gather(silu_cond, "dp", axis=0, tiled=True)
    slice_width = width // lax.axis_size("dp")
    cond_slice = lax.dynamic_slice_in_dim(
        all_cond, lax.axis_index("dp") * slice_width, slice_width, 1
    )
    grad_ada_weight = lax.dot_general(
        cond_slice.astype(F32), all_columns, (((0,), (0,)), ((), ())), precision=PRECISE
    )
    grad_ada_bias = jnp.sum(all_columns, axis=0)
    silu_part = lax.dot_general(
        dcolumns, ada_weight.astype(F32), (((1,), (1,)), ((), ())), precision=PRECISE
    )
    shares = lax.all_to_all(
        silu_part.astype(BF).reshape(ways, images, width), "mp", split_axis=0, concat_axis=0,
        tiled=True,
    )
    grad_silu = jnp.sum(shares.astype(F32), axis=0)
    own_cond = lax.dynamic_slice_in_dim(conditioning, place * images, images, 0).astype(F32)
    grad_cond = jax.vjp(jax.nn.silu, own_cond)[1](grad_silu)[0].astype(BF)

    out = out.reshape(images, PATCHES + padded, width)
    out_full = out[:, :PATCHES].reshape(-1, width)
    out_kept = out[:, PATCHES : PATCHES + keep].reshape(-1, width)
    return (
        out_kept, out_full, dtok, grad_cond, grad_ada_weight, grad_ada_bias, grad_qkv, grad_out,
        grad_up, jnp.transpose(grad_down_t), dtable,
    )


def solution(mesh):
    both = P(("dp", "mp"), None)
    return jax.shard_map(
        local,
        mesh=mesh,
        in_specs=(
            both, P("dp", None), P("dp", None), P(None, "mp"), P("mp"), P(None, None, "mp"),
            P("mp", None), P(None, "mp"), P("mp", None), P("mp", None), both, both,
        ),
        out_specs=(
            both, both, both, both, P("dp", "mp"), P("mp"), P("dp", None, "mp"), P("mp", "dp"),
            P("dp", "mp"), P("mp", "dp"), P("mp", None),
        ),
        check_vma=False,
    )
```

time: 3870 us -> 796 us (0.21)
  other arithmetic: 1890 us -> 33.2 us
  local copies, waits for them, and re-layouts: 1140 us -> 94.2 us
  matrix products: 445 us -> 39.3 us
  Pallas kernels: 0 us -> 311 us
  blocking collectives: 266 us -> 23.6 us
  waiting for transfers between devices: 75.6 us -> 252 us
    scatter-add x2 -> x0, other arithmetic: 1710 us -> none  [the longest x1 1360 us: local(): jax.ops.segment_sum(kept_scores, kept_index.reshape(-1), num_segments=BUC...]
    gather x6 -> x0, local copies, waits for them, and re-layouts: 800 us -> none  [the longest x4 565 us: local(): jnp.take(table_whole, kept_index, axis=1)]
    dot_general x41 -> x5, matrix products: 445 us -> 39.3 us  [the longest x2 24.3 us: dot(): lax.dot_general(a, b, ((dims[0:1], dims[1:2]), ((), ())), preferred_eleme...]
    pallas_call x0 -> x5, Pallas kernels: none -> 311 us  [the longest x2 164 us: mlp(): pl.pallas_call(functools.partial(mlp_kernel, chunk, fresh), grid=(hidden...]
    unnamed x4 -> x0, blocking collectives: 195 us -> none
    ppermute x0 -> x12, waiting for transfers between devices: none -> 143 us  [the longest x8 143 us: shift_mp(): lax.ppermute(value, 'mp', [(i, (i - steps) % ways) for i in range(ways)])]
    unnamed x270 -> x28, local copies, waits for them, and re-layouts: 128 us -> 4.98 us
    reshape x10 -> x11, local copies, waits for them, and re-layouts: 120 us -> 14.1 us  [the longest x1 3.96 us: table_of_strips(): parts = strips[:, :, :SPAN * GRID].reshape(heads, GRID, SPAN, GRID)]
  transfers between devices with their start and end apart: 22 -> 19, of which waited for: 3 -> 7; matrix products, arithmetic and copies ran while one was open for 92% -> 19% of each run, Pallas kernels for 0% -> 22%
where the time goes in v1:
time: 796 us; the launch traced here: 791 us
  Pallas kernels  311 us (39%)
  waiting for transfers between devices  252 us (32%)
  local copies, waits for them, and re-layouts  94.2 us (12%)
  matrix products  39.3 us (5%)
  other arithmetic  33.2 us (4%)
  starting transfers between devices  23.7 us (3%)
  blocking collectives  23.6 us (3%)
  between operations  14.5 us (2%)
    pallas_call x2, Pallas kernels, mlp(): pl.pallas_call(functools.partial(mlp_kernel, chunk, fresh), grid=(hidden...  164 us
    ppermute x8, waiting for transfers between devices, shift_mp(): lax.ppermute(value, 'mp', [(i, (i - steps) % ways) for i in range(ways)])  143 us
    reduce_scatter x3, waiting for transfers between devices, scatter_dp(): return lax.psum_scatter(part, 'dp', scatter_dimension=0, tiled=True)  94.8 us
    pallas_call x1, Pallas kernels, backward(): pl.pallas_call(functools.partial(backward_kernel, per_block), grid=(image...  86.8 us
    pallas_call x1, Pallas kernels, forward(): pl.pallas_call(functools.partial(forward_kernel, per_block), grid=(images...  50.9 us
    dot_general x2, matrix products, dot(): lax.dot_general(a, b, ((dims[0:1], dims[1:2]), ((), ())), preferred_eleme...  24.3 us
    all_gather x1, blocking collectives, local(): all_cond = lax.all_gather(silu_cond, 'dp', axis=0, tiled=True)  23.6 us
    another operation x17, local copies, waits for them, and re-layouts, bias_whole(): jnp.stack([grid_table[:, :, GRID - 1 - c:2 * GRID - 1 - c] for c in range...  17.7 us
  transfers between devices with their start and end apart: 19, of which 7 were waited for; matrix products, arithmetic and copies ran while one was open for 19% of the time, Pallas kernels for 22%

profile of v1, /device:TPU:0, one launch (start us, length us, event | category | flops | bytes accessed | tf_op | source)
XLA Modules:
  0.0 791.4 jit_solution(6662697696789050777)
XLA Ops:
  7.3 3.1 dynamic-slice_bitcast_fusion
  10.3 2.9 collective-permute-start
  14.2 2.0 collective-permute-start.4
  16.2 4.4 fusion.2
  21.3 3.3 all-to-all-start
  24.6 1.9 reshape.130
  26.5 3.4 fusion.3
  30.8 26.9 %collective-permute-done = bf16[864,1152]{1,0:T(8,128)(2,1)} collective-permute-done((bf16[864,1152]{1,0:T(8,128)(2,1)}, bf16[864,1152]{1,0:T(8,128)(2,1)}, u32[]{:S(2)}, u32[]{:S(2)}) %collective-permute-start) | collective-permute-done | bytes 1990688 | tf_op jit(solution)/shard_map/ppermute | solution.py:496
  57.8 14.6 %all-to-all-done = bf16[2,4,3456]{2,1,0:T(4,128)(2,1)S(1)} async-done(((bf16[2,4,3456]{2,1,0:T(4,128)(2,1)}), bf16[2,4,3456]{2,1,0:T(4,128)(2,1)S(1)}, u32[]{:S(2)}, u32[]{:S(2)}) %all-to-all-start) | async-done | bytes 55328 | tf_op jit(solution)/shard_map/all_to_all | solution.py:542
  73.2 4.9 fusion.dmlp_ref
  78.5 2.5 fusion.23
  84.3 1.7 stack.71
  86.0 1.7 stack.72
  87.7 1.7 stack.73
  89.4 1.7 stack.74
  91.2 1.7 stack.75
  92.9 1.7 stack.76
  96.3 2.3 stack.67
  99.5 9.6 %shard_map.203.bias_ref = f32[16,256,256]{2,1,0:T(8,128)} custom-call(f32[16,16,512]{2,1,0:T(8,128)} %pad.86.strip_ref), custom_call_target="tpu_custom_call" | custom-call | bytes 4194304 | tf_op jit(solution)/shard_map/pallas_call | solution.py:84
  111.6 1.7 pad_maximum_fusion.2.out_w_ref
  113.3 2.2 broadcast_in_dim.15
  115.5 3.0 constant_dynamic-update-slice_fusion.7
  118.5 3.0 constant_dynamic-update-slice_fusion.6
  121.5 7.0 pad_maximum_fusion.1.weight_ref
  128.5 50.9 %shard_map.204 = (bf16[1024,1152]{1,0:T(8,128)(2,1)}, bf16[3456,1024]{1,0:T(8,128)(2,1)}, bf16[1152,2048]{1,0:T(8,128)(2,1)}, f32[4,32,256]{2,1,0:T(8,128)}, f32...) custom-call(bf16[1024,1152]{1,0:T(8,128)(2,1)} %tok_ref.3, f32[4,8,1152]{2,1,0:T(8,128)} %pad.84.mod_ref, ...), custom_call_target="tpu_custom_call" | custom-call | flops 51999997952 | bytes 32000000 | tf_op jit(solution)/shard_map/pallas_call | solution.py:180
  179.5 85.3 %shard_map.205 = (f32[1792,1152]{1,0:T(8,128)}, f32[1792,1152]{1,0:T(8,128)}, bf16[1152,4608]{1,0:T(8,128)(2,1)}) custom-call(bf16[1792,1152]{1,0:T(8,128)(2,1)} %get-tuple-element.44.second_ref, bf16[1792,1152]{1,0:T(8,128)(2,1)} %fusion.dmlp_ref, bf16[1152,2304]{1,0:T(8,128)(2,1)} %up_ref.1, bf16[2304,1152]{1,0:T(8,128)(2,1)} %down_ref.1), custom_call_target="tpu_custom_call" | custom-call | flops 97029349376 | bytes 30000000 | tf_op jit(solution)/shard_map/pallas_call | solution.py:301
  264.9 2.1 constant_dynamic-slice_fusion.1
  266.9 1.8 collective-permute-start.5
  269.0 1.2 collective-permute-start.7
  270.2 57.3 %collective-permute-done.5 = bf16[576,2304]{1,0:T(8,128)(2,1)} collective-permute-done((bf16[576,2304]{1,0:T(8,128)(2,1)S(1)}, bf16[576,2304]{1,0:T(8,128)(2,1)}, u32[]{:S(2)}, u32[]{:S(2)}) %collective-permute-start.5) | collective-permute-done | bytes 2654240 | tf_op jit(solution)/shard_map/ppermute | solution.py:496
  327.5 56.4 %collective-permute-done.7 = bf16[1152,1152]{1,0:T(8,128)(2,1)S(1)} collective-permute-done((bf16[1152,1152]{1,0:T(8,128)(2,1)S(1)}, bf16[1152,1152]{1,0:T(8,128)(2,1)S(1)}, u32[]{:S(2)}, u32[]{:S(2)}) %collective-permute-start.7) | collective-permute-done | bytes 2654240 | tf_op jit(solution)/shard_map/ppermute | solution.py:496
  383.9 2.8 broadcast_in_dim.17
  386.6 3.6 constant_dynamic-update-slice_fusion.3
  390.2 2.7 broadcast_in_dim.18
  392.9 1.7 constant_dynamic-update-slice_fusion.1
  394.6 3.4 constant_dynamic-update-slice_fusion.2.up_ref
  398.1 3.5 constant_dynamic-update-slice_fusion.down_ref
  401.5 78.2 %shard_map.206 = (f32[1792,1152]{1,0:T(8,128)}, f32[1792,1152]{1,0:T(8,128)}, bf16[1152,4608]{1,0:T(8,128)(2,1)}) custom-call(bf16[1792,1152]{1,0:T(8,128)(2,1)} %get-tuple-element.44.second_ref, bf16[1792,1152]{1,0:T(8,128)(2,1)} %fusion.dmlp_ref, bf16[1152,2304]{1,0:T(8,128)(2,1)} %constant_dynamic-update-slice_fusion.2.up_ref, ...), custom_call_target="tpu_custom_call" | custom-call | flops 97029349376 | bytes 30000000 | tf_op jit(solution)/shard_map/pallas_call | solution.py:301
  479.8 86.8 %shard_map.207 = (bf16[1792,1152]{1,0:T(8,128)(2,1)}, bf16[1024,1152]{1,0:T(8,128)(2,1)}, f32[4,8,1152]{2,1,0:T(8,128)}, bf16[2048,1152]{1,0:T(8,128)(2,1)}, bf1...) custom-call(bf16[1024,1152]{1,0:T(8,128)(2,1)} %tok_ref.3, f32[4,8,1152]{2,1,0:T(8,128)} %pad.84.mod_ref, ...), custom_call_target="tpu_custom_call" | custom-call | flops 88000004096 | bytes 40000000 | tf_op jit(solution)/shard_map/pallas_call | solution.py:446
  566.6 4.0 reshape.136
  571.3 3.4 all-to-all-start.1
  574.7 2.9 slice_bitcast_fusion.15
  578.8 2.1 collective-permute-start.9
  581.0 1.9 collective-permute-done.9
  584.0 10.3 %convolution_convert_fusion.1 = bf16[1152,1152]{1,0:T(8,128)(2,1)S(1)} fusion(bf16[2048,1152]{1,0:T(8,128)(2,1)} %get-tuple-element.57, bf16[1152,2048]{1,0:T(8,128)(2,1)} %get-tuple-element.58), kind=kOutput, calls=%fused_computation.7 | convolution fusion | flops 5437145088 | bytes 12091392 | tf_op jit(solution)/shard_map/dot_general | solution.py:25
  594.4 13.9 %convolution_convert_fusion = bf16[1152,3456]{1,0:T(8,128)(2,1)} fusion(bf16[1024,1152]{1,0:T(8,128)(2,1)S(1)} %copy-done.11, bf16[3456,1024]{1,0:T(8,128)(2,1)} %get-tuple-element.56), kind=kOutput, calls=%fused_computation | convolution fusion | flops 8157708288 | bytes 17399808 | tf_op jit(solution)/shard_map/dot_general | solution.py:25
  608.3 8.7 %pad_maximum_fusion = bf16[1152,4608]{1,0:T(8,128)(2,1)} fusion(bf16[1152,1152]{1,0:T(8,128)(2,1)S(1)} %convolution_convert_fusion.1, bf16[1152,3456]{1,0:T(8,128)(2,1)} %convolution_convert_fusion), kind=kLoop, calls=%fused_computation.1 | loop fusion | flops 21233664 | bytes 21233664 | tf_op jit(solution)/shard_map/concatenate | solution.py:591
  617.8 8.8 %convolution_convert_fusion.2 = bf16[8,1152]{1,0:T(8,128)(2,1)S(1)} fusion(f32[8,3456]{1,0:T(8,128)S(1)} %all_to_all.32, bf16[1152,3456]{1,0:T(8,128)(2,1)} %param.15), kind=kOutput, calls=%fused_computation.12 | convolution fusion | flops 382215168 | bytes 8091648 | tf_op jit(solution)/shard_map/dot_general | solution.py:628
  627.3 3.2 all-to-all-start.2
  630.5 23.6 %all_gather.6 = bf16[128,1152]{1,0:T(8,128)(2,1)S(1)} all-gather(bf16[8,1152]{1,0:T(8,128)(2,1)S(1)} %fusion.9), channel_id=1, replica_groups=mesh['dp'=16,'mp'=2] {'dp'}, dimensions={0}, use_global_device_ids=true | all-gather | bytes 313344 | tf_op jit(solution)/shard_map/all_gather | solution.py:619
  654.1 2.0 slice.211
  656.1 3.6 slice.212
  659.6 1.6 reshape.132
  661.9 2.1 reshape.139
  664.0 1.5 copy-done.2
  665.5 1.3 slice.229
  666.8 2.0 reshape.140
  671.3 1.8 fusion.10
  673.1 1.9 collective-permute-start.11
  675.1 94.8 %reduce-scatter.8.cloned.1.call-done = bf16[72,4608]{1,0:T(8,128)(2,1)} async-done(((bf16[1152,4608]{1,0:T(8,128)(2,1)}), bf16[72,4608]{1,0:T(8,128)(2,1)}) %reduce-scatter.8.cloned.1.call-update) | async-done | bytes 663568 | tf_op jit(solution)/shard_map/reduce_scatter | solution.py:523
  769.9 1.2 fusion.20
  773.0 1.5 collective-permute-start.10
  774.5 1.3 convert_add_fusion
  776.6 3.9 slice_reduce_fusion
  (105 shorter events, 26.9 us)
Async XLA Ops:
  7.2 19.3 %copy-start = (s32[8,179]{1,0:T(8,128)S(1)}, s32[8,179]{1,0:T(8,128)}, u32[]{:S(2)}) copy-start(s32[8,179]{1,0:T(8,128)} %param.14) | copy-start | bytes 17188
  7.2 6.1 copy-start.3
  7.2 7.0 copy-start.9
  7.2 9.0 %copy-start.6 = (bf16[8,1152]{1,0:T(8,128)(2,1)S(1)}, bf16[8,1152]{1,0:T(8,128)(2,1)}, u32[]{:S(2)}) copy-start(bf16[8,1152]{1,0:T(8,128)(2,1)} %param.13) | copy-start | bytes 55300
  7.2 9.0 %copy-start.10 = (f32[3456]{0:T(1024)S(1)}, f32[3456]{0:T(1024)}, u32[]{:S(2)}) copy-start(f32[3456]{0:T(1024)} %param.16) | copy-start | bytes 41476
  10.3 47.4 %collective-permute-start = (bf16[864,1152]{1,0:T(8,128)(2,1)}, bf16[864,1152]{1,0:T(8,128)(2,1)}, u32[]{:S(2)}, u32[]{:S(2)}) collective-permute-start(bf16[864,1152]{1,0:T(8,128)(2,1)} %dynamic-slice_bitcast_fusion), channel_id=1, source_target_pairs={{0,1},{1,0},{2,3},{3,2},{4,5},{5,4},{6,7},{7,6},{8,9},{9,8},{10,11... | collective-permute-start | bytes 5971976 | tf_op jit(solution)/shard_map/ppermute | solution.py:496
  14.2 64.0 %collective-permute-start.2 = (bf16[288,1152]{1,0:T(8,128)(2,1)}, bf16[288,1152]{1,0:T(8,128)(2,1)}, u32[]{:S(2)}, u32[]{:S(2)}) collective-permute-start(bf16[288,1152]{1,0:T(8,128)(2,1)} %constant_dynamic-slice_fusion.2), channel_id=1, source_target_pairs={{0,1},{1,0},{2,3},{3,2},{4,5},{5,4},{6,7},{7,6},{8,9},{9,8},{10,11... | collective-permute-start | bytes 1990664 | tf_op jit(solution)/shard_map/ppermute | solution.py:496
  14.2 64.0 %collective-permute-start.4 = (f32[8,961]{1,0:T(8,128)S(1)}, f32[8,961]{1,0:T(8,128)S(1)}, u32[]{:S(2)}, u32[]{:S(2)}) collective-permute-start(f32[8,961]{1,0:T(8,128)S(1)} %copy-done.9), channel_id=1, source_target_pairs={{0,1},{1,0},{2,3},{3,2},{4,5},{5,4},{6,7},{7,6},{8,9},{9,8},{10,11... | collective-permute-start | bytes 92264 | tf_op jit(solution)/shard_map/ppermute | solution.py:496
  21.3 51.1 %all-to-all-start = ((bf16[2,4,3456]{2,1,0:T(4,128)(2,1)}), bf16[2,4,3456]{2,1,0:T(4,128)(2,1)S(1)}, u32[]{:S(2)}, u32[]{:S(2)}) async-start(bf16[2,4,3456]{2,1,0:T(4,128)(2,1)} %all_to_all.27), calls=%async_computation | async-start | bytes 110592 | tf_op jit(solution)/shard_map/all_to_all | solution.py:542
  24.6 583.8 %reduce-scatter.4.cloned.1.call-start = ((), (), s32[]{:S(2)}) async-start(), calls=%async_computation.7 | async-start | bytes 11280384 | tf_op jit(solution)/shard_map/reduce_scatter | solution.py:523
  57.8 60.7 %collective-permute-start.1 = (bf16[864,1152]{1,0:T(8,128)(2,1)}, bf16[864,1152]{1,0:T(8,128)(2,1)}, u32[]{:S(2)}, u32[]{:S(2)}) collective-permute-start(bf16[864,1152]{1,0:T(8,128)(2,1)} %collective-permute-done), channel_id=1, source_target_pairs={{0,2},{2,0},{4,6},{6,4},{8,10},{10,8},{12,14},{14,12},{16,18},{18,... | collective-permute-start | bytes 5971976 | tf_op jit(solution)/shard_map/ppermute | solution.py:507
  78.2 32.2 %collective-permute-start.3 = (bf16[288,1152]{1,0:T(8,128)(2,1)}, bf16[288,1152]{1,0:T(8,128)(2,1)}, u32[]{:S(2)}, u32[]{:S(2)}) collective-permute-start(bf16[288,1152]{1,0:T(8,128)(2,1)} %collective-permute-done.2), channel_id=1, source_target_pairs={{0,2},{2,0},{4,6},{6,4},{8,10},{10,8},{12,14},{14,12},{16,18},{18,... | collective-permute-start | bytes 1990664 | tf_op jit(solution)/shard_map/ppermute | solution.py:507
  264.8 343.5 %reduce-scatter.6.cloned.1.call-start = ((), (), s32[]{:S(2)}) async-start(), calls=%async_computation.8 | async-start | bytes 11280384 | tf_op jit(solution)/shard_map/reduce_scatter | solution.py:523
  264.9 3.9 copy-start.4
  266.9 60.5 %collective-permute-start.5 = (bf16[576,2304]{1,0:T(8,128)(2,1)S(1)}, bf16[576,2304]{1,0:T(8,128)(2,1)}, u32[]{:S(2)}, u32[]{:S(2)}) collective-permute-start(bf16[576,2304]{1,0:T(8,128)(2,1)S(1)} %constant_dynamic-slice_fusion.1), channel_id=1, source_target_pairs={{0,1},{1,0},{2,3},{3,2},{4,5},{5,4},{6,7},{7,6},{8,9},{9,8},{10,11... | collective-permute-start | bytes 7962632 | tf_op jit(solution)/shard_map/ppermute | solution.py:496
  269.0 114.9 %collective-permute-start.7 = (bf16[1152,1152]{1,0:T(8,128)(2,1)S(1)}, bf16[1152,1152]{1,0:T(8,128)(2,1)S(1)}, u32[]{:S(2)}, u32[]{:S(2)}) collective-permute-start(bf16[1152,1152]{1,0:T(8,128)(2,1)S(1)} %constant_dynamic-slice_fusion), channel_id=1, source_target_pairs={{0,1},{1,0},{2,3},{3,2},{4,5},{5,4},{6,7},{7,6},{8,9},{9,8},{10,11... | collective-permute-start | bytes 7962632 | tf_op jit(solution)/shard_map/ppermute | solution.py:496
  327.5 67.2 %collective-permute-start.6 = (bf16[576,2304]{1,0:T(8,128)(2,1)}, bf16[576,2304]{1,0:T(8,128)(2,1)}, u32[]{:S(2)}, u32[]{:S(2)}) collective-permute-start(bf16[576,2304]{1,0:T(8,128)(2,1)} %collective-permute-done.5), channel_id=1, source_target_pairs={{0,2},{2,0},{4,6},{6,4},{8,10},{10,8},{12,14},{14,12},{16,18},{18,... | collective-permute-start | bytes 7962632 | tf_op jit(solution)/shard_map/ppermute | solution.py:507
  383.9 14.2 %collective-permute-start.8 = (bf16[1152,1152]{1,0:T(8,128)(2,1)S(1)}, bf16[1152,1152]{1,0:T(8,128)(2,1)}, u32[]{:S(2)}, u32[]{:S(2)}) collective-permute-start(bf16[1152,1152]{1,0:T(8,128)(2,1)S(1)} %collective-permute-done.7), channel_id=1, source_target_pairs={{0,2},{2,0},{4,6},{6,4},{8,10},{10,8},{12,14},{14,12},{16,18},{18,... | collective-permute-start | bytes 7962632 | tf_op jit(solution)/shard_map/ppermute | solution.py:507
  566.6 4.0 copy-start.8
  571.3 11.8 %all-to-all-start.1 = ((f32[4,2,3456]{2,0,1:T(4,128)}), f32[4,2,3456]{2,0,1:T(4,128)S(1)}, u32[]{:S(2)}, u32[]{:S(2)}) async-start(f32[4,2,3456]{2,0,1:T(4,128)} %copy.126), calls=%async_computation.1 | async-start | bytes 221184 | tf_op jit(solution)/shard_map/all_to_all | solution.py:610
  574.6 87.3 %all-gather.2.cloned.1.call-start = ((), (), s32[]{:S(2)}) async-start(), calls=%async_computation.6 | async-start | bytes 2437120 | tf_op jit(solution)/shard_map/all_gather | solution.py:615
  578.8 4.1 collective-permute-start.9
  583.8 186.1 %reduce-scatter.8.cloned.1.call-start = ((), (), s32[]{:S(2)}) async-start(), calls=%async_computation.9 | async-start | bytes 11280384 | tf_op jit(solution)/shard_map/reduce_scatter | solution.py:523
  584.0 10.3 %copy-start.11 = (bf16[1024,1152]{1,0:T(8,128)(2,1)S(1)}, bf16[1024,1152]{1,0:T(8,128)(2,1)}, u32[]{:S(2)}) copy-start(bf16[1024,1152]{1,0:T(8,128)(2,1)} %get-tuple-element.55) | copy-start | bytes 7077892
  617.0 0.7 copy-start.7
  627.3 34.0 %all-to-all-start.2 = ((bf16[2,4,1152]{2,1,0:T(4,128)(2,1)}), bf16[2,4,1152]{2,1,0:T(4,128)(2,1)S(1)}, u32[]{:S(2)}, u32[]{:S(2)}) async-start(bf16[2,4,1152]{2,1,0:T(4,128)(2,1)} %reshape.134), calls=%async_computation.2 | async-start | bytes 36864 | tf_op jit(solution)/shard_map/all_to_all | solution.py:631
  664.0 1.5 copy-start.2
  668.8 105.7 %copy-start.5 = (bf16[72,4608]{1,0:T(8,128)(2,1)S(1)}, bf16[72,4608]{1,0:T(8,128)(2,1)}, u32[]{:S(2)}) copy-start(bf16[72,4608]{1,0:T(8,128)(2,1)} %reduce-scatter.4.cloned.1.call-done) | copy-start | bytes 1990660
  673.1 101.3 %collective-permute-start.11 = (bf16[72,4608]{1,0:T(8,128)(2,1)}, bf16[72,4608]{1,0:T(8,128)(2,1)}, u32[]{:S(2)}, u32[]{:S(2)}) collective-permute-start(bf16[72,4608]{1,0:T(8,128)(2,1)} %reduce-scatter.6.cloned.1.call-done), channel_id=1, source_target_pairs={{0,1},{1,0},{2,3},{3,2},{4,5},{5,4},{6,7},{7,6},{8,9},{9,8},{10,11... | collective-permute-start | bytes 1990664 | tf_op jit(solution)/shard_map/ppermute | solution.py:496
  773.0 9.6 %collective-permute-start.10 = (bf16[72,2304]{1,0:T(8,128)(2,1)}, bf16[72,2304]{1,0:T(8,128)(2,1)S(1)}, u32[]{:S(2)}, u32[]{:S(2)}) collective-permute-start(bf16[72,2304]{1,0:T(8,128)(2,1)} %pad_maximum_fusion.3), channel_id=1, source_target_pairs={{0,1},{1,0},{2,3},{3,2},{4,5},{5,4},{6,7},{7,6},{8,9},{9,8},{10,11... | collective-permute-start | bytes 995336 | tf_op jit(solution)/shard_map/ppermute | solution.py:496
  780.5 4.1 copy-start.1
Sparse Core Ops, SparseCore 0:
  264.9 121.8 reduce-scatter.3
  479.9 121.9 reduce-scatter.5
  604.6 42.4 all-gather.1
  651.0 118.8 reduce-scatter.7

commit v2 on v1

--- a/solution.py
+++ b/solution.py
@@ -212,7 +212,7 @@
             pltpu.VMEM((width, PATCHES), F32),
         ],
         compiler_params=params(),
-        cost_estimate=cost(images * 1.3e10, images * 8e6, images * heads * PATCHES * PATCHES * 2),
+        cost_estimate=cost(images * 2e9, images * 8e6),
     )(tokens, mod, pick, weight_t, out_w, bias)
 
 
@@ -320,7 +320,7 @@
             pltpu.SemaphoreType.DMA((2,)),
         ],
         compiler_params=params(),
-        cost_estimate=cost(12 * rows * width * hidden * 1.7, 30e6, rows * hidden),
+        cost_estimate=cost(6e10, 6e7) if fresh else cost(1e7, 1e5),
     )(*operands), tile
 
 
@@ -484,32 +484,281 @@
             pltpu.VMEM((heads, PATCHES, PATCHES), F32),
         ],
         compiler_params=params(),
-        cost_estimate=cost(images * 2.2e10, images * 1e7, images * heads * PATCHES * PATCHES * 2),
+        cost_estimate=cost(1e7, 1e5),
     )(
         tokens, mod, pick, weight_t, out_w, bias, qkv, lse, middle, branch, branch_mlp,
         dsecond, grads,
     )
 
 
+SUM_PLACES = 16
+HALVING = (1, 2, 8)
+FINAL = 4
+
+
+def place_bit(place, bit):
+    return (place // bit) % 2
+
+
+def unit_start(owner, share):
+    index = 0
+    for bit in HALVING + (FINAL,):
+        index = index * 2 + place_bit(owner, bit)
+    return index * share
+
+
+def store_by_owner(buffer, tile, at, block, share):
+    first_owner = at // share
+    owners = block.shape[0] // share
+    for k in range(owners):
+        owner = first_owner + k
+        if place_bit(owner, FINAL):
+            continue
+        pair = k + FINAL
+        both = jnp.concatenate(
+            [block[k * share : (k + 1) * share], block[pair * share : (pair + 1) * share]], axis=0
+        )
+        start = unit_start(owner, share)
+        buffer[tile, start : start + 2 * share, :] = both.astype(BF)
+
+
+class DpSum:
+    def __init__(self, buffer, lands, sends, recvs):
+        self.buffer, self.lands, self.sends, self.recvs = buffer, lands, sends, recvs
+        self.place = lax.axis_index("dp")
+        self.rows = buffer.shape[1]
+
+    def partner(self, bit):
+        return self.place + bit - 2 * bit * place_bit(self.place, bit)
+
+    def greet(self, barrier):
+        for bit in HALVING + (FINAL,):
+            pl.semaphore_signal(
+                barrier, inc=1, device_id={"dp": self.partner(bit)},
+                device_id_type=pl.DeviceIdType.MESH,
+            )
+
+    def spans(self, stage):
+        start, size = 0, self.rows
+        for k, bit in enumerate(HALVING):
+            size = size // 2
+            mine = place_bit(self.place, bit)
+            if k == stage:
+                return start + mine * size, start + (1 - mine) * size, size
+            start = start + mine * size
+        return start, start, size
+
+    def copy(self, stage, tile):
+        bit = (HALVING + (FINAL,))[stage]
+        _, away, size = self.spans(stage)
+        return pltpu.make_async_remote_copy(
+            src_ref=self.buffer.at[tile, pl.ds(pl.multiple_of(away, 16), size), :],
+            dst_ref=self.lands[stage].at[tile],
+            send_sem=self.sends.at[stage, tile],
+            recv_sem=self.recvs.at[stage, tile],
+            device_id={"dp": self.partner(bit)},
+            device_id_type=pl.DeviceIdType.MESH,
+        )
+
+    def gather_stage(self, stage, tile):
+        self.copy(stage, tile).wait_recv()
+        keep, _, size = self.spans(stage)
+        at = pl.ds(pl.multiple_of(keep, 16), size)
+        return at, self.buffer[tile, at, :].astype(F32) + self.lands[stage][tile].astype(F32)
+
+    def advance(self, stage, tile):
+        at, total = self.gather_stage(stage, tile)
+        self.buffer[tile, at, :] = total.astype(BF)
+        self.copy(stage + 1, tile).start()
+
+
+class PackGather:
+    def __init__(self, own, other, packs, sends, recvs):
+        self.own, self.other, self.packs, self.sends, self.recvs = own, other, packs, sends, recvs
+        self.place, self.side = lax.axis_index("dp"), lax.axis_index("mp")
+        self.stages = SUM_PLACES.bit_length() - 1
+
+    def greet(self, barrier):
+        pl.semaphore_signal(
+            barrier, inc=1, device_id={"mp": 1 - self.side}, device_id_type=pl.DeviceIdType.MESH
+        )
+
+    def cross(self):
+        return pltpu.make_async_remote_copy(
+            src_ref=self.other,
+            dst_ref=self.packs.at[self.place, self.side],
+            send_sem=self.sends.at[self.stages],
+            recv_sem=self.recvs.at[self.stages],
+            device_id={"mp": 1 - self.side},
+            device_id_type=pl.DeviceIdType.MESH,
+        )
+
+    def copy(self, stage):
+        bit = 1 << stage
+        rows = self.packs.at[pl.ds((self.place // bit) * bit, bit)]
+        return pltpu.make_async_remote_copy(
+            src_ref=rows,
+            dst_ref=rows,
+            send_sem=self.sends.at[stage],
+            recv_sem=self.recvs.at[stage],
+            device_id={"dp": self.place + bit - 2 * bit * place_bit(self.place, bit)},
+            device_id_type=pl.DeviceIdType.MESH,
+        )
+
+    def start(self):
+        self.packs[self.place, self.side] = self.own[...]
+        self.cross().start()
+
+    def advance(self, stage):
+        (self.cross() if stage == 0 else self.copy(stage - 1)).wait_recv()
+        self.copy(stage).start()
+
+    def finish(self):
+        self.copy(self.stages - 1).wait_recv()
+        self.cross().wait_send()
+        for stage in range(self.stages):
+            self.copy(stage).wait_send()
+
+
+def attn_grads_kernel(
+    first_ref, dattn_ref, dqkv_ref, att_ref, pack_own_ref, pack_other_ref, sums_ref, every_ref,
+    first_t, dattn_t, buffer, land0, land1, land2, land3, sends, recvs,
+    packs, pack_sends, pack_recvs,
+):
+    width = first_t.shape[0]
+    tiles, _, columns = buffer.shape
+    proj_tiles = dqkv_ref.shape[0] // columns
+    share = width // SUM_PLACES
+    total = DpSum(buffer, (land0, land1, land2, land3), sends, recvs)
+    ring = PackGather(pack_own_ref, pack_other_ref, packs, pack_sends, pack_recvs)
+    barrier = pltpu.get_barrier_semaphore()
+    total.greet(barrier)
+    ring.greet(barrier)
+    pl.semaphore_wait(barrier, len(HALVING) + 2)
+    ring.start()
+    for source, target in ((first_ref, first_t), (dattn_ref, dattn_t)):
+        for at in range(0, source.shape[0], 512):
+            target[:, at : at + 512] = source[at : at + 512, :].T
+    half = width // 2
+
+    def step(s, carry):
+        @pl.when(s < proj_tiles)
+        def _():
+            right = dqkv_ref[pl.ds(pl.multiple_of(s * columns, 128), columns), :]
+            for at in (0, half):
+                store_by_owner(buffer, s, at, nt(first_t[at : at + half, :], right), share)
+            total.copy(0, s).start()
+
+        @pl.when(jnp.logical_and(s >= proj_tiles, s < tiles))
+        def _():
+            right = att_ref[pl.ds(pl.multiple_of((s - proj_tiles) * columns, 128), columns), :]
+            for at in (0, half):
+                store_by_owner(buffer, s, at, nt(dattn_t[at : at + half, :], right), share)
+            total.copy(0, s).start()
+
+        for stage in range(3):
+            tile = s - 1 - stage
+
+            @pl.when(jnp.logical_and(tile >= 0, tile < tiles))
+            def _():
+                total.advance(stage, tile)
+
+        for stage in range(ring.stages):
+
+            @pl.when(s == 2 + 2 * stage)
+            def _():
+                ring.advance(stage)
+
+        tile = s - 4
+
+        @pl.when(tile >= 0)
+        def _():
+            sums_ref[tile] = total.gather_stage(3, tile)[1].astype(BF)
+
+        return carry
+
+    lax.fori_loop(0, tiles + 4, step, 0)
+    ring.finish()
+    every_ref[...] = packs[...]
+
+    def finish(tile, carry):
+        for stage in range(4):
+            total.copy(stage, tile).wait_send()
+        return carry
+
+    lax.fori_loop(0, tiles, finish, 0)
+
+
+def can_sum_here(width, columns):
+    places = lax.axis_size("dp")
+    return places == SUM_PLACES and width % (8 * places) == 0 and columns % 384 == 0
+
+
+def attn_grads(first, dattn, dqkv, att, pack_own, pack_other):
+    width = first.shape[1]
+    tile = 384
+    tiles = (dqkv.shape[0] + att.shape[0]) // tile
+    share = width // SUM_PLACES
+    vmem = pl.BlockSpec(memory_space=pltpu.VMEM)
+    sums, every = pl.pallas_call(
+        attn_grads_kernel,
+        in_specs=[vmem] * 6,
+        out_specs=[vmem] * 2,
+        out_shape=[
+            jax.ShapeDtypeStruct((tiles, 2 * share, tile), BF),
+            jax.ShapeDtypeStruct((SUM_PLACES, 2) + pack_own.shape, F32),
+        ],
+        scratch_shapes=[
+            pltpu.VMEM((width, first.shape[0]), BF),
+            pltpu.VMEM((width, dattn.shape[0]), BF),
+            pltpu.VMEM((tiles, width, tile), BF),
+            pltpu.VMEM((tiles, width // 2, tile), BF),
+            pltpu.VMEM((tiles, width // 4, tile), BF),
+            pltpu.VMEM((tiles, width // 8, tile), BF),
+            pltpu.VMEM((tiles, width // 8, tile), BF),
+            pltpu.SemaphoreType.DMA((4, tiles)),
+            pltpu.SemaphoreType.DMA((4, tiles)),
+            pltpu.VMEM((SUM_PLACES, 2) + pack_own.shape, F32),
+            pltpu.SemaphoreType.DMA((SUM_PLACES.bit_length(),)),
+            pltpu.SemaphoreType.DMA((SUM_PLACES.bit_length(),)),
+        ],
+        compiler_params=pltpu.CompilerParams(
+            vmem_limit_bytes=VMEM_LIMIT, collective_id=1, has_side_effects=True
+        ),
+        cost_estimate=cost(1e7, 1e5),
+    )(first, dattn, dqkv, att, pack_own, pack_other)
+    here = place_bit(lax.axis_index("dp"), FINAL) * share
+    mine = lax.dynamic_slice_in_dim(sums, here, share, 1)
+    return jnp.transpose(mine, (1, 0, 2)).reshape(share, -1), every
+
+
 def shift_mp(value, steps):
     ways = lax.axis_size("mp")
     return lax.ppermute(value, "mp", [(i, (i - steps) % ways) for i in range(ways)])
 
 
-def from_others(block):
-    ways, places = lax.axis_size("mp"), lax.axis_size("dp")
+def near_halves(block):
     half = block.shape[0] // 2
     core = lax.axis_index("dp") % 2
     mine = lax.dynamic_slice_in_dim(block, core * half, half, 0)
+    return [shift_mp(mine, steps) for steps in range(1, lax.axis_size("mp"))]
+
+
+def with_far_halves(nears):
+    places = lax.axis_size("dp")
+    core = lax.axis_index("dp") % 2
     got = []
-    for steps in range(1, ways):
-        near = shift_mp(mine, steps)
+    for near in nears:
+        half = near.shape[0]
         far = lax.ppermute(near, "dp", [(i, i ^ 1) for i in range(places)])
-        whole = jnp.zeros_like(block)
+        whole = jnp.zeros((2 * half,) + near.shape[1:], near.dtype)
         whole = lax.dynamic_update_slice_in_dim(whole, near, core * half, 0)
-        whole = lax.dynamic_update_slice_in_dim(whole, far, (1 - core) * half, 0)
-        got.append(whole)
+        got.append(lax.dynamic_update_slice_in_dim(whole, far, (1 - core) * half, 0))
     return got
+
+
+def from_others(block):
+    return with_far_halves(near_halves(block))
 
 
 def home(parts):
@@ -517,6 +766,16 @@
     for steps in range(1, len(parts)):
         total = total + shift_mp(parts[steps], -steps).astype(F32)
     return total
+
+
+def to_lanes_rows(size):
+    return -(-size // 1024) * 8
+
+
+def to_lanes(part):
+    flat = part.reshape(-1)
+    rows = to_lanes_rows(flat.shape[0])
+    return jnp.pad(flat, (0, rows * 128 - flat.shape[0])).reshape(rows, 128)
 
 
 def scatter_dp(part):
@@ -552,8 +811,7 @@
     weight_t, out_w, late_up, late_down = lax.optimization_barrier(
         (weight_t, out_w, mlp_up, mlp_down)
     )
-    up_others = from_others(late_up)
-    down_others = from_others(late_down)
+    near_up = near_halves(late_up)
 
     own_kept = lax.dynamic_slice_in_dim(kept_ids, place * images, images, 0)
     own_kept = jnp.pad(own_kept, ((0, 0), (0, padded - keep)), constant_values=-1)
@@ -570,9 +828,14 @@
     dmlp = (mod[:, 5:6] * grads.astype(F32)).astype(BF).reshape(-1, width)
     grads = grads.reshape(-1, width)
 
+    near_up, bias, mod, late_down = lax.optimization_barrier((near_up, bias, mod, late_down))
+    near_down = near_halves(late_down)
+    up_others = with_far_halves(near_up)
     first, qkv, att, lse, middle, second, branch = forward(
         tokens, mod, pick, weight_t, out_w, bias, per_block
     )
+    near_down, second = lax.optimization_barrier((near_down, second))
+    down_others = with_far_halves(near_down)
     (branch_mlp, dsecond, grads_own), tile_own = mlp(second, dmlp, mlp_up, mlp_down)
     reduced = [scatter_dp(grads_own)]
     for up, down in zip(up_others, down_others):
@@ -584,11 +847,44 @@
         tokens, mod, pick, weight_t, out_w, bias, qkv, lse, middle, branch, branch_mlp, dsecond,
         grads, per_block,
     )
-    dweight = dot(first, dqkv, (0, 1)).astype(BF)
-    dout_t = dot(dattn, att, (0, 1)).astype(BF)
     proj_block, out_block = weight_own.shape[0], attn_out.shape[0]
-    dweight, dout_t, *reduced = lax.optimization_barrier((dweight, dout_t, *reduced))
-    attn_sums = scatter_dp(jnp.concatenate([dweight, dout_t], axis=1))
+    dqkv, reduced[0] = lax.optimization_barrier((dqkv, reduced[0]))
+    dmod_rows = dmod[:, :6].reshape(images, 6 * width)
+    dtables = table_of_strips(strips)
+    here = can_sum_here(width, dqkv.shape[0]) and att.shape[0] % 384 == 0 and ways == 2
+    if here:
+        own_cond_rows = lax.dynamic_slice_in_dim(silu_cond, place * images, images, 0)
+        packs = []
+        for steps in range(ways):
+            at = (place + steps) % ways
+            parts = (
+                lax.dynamic_slice_in_dim(dmod_rows, at * cols, cols, 1),
+                dtables[steps * per_block : (steps + 1) * per_block],
+                own_cond_rows.astype(F32),
+            )
+            packs.append(jnp.concatenate([to_lanes(part) for part in parts], axis=0))
+        attn_sums, every = attn_grads(first, dattn, dqkv, att, *packs)
+        places = every.shape[0]
+        every = every.reshape(places * ways, -1, 128)
+        got, end = [], 0
+        for part in parts:
+            start, end = end, end + to_lanes_rows(part.size)
+            got.append(every[:, start:end].reshape(places * ways, -1)[:, : part.size])
+        all_columns = got[0].reshape(-1, cols)
+        dtable = jnp.sum(got[1], axis=0).reshape(rel_table.shape)
+        all_cond = got[2].reshape(-1, width)
+        dcolumns = lax.dynamic_slice_in_dim(
+            all_columns, lax.axis_index("dp") * images_group, images_group, 0
+        )
+    else:
+        dweight = dot(first, dqkv, (0, 1)).astype(BF)
+        dout_t = dot(dattn, att, (0, 1)).astype(BF)
+        attn_sums = scatter_dp(jnp.concatenate([dweight, dout_t], axis=1))
+        dcolumns = lax.all_to_all(dmod_rows, "mp", split_axis=1, concat_axis=0, tiled=True)
+        dtable = home(list(jnp.split(dtables, ways, axis=0)))
+        all_columns = lax.all_gather(dcolumns, "dp", axis=0, tiled=True)
+        dtable = lax.psum(dtable, "dp")
+        all_cond = lax.all_gather(silu_cond, "dp", axis=0, tiled=True).astype(F32)
     split = ways * proj_block
     attn_parts = [
         jnp.concatenate(
@@ -601,33 +897,23 @@
         for j in range(ways)
     ]
     mlp_grads = home(reduced)
-    attn_grads = home(attn_parts)
+    attn_total = home(attn_parts)
     grad_up, grad_down_t = split_mlp_grads(mlp_grads, tile_own)
-    grad_qkv = attn_grads[:, :proj_block].reshape(-1, 3, proj_block // 3)
-    grad_out = jnp.transpose(attn_grads[:, proj_block:])
-
-    dmod_rows = dmod[:, :6].reshape(images, 6 * width)
-    dcolumns = lax.all_to_all(dmod_rows, "mp", split_axis=1, concat_axis=0, tiled=True)
-    dtable = home(list(jnp.split(table_of_strips(strips), ways, axis=0)))
-    flat = jnp.concatenate([dcolumns.reshape(-1), dtable.reshape(-1)])
-    count = flat.shape[0]
-    packed = jnp.pad(flat, (0, -count % 1024)).reshape(-1, 128)
-    every = lax.all_gather(packed, "dp", axis=0, tiled=True)
-    every = every.reshape(lax.axis_size("dp"), -1)[:, :count]
-    all_columns = every[:, : images_group * cols].reshape(-1, cols)
-    dtable = jnp.sum(every[:, images_group * cols :], axis=0).reshape(rel_table.shape)
-    all_cond = lax.all_gather(silu_cond, "dp", axis=0, tiled=True)
+    grad_qkv = attn_total[:, :proj_block].reshape(-1, 3, proj_block // 3)
+    grad_out = jnp.transpose(attn_total[:, proj_block:])
+
     slice_width = width // lax.axis_size("dp")
     cond_slice = lax.dynamic_slice_in_dim(
         all_cond, lax.axis_index("dp") * slice_width, slice_width, 1
     )
     grad_ada_weight = lax.dot_general(
-        cond_slice.astype(F32), all_columns, (((0,), (0,)), ((), ())), precision=PRECISE
+        cond_slice, all_columns, (((0,), (0,)), ((), ())), precision=PRECISE
     )
     grad_ada_bias = jnp.sum(all_columns, axis=0)
-    silu_part = lax.dot_general(
-        dcolumns, ada_weight.astype(F32), (((1,), (1,)), ((), ())), precision=PRECISE
-    )
+    dcolumns_high = dcolumns.astype(BF)
+    dcolumns_low = (dcolumns - dcolumns_high.astype(F32)).astype(BF)
+    silu_part = nt(jnp.concatenate([dcolumns_high, dcolumns_low], axis=0), ada_weight)
+    silu_part = silu_part[:images_group] + silu_part[images_group:]
     shares = lax.all_to_all(
         silu_part.astype(BF).reshape(ways, images, width), "mp", split_axis=0, concat_axis=0,
         tiled=True,

time: 796 us -> 814 us (1.023)
  Pallas kernels: 311 us -> 506 us
  waiting for transfers between devices: 252 us -> 124 us
  matrix products: 39.3 us -> 12.9 us
  blocking collectives: 23.6 us -> 0 us
  other arithmetic: 33.2 us -> 21 us
  local copies, waits for them, and re-layouts: 94.2 us -> 105 us
    pallas_call x0 -> x1, Pallas kernels: none -> 205 us  [attn_grads(): pl.pallas_call(attn_grads_kernel, in_specs=[vmem] * 6, out_specs=[vmem] *...]
    reduce_scatter x3 -> x2, waiting for transfers between devices: 94.8 us -> 0.01 us  [scatter_dp(): return lax.psum_scatter(part, 'dp', scatter_dimension=0, tiled=True)]
    ppermute x8 -> x7, waiting for transfers between devices: 143 us -> 66.8 us  [shift_mp(): lax.ppermute(value, 'mp', [(i, (i - steps) % ways) for i in range(ways)])]
    all_to_all x1, waiting for transfers between devices: 14.6 us -> 48.4 us  [local(): mod = lax.all_to_all(columns, 'mp', split_axis=0, concat_axis=1, tiled=True)]
    all_gather x1 -> x0, blocking collectives: 23.6 us -> none  [local(): all_cond = lax.all_gather(silu_cond, 'dp', axis=0, tiled=True)]
    dot_general x2 -> x1, matrix products: 24.3 us -> 5.51 us  [dot(): lax.dot_general(a, b, ((dims[0:1], dims[1:2]), ((), ())), preferred_eleme...]
    pallas_call x2, Pallas kernels: 164 us -> 155 us  [mlp(): pl.pallas_call(functools.partial(mlp_kernel, chunk, fresh), grid=(hidden...]
    ppermute x4, waiting for transfers between devices: 0.01 us -> 8.84 us  [with_far_halves(): far = lax.ppermute(near, 'dp', [(i, i ^ 1) for i in range(places)])]
  transfers between devices with their start and end apart: 19 -> 15, of which waited for: 7 -> 6; matrix products, arithmetic and copies ran while one was open for 19% -> 13% of each run, Pallas kernels for 22% -> 54%
where the time goes in v2:
time: 814 us; the launch traced here: 802 us
  Pallas kernels  506 us (62%)
  waiting for transfers between devices  124 us (15%)
  local copies, waits for them, and re-layouts  105 us (13%)
  other arithmetic  21 us (3%)
  starting transfers between devices  18.2 us (2%)
  between operations  14.9 us (2%)
  matrix products  12.9 us (2%)
    pallas_call x1, Pallas kernels, attn_grads(): pl.pallas_call(attn_grads_kernel, in_specs=[vmem] * 6, out_specs=[vmem] *...  205 us
    pallas_call x2, Pallas kernels, mlp(): pl.pallas_call(functools.partial(mlp_kernel, chunk, fresh), grid=(hidden...  155 us
    pallas_call x1, Pallas kernels, backward(): pl.pallas_call(functools.partial(backward_kernel, per_block), grid=(image...  85.9 us
    ppermute x7, waiting for transfers between devices, shift_mp(): lax.ppermute(value, 'mp', [(i, (i - steps) % ways) for i in range(ways)])  66.8 us
    pallas_call x1, Pallas kernels, forward(): pl.pallas_call(functools.partial(forward_kernel, per_block), grid=(images...  50.6 us
    all_to_all x1, waiting for transfers between devices, local(): mod = lax.all_to_all(columns, 'mp', split_axis=0, concat_axis=1, tiled=True)  48.4 us
    another operation x17, local copies, waits for them, and re-layouts, bias_whole(): jnp.stack([grid_table[:, :, GRID - 1 - c:2 * GRID - 1 - c] for c in range...  24.6 us
  transfers between devices with their start and end apart: 15, of which 6 were waited for; matrix products, arithmetic and copies ran while one was open for 13% of the time, Pallas kernels for 54%

profile of v2, /device:TPU:0, one launch (start us, length us, event | category | flops | bytes accessed | tf_op | source)
XLA Modules:
  0.0 802.3 jit_solution(15392679893803971235)
XLA Ops:
  7.2 3.1 dynamic-slice_bitcast_fusion
  10.3 2.9 collective-permute-start
  13.4 44.2 %collective-permute-done = bf16[864,1152]{1,0:T(8,128)(2,1)S(1)} collective-permute-done((bf16[864,1152]{1,0:T(8,128)(2,1)}, bf16[864,1152]{1,0:T(8,128)(2,1)S(1)}, u32[]{:S(2)}, u32[]{:S(2)}) %collective-permute-start) | collective-permute-done | bytes 1990688 | tf_op jit(solution)/shard_map/ppermute | solution.py:737
  57.6 13.5 %collective-permute-done.2 = bf16[288,1152]{1,0:T(8,128)(2,1)} collective-permute-done((bf16[288,1152]{1,0:T(8,128)(2,1)S(1)}, bf16[288,1152]{1,0:T(8,128)(2,1)}, u32[]{:S(2)}, u32[]{:S(2)}) %collective-permute-start.2) | collective-permute-done | bytes 663584 | tf_op jit(solution)/shard_map/ppermute | solution.py:737
  71.2 1.2 constant_dynamic-update-slice_fusion.5
  72.4 1.2 collective-permute-done.3
  73.6 1.2 constant_dynamic-update-slice_fusion.4
  74.8 1.7 pad_maximum_fusion.1.out_w_ref
  76.5 2.2 broadcast_in_dim.15
  78.6 1.5 constant_dynamic-update-slice_fusion.7
  80.1 3.0 constant_dynamic-update-slice_fusion.6
  83.1 7.0 pad_maximum_fusion.weight_ref
  90.1 3.4 constant_dynamic-slice_fusion.5
  93.5 1.7 collective-permute-start.4
  95.3 4.4 fusion.2
  100.3 3.3 all-to-all-start
  103.8 2.0 collective-permute-start.5
  105.9 48.4 %all-to-all-done = bf16[2,4,3456]{2,1,0:T(4,128)(2,1)S(1)} async-done(((bf16[2,4,3456]{2,1,0:T(4,128)(2,1)}), bf16[2,4,3456]{2,1,0:T(4,128)(2,1)S(1)}, u32[]{:S(2)}, u32[]{:S(2)}) %all-to-all-start) | async-done | bytes 55328 | tf_op jit(solution)/shard_map/all_to_all | solution.py:801
  155.5 2.9 fusion.28
  160.6 1.7 stack.70
  162.4 1.7 stack.71
  164.1 1.7 stack.72
  165.8 1.7 stack.73
  167.5 1.7 stack.74
  169.2 1.7 stack.75
  170.9 1.7 stack.76
  172.7 1.7 stack.77
  174.4 1.7 stack.78
  176.1 1.7 stack.79
  177.8 1.7 stack.80
  180.6 2.4 stack.67
  183.9 9.6 %shard_map.203.bias_ref = f32[16,256,256]{2,1,0:T(8,128)} custom-call(f32[16,16,512]{2,1,0:T(8,128)} %pad.100.strip_ref), custom_call_target="tpu_custom_call" | custom-call | bytes 4194304 | tf_op jit(solution)/shard_map/pallas_call | solution.py:84
  193.5 4.4 constant_dynamic-slice_fusion.3
  197.9 1.7 collective-permute-start.6
  199.6 1.9 reshape.171
  202.5 1.8 fusion.3
  206.2 3.1 fusion.dmlp_ref
  209.3 50.6 %shard_map.204 = (bf16[1024,1152]{1,0:T(8,128)(2,1)}, bf16[3456,1024]{1,0:T(8,128)(2,1)}, bf16[1152,2048]{1,0:T(8,128)(2,1)}, f32[4,32,256]{2,1,0:T(8,128)}, f32...) custom-call(bf16[1024,1152]{1,0:T(8,128)(2,1)} %tok_ref.3, f32[4,8,1152]{2,1,0:T(8,128)} %pad.101.mod_ref, ...), custom_call_target="tpu_custom_call" | custom-call | flops 8000000000 | bytes 32000000 | tf_op jit(solution)/shard_map/pallas_call | solution.py:180
  259.9 75.6 %shard_map.205 = (f32[1792,1152]{1,0:T(8,128)}, f32[1792,1152]{1,0:T(8,128)}, bf16[1152,4608]{1,0:T(8,128)(2,1)}) custom-call(bf16[1792,1152]{1,0:T(8,128)(2,1)} %get-tuple-element.56.second_ref, bf16[1792,1152]{1,0:T(8,128)(2,1)} %fusion.dmlp_ref, bf16[1152,2304]{1,0:T(8,128)(2,1)} %up_ref.1, bf16[2304,1152]{1,0:T(8,128)(2,1)} %down_ref.1), custom_call_target="tpu_custom_call" | custom-call | flops 60000002048 | bytes 60000000 | tf_op jit(solution)/shard_map/pallas_call | solution.py:301
  335.6 1.7 copy-done.7
  338.5 7.7 collective-permute-done.7
  346.1 2.1 constant_dynamic-update-slice_fusion.2.up_ref
  348.2 2.9 broadcast_in_dim.18
  351.1 5.2 constant_dynamic-update-slice_fusion.1
  356.3 3.8 constant_dynamic-update-slice_fusion.down_ref
  360.1 79.1 %shard_map.206 = (f32[1792,1152]{1,0:T(8,128)}, f32[1792,1152]{1,0:T(8,128)}, bf16[1152,4608]{1,0:T(8,128)(2,1)}) custom-call(bf16[1792,1152]{1,0:T(8,128)(2,1)} %get-tuple-element.56.second_ref, bf16[1792,1152]{1,0:T(8,128)(2,1)} %fusion.dmlp_ref, bf16[1152,2304]{1,0:T(8,128)(2,1)} %copy-done.3, ...), custom_call_target="tpu_custom_call" | custom-call | flops 10000000 | bytes 100000 | tf_op jit(solution)/shard_map/pallas_call | solution.py:301
  439.3 85.9 %shard_map.207 = (bf16[1792,1152]{1,0:T(8,128)(2,1)}, bf16[1024,1152]{1,0:T(8,128)(2,1)}, f32[4,8,1152]{2,1,0:T(8,128)}, bf16[2048,1152]{1,0:T(8,128)(2,1)}, bf1...) custom-call(bf16[1024,1152]{1,0:T(8,128)(2,1)} %tok_ref.3, f32[4,8,1152]{2,1,0:T(8,128)} %pad.101.mod_ref, ...), custom_call_target="tpu_custom_call" | custom-call | flops 10000000 | bytes 100000 | tf_op jit(solution)/shard_map/pallas_call | solution.py:446
  525.3 1.7 slice.240
  526.9 3.3 slice.241
  530.4 3.4 reshape.178
  533.8 2.9 slice_bitcast_fusion.15
  538.2 1.6 reshape.173
  540.6 205.1 %shard_map.208 = (bf16[12,144,384]{2,1,0:T(8,128)(2,1)}, f32[16,2,216,128]{3,2,1,0:T(8,128)}) custom-call(bf16[1024,1152]{1,0:T(8,128)(2,1)} %get-tuple-element.65.first_ref, bf16[2048,1152]{1,0:T(8,128)(2,1)} %get-tuple-element.66.dattn_ref, bf16[3456,1024]{1,0:T(8,128)(2,1)} %get-tuple-element.69.dqkv_ref, bf16[1152,2048]{1,0:T(8,128)(2,1)} %get-tuple-element.70.att_ref, ...), custom_call_target="tpu_custom_call" | custom-call | flops 10000000 | bytes 100000 | tf_op jit(solution)/shard_map/pallas_call | solution.py:703
  745.7 1.7 slice.260
  747.4 2.0 slice.264
  749.4 2.3 slice.274
  755.5 1.2 copy.136
  757.8 5.5 fusion.5
  763.9 3.4 all-to-all-start.1
  768.0 3.0 fusion.9
  773.1 2.0 collective-permute-start.10
  778.2 9.1 %collective-permute-done.10 = bf16[72,4608]{1,0:T(8,128)(2,1)} collective-permute-done((bf16[72,4608]{1,0:T(8,128)(2,1)}, bf16[72,4608]{1,0:T(8,128)(2,1)}, u32[]{:S(2)}, u32[]{:S(2)}) %collective-permute-start.10) | collective-permute-done | bytes 663584 | tf_op jit(solution)/shard_map/ppermute | solution.py:737
  787.3 1.3 convert_add_fusion
  789.4 3.9 slice_reduce_fusion.1
  (123 shorter events, 27.0 us)
Async XLA Ops:
  7.2 194.3 %copy-start = (s32[8,179]{1,0:T(8,128)S(1)}, s32[8,179]{1,0:T(8,128)}, u32[]{:S(2)}) copy-start(s32[8,179]{1,0:T(8,128)} %param.14) | copy-start | bytes 17188
  7.2 6.1 copy-start.5
  10.3 47.3 %collective-permute-start = (bf16[864,1152]{1,0:T(8,128)(2,1)}, bf16[864,1152]{1,0:T(8,128)(2,1)S(1)}, u32[]{:S(2)}, u32[]{:S(2)}) collective-permute-start(bf16[864,1152]{1,0:T(8,128)(2,1)} %dynamic-slice_bitcast_fusion), channel_id=1, source_target_pairs={{0,1},{1,0},{2,3},{3,2},{4,5},{5,4},{6,7},{7,6},{8,9},{9,8},{10,11... | collective-permute-start | bytes 5971976 | tf_op jit(solution)/shard_map/ppermute | solution.py:737
  13.3 57.8 %collective-permute-start.2 = (bf16[288,1152]{1,0:T(8,128)(2,1)S(1)}, bf16[288,1152]{1,0:T(8,128)(2,1)}, u32[]{:S(2)}, u32[]{:S(2)}) collective-permute-start(bf16[288,1152]{1,0:T(8,128)(2,1)S(1)} %constant_dynamic-slice_fusion.6), channel_id=1, source_target_pairs={{0,1},{1,0},{2,3},{3,2},{4,5},{5,4},{6,7},{7,6},{8,9},{9,8},{10,11... | collective-permute-start | bytes 1990664 | tf_op jit(solution)/shard_map/ppermute | solution.py:737
  57.6 22.5 %collective-permute-start.1 = (bf16[864,1152]{1,0:T(8,128)(2,1)S(1)}, bf16[864,1152]{1,0:T(8,128)(2,1)}, u32[]{:S(2)}, u32[]{:S(2)}) collective-permute-start(bf16[864,1152]{1,0:T(8,128)(2,1)S(1)} %collective-permute-done), channel_id=1, source_target_pairs={{0,2},{2,0},{4,6},{6,4},{8,10},{10,8},{12,14},{14,12},{16,18},{18,... | collective-permute-start | bytes 5971976 | tf_op jit(solution)/shard_map/ppermute | solution.py:753
  71.1 2.5 collective-permute-start.3
  90.1 5.2 copy-start.15
  90.1 5.2 copy-start.19
  93.5 10.3 %copy-start.18 = (f32[8,961]{1,0:T(8,128)S(1)}, f32[8,961]{1,0:T(8,128)}, u32[]{:S(2)}) copy-start(f32[8,961]{1,0:T(8,128)} %param.21) | copy-start | bytes 92260
  93.5 100.0 %collective-permute-start.4 = (bf16[576,2304]{1,0:T(8,128)(2,1)}, bf16[576,2304]{1,0:T(8,128)(2,1)S(1)}, u32[]{:S(2)}, u32[]{:S(2)}) collective-permute-start(bf16[576,2304]{1,0:T(8,128)(2,1)} %constant_dynamic-slice_fusion.5), channel_id=1, source_target_pairs={{0,1},{1,0},{2,3},{3,2},{4,5},{5,4},{6,7},{7,6},{8,9},{9,8},{10,11... | collective-permute-start | bytes 7962632 | tf_op jit(solution)/shard_map/ppermute | solution.py:737
  100.3 54.0 %all-to-all-start = ((bf16[2,4,3456]{2,1,0:T(4,128)(2,1)}), bf16[2,4,3456]{2,1,0:T(4,128)(2,1)S(1)}, u32[]{:S(2)}, u32[]{:S(2)}) async-start(bf16[2,4,3456]{2,1,0:T(4,128)(2,1)} %all_to_all.13), calls=%async_computation | async-start | bytes 110592 | tf_op jit(solution)/shard_map/all_to_all | solution.py:801
  103.6 437.0 %reduce-scatter.3.cloned.1.call-start = ((), (), s32[]{:S(2)}) async-start(), calls=%async_computation.4 | async-start | bytes 11280384 | tf_op jit(solution)/shard_map/reduce_scatter | solution.py:782
  103.8 51.3 %collective-permute-start.5 = (f32[8,961]{1,0:T(8,128)S(1)}, f32[8,961]{1,0:T(8,128)S(1)}, u32[]{:S(2)}, u32[]{:S(2)}) collective-permute-start(f32[8,961]{1,0:T(8,128)S(1)} %copy-done.18), channel_id=1, source_target_pairs={{0,1},{1,0},{2,3},{3,2},{4,5},{5,4},{6,7},{7,6},{8,9},{9,8},{10,11... | collective-permute-start | bytes 92264 | tf_op jit(solution)/shard_map/ppermute | solution.py:737
  154.5 0.7 copy-start.10
  158.4 21.2 %copy-start.8 = (f32[16,31,16]{2,1,0:T(8,128)S(1)}, f32[16,31,16]{2,1,0:T(8,128)}, u32[]{:S(2)}) copy-start(f32[16,31,16]{2,1,0:T(8,128)} %get-tuple-element.127) | copy-start | bytes 95236
  193.5 6.2 copy-start.6
  197.9 62.0 %collective-permute-start.6 = (bf16[1152,1152]{1,0:T(8,128)(2,1)}, bf16[1152,1152]{1,0:T(8,128)(2,1)}, u32[]{:S(2)}, u32[]{:S(2)}) collective-permute-start(bf16[1152,1152]{1,0:T(8,128)(2,1)} %constant_dynamic-slice_fusion.3), channel_id=1, source_target_pairs={{0,1},{1,0},{2,3},{3,2},{4,5},{5,4},{6,7},{7,6},{8,9},{9,8},{10,11... | collective-permute-start | bytes 7962632 | tf_op jit(solution)/shard_map/ppermute | solution.py:737
  204.3 1.9 copy-start.2
  335.5 1.8 copy-start.7
  335.6 437.6 %reduce-scatter.5.cloned.1.call-start = ((), (), s32[]{:S(2)}) async-start(), calls=%async_computation.5 | async-start | bytes 11280384 | tf_op jit(solution)/shard_map/reduce_scatter | solution.py:782
  337.3 8.8 %collective-permute-start.7 = (bf16[576,2304]{1,0:T(8,128)(2,1)S(1)}, bf16[576,2304]{1,0:T(8,128)(2,1)}, u32[]{:S(2)}, u32[]{:S(2)}) collective-permute-start(bf16[576,2304]{1,0:T(8,128)(2,1)S(1)} %copy-done.7), channel_id=1, source_target_pairs={{0,2},{2,0},{4,6},{6,4},{8,10},{10,8},{12,14},{14,12},{16,18},{18,... | collective-permute-start | bytes 7962632 | tf_op jit(solution)/shard_map/ppermute | solution.py:753
  337.3 19.0 %collective-permute-start.8 = (bf16[1152,1152]{1,0:T(8,128)(2,1)}, bf16[1152,1152]{1,0:T(8,128)(2,1)}, u32[]{:S(2)}, u32[]{:S(2)}) collective-permute-start(bf16[1152,1152]{1,0:T(8,128)(2,1)} %collective-permute-done.6), channel_id=1, source_target_pairs={{0,2},{2,0},{4,6},{6,4},{8,10},{10,8},{12,14},{14,12},{16,18},{18,... | collective-permute-start | bytes 7962632 | tf_op jit(solution)/shard_map/ppermute | solution.py:753
  348.2 8.1 %copy-start.3 = (bf16[1152,2304]{1,0:T(8,128)(2,1)}, bf16[1152,2304]{1,0:T(8,128)(2,1)S(1)}, u32[]{:S(2)}) copy-start(bf16[1152,2304]{1,0:T(8,128)(2,1)S(1)} %constant_dynamic-update-slice_fusion.2.up_ref) | copy-start | bytes 15925252
  525.3 4.9 copy-start.17
  525.3 5.1 copy-start.12
  745.7 6.0 copy-start.14
  754.1 21.0 %collective-permute-start.9 = (bf16[72,2304]{1,0:T(8,128)(2,1)}, bf16[72,2304]{1,0:T(8,128)(2,1)}, u32[]{:S(2)}, u32[]{:S(2)}) collective-permute-start(bf16[72,2304]{1,0:T(8,128)(2,1)} %pad_maximum_fusion.2), channel_id=1, source_target_pairs={{0,1},{1,0},{2,3},{3,2},{4,5},{5,4},{6,7},{7,6},{8,9},{9,8},{10,11... | collective-permute-start | bytes 995336 | tf_op jit(solution)/shard_map/ppermute | solution.py:737
  757.7 9.6 %copy-start.4 = (f32[32,64,128]{2,1,0:T(8,128)S(1)}, f32[32,64,128]{2,1,0:T(8,128)}, u32[]{:S(2)}) copy-start(f32[32,64,128]{2,1,0:T(8,128)} %slice.274) | copy-start | bytes 3145732
  763.3 9.2 %copy-start.16 = (bf16[8,1152]{1,0:T(8,128)(2,1)S(1)}, bf16[8,1152]{1,0:T(8,128)(2,1)}, u32[]{:S(2)}) copy-start(bf16[8,1152]{1,0:T(8,128)(2,1)} %param.13) | copy-start | bytes 55300
  763.3 11.8 %copy-start.9 = (bf16[72,1728]{1,0:T(8,128)(2,1)S(1)}, bf16[72,1728]{1,0:T(8,128)(2,1)}, u32[]{:S(2)}) copy-start(bf16[72,1728]{1,0:T(8,128)(2,1)} %get-tuple-element.119) | copy-start | bytes 746500
  763.3 11.8 %copy-start.13 = (bf16[72,576]{1,0:T(8,128)(2,1)S(1)}, bf16[72,576]{1,0:T(8,128)(2,1)}, u32[]{:S(2)}) copy-start(bf16[72,576]{1,0:T(8,128)(2,1)} %get-tuple-element.121) | copy-start | bytes 248836
  763.9 8.5 %all-to-all-start.1 = ((bf16[2,4,1152]{2,1,0:T(4,128)(2,1)}), bf16[2,4,1152]{2,1,0:T(4,128)(2,1)S(1)}, u32[]{:S(2)}, u32[]{:S(2)}) async-start(bf16[2,4,1152]{2,1,0:T(4,128)(2,1)} %reshape.191), calls=%async_computation.2 | async-start | bytes 36864 | tf_op jit(solution)/shard_map/all_to_all | solution.py:917
  771.0 16.3 %copy-start.11 = (bf16[72,4608]{1,0:T(8,128)(2,1)S(1)}, bf16[72,4608]{1,0:T(8,128)(2,1)}, u32[]{:S(2)}) copy-start(bf16[72,4608]{1,0:T(8,128)(2,1)} %reduce-scatter.3.cloned.1.call-done) | copy-start | bytes 1990660
  773.1 14.1 %collective-permute-start.10 = (bf16[72,4608]{1,0:T(8,128)(2,1)}, bf16[72,4608]{1,0:T(8,128)(2,1)}, u32[]{:S(2)}, u32[]{:S(2)}) collective-permute-start(bf16[72,4608]{1,0:T(8,128)(2,1)} %reduce-scatter.5.cloned.1.call-done), channel_id=1, source_target_pairs={{0,1},{1,0},{2,3},{3,2},{4,5},{5,4},{6,7},{7,6},{8,9},{9,8},{10,11... | collective-permute-start | bytes 1990664 | tf_op jit(solution)/shard_map/ppermute | solution.py:737
  787.3 8.0 copy-start.1
Sparse Core Ops, SparseCore 0:
  335.7 124.1 reduce-scatter.2
  464.0 139.4 reduce-scatter.4

commit v3 on v2

--- a/solution.py
+++ b/solution.py
@@ -112,7 +112,84 @@
     return (tn(pick, ones) - 1.0) * 1e30
 
 
-def forward_kernel(
+def part_copies(layout, parts, whole, sems):
+    core = lax.axis_index("dp") % 2
+    copies = []
+    for index, ((base, half, near), part) in enumerate(zip(layout, parts)):
+        start = base + (core if near else 1 - core) * half
+        rows = pl.ds(pl.multiple_of(start, 16), part.shape[0])
+        copies.append(pltpu.make_async_copy(part, whole.at[rows, :], sems.at[index]))
+    return copies
+
+
+def run_copies(copies):
+    for copy in copies:
+        copy.start()
+    for copy in copies:
+        copy.wait()
+
+
+def start_fetch(own, target, sems):
+    half = target.shape[0]
+    start = (lax.axis_index("dp") % 2) * half
+    return pltpu.make_async_remote_copy(
+        src_ref=own.at[pl.ds(pl.multiple_of(start, 16), half), :],
+        dst_ref=target,
+        send_sem=sems.at[0],
+        recv_sem=sems.at[1],
+        device_id={"mp": 1 - lax.axis_index("mp")},
+        device_id_type=pl.DeviceIdType.MESH,
+    )
+
+
+def greet_peers(with_core):
+    barrier = pltpu.get_barrier_semaphore()
+    peers = [{"mp": 1 - lax.axis_index("mp")}]
+    if with_core:
+        place = lax.axis_index("dp")
+        peers.append({"dp": place + 1 - 2 * (place % 2)})
+    for peer in peers:
+        pl.semaphore_signal(
+            barrier, inc=1, device_id=peer, device_id_type=pl.DeviceIdType.MESH
+        )
+    pl.semaphore_wait(barrier, len(peers))
+
+
+def forward_kernel(per_block, weight_layout, out_layout, fetch, *refs):
+    tok_ref, mod_ref, pick_ref, bias_ref = refs[:4]
+    refs = refs[4:]
+    weight_parts, refs = refs[: len(weight_layout)], refs[len(weight_layout) :]
+    out_parts, refs = refs[: len(out_layout)], refs[len(out_layout) :]
+    if fetch:
+        send_ref, refs = refs[0], refs[1:]
+    first_ref, qkv_ref, att_ref, lse_ref, middle_ref, second_ref, branch_ref = refs[:7]
+    refs = refs[7:]
+    if fetch:
+        got_ref, refs = refs[0], refs[1:]
+    qkv_s, att_s, attk_s, weight_ref, out_w_ref, part_sems, fetch_sems = refs
+
+    @pl.when(pl.program_id(0) == 0)
+    def _():
+        copies = part_copies(weight_layout, weight_parts, weight_ref, part_sems.at[0])
+        copies += part_copies(out_layout, out_parts, out_w_ref, part_sems.at[1])
+        if fetch:
+            greet_peers(False)
+            start_fetch(send_ref, got_ref, fetch_sems).start()
+        run_copies(copies)
+
+    forward_body(
+        per_block, tok_ref, mod_ref, pick_ref, weight_ref, out_w_ref, bias_ref,
+        first_ref, qkv_ref, att_ref, lse_ref, middle_ref, second_ref, branch_ref,
+        qkv_s, att_s, attk_s,
+    )
+    if fetch:
+
+        @pl.when(pl.program_id(0) == pl.num_programs(0) - 1)
+        def _():
+            start_fetch(send_ref, got_ref, fetch_sems).wait()
+
+
+def forward_body(
     per_block, tok_ref, mod_ref, pick_ref, weight_ref, out_w_ref, bias_ref,
     first_ref, qkv_ref, att_ref, lse_ref, middle_ref, second_ref, branch_ref,
     qkv_s, att_s, attk_s,
@@ -171,23 +248,41 @@
         second_ref[rows, :] = (normalize(middle)[0] * (1.0 + scale_two) + shift_two).astype(BF)
 
 
-def forward(tokens, mod, pick, weight_t, out_w, bias, per_block):
+def whole_rows(layout, parts):
+    return sum(part.shape[0] for part in parts)
+
+
+ANYWHERE = pl.BlockSpec(memory_space=pl.ANY)
+
+
+def forward(tokens, mod, pick, bias, weight, out_weight, per_block, send=None):
     images, padded = pick.shape[0], pick.shape[1]
     width = tokens.shape[1]
     rows = PATCHES + padded
     heads = bias.shape[0]
-    proj = weight_t.shape[0]
+    (weight_layout, weight_parts), (out_layout, out_parts) = weight, out_weight
+    proj = whole_rows(*weight)
+    fetch = send is not None
+    most = max(len(weight_parts), len(out_parts))
+    extra_shapes, extra = [], []
+    compiler_params = params()
+    if fetch:
+        extra_shapes = [jax.ShapeDtypeStruct((send.shape[0] // 2, send.shape[1]), BF)]
+        extra = [send]
+        compiler_params = pltpu.CompilerParams(
+            vmem_limit_bytes=VMEM_LIMIT, dimension_semantics=("arbitrary",),
+            collective_id=2, has_side_effects=True,
+        )
     return pl.pallas_call(
-        functools.partial(forward_kernel, per_block),
+        functools.partial(forward_kernel, per_block, weight_layout, out_layout, fetch),
         grid=(images,),
         in_specs=[
             pl.BlockSpec((PATCHES, width), lambda i: (i, 0)),
             pl.BlockSpec((1, 8, width), lambda i: (i, 0, 0)),
             pl.BlockSpec((1, padded, PATCHES), lambda i: (i, 0, 0)),
-            const_spec(weight_t.shape),
-            const_spec(out_w.shape),
             const_spec(bias.shape),
-        ],
+        ]
+        + [ANYWHERE] * (len(weight_parts) + len(out_parts) + len(extra)),
         out_specs=[
             pl.BlockSpec((PATCHES, width), lambda i: (i, 0)),
             pl.BlockSpec((proj, PATCHES), lambda i: (0, i)),
@@ -196,7 +291,8 @@
             pl.BlockSpec((rows, width), lambda i: (i, 0)),
             pl.BlockSpec((rows, width), lambda i: (i, 0)),
             pl.BlockSpec((rows, width), lambda i: (i, 0)),
-        ],
+        ]
+        + [ANYWHERE] * len(extra),
         out_shape=[
             jax.ShapeDtypeStruct((images * PATCHES, width), BF),
             jax.ShapeDtypeStruct((proj, images * PATCHES), BF),
@@ -205,15 +301,20 @@
             jax.ShapeDtypeStruct((images * rows, width), F32),
             jax.ShapeDtypeStruct((images * rows, width), BF),
             jax.ShapeDtypeStruct((images * rows, width), BF),
-        ],
+        ]
+        + extra_shapes,
         scratch_shapes=[
             pltpu.VMEM((proj, PATCHES), F32),
             pltpu.VMEM((width, PATCHES), F32),
             pltpu.VMEM((width, PATCHES), F32),
+            pltpu.VMEM((proj, width), BF),
+            pltpu.VMEM((width, width), BF),
+            pltpu.SemaphoreType.DMA((2, most)),
+            pltpu.SemaphoreType.DMA((2,)),
         ],
-        compiler_params=params(),
+        compiler_params=compiler_params,
         cost_estimate=cost(images * 2e9, images * 8e6),
-    )(tokens, mod, pick, weight_t, out_w, bias)
+    )(tokens, mod, pick, bias, *weight_parts, *out_parts, *extra)
 
 
 def gelu_pair(pre):
@@ -226,8 +327,13 @@
 
 
 def mlp_kernel(
-    chunk, fresh, second_ref, dmlp_ref, up_ref, down_ref, *refs
+    chunk, fresh, fetch, second_ref, dmlp_ref, up_ref, down_ref, *refs
 ):
+    if fetch:
+        near_ref, send_ref = refs[:2]
+        *refs, moves, fetch_sems = refs[2:]
+        up_all, down_all = refs[3:5]
+        refs = refs[:3] + refs[5:]
     if fresh:
         branch_ref, dsecond_ref, grads_ref, second_t, dmlp_t, hidden_s, dpre_s, sem = refs
     else:
@@ -237,8 +343,31 @@
     tile = up_ref.shape[1]
     width = second_ref.shape[1]
 
+    def half_moves(source, target, at):
+        place = lax.axis_index("dp")
+        half = source.shape[0]
+        rows = target.at[pl.ds(pl.multiple_of((place % 2) * half, 16), half), :]
+        return pltpu.make_async_remote_copy(
+            src_ref=source,
+            dst_ref=rows,
+            send_sem=moves.at[at],
+            recv_sem=moves.at[at + 1],
+            device_id={"dp": place + 1 - 2 * (place % 2)},
+            device_id_type=pl.DeviceIdType.MESH,
+        ), pltpu.make_async_copy(source, rows, moves.at[at + 2])
+
+    def down_half():
+        half = down_all.shape[0] // 2
+        start = (lax.axis_index("dp") % 2) * half
+        return down_all.at[pl.ds(pl.multiple_of(start, 16), half), :]
+
     @pl.when(pl.program_id(0) == 0)
     def _():
+        if fetch:
+            greet_peers(True)
+            start_fetch(send_ref, down_half(), fetch_sems).start()
+            for copy in half_moves(near_ref, up_all, 0):
+                copy.start()
         if fresh:
             branch_ref[...] = jnp.zeros_like(branch_ref)
             dsecond_ref[...] = jnp.zeros_like(dsecond_ref)
@@ -274,6 +403,17 @@
         grads_ref[at, :tile] = nn(second_t[at, :], dpre_s[...]).astype(BF)
         grads_ref[at, tile:] = nn(dmlp_t[at, :], hidden_s[...]).astype(BF)
 
+    if fetch:
+
+        @pl.when(pl.program_id(0) == pl.num_programs(0) - 1)
+        def _():
+            start_fetch(send_ref, down_half(), fetch_sems).wait()
+            last = half_moves(down_half(), down_all, 3)[0]
+            last.start()
+            for copy in half_moves(near_ref, up_all, 0):
+                copy.wait()
+            last.wait()
+
 
 def mlp_chunk(rows):
     for chunk in (896, 448, 64):
@@ -282,7 +422,7 @@
     return rows
 
 
-def mlp(second, dmlp, up, down, sums=None):
+def mlp(second, dmlp, up, down, sums=None, fetch=None):
     rows, width = second.shape
     hidden = up.shape[1]
     tile = 768 if hidden % 768 == 0 else hidden
@@ -295,31 +435,45 @@
         pl.BlockSpec((tile, width), lambda f: (f, 0)),
     ]
     operands = [second, dmlp, up, down]
+    out_specs = [
+        const_spec(second.shape),
+        const_spec(second.shape),
+        pl.BlockSpec((width, 2 * tile), lambda f: (0, f)),
+    ]
+    out_shape = [
+        jax.ShapeDtypeStruct(second.shape, F32),
+        jax.ShapeDtypeStruct(second.shape, F32),
+        jax.ShapeDtypeStruct((width, 2 * hidden), BF),
+    ]
+    scratch = [
+        pltpu.VMEM((width, rows), BF),
+        pltpu.VMEM((width, rows), BF),
+        pltpu.VMEM((rows, tile), BF),
+        pltpu.VMEM((rows, tile), BF),
+        pltpu.SemaphoreType.DMA((2,)),
+    ]
+    compiler_params = params()
     if not fresh:
-        in_specs += [pl.BlockSpec(memory_space=pl.ANY)] * 2
+        in_specs += [ANYWHERE] * 2
         operands += list(sums)
+    if fetch is not None:
+        in_specs += [ANYWHERE] * 2
+        operands += list(fetch)
+        out_specs += [ANYWHERE] * 2
+        out_shape += [jax.ShapeDtypeStruct(up.shape, BF), jax.ShapeDtypeStruct(down.shape, BF)]
+        scratch += [pltpu.SemaphoreType.DMA((6,)), pltpu.SemaphoreType.DMA((2,))]
+        compiler_params = pltpu.CompilerParams(
+            vmem_limit_bytes=VMEM_LIMIT, dimension_semantics=("arbitrary",),
+            collective_id=3, has_side_effects=True,
+        )
     return pl.pallas_call(
-        functools.partial(mlp_kernel, chunk, fresh),
+        functools.partial(mlp_kernel, chunk, fresh, fetch is not None),
         grid=(hidden // tile,),
         in_specs=in_specs,
-        out_specs=[
-            const_spec(second.shape),
-            const_spec(second.shape),
-            pl.BlockSpec((width, 2 * tile), lambda f: (0, f)),
-        ],
-        out_shape=[
-            jax.ShapeDtypeStruct(second.shape, F32),
-            jax.ShapeDtypeStruct(second.shape, F32),
-            jax.ShapeDtypeStruct((width, 2 * hidden), BF),
-        ],
-        scratch_shapes=[
-            pltpu.VMEM((width, rows), BF),
-            pltpu.VMEM((width, rows), BF),
-            pltpu.VMEM((rows, tile), BF),
-            pltpu.VMEM((rows, tile), BF),
-            pltpu.SemaphoreType.DMA((2,)),
-        ],
-        compiler_params=params(),
+        out_specs=out_specs,
+        out_shape=out_shape,
+        scratch_shapes=scratch,
+        compiler_params=compiler_params,
         cost_estimate=cost(6e10, 6e7) if fresh else cost(1e7, 1e5),
     )(*operands), tile
 
@@ -332,8 +486,24 @@
     )
 
 
-def backward_kernel(
-    per_block, tok_ref, mod_ref, pick_ref, weight_ref, out_w_ref, bias_ref,
+def backward_kernel(per_block, weight_layout, out_layout, *refs):
+    count = len(weight_layout) + len(out_layout)
+    weight_parts = refs[: len(weight_layout)]
+    out_parts = refs[len(weight_layout) : count]
+    weight_ref, out_w_ref, sems = refs[-3:]
+
+    @pl.when(pl.program_id(0) == 0)
+    def _():
+        run_copies(
+            part_copies(weight_layout, weight_parts, weight_ref, sems.at[0])
+            + part_copies(out_layout, out_parts, out_w_ref, sems.at[1])
+        )
+
+    backward_body(per_block, weight_ref, out_w_ref, *refs[count:-3])
+
+
+def backward_body(
+    per_block, weight_ref, out_w_ref, tok_ref, mod_ref, pick_ref, bias_ref,
     qkv_ref, lse_ref, middle_ref, branch_ref, mlp_ref, dsecond_ref, grad_ref,
     out_ref, dtok_ref, dmod_ref, dattn_ref, dqkv_ref, strips_ref,
     qkv_s, datt_s, dattk_s, dscores_s,
@@ -433,25 +603,25 @@
 
 
 def backward(
-    tokens, mod, pick, weight_t, out_w, bias, qkv, lse, middle, branch, branch_mlp, dsecond,
-    grads, per_block,
+    tokens, mod, pick, bias, qkv, lse, middle, branch, branch_mlp, dsecond, grads,
+    weight, out_weight, per_block,
 ):
+    (weight_layout, weight_parts), (out_layout, out_parts) = weight, out_weight
+    most = max(len(weight_parts), len(out_parts))
+    proj = whole_rows(*weight)
     images, padded = pick.shape[0], pick.shape[1]
     width = tokens.shape[1]
     rows = PATCHES + padded
     heads = bias.shape[0]
-    proj = weight_t.shape[0]
     by_row = pl.BlockSpec((rows, width), lambda i: (i, 0))
-    one_row = pl.BlockSpec((rows, width), lambda i: (i, 0), pipeline_mode=pl.Buffered(1))
     return pl.pallas_call(
-        functools.partial(backward_kernel, per_block),
+        functools.partial(backward_kernel, per_block, weight_layout, out_layout),
         grid=(images,),
-        in_specs=[
+        in_specs=[ANYWHERE] * (len(weight_parts) + len(out_parts))
+        + [
             pl.BlockSpec((PATCHES, width), lambda i: (i, 0)),
             pl.BlockSpec((1, 8, width), lambda i: (i, 0, 0)),
             pl.BlockSpec((1, padded, PATCHES), lambda i: (i, 0, 0)),
-            const_spec(weight_t.shape),
-            const_spec(out_w.shape),
             const_spec(bias.shape),
             pl.BlockSpec((proj, PATCHES), lambda i: (0, i)),
             pl.BlockSpec((1, 2 * heads, PATCHES), lambda i: (i, 0, 0)),
@@ -482,11 +652,14 @@
             pltpu.VMEM((width, PATCHES), F32),
             pltpu.VMEM((width, PATCHES), F32),
             pltpu.VMEM((heads, PATCHES, PATCHES), F32),
+            pltpu.VMEM((proj, width), BF),
+            pltpu.VMEM((width, width), BF),
+            pltpu.SemaphoreType.DMA((2, most)),
         ],
         compiler_params=params(),
         cost_estimate=cost(1e7, 1e5),
     )(
-        tokens, mod, pick, weight_t, out_w, bias, qkv, lse, middle, branch, branch_mlp,
+        *weight_parts, *out_parts, tokens, mod, pick, bias, qkv, lse, middle, branch, branch_mlp,
         dsecond, grads,
     )
 
@@ -572,11 +745,18 @@
         self.copy(stage + 1, tile).start()
 
 
+def pack_slot(place):
+    return sum(
+        place_bit(place, SUM_PLACES >> (k + 1)) << k for k in range(SUM_PLACES.bit_length() - 1)
+    )
+
+
 class PackGather:
     def __init__(self, own, other, packs, sends, recvs):
         self.own, self.other, self.packs, self.sends, self.recvs = own, other, packs, sends, recvs
         self.place, self.side = lax.axis_index("dp"), lax.axis_index("mp")
         self.stages = SUM_PLACES.bit_length() - 1
+        self.slot = pack_slot(self.place)
 
     def greet(self, barrier):
         pl.semaphore_signal(
@@ -586,7 +766,7 @@
     def cross(self):
         return pltpu.make_async_remote_copy(
             src_ref=self.other,
-            dst_ref=self.packs.at[self.place, self.side],
+            dst_ref=self.packs.at[self.slot, self.side],
             send_sem=self.sends.at[self.stages],
             recv_sem=self.recvs.at[self.stages],
             device_id={"mp": 1 - self.side},
@@ -594,8 +774,9 @@
         )
 
     def copy(self, stage):
-        bit = 1 << stage
-        rows = self.packs.at[pl.ds((self.place // bit) * bit, bit)]
+        size = 1 << stage
+        bit = SUM_PLACES >> (stage + 1)
+        rows = self.packs.at[pl.ds((self.slot // size) * size, size)]
         return pltpu.make_async_remote_copy(
             src_ref=rows,
             dst_ref=rows,
@@ -606,7 +787,7 @@
         )
 
     def start(self):
-        self.packs[self.place, self.side] = self.own[...]
+        self.packs[self.slot, self.side] = self.own[...]
         self.cross().start()
 
     def advance(self, stage):
@@ -706,7 +887,7 @@
         out_specs=[vmem] * 2,
         out_shape=[
             jax.ShapeDtypeStruct((tiles, 2 * share, tile), BF),
-            jax.ShapeDtypeStruct((SUM_PLACES, 2) + pack_own.shape, F32),
+            jax.ShapeDtypeStruct((SUM_PLACES, 2) + pack_own.shape, BF),
         ],
         scratch_shapes=[
             pltpu.VMEM((width, first.shape[0]), BF),
@@ -718,7 +899,7 @@
             pltpu.VMEM((tiles, width // 8, tile), BF),
             pltpu.SemaphoreType.DMA((4, tiles)),
             pltpu.SemaphoreType.DMA((4, tiles)),
-            pltpu.VMEM((SUM_PLACES, 2) + pack_own.shape, F32),
+            pltpu.VMEM((SUM_PLACES, 2) + pack_own.shape, BF),
             pltpu.SemaphoreType.DMA((SUM_PLACES.bit_length(),)),
             pltpu.SemaphoreType.DMA((SUM_PLACES.bit_length(),)),
         ],
@@ -757,8 +938,18 @@
     return got
 
 
-def from_others(block):
-    return with_far_halves(near_halves(block))
+def gathered_parts(own, nears):
+    half = own.shape[0] // 2
+    if half % 16:
+        return [(0, 0, True)], [jnp.concatenate([own] + with_far_halves(nears), axis=0)]
+    places = lax.axis_size("dp")
+    layout, parts = [(0, 0, True)], [own]
+    for j, near in enumerate(nears):
+        base = (j + 1) * own.shape[0]
+        far = lax.ppermute(near, "dp", [(i, i ^ 1) for i in range(places)])
+        layout += [(base, half, True), (base, half, False)]
+        parts += [near, far]
+    return layout, parts
 
 
 def home(parts):
@@ -769,7 +960,7 @@
 
 
 def to_lanes_rows(size):
-    return -(-size // 1024) * 8
+    return -(-size // 2048) * 16
 
 
 def to_lanes(part):
@@ -802,16 +993,16 @@
     mod = jnp.pad(mod.astype(F32).reshape(images, 6, width), ((0, 0), (0, 2), (0, 0)))
 
     weight_own = jnp.transpose(attn_qkv.reshape(width, -1))
-    weight_t = jnp.concatenate([weight_own] + from_others(weight_own), axis=0)
-    out_w = jnp.concatenate([attn_out] + from_others(attn_out), axis=0)
-    table = jnp.concatenate(
-        [rel_table] + [shift_mp(rel_table, s) for s in range(1, ways)], axis=0
-    )
-    bias = bias_whole(table)
-    weight_t, out_w, late_up, late_down = lax.optimization_barrier(
-        (weight_t, out_w, mlp_up, mlp_down)
-    )
-    near_up = near_halves(late_up)
+    tables = [rel_table] + [shift_mp(rel_table, s) for s in range(1, ways)]
+    mod, tables, weight_sent, out_sent = lax.optimization_barrier(
+        (mod, tables, weight_own, attn_out)
+    )
+    near_w, near_o = near_halves(weight_sent), near_halves(out_sent)
+    weight = gathered_parts(weight_own, near_w)
+    out_weight = gathered_parts(attn_out, near_o)
+    fetch = ways == 2 and lax.axis_size("dp") % 2 == 0 and mlp_up.shape[0] % 32 == 0
+    fetch = fetch and mlp_down.shape[0] % 32 == 0
+    bias = bias_whole(jnp.concatenate(tables, axis=0))
 
     own_kept = lax.dynamic_slice_in_dim(kept_ids, place * images, images, 0)
     own_kept = jnp.pad(own_kept, ((0, 0), (0, padded - keep)), constant_values=-1)
@@ -828,15 +1019,17 @@
     dmlp = (mod[:, 5:6] * grads.astype(F32)).astype(BF).reshape(-1, width)
     grads = grads.reshape(-1, width)
 
-    near_up, bias, mod, late_down = lax.optimization_barrier((near_up, bias, mod, late_down))
-    near_down = near_halves(late_down)
-    up_others = with_far_halves(near_up)
-    first, qkv, att, lse, middle, second, branch = forward(
-        tokens, mod, pick, weight_t, out_w, bias, per_block
-    )
-    near_down, second = lax.optimization_barrier((near_down, second))
-    down_others = with_far_halves(near_down)
-    (branch_mlp, dsecond, grads_own), tile_own = mlp(second, dmlp, mlp_up, mlp_down)
+    first, qkv, att, lse, middle, second, branch, *near_up = forward(
+        tokens, mod, pick, bias, weight, out_weight, per_block, mlp_up if fetch else None
+    )
+    (branch_mlp, dsecond, grads_own, *whole), tile_own = mlp(
+        second, dmlp, mlp_up, mlp_down, None, (near_up[0], mlp_down) if fetch else None
+    )
+    if fetch:
+        up_others, down_others = [whole[0]], [whole[1]]
+    else:
+        up_others = with_far_halves(near_halves(mlp_up))
+        down_others = with_far_halves(near_halves(mlp_down))
     reduced = [scatter_dp(grads_own)]
     for up, down in zip(up_others, down_others):
         (branch_mlp, dsecond, grads_next), _ = mlp(
@@ -844,8 +1037,8 @@
         )
         reduced.append(scatter_dp(grads_next))
     out, dtok, dmod, dattn, dqkv, strips = backward(
-        tokens, mod, pick, weight_t, out_w, bias, qkv, lse, middle, branch, branch_mlp, dsecond,
-        grads, per_block,
+        tokens, mod, pick, bias, qkv, lse, middle, branch, branch_mlp, dsecond, grads,
+        weight, out_weight, per_block,
     )
     proj_block, out_block = weight_own.shape[0], attn_out.shape[0]
     dqkv, reduced[0] = lax.optimization_barrier((dqkv, reduced[0]))
@@ -860,12 +1053,12 @@
             parts = (
                 lax.dynamic_slice_in_dim(dmod_rows, at * cols, cols, 1),
                 dtables[steps * per_block : (steps + 1) * per_block],
-                own_cond_rows.astype(F32),
+                own_cond_rows,
             )
-            packs.append(jnp.concatenate([to_lanes(part) for part in parts], axis=0))
+            packs.append(jnp.concatenate([to_lanes(part.astype(BF)) for part in parts], axis=0))
         attn_sums, every = attn_grads(first, dattn, dqkv, att, *packs)
         places = every.shape[0]
-        every = every.reshape(places * ways, -1, 128)
+        every = every.astype(F32).reshape(places * ways, -1, 128)
         got, end = [], 0
         for part in parts:
             start, end = end, end + to_lanes_rows(part.size)
@@ -874,7 +1067,7 @@
         dtable = jnp.sum(got[1], axis=0).reshape(rel_table.shape)
         all_cond = got[2].reshape(-1, width)
         dcolumns = lax.dynamic_slice_in_dim(
-            all_columns, lax.axis_index("dp") * images_group, images_group, 0
+            all_columns, pack_slot(lax.axis_index("dp")) * images_group, images_group, 0
         )
     else:
         dweight = dot(first, dqkv, (0, 1)).astype(BF)

time: 814 us -> 656 us (0.81)
  waiting for transfers between devices: 124 us -> 66.7 us
  local copies, waits for them, and re-layouts: 105 us -> 52.6 us
  Pallas kernels: 506 us -> 464 us
    pallas_call x1, Pallas kernels: 205 us -> 127 us  [attn_grads(): pl.pallas_call(attn_grads_kernel, in_specs=[vmem] * 6, out_specs=[vmem] *...]
    all_to_all x1, waiting for transfers between devices: 48.4 us -> 1.92 us  [local(): mod = lax.all_to_all(columns, 'mp', split_axis=0, concat_axis=1, tiled=True)]
    pallas_call x4, Pallas kernels: 291 us -> 327 us  [the longest x2 174 us: mlp(): pl.pallas_call(functools.partial(mlp_kernel, chunk, fresh, fetch is not N...]
    dynamic_update_slice x8 -> x0, local copies, waits for them, and re-layouts: 18.1 us -> none  [the longest x4 10 us: with_far_halves(): lax.dynamic_update_slice_in_dim(whole, far, (1 - core) * half, 0)]
    another operation x17, local copies, waits for them, and re-layouts: 24.6 us -> 8.39 us  [bias_whole(): jnp.stack([grid_table[:, :, GRID - 1 - c:2 * GRID - 1 - c] for c in range...]
    dynamic_slice x4 -> x2, local copies, waits for them, and re-layouts: 11 us -> 1.77 us  [near_halves(): mine = lax.dynamic_slice_in_dim(block, core * half, half, 0)]
    ppermute x4 -> x2, waiting for transfers between devices: 8.84 us -> 0.01 us  [gathered_parts(): far = lax.ppermute(near, 'dp', [(i, i ^ 1) for i in range(places)])]
    concatenate x3 -> x1, other arithmetic: 9.42 us -> 0.65 us  [local(): jnp.concatenate([to_lanes(part.astype(BF)) for part in parts], axis=0)]
  transfers between devices with their start and end apart: 15 -> 11, of which waited for: 6 -> 4; matrix products, arithmetic and copies ran while one was open for 13% -> 10% of each run, Pallas kernels for 54% -> 47%
where the time goes in v3:
time: 656 us; the launch traced here: 645 us
  Pallas kernels  464 us (71%)
  waiting for transfers between devices  66.7 us (10%)
  local copies, waits for them, and re-layouts  52.6 us (8%)
  other arithmetic  18.3 us (3%)
  starting transfers between devices  15.7 us (2%)
  between operations  15 us (2%)
  matrix products  12.4 us (2%)
    pallas_call x2, Pallas kernels, mlp(): pl.pallas_call(functools.partial(mlp_kernel, chunk, fresh, fetch is not N...  174 us
    pallas_call x1, Pallas kernels, attn_grads(): pl.pallas_call(attn_grads_kernel, in_specs=[vmem] * 6, out_specs=[vmem] *...  127 us
    pallas_call x1, Pallas kernels, backward(): pl.pallas_call(functools.partial(backward_kernel, per_block, weight_layou...  87.7 us
    pallas_call x1, Pallas kernels, forward(): pl.pallas_call(functools.partial(forward_kernel, per_block, weight_layout...  65.9 us
    ppermute x5, waiting for transfers between devices, shift_mp(): lax.ppermute(value, 'mp', [(i, (i - steps) % ways) for i in range(ways)])  64.8 us
  transfers between devices with their start and end apart: 11, of which 4 were waited for; matrix products, arithmetic and copies ran while one was open for 10% of the time, Pallas kernels for 47%

profile of v3, /device:TPU:0, one launch (start us, length us, event | category | flops | bytes accessed | tf_op | source)
XLA Modules:
  0.0 644.7 jit_solution(13870863660187036042)
XLA Ops:
  7.2 4.4 fusion.2
  11.6 0.7 all_to_all.13
  12.3 4.2 all-to-all-start
  16.5 2.1 collective-permute-start
  18.6 1.9 all-to-all-done
  20.6 0.7 pad_convert_fusion.refs_1_.refs_7_
  21.3 1.7 constant_dynamic-slice_fusion.3
  23.0 1.3 collective-permute-start.1
  24.3 43.1 %collective-permute-done.1.refs_5_.refs_1_ = bf16[864,1152]{1,0:T(8,128)(2,1)} collective-permute-done((bf16[864,1152]{1,0:T(8,128)(2,1)S(1)}, bf16[864,1152]{1,0:T(8,128)(2,1)}, u32[]{:S(2)}, u32[]{:S(2)}) %collective-permute-start.1) | collective-permute-done | bytes 1990688 | tf_op jit(solution)/shard_map/ppermute | solution.py:918
  67.4 1.9 reshape.172
  69.4 1.0 collective-permute-start.3
  70.4 3.4 fusion.3
  73.8 13.0 %collective-permute-done.3.refs_8_.refs_4_ = bf16[288,1152]{1,0:T(8,128)(2,1)} collective-permute-done((bf16[288,1152]{1,0:T(8,128)(2,1)S(1)}, bf16[288,1152]{1,0:T(8,128)(2,1)}, u32[]{:S(2)}, u32[]{:S(2)}) %collective-permute-start.3) | collective-permute-done | bytes 663584 | tf_op jit(solution)/shard_map/ppermute | solution.py:918
  86.9 0.9 fusion.4.refs_2_.refs_8_
  88.1 2.0 fusion.27
  90.1 1.1 stack.68
  91.2 1.1 stack.69
  92.3 1.1 stack.70
  93.4 1.1 stack.71
  94.5 0.8 stack.72
  97.1 1.5 stack.67
  98.6 0.8 pad.105.strip_ref
  99.5 9.5 %shard_map.203.refs_3_.refs_9_ = f32[16,256,256]{2,1,0:T(8,128)} custom-call(f32[16,16,512]{2,1,0:T(8,128)} %pad.105.strip_ref), custom_call_target="tpu_custom_call" | custom-call | bytes 4194304 | tf_op jit(solution)/shard_map/pallas_call | solution.py:84
  109.0 0.9 slice.189
  109.9 4.9 fusion.dmlp_ref
  114.9 65.9 %shard_map.204 = (bf16[1024,1152]{1,0:T(8,128)(2,1)}, bf16[3456,1024]{1,0:T(8,128)(2,1)}, bf16[1152,2048]{1,0:T(8,128)(2,1)}, f32[4,32,256]{2,1,0:T(8,128)}, f32...) custom-call(bf16[1024,1152]{1,0:T(8,128)(2,1)} %refs_6_.1, ...), custom_call_target="tpu_custom_call" | custom-call | flops 8000000000 | bytes 32000000 | tf_op jit(solution)/shard_map/pallas_call | solution.py:276
  180.8 94.4 %shard_map.205 = (f32[1792,1152]{1,0:T(8,128)}, f32[1792,1152]{1,0:T(8,128)}, bf16[1152,4608]{1,0:T(8,128)(2,1)}, bf16[1152,2304]{1,0:T(8,128)(2,1)}, bf16[2304,1152]{1,0:T(8,128)(2,1)}) custom-call(bf16[1792,1152]{1,0:T(8,128)(2,1)} %get-tuple-element.51.second_ref, bf16[1792,1152]{1,0:T(8,128)(2,1)} %fusion.dmlp_ref, bf16[1152,2304]{1,0:T(8,128)(2,1)} %up_ref.1, ...), custom_call_target="tpu_custom_call" | custom-call | flops 60000002048 | bytes 60000000 | tf_op jit(solution)/shard_map/pallas_call | solution.py:469
  275.2 79.3 %shard_map.206 = (f32[1792,1152]{1,0:T(8,128)}, f32[1792,1152]{1,0:T(8,128)}, bf16[1152,4608]{1,0:T(8,128)(2,1)}) custom-call(bf16[1792,1152]{1,0:T(8,128)(2,1)} %get-tuple-element.51.second_ref, bf16[1792,1152]{1,0:T(8,128)(2,1)} %fusion.dmlp_ref, bf16[1152,2304]{1,0:T(8,128)(2,1)} %get-tuple-element.53.up_ref, ...), custom_call_target="tpu_custom_call" | custom-call | flops 10000000 | bytes 100000 | tf_op jit(solution)/shard_map/pallas_call | solution.py:469
  355.4 87.7 %shard_map.207 = (bf16[1792,1152]{1,0:T(8,128)(2,1)}, bf16[1024,1152]{1,0:T(8,128)(2,1)}, f32[4,8,1152]{2,1,0:T(8,128)}, bf16[2048,1152]{1,0:T(8,128)(2,1)}, bf1...) custom-call(bf16[1728,1152]{1,0:T(8,128)(2,1)} %bitcast.130, bf16[864,1152]{1,0:T(8,128)(2,1)} %collective-permute-done.1.refs_5_.refs_1_, ...), custom_call_target="tpu_custom_call" | custom-call | flops 10000000 | bytes 100000 | tf_op jit(solution)/shard_map/pallas_call | solution.py:617
  443.2 1.6 slice.246
  444.8 3.3 slice.247
  448.3 3.3 reshape.179
  451.6 2.9 slice_bitcast_fusion.15
  454.5 1.1 add_convert_fusion
  456.1 1.6 reshape.174
  457.7 0.6 pad_maximum_fusion.1
  458.3 127.1 %shard_map.208 = (bf16[12,144,384]{2,1,0:T(8,128)(2,1)}, bf16[16,2,224,128]{3,2,1,0:T(8,128)(2,1)}) custom-call(bf16[1024,1152]{1,0:T(8,128)(2,1)} %get-tuple-element.61.first_ref, bf16[2048,1152]{1,0:T(8,128)(2,1)} %get-tuple-element.62.dattn_ref, bf16[3456,1024]{1,0:T(8,128)(2,1)} %get-tuple-element.65.dqkv_ref, ...), custom_call_target="tpu_custom_call" | custom-call | flops 10000000 | bytes 100000 | tf_op jit(solution)/shard_map/pallas_call | solution.py:884
  585.4 1.2 slice.272
  586.7 1.0 slice.270
  587.7 1.9 bitcast_convert_fusion
  589.7 2.3 copy-done.5
  592.4 0.8 pad_maximum_fusion
  593.2 1.7 collective-permute-start.5
  595.3 1.7 reshape.194
  597.8 1.3 slice.267
  599.2 2.0 reshape.189
  601.3 5.5 fusion.5
  606.8 0.6 reshape.190
  607.4 3.2 all-to-all-start.1
  610.7 0.6 copy.137
  611.3 2.5 fusion.14
  613.9 0.7 reduce_sum.28
  614.6 0.7 reshape.199
  615.3 2.0 collective-permute-start.6
  617.3 0.6 fusion.21
  618.0 1.1 convert_add_fusion.1
  619.4 0.8 copy.106
  620.2 0.8 slice_bitcast_fusion.16
  621.0 8.6 %collective-permute-done.6 = bf16[72,4608]{1,0:T(8,128)(2,1)S(1)} collective-permute-done((bf16[72,4608]{1,0:T(8,128)(2,1)}, bf16[72,4608]{1,0:T(8,128)(2,1)S(1)}, u32[]{:S(2)}, u32[]{:S(2)}) %collective-permute-start.6) | collective-permute-done | bytes 663584 | tf_op jit(solution)/shard_map/ppermute | solution.py:918
  629.7 1.3 convert_add_fusion
  630.9 0.9 reshape.197
  631.8 3.9 slice_reduce_fusion.1
  635.7 1.0 copy.129
  636.7 1.0 copy.128
  (83 shorter events, 5.5 us)
Async XLA Ops:
  7.2 63.2 %copy-start = (s32[8,179]{1,0:T(8,128)S(1)}, s32[8,179]{1,0:T(8,128)}, u32[]{:S(2)}) copy-start(s32[8,179]{1,0:T(8,128)} %param.14) | copy-start | bytes 17188
  7.2 9.3 %copy-start.8 = (f32[8,961]{1,0:T(8,128)S(1)}, f32[8,961]{1,0:T(8,128)}, u32[]{:S(2)}) copy-start(f32[8,961]{1,0:T(8,128)} %param.21) | copy-start | bytes 92260
  11.6 57.7 %copy-start.3 = (bf16[576,1152]{1,0:T(8,128)(2,1)S(1)}, bf16[576,1152]{1,0:T(8,128)(2,1)}, u32[]{:S(2)}) copy-start(bf16[576,1152]{1,0:T(8,128)(2,1)} %refs_3_.1) | copy-start | bytes 3981316
  12.3 8.3 %all-to-all-start = ((bf16[2,4,3456]{2,1,0:T(4,128)(2,1)}), bf16[2,4,3456]{2,1,0:T(4,128)(2,1)S(1)}, u32[]{:S(2)}, u32[]{:S(2)}) async-start(bf16[2,4,3456]{2,1,0:T(4,128)(2,1)} %all_to_all.13), calls=%async_computation | async-start | bytes 110592 | tf_op jit(solution)/shard_map/all_to_all | solution.py:992
  16.5 441.9 %reduce-scatter.3.cloned.1.call-start = ((), (), s32[]{:S(2)}) async-start(), calls=%async_computation.4 | async-start | bytes 11280384 | tf_op jit(solution)/shard_map/reduce_scatter | solution.py:973
  16.5 4.8 collective-permute-start
  23.0 44.4 %collective-permute-start.1 = (bf16[864,1152]{1,0:T(8,128)(2,1)S(1)}, bf16[864,1152]{1,0:T(8,128)(2,1)}, u32[]{:S(2)}, u32[]{:S(2)}) collective-permute-start(bf16[864,1152]{1,0:T(8,128)(2,1)S(1)} %constant_dynamic-slice_fusion.3), channel_id=1, source_target_pairs={{0,1},{1,0},{2,3},{3,2},{4,5},{5,4},{6,7},{7,6},{8,9},{9,8},{10,11... | collective-permute-start | bytes 5971976 | tf_op jit(solution)/shard_map/ppermute | solution.py:918
  67.4 47.5 %collective-permute-start.2 = (bf16[864,1152]{1,0:T(8,128)(2,1)}, bf16[864,1152]{1,0:T(8,128)(2,1)}, u32[]{:S(2)}, u32[]{:S(2)}) collective-permute-start(bf16[864,1152]{1,0:T(8,128)(2,1)} %collective-permute-done.1.refs_5_.refs_1_), channel_id=1, source_target_pairs={{0,2},{2,0},{4,6},{6,4},{8,10},{10,8},{12,14},{14,12},{16,18},{18,... | collective-permute-start | bytes 5971976 | tf_op jit(solution)/shard_map/ppermute | solution.py:949
  69.4 17.5 %collective-permute-start.3 = (bf16[288,1152]{1,0:T(8,128)(2,1)S(1)}, bf16[288,1152]{1,0:T(8,128)(2,1)}, u32[]{:S(2)}, u32[]{:S(2)}) collective-permute-start(bf16[288,1152]{1,0:T(8,128)(2,1)S(1)} %constant_dynamic-slice_fusion.2), channel_id=1, source_target_pairs={{0,1},{1,0},{2,3},{3,2},{4,5},{5,4},{6,7},{7,6},{8,9},{9,8},{10,11... | collective-permute-start | bytes 1990664 | tf_op jit(solution)/shard_map/ppermute | solution.py:918
  86.9 28.0 %collective-permute-start.4 = (bf16[288,1152]{1,0:T(8,128)(2,1)}, bf16[288,1152]{1,0:T(8,128)(2,1)}, u32[]{:S(2)}, u32[]{:S(2)}) collective-permute-start(bf16[288,1152]{1,0:T(8,128)(2,1)} %collective-permute-done.3.refs_8_.refs_4_), channel_id=1, source_target_pairs={{0,2},{2,0},{4,6},{6,4},{8,10},{10,8},{12,14},{14,12},{16,18},{18,... | collective-permute-start | bytes 1990664 | tf_op jit(solution)/shard_map/ppermute | solution.py:949
  275.2 340.1 %reduce-scatter.5.cloned.1.call-start = ((), (), s32[]{:S(2)}) async-start(), calls=%async_computation.5 | async-start | bytes 11280384 | tf_op jit(solution)/shard_map/reduce_scatter | solution.py:973
  354.6 0.7 copy-start.6
  443.2 5.0 copy-start.7
  443.2 5.1 copy-start.4
  589.7 2.5 copy-start.2
  589.7 2.3 copy-start.5
  592.4 4.9 slice-start
  593.2 24.8 %collective-permute-start.5 = (bf16[72,2304]{1,0:T(8,128)(2,1)}, bf16[72,2304]{1,0:T(8,128)(2,1)}, u32[]{:S(2)}, u32[]{:S(2)}) collective-permute-start(bf16[72,2304]{1,0:T(8,128)(2,1)} %pad_maximum_fusion), channel_id=1, source_target_pairs={{0,1},{1,0},{2,3},{3,2},{4,5},{5,4},{6,7},{7,6},{8,9},{9,8},{10,11... | collective-permute-start | bytes 995336 | tf_op jit(solution)/shard_map/ppermute | solution.py:918
  601.3 9.4 %slice-start.1 = ((f32[32,224,128]{2,1,0:T(8,128)}), f32[32,64,128]{2,1,0:T(8,128)S(1)}, s32[]{:S(2)}) async-start(f32[32,224,128]{2,1,0:T(8,128)} %copy-done.2), calls=%async_computation.7 | async-start | bytes 2097152 | tf_op jit(solution)/shard_map/slice | solution.py:1065
  607.4 9.9 %all-to-all-start.1 = ((bf16[2,4,1152]{2,1,0:T(4,128)(2,1)}), bf16[2,4,1152]{2,1,0:T(4,128)(2,1)S(1)}, u32[]{:S(2)}, u32[]{:S(2)}) async-start(bf16[2,4,1152]{2,1,0:T(4,128)(2,1)} %reshape.190), calls=%async_computation.2 | async-start | bytes 36864 | tf_op jit(solution)/shard_map/all_to_all | solution.py:1110
  615.3 14.3 %collective-permute-start.6 = (bf16[72,4608]{1,0:T(8,128)(2,1)}, bf16[72,4608]{1,0:T(8,128)(2,1)S(1)}, u32[]{:S(2)}, u32[]{:S(2)}) collective-permute-start(bf16[72,4608]{1,0:T(8,128)(2,1)} %reduce-scatter.5.cloned.1.call-done), channel_id=1, source_target_pairs={{0,1},{1,0},{2,3},{3,2},{4,5},{5,4},{6,7},{7,6},{8,9},{9,8},{10,11... | collective-permute-start | bytes 1990664 | tf_op jit(solution)/shard_map/ppermute | solution.py:918
  629.7 8.0 %copy-start.1 = (s32[8,179]{1,0:T(8,128)S(1)}, s32[8,179]{1,0:T(8,128)}, u32[]{:S(2)}) copy-start(s32[8,179]{1,0:T(8,128)} %param.14) | copy-start | bytes 17188
Sparse Core Ops, SparseCore 0:
  275.3 121.3 reduce-scatter.2
  400.7 149.6 reduce-scatter.4

commit v4 on v3

--- a/solution.py
+++ b/solution.py
@@ -88,7 +88,7 @@
         out_specs=pl.BlockSpec((1, PATCHES, PATCHES), lambda h: (h, 0, 0)),
         out_shape=jax.ShapeDtypeStruct((heads, PATCHES, PATCHES), F32),
         compiler_params=params(),
-        cost_estimate=cost(0, heads * PATCHES * PATCHES * 4),
+        cost_estimate=cost(1e6, 1e5),
     )(strip)
 
 
@@ -129,15 +129,30 @@
         copy.wait()
 
 
-def start_fetch(own, target, sems):
-    half = target.shape[0]
-    start = (lax.axis_index("dp") % 2) * half
+def core_rows(half, skip, count):
+    start = (lax.axis_index("dp") % 2) * half + skip
+    return pl.ds(pl.multiple_of(start, 16), count)
+
+
+def fetch_copy(own, rows, target, sems, at):
     return pltpu.make_async_remote_copy(
-        src_ref=own.at[pl.ds(pl.multiple_of(start, 16), half), :],
+        src_ref=own.at[rows, :],
         dst_ref=target,
-        send_sem=sems.at[0],
-        recv_sem=sems.at[1],
+        send_sem=sems.at[at],
+        recv_sem=sems.at[at + 1],
         device_id={"mp": 1 - lax.axis_index("mp")},
+        device_id_type=pl.DeviceIdType.MESH,
+    )
+
+
+def core_copy(source, target, sems, at):
+    place = lax.axis_index("dp")
+    return pltpu.make_async_remote_copy(
+        src_ref=source,
+        dst_ref=target,
+        send_sem=sems.at[at],
+        recv_sem=sems.at[at + 1],
+        device_id={"dp": place + 1 - 2 * (place % 2)},
         device_id_type=pl.DeviceIdType.MESH,
     )
 
@@ -155,18 +170,111 @@
     pl.semaphore_wait(barrier, len(peers))
 
 
+def project(weight_ref, first, qkv_s, qkv_ref, base):
+    step = weight_ref.shape[0] // 3
+    for c in range(3):
+        part = nt(weight_ref[c * step : (c + 1) * step, :], first)
+        qkv_s[c * step : (c + 1) * step, :] = part
+        qkv_ref[base + c * step : base + (c + 1) * step, :] = part.astype(BF)
+
+
+def attend_heads(per_block, first_head, qkv_s, bias_ref, mask, att_s, attk_s, lse_s):
+    scale = HEAD_DIM ** (-0.5) * LOG2E
+    heads = qkv_s.shape[0] // (3 * HEAD_DIM)
+
+    def one_head(head, carry):
+        q_at, k_at, v_at = head_rows(head, per_block)
+        queries = qkv_s[q_at, :].astype(BF)
+        keys = qkv_s[k_at, :].astype(BF)
+        values = qkv_s[v_at, :].astype(BF)
+        scores = tn(keys, queries) * scale + bias_ref[first_head + head]
+        here = pl.ds(pl.multiple_of(head * HEAD_DIM, 8), HEAD_DIM)
+
+        def attend(scores):
+            top = jnp.max(scores, axis=0, keepdims=True)
+            weights = jnp.exp2(scores - top)
+            total = jnp.sum(weights, axis=0, keepdims=True)
+            probs = (weights * (1.0 / total)).astype(BF)
+            return nn(values, probs), top + jnp.log2(total)
+
+        att_s[here, :], lse_s[pl.ds(head, 1), :] = attend(scores)
+        attk_s[here, :], lse_s[pl.ds(heads + head, 1), :] = attend(scores + mask)
+        return carry
+
+    lax.fori_loop(0, heads, one_head, 0, unroll=4 if heads % 4 == 0 else 2)
+
+
+def own_heads_kernel(
+    per_block, tok_ref, mod_ref, pick_ref, bias_ref, weight_ref,
+    first_ref, qkv_ref, att_ref, lse_ref, qkv_s, att_s, attk_s, lse_s,
+):
+    shift_one, scale_one = mod_ref[0, 0:1], mod_ref[0, 1:2]
+    normed, _ = normalize(tok_ref[...].astype(F32))
+    first = (normed * (1.0 + scale_one) + shift_one).astype(BF)
+    first_ref[...] = first
+    project(weight_ref, first, qkv_s, qkv_ref, 0)
+    mask = key_mask(pick_ref[0])
+    attend_heads(per_block, 0, qkv_s, bias_ref, mask, att_s, attk_s, lse_s)
+    att_ref[:, :PATCHES] = att_s[...].astype(BF)
+    att_ref[:, PATCHES:] = attk_s[...].astype(BF)
+    lse_ref[0] = lse_s[...]
+
+
+def own_heads(tokens, mod, pick, bias, weight, per_block):
+    images, padded = pick.shape[0], pick.shape[1]
+    width = tokens.shape[1]
+    proj = weight.shape[0]
+    heads = proj // (3 * HEAD_DIM)
+    inner = heads * HEAD_DIM
+    return pl.pallas_call(
+        functools.partial(own_heads_kernel, per_block),
+        grid=(images,),
+        in_specs=[
+            pl.BlockSpec((PATCHES, width), lambda i: (i, 0)),
+            pl.BlockSpec((1, 8, width), lambda i: (i, 0, 0)),
+            pl.BlockSpec((1, padded, PATCHES), lambda i: (i, 0, 0)),
+            const_spec(bias.shape),
+            const_spec(weight.shape),
+        ],
+        out_specs=[
+            pl.BlockSpec((PATCHES, width), lambda i: (i, 0)),
+            pl.BlockSpec((proj, PATCHES), lambda i: (0, i)),
+            pl.BlockSpec((inner, 2 * PATCHES), lambda i: (0, i)),
+            pl.BlockSpec((1, 2 * heads, PATCHES), lambda i: (i, 0, 0)),
+        ],
+        out_shape=[
+            jax.ShapeDtypeStruct((images * PATCHES, width), BF),
+            jax.ShapeDtypeStruct((proj, images * PATCHES), BF),
+            jax.ShapeDtypeStruct((inner, images * 2 * PATCHES), BF),
+            jax.ShapeDtypeStruct((images, 2 * heads, PATCHES), F32),
+        ],
+        scratch_shapes=[
+            pltpu.VMEM((proj, PATCHES), F32),
+            pltpu.VMEM((inner, PATCHES), F32),
+            pltpu.VMEM((inner, PATCHES), F32),
+            pltpu.VMEM((2 * heads, PATCHES), F32),
+        ],
+        compiler_params=params(),
+        cost_estimate=cost(1e7, 1e5),
+    )(tokens, mod, pick, bias, weight)
+
+
 def forward_kernel(per_block, weight_layout, out_layout, fetch, *refs):
-    tok_ref, mod_ref, pick_ref, bias_ref = refs[:4]
-    refs = refs[4:]
+    first_ref, own_qkv, own_att, own_lse, tok_ref, mod_ref, pick_ref, bias_ref = refs[:8]
+    refs = refs[8:]
     weight_parts, refs = refs[: len(weight_layout)], refs[len(weight_layout) :]
     out_parts, refs = refs[: len(out_layout)], refs[len(out_layout) :]
     if fetch:
         send_ref, refs = refs[0], refs[1:]
-    first_ref, qkv_ref, att_ref, lse_ref, middle_ref, second_ref, branch_ref = refs[:7]
-    refs = refs[7:]
+    qkv_ref, att_ref, lse_ref, middle_ref, second_ref, branch_ref = refs[:6]
+    refs = refs[6:]
     if fetch:
         got_ref, refs = refs[0], refs[1:]
-    qkv_s, att_s, attk_s, weight_ref, out_w_ref, part_sems, fetch_sems = refs
+    qkv_s, att_s, attk_s, lse_s, weight_ref, out_w_ref, part_sems, fetch_sems = refs
+
+    def fetching():
+        half = send_ref.shape[0] // 2
+        return fetch_copy(send_ref, core_rows(half, 0, got_ref.shape[0]), got_ref, fetch_sems, 0)
 
     @pl.when(pl.program_id(0) == 0)
     def _():
@@ -174,71 +282,32 @@
         copies += part_copies(out_layout, out_parts, out_w_ref, part_sems.at[1])
         if fetch:
             greet_peers(False)
-            start_fetch(send_ref, got_ref, fetch_sems).start()
+            fetching().start()
         run_copies(copies)
 
-    forward_body(
-        per_block, tok_ref, mod_ref, pick_ref, weight_ref, out_w_ref, bias_ref,
-        first_ref, qkv_ref, att_ref, lse_ref, middle_ref, second_ref, branch_ref,
-        qkv_s, att_s, attk_s,
-    )
-    if fetch:
-
-        @pl.when(pl.program_id(0) == pl.num_programs(0) - 1)
-        def _():
-            start_fetch(send_ref, got_ref, fetch_sems).wait()
-
-
-def forward_body(
-    per_block, tok_ref, mod_ref, pick_ref, weight_ref, out_w_ref, bias_ref,
-    first_ref, qkv_ref, att_ref, lse_ref, middle_ref, second_ref, branch_ref,
-    qkv_s, att_s, attk_s,
-):
+    own = own_qkv.shape[0]
+    own_inner = own // 3
+    own_count = own_inner // HEAD_DIM
     heads = bias_ref.shape[0]
-    tok = tok_ref[...].astype(F32)
-    shift_one, scale_one, gate_one = mod_ref[0, 0:1], mod_ref[0, 1:2], mod_ref[0, 2:3]
+    others = heads - own_count
+    pick = pick_ref[0]
+    qkv_ref[:own, :] = own_qkv[...]
+    project(weight_ref, first_ref[...], qkv_s, qkv_ref, own)
+    mask = key_mask(pick)
+    attend_heads(per_block, own_count, qkv_s, bias_ref, mask, att_s, attk_s, lse_s)
+    att_ref[:own_inner, :] = own_att[...]
+    att_ref[own_inner:, :PATCHES] = att_s[...].astype(BF)
+    att_ref[own_inner:, PATCHES:] = attk_s[...].astype(BF)
+    lse_ref[0, :own_count, :] = own_lse[0, :own_count]
+    lse_ref[0, own_count:heads, :] = lse_s[:others]
+    lse_ref[0, heads : heads + own_count, :] = own_lse[0, own_count:]
+    lse_ref[0, heads + own_count :, :] = lse_s[others:]
+    gate_one = mod_ref[0, 2:3]
     shift_two, scale_two = mod_ref[0, 3:4], mod_ref[0, 4:5]
-    normed, _ = normalize(tok)
-    first = (normed * (1.0 + scale_one) + shift_one).astype(BF)
-    first_ref[...] = first
-    step = weight_ref.shape[0] // 6
-    for c in range(6):
-        rows = slice(c * step, (c + 1) * step)
-        part = nt(weight_ref[rows, :], first)
-        qkv_s[rows, :] = part
-        qkv_ref[rows, :] = part.astype(BF)
-    pick = pick_ref[0]
-    mask = key_mask(pick)
-    scale = HEAD_DIM ** (-0.5) * LOG2E
-
-    def one_head(head, carry):
-        q_at, k_at, v_at = head_rows(head, per_block)
-        queries = qkv_s[q_at, :].astype(BF)
-        keys = qkv_s[k_at, :].astype(BF)
-        values = qkv_s[v_at, :].astype(BF)
-        scores = tn(keys, queries) * scale + bias_ref[head]
-        here = pl.ds(pl.multiple_of(head * HEAD_DIM, 8), HEAD_DIM)
-
-        def attend(scores):
-            top = jnp.max(scores, axis=0, keepdims=True)
-            weights = jnp.exp2(scores - top)
-            total = jnp.sum(weights, axis=0, keepdims=True)
-            probs = (weights * (1.0 / total)).astype(BF)
-            return nn(values, probs), top + jnp.log2(total)
-
-        att_s[here, :], lse_ref[0, pl.ds(head, 1), :] = attend(scores)
-        attk_s[here, :], lse_ref[0, pl.ds(heads + head, 1), :] = attend(scores + mask)
-        return carry
-
-    lax.fori_loop(0, heads, one_head, 0, unroll=2)
-    att = att_s[...].astype(BF)
-    att_kept = attk_s[...].astype(BF)
-    att_ref[:, :PATCHES] = att
-    att_ref[:, PATCHES:] = att_kept
     out_w = out_w_ref[...]
-    kept_att = nt(pick, att_kept).astype(BF)
+    kept_att = nt(pick, att_ref[:, PATCHES:]).astype(BF)
     for rows, source, residual in (
-        (slice(0, PATCHES), att.T, tok),
+        (slice(0, PATCHES), att_ref[:, :PATCHES].T, tok_ref[...].astype(F32)),
         (slice(PATCHES, PATCHES + pick.shape[0]), kept_att, nn(pick, tok_ref[...])),
     ):
         branch = nn(source, out_w)
@@ -246,6 +315,11 @@
         middle = residual + gate_one * branch
         middle_ref[rows, :] = middle
         second_ref[rows, :] = (normalize(middle)[0] * (1.0 + scale_two) + shift_two).astype(BF)
+    if fetch:
+
+        @pl.when(pl.program_id(0) == pl.num_programs(0) - 1)
+        def _():
+            fetching().wait()
 
 
 def whole_rows(layout, parts):
@@ -255,28 +329,36 @@
 ANYWHERE = pl.BlockSpec(memory_space=pl.ANY)
 
 
-def forward(tokens, mod, pick, bias, weight, out_weight, per_block, send=None):
+def forward(own, tokens, mod, pick, bias, weight, out_weight, per_block, send=None, count=0):
     images, padded = pick.shape[0], pick.shape[1]
     width = tokens.shape[1]
     rows = PATCHES + padded
     heads = bias.shape[0]
     (weight_layout, weight_parts), (out_layout, out_parts) = weight, out_weight
-    proj = whole_rows(*weight)
+    proj_others = whole_rows(*weight)
+    proj = own[1].shape[0] + proj_others
+    own_inner, own_heads_count = own[2].shape[0], own[3].shape[1] // 2
+    others = heads - own_heads_count
     fetch = send is not None
     most = max(len(weight_parts), len(out_parts))
     extra_shapes, extra = [], []
     compiler_params = params()
     if fetch:
-        extra_shapes = [jax.ShapeDtypeStruct((send.shape[0] // 2, send.shape[1]), BF)]
+        extra_shapes = [jax.ShapeDtypeStruct((count, send.shape[1]), BF)]
         extra = [send]
         compiler_params = pltpu.CompilerParams(
             vmem_limit_bytes=VMEM_LIMIT, dimension_semantics=("arbitrary",),
             collective_id=2, has_side_effects=True,
         )
+    by_row = pl.BlockSpec((rows, width), lambda i: (i, 0))
     return pl.pallas_call(
         functools.partial(forward_kernel, per_block, weight_layout, out_layout, fetch),
         grid=(images,),
         in_specs=[
+            pl.BlockSpec((PATCHES, width), lambda i: (i, 0)),
+            pl.BlockSpec((own[1].shape[0], PATCHES), lambda i: (0, i)),
+            pl.BlockSpec((own_inner, 2 * PATCHES), lambda i: (0, i)),
+            pl.BlockSpec((1, 2 * own_heads_count, PATCHES), lambda i: (i, 0, 0)),
             pl.BlockSpec((PATCHES, width), lambda i: (i, 0)),
             pl.BlockSpec((1, 8, width), lambda i: (i, 0, 0)),
             pl.BlockSpec((1, padded, PATCHES), lambda i: (i, 0, 0)),
@@ -284,17 +366,15 @@
         ]
         + [ANYWHERE] * (len(weight_parts) + len(out_parts) + len(extra)),
         out_specs=[
-            pl.BlockSpec((PATCHES, width), lambda i: (i, 0)),
             pl.BlockSpec((proj, PATCHES), lambda i: (0, i)),
             pl.BlockSpec((width, 2 * PATCHES), lambda i: (0, i)),
             pl.BlockSpec((1, 2 * heads, PATCHES), lambda i: (i, 0, 0)),
-            pl.BlockSpec((rows, width), lambda i: (i, 0)),
-            pl.BlockSpec((rows, width), lambda i: (i, 0)),
-            pl.BlockSpec((rows, width), lambda i: (i, 0)),
+            by_row,
+            by_row,
+            by_row,
         ]
         + [ANYWHERE] * len(extra),
         out_shape=[
-            jax.ShapeDtypeStruct((images * PATCHES, width), BF),
             jax.ShapeDtypeStruct((proj, images * PATCHES), BF),
             jax.ShapeDtypeStruct((width, images * 2 * PATCHES), BF),
             jax.ShapeDtypeStruct((images, 2 * heads, PATCHES), F32),
@@ -304,17 +384,18 @@
         ]
         + extra_shapes,
         scratch_shapes=[
-            pltpu.VMEM((proj, PATCHES), F32),
-            pltpu.VMEM((width, PATCHES), F32),
-            pltpu.VMEM((width, PATCHES), F32),
-            pltpu.VMEM((proj, width), BF),
+            pltpu.VMEM((proj_others, PATCHES), F32),
+            pltpu.VMEM((others * HEAD_DIM, PATCHES), F32),
+            pltpu.VMEM((others * HEAD_DIM, PATCHES), F32),
+            pltpu.VMEM((2 * others, PATCHES), F32),
+            pltpu.VMEM((proj_others, width), BF),
             pltpu.VMEM((width, width), BF),
             pltpu.SemaphoreType.DMA((2, most)),
             pltpu.SemaphoreType.DMA((2,)),
         ],
         compiler_params=compiler_params,
         cost_estimate=cost(images * 2e9, images * 8e6),
-    )(tokens, mod, pick, bias, *weight_parts, *out_parts, *extra)
+    )(*own, tokens, mod, pick, bias, *weight_parts, *out_parts, *extra)
 
 
 def gelu_pair(pre):
@@ -330,8 +411,8 @@
     chunk, fresh, fetch, second_ref, dmlp_ref, up_ref, down_ref, *refs
 ):
     if fetch:
-        near_ref, send_ref = refs[:2]
-        *refs, moves, fetch_sems = refs[2:]
+        near_ref, send_up, send_down = refs[:3]
+        *refs, moves, fetch_sems = refs[3:]
         up_all, down_all = refs[3:5]
         refs = refs[:3] + refs[5:]
     if fresh:
@@ -343,31 +424,32 @@
     tile = up_ref.shape[1]
     width = second_ref.shape[1]
 
-    def half_moves(source, target, at):
-        place = lax.axis_index("dp")
-        half = source.shape[0]
-        rows = target.at[pl.ds(pl.multiple_of((place % 2) * half, 16), half), :]
-        return pltpu.make_async_remote_copy(
-            src_ref=source,
-            dst_ref=rows,
-            send_sem=moves.at[at],
-            recv_sem=moves.at[at + 1],
-            device_id={"dp": place + 1 - 2 * (place % 2)},
-            device_id_type=pl.DeviceIdType.MESH,
-        ), pltpu.make_async_copy(source, rows, moves.at[at + 2])
-
-    def down_half():
-        half = down_all.shape[0] // 2
-        start = (lax.axis_index("dp") % 2) * half
-        return down_all.at[pl.ds(pl.multiple_of(start, 16), half), :]
-
-    @pl.when(pl.program_id(0) == 0)
+    if fetch:
+        up_half, down_half = up_all.shape[0] // 2, down_all.shape[0] // 2
+        cut = near_ref.shape[0]
+        up_a = up_all.at[core_rows(up_half, 0, cut), :]
+        up_b = up_all.at[core_rows(up_half, cut, up_half - cut), :]
+        down_a = down_all.at[core_rows(down_half, 0, down_half), :]
+        lay_a = pltpu.make_async_copy(near_ref, up_a, moves.at[0])
+        pass_a = core_copy(near_ref, up_a, moves, 1)
+        pass_b = core_copy(up_b, up_b, moves, 3)
+        pass_down = core_copy(down_a, down_a, moves, 5)
+        fetch_b = fetch_copy(
+            send_up, core_rows(up_half, cut, up_half - cut), up_b, fetch_sems, 0
+        )
+        fetch_down = fetch_copy(
+            send_down, core_rows(down_half, 0, down_half), down_a, fetch_sems, 2
+        )
+    step, last = pl.program_id(0), pl.num_programs(0) - 1
+
+    @pl.when(step == 0)
     def _():
         if fetch:
             greet_peers(True)
-            start_fetch(send_ref, down_half(), fetch_sems).start()
-            for copy in half_moves(near_ref, up_all, 0):
-                copy.start()
+            fetch_b.start()
+            fetch_down.start()
+            lay_a.start()
+            pass_a.start()
         if fresh:
             branch_ref[...] = jnp.zeros_like(branch_ref)
             dsecond_ref[...] = jnp.zeros_like(dsecond_ref)
@@ -397,6 +479,18 @@
         return carry
 
     lax.fori_loop(0, rows // chunk, one_chunk, 0)
+    if fetch:
+
+        @pl.when(step == last // 2)
+        def _():
+            fetch_b.wait_recv()
+            pass_b.start()
+
+        @pl.when(step == last)
+        def _():
+            fetch_down.wait_recv()
+            pass_down.start()
+
     part = width // 3
     for c in range(3):
         at = slice(c * part, (c + 1) * part)
@@ -405,14 +499,12 @@
 
     if fetch:
 
-        @pl.when(pl.program_id(0) == pl.num_programs(0) - 1)
+        @pl.when(step == last)
         def _():
-            start_fetch(send_ref, down_half(), fetch_sems).wait()
-            last = half_moves(down_half(), down_all, 3)[0]
-            last.start()
-            for copy in half_moves(near_ref, up_all, 0):
+            for copy in (lay_a, pass_a, pass_b, pass_down):
                 copy.wait()
-            last.wait()
+            fetch_b.wait_send()
+            fetch_down.wait_send()
 
 
 def mlp_chunk(rows):
@@ -457,11 +549,11 @@
         in_specs += [ANYWHERE] * 2
         operands += list(sums)
     if fetch is not None:
-        in_specs += [ANYWHERE] * 2
+        in_specs += [ANYWHERE] * 3
         operands += list(fetch)
         out_specs += [ANYWHERE] * 2
         out_shape += [jax.ShapeDtypeStruct(up.shape, BF), jax.ShapeDtypeStruct(down.shape, BF)]
-        scratch += [pltpu.SemaphoreType.DMA((6,)), pltpu.SemaphoreType.DMA((2,))]
+        scratch += [pltpu.SemaphoreType.DMA((7,)), pltpu.SemaphoreType.DMA((4,))]
         compiler_params = pltpu.CompilerParams(
             vmem_limit_bytes=VMEM_LIMIT, dimension_semantics=("arbitrary",),
             collective_id=3, has_side_effects=True,
@@ -577,7 +669,7 @@
         qkv_s[v_at, :] = dvalues + dvalues_kept
         return carry
 
-    lax.fori_loop(0, heads, one_head, 0, unroll=2)
+    lax.fori_loop(0, heads, one_head, 0, unroll=4)
     dqkv = qkv_s[...].astype(BF)
     dqkv_ref[...] = dqkv
     dfirst = tn(dqkv, weight_ref[...])
@@ -938,18 +1030,27 @@
     return got
 
 
-def gathered_parts(own, nears):
-    half = own.shape[0] // 2
+def gathered_parts(nears, own=None):
+    half = nears[0].shape[0]
+    layout, parts, base = [], [], 0
+    if own is not None:
+        layout, parts, base = [(0, 0, True)], [own], own.shape[0]
     if half % 16:
-        return [(0, 0, True)], [jnp.concatenate([own] + with_far_halves(nears), axis=0)]
+        return [(0, 0, True)], [jnp.concatenate(parts + with_far_halves(nears), axis=0)]
     places = lax.axis_size("dp")
-    layout, parts = [(0, 0, True)], [own]
-    for j, near in enumerate(nears):
-        base = (j + 1) * own.shape[0]
+    for near in nears:
         far = lax.ppermute(near, "dp", [(i, i ^ 1) for i in range(places)])
         layout += [(base, half, True), (base, half, False)]
         parts += [near, far]
+        base += 2 * half
     return layout, parts
+
+
+def after_own(gathered, own):
+    layout, parts = gathered
+    return [(0, 0, True)] + [(base + own.shape[0], half, near) for base, half, near in layout], [
+        own
+    ] + parts
 
 
 def home(parts):
@@ -998,8 +1099,6 @@
         (mod, tables, weight_own, attn_out)
     )
     near_w, near_o = near_halves(weight_sent), near_halves(out_sent)
-    weight = gathered_parts(weight_own, near_w)
-    out_weight = gathered_parts(attn_out, near_o)
     fetch = ways == 2 and lax.axis_size("dp") % 2 == 0 and mlp_up.shape[0] % 32 == 0
     fetch = fetch and mlp_down.shape[0] % 32 == 0
     bias = bias_whole(jnp.concatenate(tables, axis=0))
@@ -1019,11 +1118,19 @@
     dmlp = (mod[:, 5:6] * grads.astype(F32)).astype(BF).reshape(-1, width)
     grads = grads.reshape(-1, width)
 
-    first, qkv, att, lse, middle, second, branch, *near_up = forward(
-        tokens, mod, pick, bias, weight, out_weight, per_block, mlp_up if fetch else None
+    own = own_heads(tokens, mod, pick, bias, weight_own, per_block)
+    near_w, near_o, own = lax.optimization_barrier((near_w, near_o, own))
+    first = own[0]
+    weight_others = gathered_parts(near_w)
+    weight = after_own(weight_others, weight_own)
+    out_weight = gathered_parts(near_o, attn_out)
+    cut = (mlp_up.shape[0] * 5 // 18) // 16 * 16
+    qkv, att, lse, middle, second, branch, *near_up = forward(
+        own, tokens, mod, pick, bias, weight_others, out_weight, per_block,
+        mlp_up if fetch else None, cut,
     )
     (branch_mlp, dsecond, grads_own, *whole), tile_own = mlp(
-        second, dmlp, mlp_up, mlp_down, None, (near_up[0], mlp_down) if fetch else None
+        second, dmlp, mlp_up, mlp_down, None, (near_up[0], mlp_up, mlp_down) if fetch else None
     )
     if fetch:
         up_others, down_others = [whole[0]], [whole[1]]

time: 656 us -> 609 us (0.928)
  waiting for transfers between devices: 66.7 us -> 23.7 us
    ppermute x5, waiting for transfers between devices: 64.8 us -> 21.7 us  [shift_mp(): lax.ppermute(value, 'mp', [(i, (i - steps) % ways) for i in range(ways)])]
    pallas_call x1, Pallas kernels: 65.9 us -> 41.2 us  [forward(): pl.pallas_call(functools.partial(forward_kernel, per_block, weight_layout...]
    pallas_call x0 -> x1, Pallas kernels: none -> 19.9 us  [own_heads(): pl.pallas_call(functools.partial(own_heads_kernel, per_block), grid=(imag...]
    pallas_call x2, Pallas kernels: 174 us -> 183 us  [mlp(): pl.pallas_call(functools.partial(mlp_kernel, chunk, fresh, fetch is not N...]
  transfers between devices with their start and end apart: 11 -> 11, of which waited for: 4 -> 3; matrix products, arithmetic and copies ran while one was open for 10% -> 10% of each run, Pallas kernels for 47% -> 54%
where the time goes in v4:
time: 609 us; the launch traced here: 603 us
  Pallas kernels  468 us (77%)
  local copies, waits for them, and re-layouts  53.2 us (9%)
  waiting for transfers between devices  23.7 us (4%)
  starting transfers between devices  15.5 us (3%)
  between operations  15 us (2%)
  other arithmetic  14.8 us (2%)
  matrix products  12.4 us (2%)
    pallas_call x2, Pallas kernels, mlp(): pl.pallas_call(functools.partial(mlp_kernel, chunk, fresh, fetch is not N...  183 us
    pallas_call x1, Pallas kernels, attn_grads(): pl.pallas_call(attn_grads_kernel, in_specs=[vmem] * 6, out_specs=[vmem] *...  128 us
    pallas_call x1, Pallas kernels, backward(): pl.pallas_call(functools.partial(backward_kernel, per_block, weight_layou...  86.5 us
    pallas_call x1, Pallas kernels, forward(): pl.pallas_call(functools.partial(forward_kernel, per_block, weight_layout...  41.2 us
    ppermute x5, waiting for transfers between devices, shift_mp(): lax.ppermute(value, 'mp', [(i, (i - steps) % ways) for i in range(ways)])  21.7 us
    pallas_call x1, Pallas kernels, own_heads(): pl.pallas_call(functools.partial(own_heads_kernel, per_block), grid=(imag...  19.9 us
  transfers between devices with their start and end apart: 11, of which 3 were waited for; matrix products, arithmetic and copies ran while one was open for 10% of the time, Pallas kernels for 54%

profile of v4, /device:TPU:0, one launch (start us, length us, event | category | flops | bytes accessed | tf_op | source)
XLA Modules:
  0.0 602.6 jit_solution(11437685861370684310)
XLA Ops:
  7.2 4.4 fusion.2
  11.6 0.7 all_to_all.13
  12.3 4.2 all-to-all-start
  16.5 2.1 collective-permute-start
  18.6 1.9 all-to-all-done
  20.6 0.7 pad_convert_fusion.mod_ref.refs_5_.refs_7_
  21.3 3.0 constant_dynamic-slice_fusion.3
  24.3 1.2 collective-permute-start.1
  25.6 0.9 constant_dynamic-slice_fusion.2
  26.4 0.8 collective-permute-start.2
  27.3 0.9 fusion.4.pick_ref.refs_6_.refs_8_
  28.5 2.0 fusion.27
  30.5 1.1 stack.68
  31.6 1.1 stack.69
  32.7 1.1 stack.70
  33.8 1.1 stack.71
  34.9 0.8 stack.72
  37.5 1.5 stack.67
  39.0 0.8 pad.105.strip_ref
  39.9 10.1 %shard_map.203.bias_ref.refs_7_.refs_9_ = f32[16,256,256]{2,1,0:T(8,128)} custom-call(f32[16,16,512]{2,1,0:T(8,128)} %pad.105.strip_ref), custom_call_target="tpu_custom_call" | custom-call | flops 1000000 | bytes 100000 | tf_op jit(solution)/shard_map/pallas_call | solution.py:84
  49.9 19.9 %shard_map.204 = (bf16[1024,1152]{1,0:T(8,128)(2,1)}, bf16[1728,1024]{1,0:T(8,128)(2,1)}, bf16[576,2048]{1,0:T(8,128)(2,1)}, f32[4,16,256]{2,1,0:T(8,128)}) custom-call(bf16[1024,1152]{1,0:T(8,128)(2,1)} %refs_6_.1, f32[4,8,1152]{2,1,0:T(8,128)} %pad_convert_fusion.mod_ref.refs_5_.refs_7_, bf16[4,192,256]{2,1,0:T(8,128)(2,1)} %fusion.4.pick_ref.refs_6_.refs_8_, ...), custom_call_target="tpu_custom_call" | custom-call | flops 10000000 | bytes 100000 | tf_op jit(solution)/shard_map/pallas_call | solution.py:229
  69.8 13.2 %collective-permute-done.2.refs_11_.refs_4_ = bf16[288,1152]{1,0:T(8,128)(2,1)} collective-permute-done((bf16[288,1152]{1,0:T(8,128)(2,1)}, bf16[288,1152]{1,0:T(8,128)(2,1)}, u32[]{:S(2)}, u32[]{:S(2)}) %collective-permute-start.2) | collective-permute-done | bytes 663584 | tf_op jit(solution)/shard_map/ppermute | solution.py:1010
  84.0 1.8 fusion.3
  85.8 1.1 slice.189
  87.0 3.0 fusion.dmlp_ref
  90.0 41.2 %shard_map.205 = (bf16[3456,1024]{1,0:T(8,128)(2,1)}, bf16[1152,2048]{1,0:T(8,128)(2,1)}, f32[4,32,256]{2,1,0:T(8,128)}, f32[1792,1152]{1,0:T(8,128)}, bf16[1792...) custom-call(bf16[1024,1152]{1,0:T(8,128)(2,1)} %get-tuple-element.62.refs_0_.first_ref, ...), custom_call_target="tpu_custom_call" | custom-call | flops 8000000000 | bytes 32000000 | tf_op jit(solution)/shard_map/pallas_call | solution.py:354
  131.2 103.1 %shard_map.206 = (f32[1792,1152]{1,0:T(8,128)}, f32[1792,1152]{1,0:T(8,128)}, bf16[1152,4608]{1,0:T(8,128)(2,1)}, bf16[1152,2304]{1,0:T(8,128)(2,1)}, bf16[2304,1152]{1,0:T(8,128)(2,1)}) custom-call(bf16[1792,1152]{1,0:T(8,128)(2,1)} %get-tuple-element.70.second_ref, bf16[1792,1152]{1,0:T(8,128)(2,1)} %fusion.dmlp_ref, bf16[1152,2304]{1,0:T(8,128)(2,1)} %refs_1_.1, ...), custom_call_target="tpu_custom_call" | custom-call | flops 60000002048 | bytes 60000000 | tf_op jit(solution)/shard_map/pallas_call | solution.py:561
  234.4 79.5 %shard_map.207 = (f32[1792,1152]{1,0:T(8,128)}, f32[1792,1152]{1,0:T(8,128)}, bf16[1152,4608]{1,0:T(8,128)(2,1)}) custom-call(bf16[1792,1152]{1,0:T(8,128)(2,1)} %get-tuple-element.70.second_ref, bf16[1792,1152]{1,0:T(8,128)(2,1)} %fusion.dmlp_ref, bf16[1152,2304]{1,0:T(8,128)(2,1)} %get-tuple-element.72.up_ref, ...), custom_call_target="tpu_custom_call" | custom-call | flops 10000000 | bytes 100000 | tf_op jit(solution)/shard_map/pallas_call | solution.py:561
  314.8 86.5 %shard_map.208 = (bf16[1792,1152]{1,0:T(8,128)(2,1)}, bf16[1024,1152]{1,0:T(8,128)(2,1)}, f32[4,8,1152]{2,1,0:T(8,128)}, bf16[2048,1152]{1,0:T(8,128)(2,1)}, bf1...) custom-call(bf16[1728,1152]{1,0:T(8,128)(2,1)} %bitcast.128, bf16[864,1152]{1,0:T(8,128)(2,1)} %collective-permute-done.1.refs_8_.refs_1_, ...), custom_call_target="tpu_custom_call" | custom-call | flops 10000000 | bytes 100000 | tf_op jit(solution)/shard_map/pallas_call | solution.py:709
  401.3 1.7 slice.246
  403.0 3.3 slice.247
  406.4 3.1 reshape.179
  409.4 2.9 slice_bitcast_fusion.15
  412.3 1.1 add_convert_fusion
  413.9 1.6 reshape.174
  415.5 0.6 pad_maximum_fusion.1
  416.1 127.8 %shard_map.209 = (bf16[12,144,384]{2,1,0:T(8,128)(2,1)}, bf16[16,2,224,128]{3,2,1,0:T(8,128)(2,1)}) custom-call(bf16[1024,1152]{1,0:T(8,128)(2,1)} %get-tuple-element.62.refs_0_.first_ref, bf16[2048,1152]{1,0:T(8,128)(2,1)} %get-tuple-element.80.dattn_ref, bf16[3456,1024]{1,0:T(8,128)(2,1)} %get-tuple-element.83.dqkv_ref, ...), custom_call_target="tpu_custom_call" | custom-call | flops 10000000 | bytes 100000 | tf_op jit(solution)/shard_map/pallas_call | solution.py:976
  544.0 1.2 slice.272
  545.2 1.0 slice.270
  546.3 1.9 bitcast_convert_fusion
  548.2 2.3 copy-done.7
  550.9 0.8 pad_maximum_fusion
  551.7 1.3 collective-permute-start.5
  553.4 1.7 reshape.194
  555.9 1.3 slice.267
  557.3 2.1 reshape.189
  559.4 5.5 fusion.5
  564.9 0.6 reshape.190
  565.6 3.2 all-to-all-start.1
  568.8 0.6 copy.137
  569.4 2.5 fusion.14
  572.1 0.7 reduce_sum.28
  572.8 0.7 reshape.199
  573.5 2.0 collective-permute-start.6
  575.5 0.6 fusion.21
  576.1 1.1 convert_add_fusion.1
  577.5 0.8 copy.106
  578.4 0.8 slice_bitcast_fusion.16
  579.1 8.4 %collective-permute-done.6 = bf16[72,4608]{1,0:T(8,128)(2,1)S(1)} collective-permute-done((bf16[72,4608]{1,0:T(8,128)(2,1)}, bf16[72,4608]{1,0:T(8,128)(2,1)S(1)}, u32[]{:S(2)}, u32[]{:S(2)}) %collective-permute-start.6) | collective-permute-done | bytes 663584 | tf_op jit(solution)/shard_map/ppermute | solution.py:1010
  587.6 1.3 convert_add_fusion
  588.9 0.9 reshape.197
  589.8 3.9 slice_reduce_fusion.1
  593.7 1.0 copy.129
  594.6 1.0 copy.128
  (88 shorter events, 6.4 us)
Async XLA Ops:
  7.2 18.3 %copy-start = (s32[8,179]{1,0:T(8,128)S(1)}, s32[8,179]{1,0:T(8,128)}, u32[]{:S(2)}) copy-start(s32[8,179]{1,0:T(8,128)} %param.14) | copy-start | bytes 17188
  7.2 9.3 %copy-start.10 = (f32[8,961]{1,0:T(8,128)S(1)}, f32[8,961]{1,0:T(8,128)}, u32[]{:S(2)}) copy-start(f32[8,961]{1,0:T(8,128)} %param.21) | copy-start | bytes 92260
  11.6 13.9 %copy-start.4 = (bf16[576,1152]{1,0:T(8,128)(2,1)S(1)}, bf16[576,1152]{1,0:T(8,128)(2,1)}, u32[]{:S(2)}) copy-start(bf16[576,1152]{1,0:T(8,128)(2,1)} %refs_3_.1) | copy-start | bytes 3981316
  12.3 8.3 %all-to-all-start = ((bf16[2,4,3456]{2,1,0:T(4,128)(2,1)}), bf16[2,4,3456]{2,1,0:T(4,128)(2,1)S(1)}, u32[]{:S(2)}, u32[]{:S(2)}) async-start(bf16[2,4,3456]{2,1,0:T(4,128)(2,1)} %all_to_all.13), calls=%async_computation | async-start | bytes 110592 | tf_op jit(solution)/shard_map/all_to_all | solution.py:1093
  16.5 399.7 %reduce-scatter.3.cloned.1.call-start = ((), (), s32[]{:S(2)}) async-start(), calls=%async_computation.4 | async-start | bytes 11280384 | tf_op jit(solution)/shard_map/reduce_scatter | solution.py:1074
  16.5 4.8 collective-permute-start
  24.3 58.7 %collective-permute-start.1 = (bf16[864,1152]{1,0:T(8,128)(2,1)}, bf16[864,1152]{1,0:T(8,128)(2,1)}, u32[]{:S(2)}, u32[]{:S(2)}) collective-permute-start(bf16[864,1152]{1,0:T(8,128)(2,1)} %constant_dynamic-slice_fusion.3), channel_id=1, source_target_pairs={{0,1},{1,0},{2,3},{3,2},{4,5},{5,4},{6,7},{7,6},{8,9},{9,8},{10,11... | collective-permute-start | bytes 5971976 | tf_op jit(solution)/shard_map/ppermute | solution.py:1010
  26.4 56.6 %collective-permute-start.2 = (bf16[288,1152]{1,0:T(8,128)(2,1)}, bf16[288,1152]{1,0:T(8,128)(2,1)}, u32[]{:S(2)}, u32[]{:S(2)}) collective-permute-start(bf16[288,1152]{1,0:T(8,128)(2,1)} %constant_dynamic-slice_fusion.2), channel_id=1, source_target_pairs={{0,1},{1,0},{2,3},{3,2},{4,5},{5,4},{6,7},{7,6},{8,9},{9,8},{10,11... | collective-permute-start | bytes 1990664 | tf_op jit(solution)/shard_map/ppermute | solution.py:1010
  49.9 33.6 %copy-start.5 = (bf16[716,1152]{1,0:T(8,128)(2,1)S(1)}, bf16[716,1152]{1,0:T(8,128)(2,1)}, u32[]{:S(2)}) copy-start(bf16[716,1152]{1,0:T(8,128)(2,1)} %param.22) | copy-start | bytes 4948996
  83.0 7.0 %collective-permute-start.3 = (bf16[864,1152]{1,0:T(8,128)(2,1)}, bf16[864,1152]{1,0:T(8,128)(2,1)}, u32[]{:S(2)}, u32[]{:S(2)}) collective-permute-start(bf16[864,1152]{1,0:T(8,128)(2,1)} %collective-permute-done.1.refs_8_.refs_1_), channel_id=1, source_target_pairs={{0,2},{2,0},{4,6},{6,4},{8,10},{10,8},{12,14},{14,12},{16,18},{18,... | collective-permute-start | bytes 5971976 | tf_op jit(solution)/shard_map/ppermute | solution.py:1042
  83.0 7.0 %collective-permute-start.4 = (bf16[288,1152]{1,0:T(8,128)(2,1)}, bf16[288,1152]{1,0:T(8,128)(2,1)}, u32[]{:S(2)}, u32[]{:S(2)}) collective-permute-start(bf16[288,1152]{1,0:T(8,128)(2,1)} %collective-permute-done.2.refs_11_.refs_4_), channel_id=1, source_target_pairs={{0,2},{2,0},{4,6},{6,4},{8,10},{10,8},{12,14},{14,12},{16,18},{18,... | collective-permute-start | bytes 1990664 | tf_op jit(solution)/shard_map/ppermute | solution.py:1042
  85.8 4.2 copy-start.2
  234.4 339.1 %reduce-scatter.5.cloned.1.call-start = ((), (), s32[]{:S(2)}) async-start(), calls=%async_computation.5 | async-start | bytes 11280384 | tf_op jit(solution)/shard_map/reduce_scatter | solution.py:1074
  313.9 0.7 copy-start.8
  401.3 4.9 copy-start.9
  401.3 5.1 copy-start.6
  548.2 2.5 copy-start.3
  548.2 2.3 copy-start.7
  550.9 4.5 slice-start
  551.7 24.4 %collective-permute-start.5 = (bf16[72,2304]{1,0:T(8,128)(2,1)}, bf16[72,2304]{1,0:T(8,128)(2,1)}, u32[]{:S(2)}, u32[]{:S(2)}) collective-permute-start(bf16[72,2304]{1,0:T(8,128)(2,1)} %pad_maximum_fusion), channel_id=1, source_target_pairs={{0,1},{1,0},{2,3},{3,2},{4,5},{5,4},{6,7},{7,6},{8,9},{9,8},{10,11... | collective-permute-start | bytes 995336 | tf_op jit(solution)/shard_map/ppermute | solution.py:1010
  559.4 9.4 %slice-start.1 = ((f32[32,224,128]{2,1,0:T(8,128)}), f32[32,64,128]{2,1,0:T(8,128)S(1)}, s32[]{:S(2)}) async-start(f32[32,224,128]{2,1,0:T(8,128)} %copy-done.3), calls=%async_computation.7 | async-start | bytes 2097152 | tf_op jit(solution)/shard_map/slice | solution.py:1172
  565.6 9.9 %all-to-all-start.1 = ((bf16[2,4,1152]{2,1,0:T(4,128)(2,1)}), bf16[2,4,1152]{2,1,0:T(4,128)(2,1)S(1)}, u32[]{:S(2)}, u32[]{:S(2)}) async-start(bf16[2,4,1152]{2,1,0:T(4,128)(2,1)} %reshape.190), calls=%async_computation.2 | async-start | bytes 36864 | tf_op jit(solution)/shard_map/all_to_all | solution.py:1217
  573.5 14.1 %collective-permute-start.6 = (bf16[72,4608]{1,0:T(8,128)(2,1)}, bf16[72,4608]{1,0:T(8,128)(2,1)S(1)}, u32[]{:S(2)}, u32[]{:S(2)}) collective-permute-start(bf16[72,4608]{1,0:T(8,128)(2,1)} %reduce-scatter.5.cloned.1.call-done), channel_id=1, source_target_pairs={{0,1},{1,0},{2,3},{3,2},{4,5},{5,4},{6,7},{7,6},{8,9},{9,8},{10,11... | collective-permute-start | bytes 1990664 | tf_op jit(solution)/shard_map/ppermute | solution.py:1010
  587.6 8.0 %copy-start.1 = (s32[8,179]{1,0:T(8,128)S(1)}, s32[8,179]{1,0:T(8,128)}, u32[]{:S(2)}) copy-start(s32[8,179]{1,0:T(8,128)} %param.14) | copy-start | bytes 17188
Sparse Core Ops, SparseCore 0:
  234.5 121.2 reduce-scatter.2
  359.8 153.4 reduce-scatter.4

commit v5 on v4

--- a/solution.py
+++ b/solution.py
@@ -157,12 +157,12 @@
     )
 
 
-def greet_peers(with_core):
+def greet_peers(bits):
     barrier = pltpu.get_barrier_semaphore()
     peers = [{"mp": 1 - lax.axis_index("mp")}]
-    if with_core:
-        place = lax.axis_index("dp")
-        peers.append({"dp": place + 1 - 2 * (place % 2)})
+    place = lax.axis_index("dp")
+    for bit in bits:
+        peers.append({"dp": place + bit - 2 * bit * place_bit(place, bit)})
     for peer in peers:
         pl.semaphore_signal(
             barrier, inc=1, device_id=peer, device_id_type=pl.DeviceIdType.MESH
@@ -281,7 +281,7 @@
         copies = part_copies(weight_layout, weight_parts, weight_ref, part_sems.at[0])
         copies += part_copies(out_layout, out_parts, out_w_ref, part_sems.at[1])
         if fetch:
-            greet_peers(False)
+            greet_peers(())
             fetching().start()
         run_copies(copies)
 
@@ -426,27 +426,36 @@
 
     if fetch:
         up_half, down_half = up_all.shape[0] // 2, down_all.shape[0] // 2
-        cut = near_ref.shape[0]
+        cut, quarter = near_ref.shape[0], down_half // 2
+        place = lax.axis_index("dp")
+        side = place_bit(place, 2)
         up_a = up_all.at[core_rows(up_half, 0, cut), :]
         up_b = up_all.at[core_rows(up_half, cut, up_half - cut), :]
         down_a = down_all.at[core_rows(down_half, 0, down_half), :]
+        down_q_rows = core_rows(down_half, side * quarter, quarter)
+        down_q = down_all.at[down_q_rows, :]
         lay_a = pltpu.make_async_copy(near_ref, up_a, moves.at[0])
         pass_a = core_copy(near_ref, up_a, moves, 1)
         pass_b = core_copy(up_b, up_b, moves, 3)
         pass_down = core_copy(down_a, down_a, moves, 5)
+        pass_y = pltpu.make_async_remote_copy(
+            src_ref=down_q,
+            dst_ref=down_q,
+            send_sem=moves.at[7],
+            recv_sem=moves.at[8],
+            device_id={"dp": place + 2 - 4 * side},
+            device_id_type=pl.DeviceIdType.MESH,
+        )
         fetch_b = fetch_copy(
             send_up, core_rows(up_half, cut, up_half - cut), up_b, fetch_sems, 0
         )
-        fetch_down = fetch_copy(
-            send_down, core_rows(down_half, 0, down_half), down_a, fetch_sems, 2
-        )
+        fetch_down = fetch_copy(send_down, down_q_rows, down_q, fetch_sems, 2)
     step, last = pl.program_id(0), pl.num_programs(0) - 1
 
     @pl.when(step == 0)
     def _():
         if fetch:
-            greet_peers(True)
-            fetch_b.start()
+            greet_peers((1, 2))
             fetch_down.start()
             lay_a.start()
             pass_a.start()
@@ -476,19 +485,24 @@
         dpre_s[at, :] = dpre
         branch_ref[at, :] += nn(hidden, down_ref[...])
         dsecond_ref[at, :] += nt(dpre, up_ref[...])
+        if fetch:
+
+            @pl.when(jnp.logical_and(step == jnp.minimum(1, last), index == 0))
+            def _():
+                fetch_down.wait_recv()
+                pass_y.start()
+                fetch_b.start()
+
         return carry
 
     lax.fori_loop(0, rows // chunk, one_chunk, 0)
     if fetch:
 
-        @pl.when(step == last // 2)
+        @pl.when(step == last)
         def _():
             fetch_b.wait_recv()
             pass_b.start()
-
-        @pl.when(step == last)
-        def _():
-            fetch_down.wait_recv()
+            pass_y.wait_recv()
             pass_down.start()
 
     part = width // 3
@@ -503,6 +517,7 @@
         def _():
             for copy in (lay_a, pass_a, pass_b, pass_down):
                 copy.wait()
+            pass_y.wait_send()
             fetch_b.wait_send()
             fetch_down.wait_send()
 
@@ -553,7 +568,7 @@
         operands += list(fetch)
         out_specs += [ANYWHERE] * 2
         out_shape += [jax.ShapeDtypeStruct(up.shape, BF), jax.ShapeDtypeStruct(down.shape, BF)]
-        scratch += [pltpu.SemaphoreType.DMA((7,)), pltpu.SemaphoreType.DMA((4,))]
+        scratch += [pltpu.SemaphoreType.DMA((9,)), pltpu.SemaphoreType.DMA((4,))]
         compiler_params = pltpu.CompilerParams(
             vmem_limit_bytes=VMEM_LIMIT, dimension_semantics=("arbitrary",),
             collective_id=3, has_side_effects=True,
@@ -1060,16 +1075,6 @@
     return total
 
 
-def to_lanes_rows(size):
-    return -(-size // 2048) * 16
-
-
-def to_lanes(part):
-    flat = part.reshape(-1)
-    rows = to_lanes_rows(flat.shape[0])
-    return jnp.pad(flat, (0, rows * 128 - flat.shape[0])).reshape(rows, 128)
-
-
 def scatter_dp(part):
     return lax.psum_scatter(part, "dp", scatter_dimension=0, tiled=True)
 
@@ -1099,8 +1104,8 @@
         (mod, tables, weight_own, attn_out)
     )
     near_w, near_o = near_halves(weight_sent), near_halves(out_sent)
-    fetch = ways == 2 and lax.axis_size("dp") % 2 == 0 and mlp_up.shape[0] % 32 == 0
-    fetch = fetch and mlp_down.shape[0] % 32 == 0
+    fetch = ways == 2 and lax.axis_size("dp") % 4 == 0 and mlp_up.shape[0] % 32 == 0
+    fetch = fetch and mlp_down.shape[0] % 64 == 0
     bias = bias_whole(jnp.concatenate(tables, axis=0))
 
     own_kept = lax.dynamic_slice_in_dim(kept_ids, place * images, images, 0)
@@ -1149,30 +1154,33 @@
     )
     proj_block, out_block = weight_own.shape[0], attn_out.shape[0]
     dqkv, reduced[0] = lax.optimization_barrier((dqkv, reduced[0]))
-    dmod_rows = dmod[:, :6].reshape(images, 6 * width)
     dtables = table_of_strips(strips)
     here = can_sum_here(width, dqkv.shape[0]) and att.shape[0] % 384 == 0 and ways == 2
+    here = here and cols % width == 0
     if here:
         own_cond_rows = lax.dynamic_slice_in_dim(silu_cond, place * images, images, 0)
+        pieces = cols // width
         packs = []
         for steps in range(ways):
             at = (place + steps) % ways
-            parts = (
-                lax.dynamic_slice_in_dim(dmod_rows, at * cols, cols, 1),
-                dtables[steps * per_block : (steps + 1) * per_block],
-                own_cond_rows,
+            table = dtables[steps * per_block : (steps + 1) * per_block]
+            pack = jnp.concatenate(
+                [
+                    lax.dynamic_slice_in_dim(dmod, at * pieces, pieces, 1)
+                    .astype(BF)
+                    .reshape(-1, width),
+                    own_cond_rows,
+                    jnp.pad(table, ((0, 0), (0, width - BUCKETS))).astype(BF),
+                ],
+                axis=0,
             )
-            packs.append(jnp.concatenate([to_lanes(part.astype(BF)) for part in parts], axis=0))
+            packs.append(jnp.pad(pack, ((0, -pack.shape[0] % 16), (0, 0))))
         attn_sums, every = attn_grads(first, dattn, dqkv, att, *packs)
-        places = every.shape[0]
-        every = every.astype(F32).reshape(places * ways, -1, 128)
-        got, end = [], 0
-        for part in parts:
-            start, end = end, end + to_lanes_rows(part.size)
-            got.append(every[:, start:end].reshape(places * ways, -1)[:, : part.size])
-        all_columns = got[0].reshape(-1, cols)
-        dtable = jnp.sum(got[1], axis=0).reshape(rel_table.shape)
-        all_cond = got[2].reshape(-1, width)
+        places, first_cond = every.shape[0], images * pieces
+        every = every.reshape((places * ways,) + every.shape[2:]).astype(F32)
+        all_columns = every[:, :first_cond].reshape(-1, cols)
+        all_cond = every[:, first_cond : first_cond + images].reshape(-1, width)
+        dtable = jnp.sum(every[:, first_cond + images :], axis=0)[:per_block, :BUCKETS]
         dcolumns = lax.dynamic_slice_in_dim(
             all_columns, pack_slot(lax.axis_index("dp")) * images_group, images_group, 0
         )
@@ -1180,6 +1188,7 @@
         dweight = dot(first, dqkv, (0, 1)).astype(BF)
         dout_t = dot(dattn, att, (0, 1)).astype(BF)
         attn_sums = scatter_dp(jnp.concatenate([dweight, dout_t], axis=1))
+        dmod_rows = dmod[:, :6].reshape(images, 6 * width)
         dcolumns = lax.all_to_all(dmod_rows, "mp", split_axis=1, concat_axis=0, tiled=True)
         dtable = home(list(jnp.split(dtables, ways, axis=0)))
         all_columns = lax.all_gather(dcolumns, "dp", axis=0, tiled=True)
@@ -1196,8 +1205,8 @@
         )
         for j in range(ways)
     ]
-    mlp_grads = home(reduced)
-    attn_total = home(attn_parts)
+    totals = home([jnp.concatenate(pair, axis=1) for pair in zip(reduced, attn_parts)])
+    mlp_grads, attn_total = totals[:, : reduced[0].shape[1]], totals[:, reduced[0].shape[1] :]
     grad_up, grad_down_t = split_mlp_grads(mlp_grads, tile_own)
     grad_qkv = attn_total[:, :proj_block].reshape(-1, 3, proj_block // 3)
     grad_out = jnp.transpose(attn_total[:, proj_block:])

time: 609 us -> 586 us (0.962)
  Pallas kernels: 468 us -> 450 us
  waiting for transfers between devices: 23.7 us -> 17.4 us
    pallas_call x2, Pallas kernels: 183 us -> 163 us  [mlp(): pl.pallas_call(functools.partial(mlp_kernel, chunk, fresh, fetch is not N...]
    ppermute x5 -> x4, waiting for transfers between devices: 21.7 us -> 13.5 us  [shift_mp(): lax.ppermute(value, 'mp', [(i, (i - steps) % ways) for i in range(ways)])]
  transfers between devices with their start and end apart: 11 -> 10, of which waited for: 3 -> 3; matrix products, arithmetic and copies ran while one was open for 10% -> 11% of each run, Pallas kernels for 54% -> 56%
where the time goes in v5:
time: 586 us; the launch traced here: 579 us
  Pallas kernels  450 us (77%)
  local copies, waits for them, and re-layouts  56.4 us (10%)
  waiting for transfers between devices  17.4 us (3%)
  other arithmetic  16.2 us (3%)
  between operations  14.9 us (3%)
  starting transfers between devices  12.9 us (2%)
  matrix products  11.3 us (2%)
    pallas_call x2, Pallas kernels, mlp(): pl.pallas_call(functools.partial(mlp_kernel, chunk, fresh, fetch is not N...  163 us
    pallas_call x1, Pallas kernels, attn_grads(): pl.pallas_call(attn_grads_kernel, in_specs=[vmem] * 6, out_specs=[vmem] *...  129 us
    pallas_call x1, Pallas kernels, backward(): pl.pallas_call(functools.partial(backward_kernel, per_block, weight_layou...  86.3 us
    pallas_call x1, Pallas kernels, forward(): pl.pallas_call(functools.partial(forward_kernel, per_block, weight_layout...  41.2 us
    pallas_call x1, Pallas kernels, own_heads(): pl.pallas_call(functools.partial(own_heads_kernel, per_block), grid=(imag...  19.8 us
    ppermute x4, waiting for transfers between devices, shift_mp(): lax.ppermute(value, 'mp', [(i, (i - steps) % ways) for i in range(ways)])  13.5 us
  transfers between devices with their start and end apart: 10, of which 3 were waited for; matrix products, arithmetic and copies ran while one was open for 11% of the time, Pallas kernels for 56%

profile of v5, /device:TPU:0, one launch (start us, length us, event | category | flops | bytes accessed | tf_op | source)
XLA Modules:
  0.0 578.9 jit_solution(16401486317059975363)
XLA Ops:
  7.2 4.4 fusion.2
  11.6 0.7 all_to_all.13
  12.3 4.2 all-to-all-start
  16.5 2.1 collective-permute-start
  18.6 1.9 all-to-all-done
  20.6 0.7 pad_convert_fusion.mod_ref.refs_5_.refs_7_
  21.3 3.0 constant_dynamic-slice_fusion.3
  24.3 1.2 collective-permute-start.1
  25.6 0.9 constant_dynamic-slice_fusion.2
  26.4 0.8 collective-permute-start.2
  27.3 0.9 fusion.4.pick_ref.refs_6_.refs_8_
  28.5 2.0 fusion.31
  30.5 1.1 stack.68
  31.6 1.1 stack.69
  32.7 1.1 stack.70
  33.8 1.1 stack.71
  34.9 0.8 stack.72
  37.5 1.5 stack.67
  39.0 0.8 pad.102.strip_ref
  39.9 9.9 %shard_map.203.bias_ref.refs_7_.refs_9_ = f32[16,256,256]{2,1,0:T(8,128)} custom-call(f32[16,16,512]{2,1,0:T(8,128)} %pad.102.strip_ref), custom_call_target="tpu_custom_call" | custom-call | flops 1000000 | bytes 100000 | tf_op jit(solution)/shard_map/pallas_call | solution.py:84
  49.7 19.8 %shard_map.204 = (bf16[1024,1152]{1,0:T(8,128)(2,1)}, bf16[1728,1024]{1,0:T(8,128)(2,1)}, bf16[576,2048]{1,0:T(8,128)(2,1)}, f32[4,16,256]{2,1,0:T(8,128)}) custom-call(bf16[1024,1152]{1,0:T(8,128)(2,1)} %refs_6_.1, f32[4,8,1152]{2,1,0:T(8,128)} %pad_convert_fusion.mod_ref.refs_5_.refs_7_, bf16[4,192,256]{2,1,0:T(8,128)(2,1)} %fusion.4.pick_ref.refs_6_.refs_8_, ...), custom_call_target="tpu_custom_call" | custom-call | flops 10000000 | bytes 100000 | tf_op jit(solution)/shard_map/pallas_call | solution.py:229
  69.6 13.5 %collective-permute-done.2.refs_11_.refs_4_ = bf16[288,1152]{1,0:T(8,128)(2,1)} collective-permute-done((bf16[288,1152]{1,0:T(8,128)(2,1)}, bf16[288,1152]{1,0:T(8,128)(2,1)}, u32[]{:S(2)}, u32[]{:S(2)}) %collective-permute-start.2) | collective-permute-done | bytes 663584 | tf_op jit(solution)/shard_map/ppermute | solution.py:1025
  84.0 1.8 fusion.3
  85.8 1.1 slice.188
  87.0 3.0 fusion.dmlp_ref
  90.0 41.2 %shard_map.205 = (bf16[3456,1024]{1,0:T(8,128)(2,1)}, bf16[1152,2048]{1,0:T(8,128)(2,1)}, f32[4,32,256]{2,1,0:T(8,128)}, f32[1792,1152]{1,0:T(8,128)}, bf16[1792...) custom-call(bf16[1024,1152]{1,0:T(8,128)(2,1)} %get-tuple-element.62.refs_0_.first_ref, ...), custom_call_target="tpu_custom_call" | custom-call | flops 8000000000 | bytes 32000000 | tf_op jit(solution)/shard_map/pallas_call | solution.py:354
  131.2 83.4 %shard_map.206 = (f32[1792,1152]{1,0:T(8,128)}, f32[1792,1152]{1,0:T(8,128)}, bf16[1152,4608]{1,0:T(8,128)(2,1)}, bf16[1152,2304]{1,0:T(8,128)(2,1)}, bf16[2304,1152]{1,0:T(8,128)(2,1)}) custom-call(bf16[1792,1152]{1,0:T(8,128)(2,1)} %get-tuple-element.70.second_ref, bf16[1792,1152]{1,0:T(8,128)(2,1)} %fusion.dmlp_ref, bf16[1152,2304]{1,0:T(8,128)(2,1)} %refs_1_.1, ...), custom_call_target="tpu_custom_call" | custom-call | flops 60000002048 | bytes 60000000 | tf_op jit(solution)/shard_map/pallas_call | solution.py:576
  214.7 79.8 %shard_map.207 = (f32[1792,1152]{1,0:T(8,128)}, f32[1792,1152]{1,0:T(8,128)}, bf16[1152,4608]{1,0:T(8,128)(2,1)}) custom-call(bf16[1792,1152]{1,0:T(8,128)(2,1)} %get-tuple-element.70.second_ref, bf16[1792,1152]{1,0:T(8,128)(2,1)} %fusion.dmlp_ref, bf16[1152,2304]{1,0:T(8,128)(2,1)} %get-tuple-element.72.up_ref, ...), custom_call_target="tpu_custom_call" | custom-call | flops 10000000 | bytes 100000 | tf_op jit(solution)/shard_map/pallas_call | solution.py:576
  295.3 86.3 %shard_map.208 = (bf16[1792,1152]{1,0:T(8,128)(2,1)}, bf16[1024,1152]{1,0:T(8,128)(2,1)}, f32[4,8,1152]{2,1,0:T(8,128)}, bf16[2048,1152]{1,0:T(8,128)(2,1)}, bf1...) custom-call(bf16[1728,1152]{1,0:T(8,128)(2,1)} %bitcast.99, bf16[864,1152]{1,0:T(8,128)(2,1)} %collective-permute-done.1.refs_8_.refs_1_, ...), custom_call_target="tpu_custom_call" | custom-call | flops 10000000 | bytes 100000 | tf_op jit(solution)/shard_map/pallas_call | solution.py:724
  381.6 1.6 slice.244
  383.3 3.3 slice.245
  386.6 3.3 reshape.133
  389.9 2.9 slice_bitcast_fusion.15
  392.8 1.1 add_convert_fusion
  394.3 0.6 pad.121.pack_own_ref
  395.0 0.6 pad.123.pack_other_ref
  395.6 1.6 reshape.130
  397.2 129.4 %shard_map.209 = (bf16[12,144,384]{2,1,0:T(8,128)(2,1)}, bf16[16,2,32,1152]{3,2,1,0:T(8,128)(2,1)}) custom-call(bf16[1024,1152]{1,0:T(8,128)(2,1)} %get-tuple-element.62.refs_0_.first_ref, bf16[2048,1152]{1,0:T(8,128)(2,1)} %get-tuple-element.80.dattn_ref, bf16[3456,1024]{1,0:T(8,128)(2,1)} %get-tuple-element.83.dqkv_ref, ...), custom_call_target="tpu_custom_call" | custom-call | flops 10000000 | bytes 100000 | tf_op jit(solution)/shard_map/pallas_call | solution.py:991
  526.6 1.5 slice.268
  528.1 1.9 slice.267
  530.1 1.2 dynamic-slice_bitcast_fusion
  531.3 0.7 fusion.29
  532.0 0.8 fusion.30
  532.8 3.0 bitcast_convert_fusion
  535.7 3.0 concatenate.31
  539.2 1.5 reshape.139
  540.6 1.0 reshape.138
  541.6 1.7 reshape.136
  543.4 1.0 subtract_convert_fusion
  544.4 5.5 fusion.7
  549.9 0.6 reshape.137
  550.5 3.5 all-to-all-start.1
  554.1 1.4 fusion.18
  555.4 1.9 slice_reduce_fusion
  557.3 0.7 reduce_sum.28
  559.0 1.9 all-to-all-done.1
  561.0 0.6 fusion.25
  561.6 1.4 convert_add_fusion
  563.2 0.8 slice_bitcast_fusion.16
  564.0 0.9 reshape.142
  564.9 3.9 slice_reduce_fusion.1
  568.8 1.0 copy.127
  569.8 1.0 copy.126
  571.0 0.8 copy.108
  (84 shorter events, 6.1 us)
Async XLA Ops:
  7.2 18.3 %copy-start = (s32[8,179]{1,0:T(8,128)S(1)}, s32[8,179]{1,0:T(8,128)}, u32[]{:S(2)}) copy-start(s32[8,179]{1,0:T(8,128)} %param.14) | copy-start | bytes 17188
  7.2 9.3 %copy-start.15 = (f32[8,961]{1,0:T(8,128)S(1)}, f32[8,961]{1,0:T(8,128)}, u32[]{:S(2)}) copy-start(f32[8,961]{1,0:T(8,128)} %param.21) | copy-start | bytes 92260
  11.6 13.9 %copy-start.6 = (bf16[576,1152]{1,0:T(8,128)(2,1)S(1)}, bf16[576,1152]{1,0:T(8,128)(2,1)}, u32[]{:S(2)}) copy-start(bf16[576,1152]{1,0:T(8,128)(2,1)} %refs_3_.1) | copy-start | bytes 3981316
  12.3 8.3 %all-to-all-start = ((bf16[2,4,3456]{2,1,0:T(4,128)(2,1)}), bf16[2,4,3456]{2,1,0:T(4,128)(2,1)S(1)}, u32[]{:S(2)}, u32[]{:S(2)}) async-start(bf16[2,4,3456]{2,1,0:T(4,128)(2,1)} %all_to_all.13), calls=%async_computation | async-start | bytes 110592 | tf_op jit(solution)/shard_map/all_to_all | solution.py:1098
  16.5 380.8 %reduce-scatter.3.cloned.1.call-start = ((), (), s32[]{:S(2)}) async-start(), calls=%async_computation.4 | async-start | bytes 11280384 | tf_op jit(solution)/shard_map/reduce_scatter | solution.py:1079
  16.5 4.8 collective-permute-start
  24.3 58.7 %collective-permute-start.1 = (bf16[864,1152]{1,0:T(8,128)(2,1)}, bf16[864,1152]{1,0:T(8,128)(2,1)}, u32[]{:S(2)}, u32[]{:S(2)}) collective-permute-start(bf16[864,1152]{1,0:T(8,128)(2,1)} %constant_dynamic-slice_fusion.3), channel_id=1, source_target_pairs={{0,1},{1,0},{2,3},{3,2},{4,5},{5,4},{6,7},{7,6},{8,9},{9,8},{10,11... | collective-permute-start | bytes 5971976 | tf_op jit(solution)/shard_map/ppermute | solution.py:1025
  26.4 56.6 %collective-permute-start.2 = (bf16[288,1152]{1,0:T(8,128)(2,1)}, bf16[288,1152]{1,0:T(8,128)(2,1)}, u32[]{:S(2)}, u32[]{:S(2)}) collective-permute-start(bf16[288,1152]{1,0:T(8,128)(2,1)} %constant_dynamic-slice_fusion.2), channel_id=1, source_target_pairs={{0,1},{1,0},{2,3},{3,2},{4,5},{5,4},{6,7},{7,6},{8,9},{9,8},{10,11... | collective-permute-start | bytes 1990664 | tf_op jit(solution)/shard_map/ppermute | solution.py:1025
  49.7 33.8 %copy-start.7 = (bf16[716,1152]{1,0:T(8,128)(2,1)S(1)}, bf16[716,1152]{1,0:T(8,128)(2,1)}, u32[]{:S(2)}) copy-start(bf16[716,1152]{1,0:T(8,128)(2,1)} %param.22) | copy-start | bytes 4948996
  83.0 7.0 %collective-permute-start.3 = (bf16[864,1152]{1,0:T(8,128)(2,1)}, bf16[864,1152]{1,0:T(8,128)(2,1)}, u32[]{:S(2)}, u32[]{:S(2)}) collective-permute-start(bf16[864,1152]{1,0:T(8,128)(2,1)} %collective-permute-done.1.refs_8_.refs_1_), channel_id=1, source_target_pairs={{0,2},{2,0},{4,6},{6,4},{8,10},{10,8},{12,14},{14,12},{16,18},{18,... | collective-permute-start | bytes 5971976 | tf_op jit(solution)/shard_map/ppermute | solution.py:1057
  83.0 7.0 %collective-permute-start.4 = (bf16[288,1152]{1,0:T(8,128)(2,1)}, bf16[288,1152]{1,0:T(8,128)(2,1)}, u32[]{:S(2)}, u32[]{:S(2)}) collective-permute-start(bf16[288,1152]{1,0:T(8,128)(2,1)} %collective-permute-done.2.refs_11_.refs_4_), channel_id=1, source_target_pairs={{0,2},{2,0},{4,6},{6,4},{8,10},{10,8},{12,14},{14,12},{16,18},{18,... | collective-permute-start | bytes 1990664 | tf_op jit(solution)/shard_map/ppermute | solution.py:1057
  85.8 4.2 copy-start.2
  214.7 321.0 %reduce-scatter.5.cloned.1.call-start = ((), (), s32[]{:S(2)}) async-start(), calls=%async_computation.5 | async-start | bytes 11280384 | tf_op jit(solution)/shard_map/reduce_scatter | solution.py:1079
  294.5 0.7 copy-start.12
  381.6 5.0 copy-start.10
  392.8 1.4 copy-start.14
  526.6 6.1 %copy-start.4 = (bf16[16,2,32,1152]{3,2,1,0:T(8,128)(2,1)S(1)}, bf16[16,2,32,1152]{3,2,1,0:T(8,128)(2,1)}, u32[]{:S(2)}) copy-start(bf16[16,2,32,1152]{3,2,1,0:T(8,128)(2,1)} %get-tuple-element.87) | copy-start | bytes 7077892
  538.8 2.9 slice-start
  538.8 22.9 %collective-permute-start.5 = (bf16[72,6912]{1,0:T(8,128)(2,1)}, bf16[72,6912]{1,0:T(8,128)(2,1)}, u32[]{:S(2)}, u32[]{:S(2)}) collective-permute-start(bf16[72,6912]{1,0:T(8,128)(2,1)} %concatenate.31), channel_id=1, source_target_pairs={{0,1},{1,0},{2,3},{3,2},{4,5},{5,4},{6,7},{7,6},{8,9},{9,8},{10,11... | collective-permute-start | bytes 2985992 | tf_op jit(solution)/shard_map/ppermute | solution.py:1025
  544.3 9.7 %copy-start.5 = (bf16[128,3456]{1,0:T(8,128)(2,1)S(1)}, bf16[128,3456]{1,0:T(8,128)(2,1)}, u32[]{:S(2)}) copy-start(bf16[128,3456]{1,0:T(8,128)(2,1)} %reshape.139) | copy-start | bytes 2654212
  549.9 7.5 %copy-start.3 = (f32[128,3456]{1,0:T(8,128)S(1)}, f32[128,3456]{1,0:T(8,128)}, u32[]{:S(2)}) copy-start(f32[128,3456]{1,0:T(8,128)} %reshape.136) | copy-start | bytes 5308420
  549.9 8.8 %copy-start.8 = (bf16[72,1728]{1,0:T(8,128)(2,1)S(1)}, bf16[72,1728]{1,0:T(8,128)(2,1)}, u32[]{:S(2)}) copy-start(bf16[72,1728]{1,0:T(8,128)(2,1)} %get-tuple-element.146) | copy-start | bytes 746500
  549.9 8.8 %copy-start.11 = (bf16[72,576]{1,0:T(8,128)(2,1)S(1)}, bf16[72,576]{1,0:T(8,128)(2,1)}, u32[]{:S(2)}) copy-start(bf16[72,576]{1,0:T(8,128)(2,1)} %get-tuple-element.144) | copy-start | bytes 248836
  550.5 10.5 %all-to-all-start.1 = ((bf16[2,4,1152]{2,1,0:T(4,128)(2,1)}), bf16[2,4,1152]{2,1,0:T(4,128)(2,1)S(1)}, u32[]{:S(2)}, u32[]{:S(2)}) async-start(bf16[2,4,1152]{2,1,0:T(4,128)(2,1)} %reshape.137), calls=%async_computation.2 | async-start | bytes 36864 | tf_op jit(solution)/shard_map/all_to_all | solution.py:1226
  554.1 6.9 %copy-start.13 = (bf16[8,1152]{1,0:T(8,128)(2,1)S(1)}, bf16[8,1152]{1,0:T(8,128)(2,1)}, u32[]{:S(2)}) copy-start(bf16[8,1152]{1,0:T(8,128)(2,1)} %param.13) | copy-start | bytes 55300
  555.4 3.2 copy-start.9
  564.0 7.8 %copy-start.1 = (s32[8,179]{1,0:T(8,128)S(1)}, s32[8,179]{1,0:T(8,128)}, u32[]{:S(2)}) copy-start(s32[8,179]{1,0:T(8,128)} %param.14) | copy-start | bytes 17188
Sparse Core Ops, SparseCore 0:
  214.8 120.2 reduce-scatter.2
  339.1 149.4 reduce-scatter.4

commit v6 on v5

--- a/solution.py
+++ b/solution.py
@@ -612,7 +612,7 @@
 def backward_body(
     per_block, weight_ref, out_w_ref, tok_ref, mod_ref, pick_ref, bias_ref,
     qkv_ref, lse_ref, middle_ref, branch_ref, mlp_ref, dsecond_ref, grad_ref,
-    out_ref, dtok_ref, dmod_ref, dattn_ref, dqkv_ref, strips_ref,
+    out_full_ref, out_kept_ref, dtok_ref, dmod_ref, dattn_ref, dqkv_ref, strips_ref,
     qkv_s, datt_s, dattk_s, dscores_s,
 ):
     heads = bias_ref.shape[0]
@@ -622,12 +622,15 @@
     pick = pick_ref[0]
     dmiddles = []
     sums = [0.0, 0.0, 0.0, 0.0]
-    for rows in (slice(0, PATCHES), slice(PATCHES, PATCHES + pick.shape[0])):
+    for rows, out_ref in (
+        (slice(0, PATCHES), out_full_ref),
+        (slice(PATCHES, PATCHES + pick.shape[0]), out_kept_ref),
+    ):
         middle = middle_ref[rows, :]
         branch_mlp = mlp_ref[rows, :]
         dsecond = dsecond_ref[rows, :]
         grad = grad_ref[rows, :].astype(F32)
-        out_ref[rows, :] = (middle + gate_two * branch_mlp).astype(BF)
+        out_ref[...] = (middle + gate_two * branch_mlp).astype(BF)
         normed, inverse = normalize(middle)
         dmiddle = grad + norm_back(normed, inverse, dsecond * (1.0 + scale_two))
         branch = branch_ref[rows, :].astype(F32)
@@ -739,7 +742,8 @@
             by_row,
         ],
         out_specs=[
-            by_row,
+            pl.BlockSpec((PATCHES, width), lambda i: (i, 0)),
+            pl.BlockSpec((padded, width), lambda i: (i, 0)),
             pl.BlockSpec((PATCHES, width), lambda i: (i, 0)),
             pl.BlockSpec((1, 8, width), lambda i: (i, 0, 0)),
             pl.BlockSpec((2 * PATCHES, width), lambda i: (i, 0)),
@@ -747,7 +751,8 @@
             const_spec((heads, GRID, 512)),
         ],
         out_shape=[
-            jax.ShapeDtypeStruct((images * rows, width), BF),
+            jax.ShapeDtypeStruct((images * PATCHES, width), BF),
+            jax.ShapeDtypeStruct((images * padded, width), BF),
             jax.ShapeDtypeStruct((images * PATCHES, width), BF),
             jax.ShapeDtypeStruct((images, 8, width), F32),
             jax.ShapeDtypeStruct((images * 2 * PATCHES, width), BF),
@@ -802,20 +807,21 @@
         buffer[tile, start : start + 2 * share, :] = both.astype(BF)
 
 
-class DpSum:
-    def __init__(self, buffer, lands, sends, recvs):
-        self.buffer, self.lands, self.sends, self.recvs = buffer, lands, sends, recvs
+class GroupSum:
+    def __init__(self, own, other, lands, land_other, land_cross, sends, recvs):
+        self.own, self.other, self.lands = own, other, lands
+        self.land_other, self.land_cross = land_other, land_cross
+        self.sends, self.recvs = sends, recvs
         self.place = lax.axis_index("dp")
-        self.rows = buffer.shape[1]
+        self.rows = own.shape[1]
 
     def partner(self, bit):
-        return self.place + bit - 2 * bit * place_bit(self.place, bit)
+        return {"dp": self.place + bit - 2 * bit * place_bit(self.place, bit)}
 
     def greet(self, barrier):
         for bit in HALVING + (FINAL,):
             pl.semaphore_signal(
-                barrier, inc=1, device_id={"dp": self.partner(bit)},
-                device_id_type=pl.DeviceIdType.MESH,
+                barrier, inc=1, device_id=self.partner(bit), device_id_type=pl.DeviceIdType.MESH
             )
 
     def spans(self, stage):
@@ -828,28 +834,63 @@
             start = start + mine * size
         return start, start, size
 
+    def remote(self, source, target, index, tile, peer):
+        return pltpu.make_async_remote_copy(
+            src_ref=source,
+            dst_ref=target,
+            send_sem=self.sends.at[index, tile],
+            recv_sem=self.recvs.at[index, tile],
+            device_id=peer,
+            device_id_type=pl.DeviceIdType.MESH,
+        )
+
     def copy(self, stage, tile):
-        bit = (HALVING + (FINAL,))[stage]
-        _, away, size = self.spans(stage)
-        return pltpu.make_async_remote_copy(
-            src_ref=self.buffer.at[tile, pl.ds(pl.multiple_of(away, 16), size), :],
-            dst_ref=self.lands[stage].at[tile],
-            send_sem=self.sends.at[stage, tile],
-            recv_sem=self.recvs.at[stage, tile],
-            device_id={"dp": self.partner(bit)},
-            device_id_type=pl.DeviceIdType.MESH,
-        )
-
-    def gather_stage(self, stage, tile):
+        bit = (HALVING + (FINAL, HALVING[0]))[stage]
+        buffer, land = (self.other, self.land_other) if stage == 4 else (self.own, self.lands[stage])
+        _, away, size = self.spans(0 if stage == 4 else stage)
+        rows = buffer.at[tile, pl.ds(pl.multiple_of(away, 16), size), :]
+        return self.remote(rows, land.at[tile], stage, tile, self.partner(bit))
+
+    def cross_rows(self, part):
+        keep, away, size = self.spans(1)
+        return (keep if part else away), size
+
+    def cross(self, part, tile):
+        start, size = self.cross_rows(part)
+        base = self.spans(0)[0]
+        return self.remote(
+            self.other.at[tile, pl.ds(pl.multiple_of(start, 16), size), :],
+            self.land_cross.at[tile, pl.ds(pl.multiple_of(start - base, 16), size), :],
+            5 + part,
+            tile,
+            {"mp": 1 - lax.axis_index("mp")},
+        )
+
+    def total(self, stage, tile):
         self.copy(stage, tile).wait_recv()
-        keep, _, size = self.spans(stage)
+        keep, _, size = self.spans(0 if stage == 4 else stage)
         at = pl.ds(pl.multiple_of(keep, 16), size)
-        return at, self.buffer[tile, at, :].astype(F32) + self.lands[stage][tile].astype(F32)
-
-    def advance(self, stage, tile):
-        at, total = self.gather_stage(stage, tile)
-        self.buffer[tile, at, :] = total.astype(BF)
-        self.copy(stage + 1, tile).start()
+        buffer, land = (self.other, self.land_other) if stage == 4 else (self.own, self.lands[stage])
+        return buffer, at, buffer[tile, at, :].astype(F32) + land[tile].astype(F32)
+
+    def add(self, stage, tile):
+        buffer, at, total = self.total(stage, tile)
+        buffer[tile, at, :] = total.astype(BF)
+
+    def add_cross(self, part, tile):
+        self.cross(part, tile).wait_recv()
+        start, size = self.cross_rows(part)
+        base = self.spans(0)[0]
+        at = pl.ds(pl.multiple_of(start, 16), size)
+        landed = pl.ds(pl.multiple_of(start - base, 16), size)
+        total = self.own[tile, at, :].astype(F32) + self.land_cross[tile, landed, :].astype(F32)
+        self.own[tile, at, :] = total.astype(BF)
+
+    def wait_sends(self, tile):
+        for stage in range(5):
+            self.copy(stage, tile).wait_send()
+        for part in range(2):
+            self.cross(part, tile).wait_send()
 
 
 def pack_slot(place):
@@ -910,58 +951,79 @@
 
 def attn_grads_kernel(
     first_ref, dattn_ref, dqkv_ref, att_ref, pack_own_ref, pack_other_ref, sums_ref, every_ref,
-    first_t, dattn_t, buffer, land0, land1, land2, land3, sends, recvs,
-    packs, pack_sends, pack_recvs,
+    first_t, dattn_t, own, other, land0, land1, land2, land3, land_other, land_cross,
+    sends, recvs, packs, pack_sends, pack_recvs,
 ):
     width = first_t.shape[0]
-    tiles, _, columns = buffer.shape
-    proj_tiles = dqkv_ref.shape[0] // columns
+    tiles, _, columns = own.shape
     share = width // SUM_PLACES
-    total = DpSum(buffer, (land0, land1, land2, land3), sends, recvs)
+    group = GroupSum(own, other, (land0, land1, land2, land3), land_other, land_cross, sends, recvs)
     ring = PackGather(pack_own_ref, pack_other_ref, packs, pack_sends, pack_recvs)
     barrier = pltpu.get_barrier_semaphore()
-    total.greet(barrier)
+    group.greet(barrier)
     ring.greet(barrier)
     pl.semaphore_wait(barrier, len(HALVING) + 2)
     ring.start()
-    for source, target in ((first_ref, first_t), (dattn_ref, dattn_t)):
+
+    def turn(source, target):
         for at in range(0, source.shape[0], 512):
             target[:, at : at + 512] = source[at : at + 512, :].T
+
+    turn(first_ref, first_t)
     half = width // 2
 
+    def produce(s, left, right_ref, row):
+        for buffer, offset, stage in ((other, right_ref.shape[0] // 2, 4), (own, 0, 0)):
+            right = right_ref[pl.ds(pl.multiple_of(row + offset, 16), columns), :]
+            for at in (0, half):
+                store_by_owner(buffer, s, at, nt(left[at : at + half, :], right), share)
+            group.copy(stage, s).start()
+
     def step(s, carry):
-        @pl.when(s < proj_tiles)
+        @pl.when(s < tiles - 1)
         def _():
-            right = dqkv_ref[pl.ds(pl.multiple_of(s * columns, 128), columns), :]
-            for at in (0, half):
-                store_by_owner(buffer, s, at, nt(first_t[at : at + half, :], right), share)
-            total.copy(0, s).start()
-
-        @pl.when(jnp.logical_and(s >= proj_tiles, s < tiles))
+            produce(s, first_t, dqkv_ref, s * columns)
+
+        @pl.when(s == tiles - 1)
         def _():
-            right = att_ref[pl.ds(pl.multiple_of((s - proj_tiles) * columns, 128), columns), :]
-            for at in (0, half):
-                store_by_owner(buffer, s, at, nt(dattn_t[at : at + half, :], right), share)
-            total.copy(0, s).start()
-
-        for stage in range(3):
+            produce(s, dattn_t, att_ref, 0)
+
+        @pl.when(s < tiles)
+        def _():
+            group.add(4, s)
+            group.cross(0, s).start()
+            group.cross(1, s).start()
+
+        @pl.when(s == 0)
+        def _():
+            turn(dattn_ref, dattn_t)
+
+        for stage in range(ring.stages):
+
+            @pl.when(s == 1 + stage)
+            def _():
+                ring.advance(stage)
+
+        @pl.when(jnp.logical_and(s >= 1, s - 1 < tiles))
+        def _():
+            group.add(0, s - 1)
+            group.add_cross(0, s - 1)
+            group.copy(1, s - 1).start()
+            group.add_cross(1, s - 1)
+
+        for stage in (1, 2):
             tile = s - 1 - stage
 
             @pl.when(jnp.logical_and(tile >= 0, tile < tiles))
             def _():
-                total.advance(stage, tile)
-
-        for stage in range(ring.stages):
-
-            @pl.when(s == 2 + 2 * stage)
-            def _():
-                ring.advance(stage)
+                group.add(stage, tile)
+                group.copy(stage + 1, tile).start()
 
         tile = s - 4
 
         @pl.when(tile >= 0)
         def _():
-            sums_ref[tile] = total.gather_stage(3, tile)[1].astype(BF)
+            sums_ref[tile] = group.total(3, tile)[2].astype(BF)
 
         return carry
 
@@ -970,22 +1032,26 @@
     every_ref[...] = packs[...]
 
     def finish(tile, carry):
-        for stage in range(4):
-            total.copy(stage, tile).wait_send()
+        group.wait_sends(tile)
         return carry
 
     lax.fori_loop(0, tiles, finish, 0)
 
 
-def can_sum_here(width, columns):
+def can_sum_here(width, proj, inner):
     places = lax.axis_size("dp")
-    return places == SUM_PLACES and width % (8 * places) == 0 and columns % 384 == 0
+    return (
+        places == SUM_PLACES
+        and lax.axis_size("mp") == 2
+        and width % (8 * places) == 0
+        and proj == 3 * inner
+        and inner % 32 == 0
+    )
 
 
 def attn_grads(first, dattn, dqkv, att, pack_own, pack_other):
     width = first.shape[1]
-    tile = 384
-    tiles = (dqkv.shape[0] + att.shape[0]) // tile
+    tiles, tile = 4, att.shape[0] // 2
     share = width // SUM_PLACES
     vmem = pl.BlockSpec(memory_space=pltpu.VMEM)
     sums, every = pl.pallas_call(
@@ -1000,12 +1066,15 @@
             pltpu.VMEM((width, first.shape[0]), BF),
             pltpu.VMEM((width, dattn.shape[0]), BF),
             pltpu.VMEM((tiles, width, tile), BF),
+            pltpu.VMEM((tiles, width, tile), BF),
             pltpu.VMEM((tiles, width // 2, tile), BF),
             pltpu.VMEM((tiles, width // 4, tile), BF),
             pltpu.VMEM((tiles, width // 8, tile), BF),
             pltpu.VMEM((tiles, width // 8, tile), BF),
-            pltpu.SemaphoreType.DMA((4, tiles)),
-            pltpu.SemaphoreType.DMA((4, tiles)),
+            pltpu.VMEM((tiles, width // 2, tile), BF),
+            pltpu.VMEM((tiles, width // 2, tile), BF),
+            pltpu.SemaphoreType.DMA((7, tiles)),
+            pltpu.SemaphoreType.DMA((7, tiles)),
             pltpu.VMEM((SUM_PLACES, 2) + pack_own.shape, BF),
             pltpu.SemaphoreType.DMA((SUM_PLACES.bit_length(),)),
             pltpu.SemaphoreType.DMA((SUM_PLACES.bit_length(),)),
@@ -1100,10 +1169,9 @@
 
     weight_own = jnp.transpose(attn_qkv.reshape(width, -1))
     tables = [rel_table] + [shift_mp(rel_table, s) for s in range(1, ways)]
-    mod, tables, weight_sent, out_sent = lax.optimization_barrier(
-        (mod, tables, weight_own, attn_out)
-    )
-    near_w, near_o = near_halves(weight_sent), near_halves(out_sent)
+    near_o = near_halves(attn_out)
+    mod, tables, weight_sent = lax.optimization_barrier((mod, tables, weight_own))
+    near_w = near_halves(weight_sent)
     fetch = ways == 2 and lax.axis_size("dp") % 4 == 0 and mlp_up.shape[0] % 32 == 0
     fetch = fetch and mlp_down.shape[0] % 64 == 0
     bias = bias_whole(jnp.concatenate(tables, axis=0))
@@ -1148,15 +1216,14 @@
             second, dmlp, up, down, (branch_mlp, dsecond)
         )
         reduced.append(scatter_dp(grads_next))
-    out, dtok, dmod, dattn, dqkv, strips = backward(
+    out_full, out_kept, dtok, dmod, dattn, dqkv, strips = backward(
         tokens, mod, pick, bias, qkv, lse, middle, branch, branch_mlp, dsecond, grads,
         weight, out_weight, per_block,
     )
     proj_block, out_block = weight_own.shape[0], attn_out.shape[0]
     dqkv, reduced[0] = lax.optimization_barrier((dqkv, reduced[0]))
     dtables = table_of_strips(strips)
-    here = can_sum_here(width, dqkv.shape[0]) and att.shape[0] % 384 == 0 and ways == 2
-    here = here and cols % width == 0
+    here = can_sum_here(width, dqkv.shape[0], att.shape[0]) and cols % width == 0
     if here:
         own_cond_rows = lax.dynamic_slice_in_dim(silu_cond, place * images, images, 0)
         pieces = cols // width
@@ -1175,7 +1242,7 @@
                 axis=0,
             )
             packs.append(jnp.pad(pack, ((0, -pack.shape[0] % 16), (0, 0))))
-        attn_sums, every = attn_grads(first, dattn, dqkv, att, *packs)
+        attn_total, every = attn_grads(first, dattn, dqkv, att, *packs)
         places, first_cond = every.shape[0], images * pieces
         every = every.reshape((places * ways,) + every.shape[2:]).astype(F32)
         all_columns = every[:, :first_cond].reshape(-1, cols)
@@ -1194,19 +1261,21 @@
         all_columns = lax.all_gather(dcolumns, "dp", axis=0, tiled=True)
         dtable = lax.psum(dtable, "dp")
         all_cond = lax.all_gather(silu_cond, "dp", axis=0, tiled=True).astype(F32)
-    split = ways * proj_block
-    attn_parts = [
-        jnp.concatenate(
+        split = ways * proj_block
+        attn_total = home(
             [
-                attn_sums[:, j * proj_block : (j + 1) * proj_block],
-                attn_sums[:, split + j * out_block : split + (j + 1) * out_block],
-            ],
-            axis=1,
-        )
-        for j in range(ways)
-    ]
-    totals = home([jnp.concatenate(pair, axis=1) for pair in zip(reduced, attn_parts)])
-    mlp_grads, attn_total = totals[:, : reduced[0].shape[1]], totals[:, reduced[0].shape[1] :]
+                jnp.concatenate(
+                    [
+                        attn_sums[:, j * proj_block : (j + 1) * proj_block],
+                        attn_sums[:, split + j * out_block : split + (j + 1) * out_block],
+                    ],
+                    axis=1,
+                )
+                for j in range(ways)
+            ]
+        )
+    mlp_grads = home(reduced)
+    attn_total = attn_total.astype(F32)
     grad_up, grad_down_t = split_mlp_grads(mlp_grads, tile_own)
     grad_qkv = attn_total[:, :proj_block].reshape(-1, 3, proj_block // 3)
     grad_out = jnp.transpose(attn_total[:, proj_block:])
@@ -1231,9 +1300,7 @@
     own_cond = lax.dynamic_slice_in_dim(conditioning, place * images, images, 0).astype(F32)
     grad_cond = jax.vjp(jax.nn.silu, own_cond)[1](grad_silu)[0].astype(BF)
 
-    out = out.reshape(images, PATCHES + padded, width)
-    out_full = out[:, :PATCHES].reshape(-1, width)
-    out_kept = out[:, PATCHES : PATCHES + keep].reshape(-1, width)
+    out_kept = out_kept.reshape(images, padded, width)[:, :keep].reshape(-1, width)
     return (
         out_kept, out_full, dtok, grad_cond, grad_ada_weight, grad_ada_bias, grad_qkv, grad_out,
         grad_up, jnp.transpose(grad_down_t), dtable,

time: 586 us -> 569 us (0.971)
  Pallas kernels: 450 us -> 430 us
  waiting for transfers between devices: 17.4 us -> 25.7 us
  local copies, waits for them, and re-layouts: 56.4 us -> 50.4 us
    pallas_call x1, Pallas kernels: 129 us -> 110 us  [attn_grads(): pl.pallas_call(attn_grads_kernel, in_specs=[vmem] * 6, out_specs=[vmem] *...]
    ppermute x4, waiting for transfers between devices: 13.5 us -> 23.8 us  [shift_mp(): lax.ppermute(value, 'mp', [(i, (i - steps) % ways) for i in range(ways)])]
    slice x5 -> x1, local copies, waits for them, and re-layouts: 6.46 us -> 0.13 us  [local(): out_kept.reshape(images, padded, width)[:, :keep].reshape(-1, width)]
  transfers between devices with their start and end apart: 10 -> 10, of which waited for: 3 -> 3; matrix products, arithmetic and copies ran while one was open for 11% -> 10% of each run, Pallas kernels for 56% -> 54%
where the time goes in v6:
time: 569 us; the launch traced here: 562 us
  Pallas kernels  430 us (76%)
  local copies, waits for them, and re-layouts  50.4 us (9%)
  waiting for transfers between devices  25.7 us (5%)
  between operations  14.9 us (3%)
  other arithmetic  14.8 us (3%)
  starting transfers between devices  14.2 us (2%)
  matrix products  12.1 us (2%)
    pallas_call x2, Pallas kernels, mlp(): pl.pallas_call(functools.partial(mlp_kernel, chunk, fresh, fetch is not N...  163 us
    pallas_call x1, Pallas kernels, attn_grads(): pl.pallas_call(attn_grads_kernel, in_specs=[vmem] * 6, out_specs=[vmem] *...  110 us
    pallas_call x1, Pallas kernels, backward(): pl.pallas_call(functools.partial(backward_kernel, per_block, weight_layou...  86.3 us
    pallas_call x1, Pallas kernels, forward(): pl.pallas_call(functools.partial(forward_kernel, per_block, weight_layout...  41.2 us
    ppermute x4, waiting for transfers between devices, shift_mp(): lax.ppermute(value, 'mp', [(i, (i - steps) % ways) for i in range(ways)])  23.8 us
    pallas_call x1, Pallas kernels, own_heads(): pl.pallas_call(functools.partial(own_heads_kernel, per_block), grid=(imag...  19.8 us
  transfers between devices with their start and end apart: 10, of which 3 were waited for; matrix products, arithmetic and copies ran while one was open for 10% of the time, Pallas kernels for 54%

profile of v6, /device:TPU:0, one launch (start us, length us, event | category | flops | bytes accessed | tf_op | source)
XLA Modules:
  0.0 562.4 jit_solution(10203053249141078759)
XLA Ops:
  7.2 4.4 fusion.2
  11.6 0.7 all_to_all.13
  12.3 4.2 all-to-all-start
  16.5 2.1 collective-permute-start
  18.6 1.9 all-to-all-done
  20.6 0.7 pad_convert_fusion.mod_ref.refs_5_.refs_7_
  21.3 3.0 constant_dynamic-slice_fusion.3
  24.3 1.2 collective-permute-start.1
  25.5 0.9 constant_dynamic-slice_fusion.2
  26.4 0.8 collective-permute-start.2
  27.2 0.9 fusion.4.pick_ref.refs_6_.refs_8_
  28.5 2.0 fusion.29
  30.5 1.1 stack.68
  31.6 1.1 stack.69
  32.7 1.1 stack.70
  33.8 1.1 stack.71
  34.9 0.8 stack.72
  37.5 1.5 stack.67
  39.0 0.8 pad.102.strip_ref
  39.8 9.7 %shard_map.203.bias_ref.refs_7_.refs_9_ = f32[16,256,256]{2,1,0:T(8,128)} custom-call(f32[16,16,512]{2,1,0:T(8,128)} %pad.102.strip_ref), custom_call_target="tpu_custom_call" | custom-call | flops 1000000 | bytes 100000 | tf_op jit(solution)/shard_map/pallas_call | solution.py:84
  49.6 19.8 %shard_map.204 = (bf16[1024,1152]{1,0:T(8,128)(2,1)}, bf16[1728,1024]{1,0:T(8,128)(2,1)}, bf16[576,2048]{1,0:T(8,128)(2,1)}, f32[4,16,256]{2,1,0:T(8,128)}) custom-call(bf16[1024,1152]{1,0:T(8,128)(2,1)} %refs_6_.1, f32[4,8,1152]{2,1,0:T(8,128)} %pad_convert_fusion.mod_ref.refs_5_.refs_7_, bf16[4,192,256]{2,1,0:T(8,128)(2,1)} %fusion.4.pick_ref.refs_6_.refs_8_, ...), custom_call_target="tpu_custom_call" | custom-call | flops 10000000 | bytes 100000 | tf_op jit(solution)/shard_map/pallas_call | solution.py:229
  69.4 13.6 %collective-permute-done.2.refs_11_.refs_4_ = bf16[288,1152]{1,0:T(8,128)(2,1)} collective-permute-done((bf16[288,1152]{1,0:T(8,128)(2,1)}, bf16[288,1152]{1,0:T(8,128)(2,1)}, u32[]{:S(2)}, u32[]{:S(2)}) %collective-permute-start.2) | collective-permute-done | bytes 663584 | tf_op jit(solution)/shard_map/ppermute | solution.py:1094
  84.0 1.8 fusion.3
  85.8 1.1 slice.167
  87.0 3.0 fusion.dmlp_ref
  90.0 41.2 %shard_map.205 = (bf16[3456,1024]{1,0:T(8,128)(2,1)}, bf16[1152,2048]{1,0:T(8,128)(2,1)}, f32[4,32,256]{2,1,0:T(8,128)}, f32[1792,1152]{1,0:T(8,128)}, bf16[1792...) custom-call(bf16[1024,1152]{1,0:T(8,128)(2,1)} %get-tuple-element.61.refs_0_.first_ref, ...), custom_call_target="tpu_custom_call" | custom-call | flops 8000000000 | bytes 32000000 | tf_op jit(solution)/shard_map/pallas_call | solution.py:354
  131.3 83.4 %shard_map.206 = (f32[1792,1152]{1,0:T(8,128)}, f32[1792,1152]{1,0:T(8,128)}, bf16[1152,4608]{1,0:T(8,128)(2,1)}, bf16[1152,2304]{1,0:T(8,128)(2,1)}, bf16[2304,1152]{1,0:T(8,128)(2,1)}) custom-call(bf16[1792,1152]{1,0:T(8,128)(2,1)} %get-tuple-element.69.second_ref, bf16[1792,1152]{1,0:T(8,128)(2,1)} %fusion.dmlp_ref, bf16[1152,2304]{1,0:T(8,128)(2,1)} %refs_1_.1, ...), custom_call_target="tpu_custom_call" | custom-call | flops 60000002048 | bytes 60000000 | tf_op jit(solution)/shard_map/pallas_call | solution.py:576
  214.7 80.1 %shard_map.207 = (f32[1792,1152]{1,0:T(8,128)}, f32[1792,1152]{1,0:T(8,128)}, bf16[1152,4608]{1,0:T(8,128)(2,1)}) custom-call(bf16[1792,1152]{1,0:T(8,128)(2,1)} %get-tuple-element.69.second_ref, bf16[1792,1152]{1,0:T(8,128)(2,1)} %fusion.dmlp_ref, bf16[1152,2304]{1,0:T(8,128)(2,1)} %get-tuple-element.71.up_ref, ...), custom_call_target="tpu_custom_call" | custom-call | flops 10000000 | bytes 100000 | tf_op jit(solution)/shard_map/pallas_call | solution.py:576
  295.0 0.6 copy-done.12
  295.6 86.3 %shard_map.208 = (bf16[1024,1152]{1,0:T(8,128)(2,1)}, bf16[768,1152]{1,0:T(8,128)(2,1)}, bf16[1024,1152]{1,0:T(8,128)(2,1)}, f32[4,8,1152]{2,1,0:T(8,128)}, bf16...) custom-call(bf16[1728,1152]{1,0:T(8,128)(2,1)} %bitcast.96, ...), custom_call_target="tpu_custom_call" | custom-call | flops 10000000 | bytes 100000 | tf_op jit(solution)/shard_map/pallas_call | solution.py:727
  381.9 3.8 reshape.129
  385.8 2.9 slice_bitcast_fusion.15
  388.7 1.1 add_convert_fusion
  390.2 0.6 pad.121.pack_own_ref
  390.8 0.6 pad.123.pack_other_ref
  391.6 1.6 reshape.127
  393.2 109.6 %shard_map.209 = (bf16[4,144,576]{2,1,0:T(8,128)(2,1)}, bf16[16,2,32,1152]{3,2,1,0:T(8,128)(2,1)}) custom-call(bf16[1024,1152]{1,0:T(8,128)(2,1)} %get-tuple-element.61.refs_0_.first_ref, bf16[2048,1152]{1,0:T(8,128)(2,1)} %get-tuple-element.80.dattn_ref, bf16[3456,1024]{1,0:T(8,128)(2,1)} %get-tuple-element.83.dqkv_ref, ...), custom_call_target="tpu_custom_call" | custom-call | flops 10000000 | bytes 100000 | tf_op jit(solution)/shard_map/pallas_call | solution.py:1057
  502.9 1.4 slice.240
  504.2 2.1 slice.239
  506.3 1.5 reshape.135
  507.8 1.7 reshape.134
  509.5 1.0 convert_bitcast_fusion
  510.8 1.3 reshape.138
  512.1 0.7 bitcast_convert_fusion
  512.8 2.2 copy-done.3
  515.2 1.6 reshape.132
  516.8 1.0 subtract_convert_fusion
  517.9 5.5 fusion.7
  523.4 0.6 reshape.133
  524.0 3.2 all-to-all-start.1
  527.3 0.8 slice_bitcast_fusion.16
  528.1 2.2 fusion.18
  530.3 2.0 collective-permute-start.5
  532.3 1.8 slice_reduce_fusion
  534.1 0.7 reduce_sum.28
  535.1 0.8 copy.107
  535.9 0.6 slice.246
  536.6 0.6 fusion.25
  537.2 10.1 %collective-permute-done.5 = bf16[72,4608]{1,0:T(8,128)(2,1)} collective-permute-done((bf16[72,4608]{1,0:T(8,128)(2,1)}, bf16[72,4608]{1,0:T(8,128)(2,1)}, u32[]{:S(2)}, u32[]{:S(2)}) %collective-permute-start.5) | collective-permute-done | bytes 663584 | tf_op jit(solution)/shard_map/ppermute | solution.py:1094
  547.3 1.2 convert_add_fusion
  548.6 0.9 reshape.137
  549.5 3.9 slice_reduce_fusion.1
  553.4 1.0 copy.125
  554.3 1.0 copy.124
  (79 shorter events, 4.4 us)
Async XLA Ops:
  7.2 20.0 %copy-start = (s32[8,179]{1,0:T(8,128)S(1)}, s32[8,179]{1,0:T(8,128)}, u32[]{:S(2)}) copy-start(s32[8,179]{1,0:T(8,128)} %param.14) | copy-start | bytes 17188
  7.2 9.3 %copy-start.15 = (f32[8,961]{1,0:T(8,128)S(1)}, f32[8,961]{1,0:T(8,128)}, u32[]{:S(2)}) copy-start(f32[8,961]{1,0:T(8,128)} %param.21) | copy-start | bytes 92260
  11.6 13.9 %copy-start.7 = (bf16[576,1152]{1,0:T(8,128)(2,1)S(1)}, bf16[576,1152]{1,0:T(8,128)(2,1)}, u32[]{:S(2)}) copy-start(bf16[576,1152]{1,0:T(8,128)(2,1)} %refs_3_.1) | copy-start | bytes 3981316
  12.3 8.3 %all-to-all-start = ((bf16[2,4,3456]{2,1,0:T(4,128)(2,1)}), bf16[2,4,3456]{2,1,0:T(4,128)(2,1)S(1)}, u32[]{:S(2)}, u32[]{:S(2)}) async-start(bf16[2,4,3456]{2,1,0:T(4,128)(2,1)} %all_to_all.13), calls=%async_computation | async-start | bytes 110592 | tf_op jit(solution)/shard_map/all_to_all | solution.py:1167
  16.5 376.7 %reduce-scatter.3.cloned.1.call-start = ((), (), s32[]{:S(2)}) async-start(), calls=%async_computation.4 | async-start | bytes 11280384 | tf_op jit(solution)/shard_map/reduce_scatter | solution.py:1148
  16.5 4.8 collective-permute-start
  24.3 58.7 %collective-permute-start.1 = (bf16[864,1152]{1,0:T(8,128)(2,1)}, bf16[864,1152]{1,0:T(8,128)(2,1)}, u32[]{:S(2)}, u32[]{:S(2)}) collective-permute-start(bf16[864,1152]{1,0:T(8,128)(2,1)} %constant_dynamic-slice_fusion.3), channel_id=1, source_target_pairs={{0,1},{1,0},{2,3},{3,2},{4,5},{5,4},{6,7},{7,6},{8,9},{9,8},{10,11... | collective-permute-start | bytes 5971976 | tf_op jit(solution)/shard_map/ppermute | solution.py:1094
  26.4 56.6 %collective-permute-start.2 = (bf16[288,1152]{1,0:T(8,128)(2,1)}, bf16[288,1152]{1,0:T(8,128)(2,1)}, u32[]{:S(2)}, u32[]{:S(2)}) collective-permute-start(bf16[288,1152]{1,0:T(8,128)(2,1)} %constant_dynamic-slice_fusion.2), channel_id=1, source_target_pairs={{0,1},{1,0},{2,3},{3,2},{4,5},{5,4},{6,7},{7,6},{8,9},{9,8},{10,11... | collective-permute-start | bytes 1990664 | tf_op jit(solution)/shard_map/ppermute | solution.py:1094
  49.6 34.0 %copy-start.9 = (bf16[716,1152]{1,0:T(8,128)(2,1)S(1)}, bf16[716,1152]{1,0:T(8,128)(2,1)}, u32[]{:S(2)}) copy-start(bf16[716,1152]{1,0:T(8,128)(2,1)} %param.22) | copy-start | bytes 4948996
  83.0 7.0 %collective-permute-start.3 = (bf16[864,1152]{1,0:T(8,128)(2,1)}, bf16[864,1152]{1,0:T(8,128)(2,1)}, u32[]{:S(2)}, u32[]{:S(2)}) collective-permute-start(bf16[864,1152]{1,0:T(8,128)(2,1)} %collective-permute-done.1.refs_8_.refs_1_), channel_id=1, source_target_pairs={{0,2},{2,0},{4,6},{6,4},{8,10},{10,8},{12,14},{14,12},{16,18},{18,... | collective-permute-start | bytes 5971976 | tf_op jit(solution)/shard_map/ppermute | solution.py:1126
  83.0 7.0 %collective-permute-start.4 = (bf16[288,1152]{1,0:T(8,128)(2,1)}, bf16[288,1152]{1,0:T(8,128)(2,1)}, u32[]{:S(2)}, u32[]{:S(2)}) collective-permute-start(bf16[288,1152]{1,0:T(8,128)(2,1)} %collective-permute-done.2.refs_11_.refs_4_), channel_id=1, source_target_pairs={{0,2},{2,0},{4,6},{6,4},{8,10},{10,8},{12,14},{14,12},{16,18},{18,... | collective-permute-start | bytes 1990664 | tf_op jit(solution)/shard_map/ppermute | solution.py:1126
  85.8 4.2 copy-start.2
  214.7 315.6 %reduce-scatter.5.cloned.1.call-start = ((), (), s32[]{:S(2)}) async-start(), calls=%async_computation.5 | async-start | bytes 11280384 | tf_op jit(solution)/shard_map/reduce_scatter | solution.py:1148
  294.8 0.7 copy-start.12
  388.6 1.4 copy-start.14
  388.6 2.8 copy-start.10
  504.2 7.8 %copy-start.5 = (bf16[16,2,32,1152]{3,2,1,0:T(8,128)(2,1)S(1)}, bf16[16,2,32,1152]{3,2,1,0:T(8,128)(2,1)}, u32[]{:S(2)}) copy-start(bf16[16,2,32,1152]{3,2,1,0:T(8,128)(2,1)} %get-tuple-element.87) | copy-start | bytes 7077892
  512.8 2.2 copy-start.3
  517.8 9.4 %copy-start.8 = (f32[72,2304]{1,0:T(8,128)S(1)}, f32[72,2304]{1,0:T(8,128)}, u32[]{:S(2)}) copy-start(f32[72,2304]{1,0:T(8,128)} %reshape.138) | copy-start | bytes 1990660
  517.8 10.2 %copy-start.6 = (bf16[128,3456]{1,0:T(8,128)(2,1)S(1)}, bf16[128,3456]{1,0:T(8,128)(2,1)}, u32[]{:S(2)}) copy-start(bf16[128,3456]{1,0:T(8,128)(2,1)} %reshape.135) | copy-start | bytes 2654212
  523.4 10.7 %copy-start.4 = (f32[128,3456]{1,0:T(8,128)S(1)}, f32[128,3456]{1,0:T(8,128)}, u32[]{:S(2)}) copy-start(f32[128,3456]{1,0:T(8,128)} %reshape.132) | copy-start | bytes 5308420
  524.0 12.5 %all-to-all-start.1 = ((bf16[2,4,1152]{2,1,0:T(4,128)(2,1)}), bf16[2,4,1152]{2,1,0:T(4,128)(2,1)S(1)}, u32[]{:S(2)}, u32[]{:S(2)}) async-start(bf16[2,4,1152]{2,1,0:T(4,128)(2,1)} %reshape.133), calls=%async_computation.2 | async-start | bytes 36864 | tf_op jit(solution)/shard_map/all_to_all | solution.py:1295
  530.3 4.5 slice-start
  530.3 6.3 %copy-start.13 = (bf16[8,1152]{1,0:T(8,128)(2,1)S(1)}, bf16[8,1152]{1,0:T(8,128)(2,1)}, u32[]{:S(2)}) copy-start(bf16[8,1152]{1,0:T(8,128)(2,1)} %param.13) | copy-start | bytes 55300
  530.3 17.1 %collective-permute-start.5 = (bf16[72,4608]{1,0:T(8,128)(2,1)}, bf16[72,4608]{1,0:T(8,128)(2,1)}, u32[]{:S(2)}, u32[]{:S(2)}) collective-permute-start(bf16[72,4608]{1,0:T(8,128)(2,1)} %reduce-scatter.5.cloned.1.call-done), channel_id=1, source_target_pairs={{0,1},{1,0},{2,3},{3,2},{4,5},{5,4},{6,7},{7,6},{8,9},{9,8},{10,11... | collective-permute-start | bytes 1990664 | tf_op jit(solution)/shard_map/ppermute | solution.py:1094
  534.1 13.3 %copy-start.11 = (bf16[72,4608]{1,0:T(8,128)(2,1)S(1)}, bf16[72,4608]{1,0:T(8,128)(2,1)}, u32[]{:S(2)}) copy-start(bf16[72,4608]{1,0:T(8,128)(2,1)} %reduce-scatter.3.cloned.1.call-done) | copy-start | bytes 1990660
  547.3 8.0 %copy-start.1 = (s32[8,179]{1,0:T(8,128)S(1)}, s32[8,179]{1,0:T(8,128)}, u32[]{:S(2)}) copy-start(s32[8,179]{1,0:T(8,128)} %param.14) | copy-start | bytes 17188
Sparse Core Ops, SparseCore 0:
  214.8 120.2 reduce-scatter.2
  339.1 153.2 reduce-scatter.4

commit v7 on v6

--- a/solution.py
+++ b/solution.py
@@ -949,10 +949,120 @@
             self.copy(stage).wait_send()
 
 
+class SmallGrads:
+    def __init__(
+        self, images, pieces, table_rows, ring, ada, ada_s, part_s, silu_own, silu_got, sems
+    ):
+        self.images, self.pieces, self.table_rows = images, pieces, table_rows
+        self.ring, self.ada, self.ada_s, self.part_s = ring, ada, ada_s, part_s
+        self.silu_own, self.silu_got, self.sems = silu_own, silu_got, sems
+        self.rows = ring.packs.shape[2]
+        self.first_cond = images * pieces
+
+    def row_of(self, shape, axis):
+        return lax.broadcasted_iota(jnp.int32, shape, axis) & (self.rows - 1)
+
+    def any_image(self, test):
+        found = test(0)
+        for image in range(1, self.images):
+            found = jnp.logical_or(found, test(image))
+        return found
+
+    def of_piece(self, row, piece):
+        return self.any_image(lambda image: row == image * self.pieces + piece)
+
+    def piece(self, index):
+        width = self.ada_s.shape[1]
+        return pltpu.make_async_copy(
+            self.ada.at[:, index * width : (index + 1) * width], self.ada_s, self.sems.at[0]
+        )
+
+    def exchange(self):
+        return pltpu.make_async_remote_copy(
+            src_ref=self.silu_own.at[1],
+            dst_ref=self.silu_got,
+            send_sem=self.sems.at[1],
+            recv_sem=self.sems.at[2],
+            device_id={"mp": 1 - self.ring.side},
+            device_id_type=pl.DeviceIdType.MESH,
+        )
+
+    def add_piece(self, index):
+        mine = self.ring.packs[self.ring.slot]
+        mine = mine.reshape(2 * self.rows, mine.shape[-1]).astype(F32)
+        masked = jnp.where(self.of_piece(self.row_of(mine.shape, 0), index), mine, 0.0)
+        self.piece(index).wait()
+        product = nt(masked.astype(BF), self.ada_s[...])
+        if index:
+            self.part_s[...] += product
+        else:
+            self.part_s[...] = product
+        if index + 1 < self.pieces:
+            self.piece(index + 1).start()
+            return
+        for k, side in enumerate((self.ring.side, 1 - self.ring.side)):
+            block = self.part_s[pl.ds(pl.multiple_of(side * self.rows, 8), self.rows), :]
+            found = [
+                jnp.sum(block[n * self.pieces : (n + 1) * self.pieces], axis=0, keepdims=True)
+                for n in range(self.images)
+            ]
+            found.append(jnp.zeros((self.silu_got.shape[0] - self.images, block.shape[1]), F32))
+            self.silu_own[k] = jnp.concatenate(found, axis=0).astype(BF)
+        self.exchange().start()
+
+    def reduce(self, ada_grad_ref, small_ref):
+        group = 128 // (2 * self.rows)
+        width, share = self.ada_s.shape[1], ada_grad_ref.shape[1]
+        left, right = self.row_of((128, 128), 0), self.row_of((128, 128), 1)
+        left_all = lax.broadcasted_iota(jnp.int32, (128, 128), 0)
+        right_all = lax.broadcasted_iota(jnp.int32, (128, 128), 1)
+        same = (left_all - left) == (right_all - right)
+        spread = jnp.logical_and(
+            same,
+            self.any_image(
+                lambda n: jnp.logical_and(
+                    jnp.logical_and(left >= n * self.pieces, left < (n + 1) * self.pieces),
+                    right == self.first_cond + n,
+                )
+            ),
+        )
+        spread = jnp.where(spread, 1.0, 0.0).astype(BF)
+        line = lax.broadcasted_iota(jnp.int32, (16, 128), 0)
+        at = self.row_of((16, 128), 1)
+        chosen = jnp.logical_and(
+            jnp.logical_and(line >= self.pieces, line < self.pieces + self.table_rows),
+            at == line - self.pieces + self.first_cond + self.images,
+        )
+        for p in range(self.pieces):
+            chosen = jnp.logical_or(chosen, jnp.logical_and(line == p, self.of_piece(at, p)))
+        chosen = jnp.where(chosen, 1.0, 0.0).astype(BF)
+        wanted = lax.broadcasted_iota(jnp.int32, (width, 128), 0) - self.ring.place * share
+        lane = lax.broadcasted_iota(jnp.int32, (width, 128), 1)
+        wanted = jnp.where(wanted == lane, 1.0, 0.0).astype(BF)
+        ada_grad_ref[...] = jnp.zeros_like(ada_grad_ref)
+        small_ref[...] = jnp.zeros_like(small_ref)
+
+        def one(k, carry):
+            block = self.ring.packs[pl.ds(k * group, group)].reshape(128, width)
+            cond = nn(spread, nn(block, wanted).astype(BF))
+            for p in range(self.pieces):
+                mine = jnp.where(self.of_piece(left, p), cond, 0.0).astype(BF)
+                ada_grad_ref[p] += tn(mine, block)[:share]
+            small_ref[...] += nn(chosen, block)
+            return carry
+
+        lax.fori_loop(0, SUM_PLACES // group, one, 0)
+
+    def finish(self, silu_ref):
+        self.exchange().wait()
+        silu_ref[...] = self.silu_own[0].astype(F32) + self.silu_got[...].astype(F32)
+
+
 def attn_grads_kernel(
-    first_ref, dattn_ref, dqkv_ref, att_ref, pack_own_ref, pack_other_ref, sums_ref, every_ref,
-    first_t, dattn_t, own, other, land0, land1, land2, land3, land_other, land_cross,
-    sends, recvs, packs, pack_sends, pack_recvs,
+    images, pieces, table_rows, first_ref, dattn_ref, dqkv_ref, att_ref, pack_own_ref,
+    pack_other_ref, ada_ref, sums_ref, ada_grad_ref, small_ref, silu_ref, first_t,
+    dattn_t, own, other, land0, land1, land2, land3, land_other, land_cross,
+    sends, recvs, packs, pack_sends, pack_recvs, ada_s, part_s, silu_own, silu_got, small_sems,
 ):
     width = first_t.shape[0]
     tiles, _, columns = own.shape
@@ -960,6 +1070,9 @@
     group = GroupSum(own, other, (land0, land1, land2, land3), land_other, land_cross, sends, recvs)
     ring = PackGather(pack_own_ref, pack_other_ref, packs, pack_sends, pack_recvs)
     barrier = pltpu.get_barrier_semaphore()
+    small = SmallGrads(
+        images, pieces, table_rows, ring, ada_ref, ada_s, part_s, silu_own, silu_got, small_sems
+    )
     group.greet(barrier)
     ring.greet(barrier)
     pl.semaphore_wait(barrier, len(HALVING) + 2)
@@ -996,13 +1109,25 @@
 
         @pl.when(s == 0)
         def _():
+            small.piece(0).start()
             turn(dattn_ref, dattn_t)
 
         for stage in range(ring.stages):
 
-            @pl.when(s == 1 + stage)
+            @pl.when(s == stage)
             def _():
                 ring.advance(stage)
+
+        for piece in range(pieces):
+
+            @pl.when(s == 1 + piece)
+            def _():
+                small.add_piece(piece)
+
+        @pl.when(s == ring.stages)
+        def _():
+            ring.finish()
+            small.reduce(ada_grad_ref, small_ref)
 
         @pl.when(jnp.logical_and(s >= 1, s - 1 < tiles))
         def _():
@@ -1028,8 +1153,7 @@
         return carry
 
     lax.fori_loop(0, tiles + 4, step, 0)
-    ring.finish()
-    every_ref[...] = packs[...]
+    small.finish(silu_ref)
 
     def finish(tile, carry):
         group.wait_sends(tile)
@@ -1049,18 +1173,21 @@
     )
 
 
-def attn_grads(first, dattn, dqkv, att, pack_own, pack_other):
+def attn_grads(first, dattn, dqkv, att, pack_own, pack_other, ada_weight, images, table_rows):
     width = first.shape[1]
     tiles, tile = 4, att.shape[0] // 2
     share = width // SUM_PLACES
+    pieces = ada_weight.shape[1] // width
     vmem = pl.BlockSpec(memory_space=pltpu.VMEM)
-    sums, every = pl.pallas_call(
-        attn_grads_kernel,
-        in_specs=[vmem] * 6,
-        out_specs=[vmem] * 2,
+    sums, ada_grad, small, silu = pl.pallas_call(
+        functools.partial(attn_grads_kernel, images, pieces, table_rows),
+        in_specs=[vmem] * 6 + [ANYWHERE],
+        out_specs=[vmem] * 4,
         out_shape=[
             jax.ShapeDtypeStruct((tiles, 2 * share, tile), BF),
-            jax.ShapeDtypeStruct((SUM_PLACES, 2) + pack_own.shape, BF),
+            jax.ShapeDtypeStruct((pieces, share, width), F32),
+            jax.ShapeDtypeStruct((16, width), F32),
+            jax.ShapeDtypeStruct((16, width), F32),
         ],
         scratch_shapes=[
             pltpu.VMEM((width, first.shape[0]), BF),
@@ -1078,15 +1205,26 @@
             pltpu.VMEM((SUM_PLACES, 2) + pack_own.shape, BF),
             pltpu.SemaphoreType.DMA((SUM_PLACES.bit_length(),)),
             pltpu.SemaphoreType.DMA((SUM_PLACES.bit_length(),)),
+            pltpu.VMEM((width, width), BF),
+            pltpu.VMEM((2 * pack_own.shape[0], width), F32),
+            pltpu.VMEM((2, 16, width), BF),
+            pltpu.VMEM((16, width), BF),
+            pltpu.SemaphoreType.DMA((3,)),
         ],
         compiler_params=pltpu.CompilerParams(
             vmem_limit_bytes=VMEM_LIMIT, collective_id=1, has_side_effects=True
         ),
         cost_estimate=cost(1e7, 1e5),
-    )(first, dattn, dqkv, att, pack_own, pack_other)
+    )(first, dattn, dqkv, att, pack_own, pack_other, ada_weight)
     here = place_bit(lax.axis_index("dp"), FINAL) * share
     mine = lax.dynamic_slice_in_dim(sums, here, share, 1)
-    return jnp.transpose(mine, (1, 0, 2)).reshape(share, -1), every
+    return (
+        jnp.transpose(mine, (1, 0, 2)).reshape(share, -1),
+        jnp.transpose(ada_grad, (1, 0, 2)).reshape(share, -1),
+        small[:pieces].reshape(-1),
+        small[pieces : pieces + table_rows, :BUCKETS],
+        silu[:images],
+    )
 
 
 def shift_mp(value, steps):
@@ -1164,12 +1302,13 @@
 
     silu_cond = jax.nn.silu(conditioning.astype(F32)).astype(BF)
     columns = (jnp.dot(silu_cond, ada_weight, preferred_element_type=F32) + ada_bias).astype(BF)
+    near_o = near_halves(attn_out)
+    columns, near_o = lax.optimization_barrier((columns, near_o))
     mod = lax.all_to_all(columns, "mp", split_axis=0, concat_axis=1, tiled=True)
     mod = jnp.pad(mod.astype(F32).reshape(images, 6, width), ((0, 0), (0, 2), (0, 0)))
 
     weight_own = jnp.transpose(attn_qkv.reshape(width, -1))
     tables = [rel_table] + [shift_mp(rel_table, s) for s in range(1, ways)]
-    near_o = near_halves(attn_out)
     mod, tables, weight_sent = lax.optimization_barrier((mod, tables, weight_own))
     near_w = near_halves(weight_sent)
     fetch = ways == 2 and lax.axis_size("dp") % 4 == 0 and mlp_up.shape[0] % 32 == 0
@@ -1223,10 +1362,12 @@
     proj_block, out_block = weight_own.shape[0], attn_out.shape[0]
     dqkv, reduced[0] = lax.optimization_barrier((dqkv, reduced[0]))
     dtables = table_of_strips(strips)
+    pieces = cols // width
+    used = images * (pieces + 1) + per_block
     here = can_sum_here(width, dqkv.shape[0], att.shape[0]) and cols % width == 0
+    here = here and used <= 32 and pieces + per_block <= 16 and pieces <= 3
     if here:
         own_cond_rows = lax.dynamic_slice_in_dim(silu_cond, place * images, images, 0)
-        pieces = cols // width
         packs = []
         for steps in range(ways):
             at = (place + steps) % ways
@@ -1241,15 +1382,9 @@
                 ],
                 axis=0,
             )
-            packs.append(jnp.pad(pack, ((0, -pack.shape[0] % 16), (0, 0))))
-        attn_total, every = attn_grads(first, dattn, dqkv, att, *packs)
-        places, first_cond = every.shape[0], images * pieces
-        every = every.reshape((places * ways,) + every.shape[2:]).astype(F32)
-        all_columns = every[:, :first_cond].reshape(-1, cols)
-        all_cond = every[:, first_cond : first_cond + images].reshape(-1, width)
-        dtable = jnp.sum(every[:, first_cond + images :], axis=0)[:per_block, :BUCKETS]
-        dcolumns = lax.dynamic_slice_in_dim(
-            all_columns, pack_slot(lax.axis_index("dp")) * images_group, images_group, 0
+            packs.append(jnp.pad(pack, ((0, 32 - used), (0, 0))))
+        attn_total, grad_ada_weight, grad_ada_bias, dtable, grad_silu = attn_grads(
+            first, dattn, dqkv, att, *packs, ada_weight, images, per_block
         )
     else:
         dweight = dot(first, dqkv, (0, 1)).astype(BF)
@@ -1261,6 +1396,23 @@
         all_columns = lax.all_gather(dcolumns, "dp", axis=0, tiled=True)
         dtable = lax.psum(dtable, "dp")
         all_cond = lax.all_gather(silu_cond, "dp", axis=0, tiled=True).astype(F32)
+        slice_width = width // lax.axis_size("dp")
+        cond_slice = lax.dynamic_slice_in_dim(
+            all_cond, lax.axis_index("dp") * slice_width, slice_width, 1
+        )
+        grad_ada_weight = lax.dot_general(
+            cond_slice, all_columns, (((0,), (0,)), ((), ())), precision=PRECISE
+        )
+        grad_ada_bias = jnp.sum(all_columns, axis=0)
+        dcolumns_high = dcolumns.astype(BF)
+        dcolumns_low = (dcolumns - dcolumns_high.astype(F32)).astype(BF)
+        silu_part = nt(jnp.concatenate([dcolumns_high, dcolumns_low], axis=0), ada_weight)
+        silu_part = silu_part[:images_group] + silu_part[images_group:]
+        shares = lax.all_to_all(
+            silu_part.astype(BF).reshape(ways, images, width), "mp", split_axis=0, concat_axis=0,
+            tiled=True,
+        )
+        grad_silu = jnp.sum(shares.astype(F32), axis=0)
         split = ways * proj_block
         attn_total = home(
             [
@@ -1280,23 +1432,6 @@
     grad_qkv = attn_total[:, :proj_block].reshape(-1, 3, proj_block // 3)
     grad_out = jnp.transpose(attn_total[:, proj_block:])
 
-    slice_width = width // lax.axis_size("dp")
-    cond_slice = lax.dynamic_slice_in_dim(
-        all_cond, lax.axis_index("dp") * slice_width, slice_width, 1
-    )
-    grad_ada_weight = lax.dot_general(
-        cond_slice, all_columns, (((0,), (0,)), ((), ())), precision=PRECISE
-    )
-    grad_ada_bias = jnp.sum(all_columns, axis=0)
-    dcolumns_high = dcolumns.astype(BF)
-    dcolumns_low = (dcolumns - dcolumns_high.astype(F32)).astype(BF)
-    silu_part = nt(jnp.concatenate([dcolumns_high, dcolumns_low], axis=0), ada_weight)
-    silu_part = silu_part[:images_group] + silu_part[images_group:]
-    shares = lax.all_to_all(
-        silu_part.astype(BF).reshape(ways, images, width), "mp", split_axis=0, concat_axis=0,
-        tiled=True,
-    )
-    grad_silu = jnp.sum(shares.astype(F32), axis=0)
     own_cond = lax.dynamic_slice_in_dim(conditioning, place * images, images, 0).astype(F32)
     grad_cond = jax.vjp(jax.nn.silu, own_cond)[1](grad_silu)[0].astype(BF)
 

time: 569 us -> 560 us (0.984)
  matrix products: 12.1 us -> 4.4 us
    another operation x17, local copies, waits for them, and re-layouts: 8.39 us -> 19.9 us  [bias_whole(): jnp.stack([grid_table[:, :, GRID - 1 - c:2 * GRID - 1 - c] for c in range...]
    dot_general x2 -> x0, matrix products: 7.72 us -> none  [the longest x1 5.53 us: dot(): lax.dot_general(a, b, ((dims[0:1], dims[1:2]), ((), ())), preferred_eleme...]
  transfers between devices with their start and end apart: 10 -> 9, of which waited for: 3 -> 3; matrix products, arithmetic and copies ran while one was open for 10% -> 10% of each run, Pallas kernels for 54% -> 55%
where the time goes in v7:
time: 560 us; the launch traced here: 552 us
  Pallas kernels  431 us (77%)
  local copies, waits for them, and re-layouts  55.1 us (10%)
  waiting for transfers between devices  24.9 us (4%)
  between operations  14.8 us (3%)
  other arithmetic  11.3 us (2%)
  starting transfers between devices  10.9 us (2%)
    pallas_call x2, Pallas kernels, mlp(): pl.pallas_call(functools.partial(mlp_kernel, chunk, fresh, fetch is not N...  163 us
    pallas_call x1, Pallas kernels, attn_grads(): pl.pallas_call(functools.partial(attn_grads_kernel, images, pieces, table...  111 us
    pallas_call x1, Pallas kernels, backward(): pl.pallas_call(functools.partial(backward_kernel, per_block, weight_layou...  86.3 us
    pallas_call x1, Pallas kernels, forward(): pl.pallas_call(functools.partial(forward_kernel, per_block, weight_layout...  41.2 us
    ppermute x4, waiting for transfers between devices, shift_mp(): lax.ppermute(value, 'mp', [(i, (i - steps) % ways) for i in range(ways)])  22.9 us
    another operation x17, local copies, waits for them, and re-layouts, bias_whole(): jnp.stack([grid_table[:, :, GRID - 1 - c:2 * GRID - 1 - c] for c in range...  19.9 us
    pallas_call x1, Pallas kernels, own_heads(): pl.pallas_call(functools.partial(own_heads_kernel, per_block), grid=(imag...  19.8 us
  transfers between devices with their start and end apart: 9, of which 3 were waited for; matrix products, arithmetic and copies ran while one was open for 10% of the time, Pallas kernels for 55%

profile of v7, /device:TPU:0, one launch (start us, length us, event | category | flops | bytes accessed | tf_op | source)
XLA Modules:
  0.0 552.4 jit_solution(742249763203184817)
XLA Ops:
  7.2 1.1 constant_dynamic-slice_fusion.3
  8.4 3.0 collective-permute-start
  11.4 4.4 fusion.2
  15.8 10.6 %collective-permute-done.refs_11_.refs_4_ = bf16[288,1152]{1,0:T(8,128)(2,1)} collective-permute-done((bf16[288,1152]{1,0:T(8,128)(2,1)S(1)}, bf16[288,1152]{1,0:T(8,128)(2,1)}, u32[]{:S(2)}, u32[]{:S(2)}) %collective-permute-start) | collective-permute-done | bytes 663584 | tf_op jit(solution)/shard_map/ppermute | solution.py:1232
  26.4 0.6 all_to_all.10
  27.0 3.3 all-to-all-start
  30.4 2.0 collective-permute-start.1
  32.3 2.0 all-to-all-done
  34.5 0.7 pad_convert_fusion.mod_ref.refs_5_.refs_7_
  35.1 1.7 constant_dynamic-slice_fusion.2
  36.9 1.2 collective-permute-start.2
  38.0 0.9 fusion.4.pick_ref.refs_6_.refs_8_
  39.3 2.7 fusion.20
  42.0 1.1 stack.68
  43.1 1.1 stack.69
  44.2 1.1 stack.70
  45.3 1.1 stack.71
  46.4 1.1 stack.72
  47.5 1.1 stack.73
  48.6 1.1 stack.74
  49.7 1.7 stack.75
  51.5 1.7 stack.76
  53.2 1.7 stack.77
  54.9 1.7 stack.78
  56.6 1.7 stack.79
  58.3 0.8 stack.80
  59.6 2.3 stack.67
  61.9 0.8 pad.102.strip_ref
  62.8 9.7 %shard_map.203.bias_ref.refs_7_.refs_9_ = f32[16,256,256]{2,1,0:T(8,128)} custom-call(f32[16,16,512]{2,1,0:T(8,128)} %pad.102.strip_ref), custom_call_target="tpu_custom_call" | custom-call | flops 1000000 | bytes 100000 | tf_op jit(solution)/shard_map/pallas_call | solution.py:84
  72.5 19.8 %shard_map.204 = (bf16[1024,1152]{1,0:T(8,128)(2,1)}, bf16[1728,1024]{1,0:T(8,128)(2,1)}, bf16[576,2048]{1,0:T(8,128)(2,1)}, f32[4,16,256]{2,1,0:T(8,128)}) custom-call(bf16[1024,1152]{1,0:T(8,128)(2,1)} %refs_6_.1, f32[4,8,1152]{2,1,0:T(8,128)} %pad_convert_fusion.mod_ref.refs_5_.refs_7_, bf16[4,192,256]{2,1,0:T(8,128)(2,1)} %fusion.4.pick_ref.refs_6_.refs_8_, ...), custom_call_target="tpu_custom_call" | custom-call | flops 10000000 | bytes 100000 | tf_op jit(solution)/shard_map/pallas_call | solution.py:229
  92.3 0.5 collective-permute-start.4
  92.8 1.9 reshape.117
  94.7 1.8 fusion.3
  96.5 1.1 slice.156
  97.7 3.0 fusion.dmlp_ref
  100.7 0.8 copy-done.5
  101.5 41.2 %shard_map.205 = (bf16[3456,1024]{1,0:T(8,128)(2,1)}, bf16[1152,2048]{1,0:T(8,128)(2,1)}, f32[4,32,256]{2,1,0:T(8,128)}, f32[1792,1152]{1,0:T(8,128)}, bf16[1792...) custom-call(bf16[1024,1152]{1,0:T(8,128)(2,1)} %get-tuple-element.67.refs_0_.first_ref, ...), custom_call_target="tpu_custom_call" | custom-call | flops 8000000000 | bytes 32000000 | tf_op jit(solution)/shard_map/pallas_call | solution.py:354
  142.8 83.3 %shard_map.206 = (f32[1792,1152]{1,0:T(8,128)}, f32[1792,1152]{1,0:T(8,128)}, bf16[1152,4608]{1,0:T(8,128)(2,1)}, bf16[1152,2304]{1,0:T(8,128)(2,1)}, bf16[2304,1152]{1,0:T(8,128)(2,1)}) custom-call(bf16[1792,1152]{1,0:T(8,128)(2,1)} %get-tuple-element.75.second_ref, bf16[1792,1152]{1,0:T(8,128)(2,1)} %fusion.dmlp_ref, bf16[1152,2304]{1,0:T(8,128)(2,1)} %refs_1_.1, ...), custom_call_target="tpu_custom_call" | custom-call | flops 60000002048 | bytes 60000000 | tf_op jit(solution)/shard_map/pallas_call | solution.py:576
  226.2 80.0 %shard_map.207 = (f32[1792,1152]{1,0:T(8,128)}, f32[1792,1152]{1,0:T(8,128)}, bf16[1152,4608]{1,0:T(8,128)(2,1)}) custom-call(bf16[1792,1152]{1,0:T(8,128)(2,1)} %get-tuple-element.75.second_ref, bf16[1792,1152]{1,0:T(8,128)(2,1)} %fusion.dmlp_ref, bf16[1152,2304]{1,0:T(8,128)(2,1)} %get-tuple-element.77.up_ref, ...), custom_call_target="tpu_custom_call" | custom-call | flops 10000000 | bytes 100000 | tf_op jit(solution)/shard_map/pallas_call | solution.py:576
  306.3 0.6 copy-done.6
  307.0 86.3 %shard_map.208 = (bf16[1024,1152]{1,0:T(8,128)(2,1)}, bf16[768,1152]{1,0:T(8,128)(2,1)}, bf16[1024,1152]{1,0:T(8,128)(2,1)}, f32[4,8,1152]{2,1,0:T(8,128)}, bf16...) custom-call(bf16[1728,1152]{1,0:T(8,128)(2,1)} %bitcast.95, ...), custom_call_target="tpu_custom_call" | custom-call | flops 10000000 | bytes 100000 | tf_op jit(solution)/shard_map/pallas_call | solution.py:727
  393.3 3.8 reshape.121
  397.2 2.9 slice_bitcast_fusion.15
  400.1 1.1 add_convert_fusion
  401.6 0.6 pad.121.pack_own_ref
  402.2 0.6 pad.123.pack_other_ref
  403.0 1.6 reshape.119
  404.6 110.7 %shard_map.209 = (bf16[4,144,576]{2,1,0:T(8,128)(2,1)}, f32[3,72,1152]{2,1,0:T(8,128)}, f32[16,1152]{1,0:T(8,128)}, f32[16,1152]{1,0:T(8,128)}) custom-call(bf16[1024,1152]{1,0:T(8,128)(2,1)} %get-tuple-element.67.refs_0_.first_ref, bf16[2048,1152]{1,0:T(8,128)(2,1)} %get-tuple-element.86.dattn_ref, bf16[3456,1024]{1,0:T(8,128)(2,1)} %get-tuple-element.89.dqkv_ref, ...), custom_call_target="tpu_custom_call" | custom-call | flops 10000000 | bytes 100000 | tf_op jit(solution)/shard_map/pallas_call | solution.py:1182
  515.3 0.9 slice.180
  516.2 1.5 slice.185
  517.6 1.0 convert_bitcast_fusion
  518.9 0.5 reshape.127
  519.7 0.8 copy.109
  520.5 1.0 copy.126
  521.5 0.6 reshape.124
  522.1 0.8 collective-permute-start.5
  522.9 0.8 slice_bitcast_fusion.16
  523.7 1.4 fusion.18
  525.1 12.2 %collective-permute-done.5 = bf16[72,4608]{1,0:T(8,128)(2,1)S(1)} collective-permute-done((bf16[72,4608]{1,0:T(8,128)(2,1)}, bf16[72,4608]{1,0:T(8,128)(2,1)S(1)}, u32[]{:S(2)}, u32[]{:S(2)}) %collective-permute-start.5) | collective-permute-done | bytes 663584 | tf_op jit(solution)/shard_map/ppermute | solution.py:1232
  537.4 1.3 convert_add_fusion
  538.6 0.9 reshape.126
  539.5 3.9 slice_reduce_fusion
  543.4 1.0 copy.128
  544.4 1.0 copy.127
  (50 shorter events, 2.2 us)
Async XLA Ops:
  7.2 30.9 %copy-start = (s32[8,179]{1,0:T(8,128)S(1)}, s32[8,179]{1,0:T(8,128)}, u32[]{:S(2)}) copy-start(s32[8,179]{1,0:T(8,128)} %param.14) | copy-start | bytes 17188
  8.4 22.0 %copy-start.8 = (f32[8,961]{1,0:T(8,128)S(1)}, f32[8,961]{1,0:T(8,128)}, u32[]{:S(2)}) copy-start(f32[8,961]{1,0:T(8,128)} %param.21) | copy-start | bytes 92260
  8.4 18.0 %collective-permute-start = (bf16[288,1152]{1,0:T(8,128)(2,1)S(1)}, bf16[288,1152]{1,0:T(8,128)(2,1)}, u32[]{:S(2)}, u32[]{:S(2)}) collective-permute-start(bf16[288,1152]{1,0:T(8,128)(2,1)S(1)} %constant_dynamic-slice_fusion.3), channel_id=1, source_target_pairs={{0,1},{1,0},{2,3},{3,2},{4,5},{5,4},{6,7},{7,6},{8,9},{9,8},{10,11... | collective-permute-start | bytes 1990664 | tf_op jit(solution)/shard_map/ppermute | solution.py:1232
  27.0 7.3 %all-to-all-start = ((bf16[2,4,3456]{2,1,0:T(4,128)(2,1)}), bf16[2,4,3456]{2,1,0:T(4,128)(2,1)S(1)}, u32[]{:S(2)}, u32[]{:S(2)}) async-start(bf16[2,4,3456]{2,1,0:T(4,128)(2,1)} %all_to_all.10), calls=%async_computation | async-start | bytes 110592 | tf_op jit(solution)/shard_map/all_to_all | solution.py:1307
  30.3 374.3 %reduce-scatter.3.cloned.1.call-start = ((), (), s32[]{:S(2)}) async-start(), calls=%async_computation.3 | async-start | bytes 11280384 | tf_op jit(solution)/shard_map/reduce_scatter | solution.py:1286
  30.4 4.8 collective-permute-start.1
  36.9 55.4 %collective-permute-start.2 = (bf16[864,1152]{1,0:T(8,128)(2,1)S(1)}, bf16[864,1152]{1,0:T(8,128)(2,1)}, u32[]{:S(2)}, u32[]{:S(2)}) collective-permute-start(bf16[864,1152]{1,0:T(8,128)(2,1)S(1)} %constant_dynamic-slice_fusion.2), channel_id=1, source_target_pairs={{0,1},{1,0},{2,3},{3,2},{4,5},{5,4},{6,7},{7,6},{8,9},{9,8},{10,11... | collective-permute-start | bytes 5971976 | tf_op jit(solution)/shard_map/ppermute | solution.py:1232
  92.3 8.5 %collective-permute-start.3 = (bf16[864,1152]{1,0:T(8,128)(2,1)}, bf16[864,1152]{1,0:T(8,128)(2,1)}, u32[]{:S(2)}, u32[]{:S(2)}) collective-permute-start(bf16[864,1152]{1,0:T(8,128)(2,1)} %collective-permute-done.2.refs_8_.refs_1_), channel_id=1, source_target_pairs={{0,2},{2,0},{4,6},{6,4},{8,10},{10,8},{12,14},{14,12},{16,18},{18,... | collective-permute-start | bytes 5971976 | tf_op jit(solution)/shard_map/ppermute | solution.py:1264
  92.3 8.4 %collective-permute-start.4 = (bf16[288,1152]{1,0:T(8,128)(2,1)}, bf16[288,1152]{1,0:T(8,128)(2,1)S(1)}, u32[]{:S(2)}, u32[]{:S(2)}) collective-permute-start(bf16[288,1152]{1,0:T(8,128)(2,1)} %collective-permute-done.refs_11_.refs_4_), channel_id=1, source_target_pairs={{0,2},{2,0},{4,6},{6,4},{8,10},{10,8},{12,14},{14,12},{16,18},{18,... | collective-permute-start | bytes 1990664 | tf_op jit(solution)/shard_map/ppermute | solution.py:1264
  96.5 4.2 copy-start.2
  100.7 0.8 copy-start.5
  226.1 296.0 %reduce-scatter.5.cloned.1.call-start = ((), (), s32[]{:S(2)}) async-start(), calls=%async_computation.4 | async-start | bytes 11280384 | tf_op jit(solution)/shard_map/reduce_scatter | solution.py:1286
  306.2 0.7 copy-start.6
  400.0 1.4 copy-start.7
  400.0 2.8 copy-start.3
  515.3 5.2 copy-start.4
  522.1 15.2 %collective-permute-start.5 = (bf16[72,4608]{1,0:T(8,128)(2,1)}, bf16[72,4608]{1,0:T(8,128)(2,1)S(1)}, u32[]{:S(2)}, u32[]{:S(2)}) collective-permute-start(bf16[72,4608]{1,0:T(8,128)(2,1)} %reduce-scatter.5.cloned.1.call-done), channel_id=1, source_target_pairs={{0,1},{1,0},{2,3},{3,2},{4,5},{5,4},{6,7},{7,6},{8,9},{9,8},{10,11... | collective-permute-start | bytes 1990664 | tf_op jit(solution)/shard_map/ppermute | solution.py:1232
  537.4 8.0 %copy-start.1 = (s32[8,179]{1,0:T(8,128)S(1)}, s32[8,179]{1,0:T(8,128)}, u32[]{:S(2)}) copy-start(s32[8,179]{1,0:T(8,128)} %param.14) | copy-start | bytes 17188
Sparse Core Ops, SparseCore 0:
  226.3 120.2 reduce-scatter.2
  350.6 145.6 reduce-scatter.4

commit v8 on v7

--- a/solution.py
+++ b/solution.py
@@ -3,6 +3,7 @@
 
 import jax
 import jax.numpy as jnp
+import numpy as np
 from jax import lax
 from jax.experimental import pallas as pl
 from jax.experimental.pallas import tpu as pltpu
@@ -76,10 +77,13 @@
 
 def bias_whole(table):
     heads = table.shape[0]
-    grid_table = table.reshape(heads, SPAN, SPAN) * LOG2E
-    strip = jnp.stack(
-        [grid_table[:, :, GRID - 1 - c : 2 * GRID - 1 - c] for c in range(GRID)], axis=1
-    ).reshape(heads, GRID, SPAN * GRID)
+    grid_table = table.reshape(heads * SPAN, SPAN) * LOG2E
+    place = np.arange(GRID)
+    gap = place[None, :] - place[:, None] + GRID - 1
+    chooser = (np.arange(SPAN)[:, None, None] == gap[None]).astype(np.float32)
+    strip = jnp.dot(grid_table, chooser.reshape(SPAN, GRID * GRID), precision=PRECISE)
+    strip = strip.reshape(heads, SPAN, GRID, GRID).transpose(0, 2, 1, 3)
+    strip = strip.reshape(heads, GRID, SPAN * GRID)
     strip = jnp.pad(strip, ((0, 0), (0, 0), (0, 512 - SPAN * GRID)))
     return pl.pallas_call(
         bias_kernel,
@@ -593,7 +597,7 @@
     )
 
 
-def backward_kernel(per_block, weight_layout, out_layout, *refs):
+def backward_kernel(per_block, keep, weight_layout, out_layout, *refs):
     count = len(weight_layout) + len(out_layout)
     weight_parts = refs[: len(weight_layout)]
     out_parts = refs[len(weight_layout) : count]
@@ -606,11 +610,11 @@
             + part_copies(out_layout, out_parts, out_w_ref, sems.at[1])
         )
 
-    backward_body(per_block, weight_ref, out_w_ref, *refs[count:-3])
+    backward_body(per_block, keep, weight_ref, out_w_ref, *refs[count:-3])
 
 
 def backward_body(
-    per_block, weight_ref, out_w_ref, tok_ref, mod_ref, pick_ref, bias_ref,
+    per_block, keep, weight_ref, out_w_ref, tok_ref, mod_ref, pick_ref, bias_ref,
     qkv_ref, lse_ref, middle_ref, branch_ref, mlp_ref, dsecond_ref, grad_ref,
     out_full_ref, out_kept_ref, dtok_ref, dmod_ref, dattn_ref, dqkv_ref, strips_ref,
     qkv_s, datt_s, dattk_s, dscores_s,
@@ -622,15 +626,21 @@
     pick = pick_ref[0]
     dmiddles = []
     sums = [0.0, 0.0, 0.0, 0.0]
-    for rows, out_ref in (
-        (slice(0, PATCHES), out_full_ref),
-        (slice(PATCHES, PATCHES + pick.shape[0]), out_kept_ref),
-    ):
+    for rows in (slice(0, PATCHES), slice(PATCHES, PATCHES + pick.shape[0])):
         middle = middle_ref[rows, :]
         branch_mlp = mlp_ref[rows, :]
         dsecond = dsecond_ref[rows, :]
         grad = grad_ref[rows, :].astype(F32)
-        out_ref[...] = (middle + gate_two * branch_mlp).astype(BF)
+        out = (middle + gate_two * branch_mlp).astype(BF)
+        if rows.start == 0:
+            out_full_ref[...] = out
+        else:
+            for image in range(out_kept_ref.shape[0] // keep):
+
+                @pl.when(step == image)
+                def _():
+                    out_kept_ref[image * keep : (image + 1) * keep, :] = out[:keep]
+
         normed, inverse = normalize(middle)
         dmiddle = grad + norm_back(normed, inverse, dsecond * (1.0 + scale_two))
         branch = branch_ref[rows, :].astype(F32)
@@ -714,7 +724,7 @@
 
 def backward(
     tokens, mod, pick, bias, qkv, lse, middle, branch, branch_mlp, dsecond, grads,
-    weight, out_weight, per_block,
+    weight, out_weight, per_block, keep,
 ):
     (weight_layout, weight_parts), (out_layout, out_parts) = weight, out_weight
     most = max(len(weight_parts), len(out_parts))
@@ -724,26 +734,27 @@
     rows = PATCHES + padded
     heads = bias.shape[0]
     by_row = pl.BlockSpec((rows, width), lambda i: (i, 0))
+    one_row = pl.BlockSpec((rows, width), lambda i: (i, 0), pipeline_mode=pl.Buffered(1))
     return pl.pallas_call(
-        functools.partial(backward_kernel, per_block, weight_layout, out_layout),
+        functools.partial(backward_kernel, per_block, keep, weight_layout, out_layout),
         grid=(images,),
         in_specs=[ANYWHERE] * (len(weight_parts) + len(out_parts))
         + [
-            pl.BlockSpec((PATCHES, width), lambda i: (i, 0)),
+            pl.BlockSpec((PATCHES, width), lambda i: (i, 0), pipeline_mode=pl.Buffered(1)),
             pl.BlockSpec((1, 8, width), lambda i: (i, 0, 0)),
             pl.BlockSpec((1, padded, PATCHES), lambda i: (i, 0, 0)),
             const_spec(bias.shape),
             pl.BlockSpec((proj, PATCHES), lambda i: (0, i)),
             pl.BlockSpec((1, 2 * heads, PATCHES), lambda i: (i, 0, 0)),
             by_row,
+            one_row,
             by_row,
             by_row,
-            by_row,
-            by_row,
+            one_row,
         ],
         out_specs=[
             pl.BlockSpec((PATCHES, width), lambda i: (i, 0)),
-            pl.BlockSpec((padded, width), lambda i: (i, 0)),
+            const_spec((images * keep, width)),
             pl.BlockSpec((PATCHES, width), lambda i: (i, 0)),
             pl.BlockSpec((1, 8, width), lambda i: (i, 0, 0)),
             pl.BlockSpec((2 * PATCHES, width), lambda i: (i, 0)),
@@ -752,7 +763,7 @@
         ],
         out_shape=[
             jax.ShapeDtypeStruct((images * PATCHES, width), BF),
-            jax.ShapeDtypeStruct((images * padded, width), BF),
+            jax.ShapeDtypeStruct((images * keep, width), BF),
             jax.ShapeDtypeStruct((images * PATCHES, width), BF),
             jax.ShapeDtypeStruct((images, 8, width), F32),
             jax.ShapeDtypeStruct((images * 2 * PATCHES, width), BF),
@@ -1059,16 +1070,21 @@
 
 
 def attn_grads_kernel(
-    images, pieces, table_rows, first_ref, dattn_ref, dqkv_ref, att_ref, pack_own_ref,
+    images, pieces, table_rows, first_ref, dattn_hbm, dqkv_ref, att_hbm, pack_own_ref,
     pack_other_ref, ada_ref, sums_ref, ada_grad_ref, small_ref, silu_ref, first_t,
     dattn_t, own, other, land0, land1, land2, land3, land_other, land_cross,
     sends, recvs, packs, pack_sends, pack_recvs, ada_s, part_s, silu_own, silu_got, small_sems,
+    dattn_ref, att_ref, load_sems,
 ):
     width = first_t.shape[0]
     tiles, _, columns = own.shape
     share = width // SUM_PLACES
     group = GroupSum(own, other, (land0, land1, land2, land3), land_other, land_cross, sends, recvs)
     ring = PackGather(pack_own_ref, pack_other_ref, packs, pack_sends, pack_recvs)
+    load_dattn = pltpu.make_async_copy(dattn_hbm, dattn_ref, load_sems.at[0])
+    load_att = pltpu.make_async_copy(att_hbm, att_ref, load_sems.at[1])
+    load_dattn.start()
+    load_att.start()
     barrier = pltpu.get_barrier_semaphore()
     small = SmallGrads(
         images, pieces, table_rows, ring, ada_ref, ada_s, part_s, silu_own, silu_got, small_sems
@@ -1110,7 +1126,9 @@
         @pl.when(s == 0)
         def _():
             small.piece(0).start()
+            load_dattn.wait()
             turn(dattn_ref, dattn_t)
+            load_att.wait()
 
         for stage in range(ring.stages):
 
@@ -1181,7 +1199,7 @@
     vmem = pl.BlockSpec(memory_space=pltpu.VMEM)
     sums, ada_grad, small, silu = pl.pallas_call(
         functools.partial(attn_grads_kernel, images, pieces, table_rows),
-        in_specs=[vmem] * 6 + [ANYWHERE],
+        in_specs=[vmem, ANYWHERE, vmem, ANYWHERE, vmem, vmem, ANYWHERE],
         out_specs=[vmem] * 4,
         out_shape=[
             jax.ShapeDtypeStruct((tiles, 2 * share, tile), BF),
@@ -1210,6 +1228,9 @@
             pltpu.VMEM((2, 16, width), BF),
             pltpu.VMEM((16, width), BF),
             pltpu.SemaphoreType.DMA((3,)),
+            pltpu.VMEM(dattn.shape, BF),
+            pltpu.VMEM(att.shape, BF),
+            pltpu.SemaphoreType.DMA((2,)),
         ],
         compiler_params=pltpu.CompilerParams(
             vmem_limit_bytes=VMEM_LIMIT, collective_id=1, has_side_effects=True
@@ -1303,13 +1324,14 @@
     silu_cond = jax.nn.silu(conditioning.astype(F32)).astype(BF)
     columns = (jnp.dot(silu_cond, ada_weight, preferred_element_type=F32) + ada_bias).astype(BF)
     near_o = near_halves(attn_out)
-    columns, near_o = lax.optimization_barrier((columns, near_o))
     mod = lax.all_to_all(columns, "mp", split_axis=0, concat_axis=1, tiled=True)
     mod = jnp.pad(mod.astype(F32).reshape(images, 6, width), ((0, 0), (0, 2), (0, 0)))
 
     weight_own = jnp.transpose(attn_qkv.reshape(width, -1))
     tables = [rel_table] + [shift_mp(rel_table, s) for s in range(1, ways)]
-    mod, tables, weight_sent = lax.optimization_barrier((mod, tables, weight_own))
+    mod, tables, near_o, weight_sent = lax.optimization_barrier(
+        (mod, tables, near_o, weight_own)
+    )
     near_w = near_halves(weight_sent)
     fetch = ways == 2 and lax.axis_size("dp") % 4 == 0 and mlp_up.shape[0] % 32 == 0
     fetch = fetch and mlp_down.shape[0] % 64 == 0
@@ -1336,7 +1358,7 @@
     weight_others = gathered_parts(near_w)
     weight = after_own(weight_others, weight_own)
     out_weight = gathered_parts(near_o, attn_out)
-    cut = (mlp_up.shape[0] * 5 // 18) // 16 * 16
+    cut = (mlp_up.shape[0] * 6 // 18) // 16 * 16
     qkv, att, lse, middle, second, branch, *near_up = forward(
         own, tokens, mod, pick, bias, weight_others, out_weight, per_block,
         mlp_up if fetch else None, cut,
@@ -1357,7 +1379,7 @@
         reduced.append(scatter_dp(grads_next))
     out_full, out_kept, dtok, dmod, dattn, dqkv, strips = backward(
         tokens, mod, pick, bias, qkv, lse, middle, branch, branch_mlp, dsecond, grads,
-        weight, out_weight, per_block,
+        weight, out_weight, per_block, keep,
     )
     proj_block, out_block = weight_own.shape[0], attn_out.shape[0]
     dqkv, reduced[0] = lax.optimization_barrier((dqkv, reduced[0]))
@@ -1435,7 +1457,6 @@
     own_cond = lax.dynamic_slice_in_dim(conditioning, place * images, images, 0).astype(F32)
     grad_cond = jax.vjp(jax.nn.silu, own_cond)[1](grad_silu)[0].astype(BF)
 
-    out_kept = out_kept.reshape(images, padded, width)[:, :keep].reshape(-1, width)
     return (
         out_kept, out_full, dtok, grad_cond, grad_ada_weight, grad_ada_bias, grad_qkv, grad_out,
         grad_up, jnp.transpose(grad_down_t), dtable,

time: 560 us -> 550 us (0.982)
  local copies, waits for them, and re-layouts: 55.1 us -> 37.8 us
  Pallas kernels: 431 us -> 442 us
    another operation x17 -> x0, local copies, waits for them, and re-layouts: 19.9 us -> none  [bias_whole(): jnp.stack([grid_table[:, :, GRID - 1 - c:2 * GRID - 1 - c] for c in range...]
    pallas_call x1, Pallas kernels: 86.3 us -> 101 us  [backward(): pl.pallas_call(functools.partial(backward_kernel, per_block, keep, weight...]
    pallas_call x1, Pallas kernels: 111 us -> 101 us  [attn_grads(): pl.pallas_call(functools.partial(attn_grads_kernel, images, pieces, table...]
    ppermute x4, waiting for transfers between devices: 22.9 us -> 16.1 us  [shift_mp(): lax.ppermute(value, 'mp', [(i, (i - steps) % ways) for i in range(ways)])]
    pallas_call x1, Pallas kernels: 41.2 us -> 47.6 us  [forward(): pl.pallas_call(functools.partial(forward_kernel, per_block, weight_layout...]
  transfers between devices with their start and end apart: 9 -> 9, of which waited for: 3 -> 3; matrix products, arithmetic and copies ran while one was open for 10% -> 8% of each run, Pallas kernels for 55% -> 57%
where the time goes in v8:
time: 550 us; the launch traced here: 544 us
  Pallas kernels  442 us (80%)
  local copies, waits for them, and re-layouts  37.8 us (7%)
  waiting for transfers between devices  21.7 us (4%)
  between operations  14.7 us (3%)
  other arithmetic  11.3 us (2%)
  starting transfers between devices  10.9 us (2%)
  matrix products  6.21 us (1%)
    pallas_call x2, Pallas kernels, mlp(): pl.pallas_call(functools.partial(mlp_kernel, chunk, fresh, fetch is not N...  163 us
    pallas_call x1, Pallas kernels, attn_grads(): pl.pallas_call(functools.partial(attn_grads_kernel, images, pieces, table...  101 us
    pallas_call x1, Pallas kernels, backward(): pl.pallas_call(functools.partial(backward_kernel, per_block, keep, weight...  101 us
    pallas_call x1, Pallas kernels, forward(): pl.pallas_call(functools.partial(forward_kernel, per_block, weight_layout...  47.6 us
    pallas_call x1, Pallas kernels, own_heads(): pl.pallas_call(functools.partial(own_heads_kernel, per_block), grid=(imag...  19.8 us
    ppermute x4, waiting for transfers between devices, shift_mp(): lax.ppermute(value, 'mp', [(i, (i - steps) % ways) for i in range(ways)])  16.1 us
  transfers between devices with their start and end apart: 9, of which 3 were waited for; matrix products, arithmetic and copies ran while one was open for 8% of the time, Pallas kernels for 57%

profile of v8, /device:TPU:0, one launch (start us, length us, event | category | flops | bytes accessed | tf_op | source)
XLA Modules:
  0.0 544.4 jit_solution(10895754417251774101)
XLA Ops:
  7.2 0.0 copy-start
  7.2 1.1 constant_dynamic-slice_fusion.3
  8.4 0.0 copy-start.8
  8.4 3.0 collective-permute-start.1
  11.4 4.4 fusion.2
  15.8 0.7 all_to_all.10
  16.4 3.3 all-to-all-start
  19.7 0.0 reduce-scatter.3.cloned.1.call-start
  19.8 2.0 collective-permute-start
  21.7 5.5 %all-to-all-done = bf16[2,4,3456]{2,1,0:T(4,128)(2,1)S(1)} async-done(((bf16[2,4,3456]{2,1,0:T(4,128)(2,1)}), bf16[2,4,3456]{2,1,0:T(4,128)(2,1)S(1)}, u32[]{:S(2)}, u32[]{:S(2)}) %all-to-all-start) | async-done | bytes 55328 | tf_op jit(solution)/shard_map/all_to_all | solution.py:1327
  27.3 0.7 pad_convert_fusion.mod_ref.refs_5_.refs_7_
  28.0 3.0 constant_dynamic-slice_fusion.2
  31.0 1.7 collective-permute-start.2
  32.8 0.9 fusion.4.pick_ref.refs_6_.refs_8_
  33.7 0.2 concatenate.19
  33.8 0.2 concatenate.20
  34.0 1.8 convolution_bitcast_fusion
  35.8 3.5 copy.63
  39.3 4.4 reshape.85
  43.7 0.8 pad.102.strip_ref
  44.6 9.5 %shard_map.212.bias_ref.refs_7_.refs_9_ = f32[16,256,256]{2,1,0:T(8,128)} custom-call(f32[16,16,512]{2,1,0:T(8,128)} %pad.102.strip_ref), custom_call_target="tpu_custom_call" | custom-call | flops 1000000 | bytes 100000 | tf_op jit(solution)/shard_map/pallas_call | solution.py:88
  54.1 19.8 %shard_map.213 = (bf16[1024,1152]{1,0:T(8,128)(2,1)}, bf16[1728,1024]{1,0:T(8,128)(2,1)}, bf16[576,2048]{1,0:T(8,128)(2,1)}, f32[4,16,256]{2,1,0:T(8,128)}) custom-call(bf16[1024,1152]{1,0:T(8,128)(2,1)} %refs_6_.1, f32[4,8,1152]{2,1,0:T(8,128)} %pad_convert_fusion.mod_ref.refs_5_.refs_7_, bf16[4,192,256]{2,1,0:T(8,128)(2,1)} %fusion.4.pick_ref.refs_6_.refs_8_, ...), custom_call_target="tpu_custom_call" | custom-call | flops 10000000 | bytes 100000 | tf_op jit(solution)/shard_map/pallas_call | solution.py:233
  74.0 1.6 collective-permute-done.2.refs_8_.refs_1_
  75.6 0.5 collective-permute-start.4
  76.1 0.4 reshape.87
  76.6 1.8 fusion.3
  78.4 1.1 slice.89
  79.5 3.0 fusion.dmlp_ref
  82.6 47.6 %shard_map.214 = (bf16[3456,1024]{1,0:T(8,128)(2,1)}, bf16[1152,2048]{1,0:T(8,128)(2,1)}, f32[4,32,256]{2,1,0:T(8,128)}, f32[1792,1152]{1,0:T(8,128)}, bf16[1792...) custom-call(bf16[1024,1152]{1,0:T(8,128)(2,1)} %get-tuple-element.65.refs_0_.first_ref, ...), custom_call_target="tpu_custom_call" | custom-call | flops 8000000000 | bytes 32000000 | tf_op jit(solution)/shard_map/pallas_call | solution.py:358
  130.1 83.1 %shard_map.215 = (f32[1792,1152]{1,0:T(8,128)}, f32[1792,1152]{1,0:T(8,128)}, bf16[1152,4608]{1,0:T(8,128)(2,1)}, bf16[1152,2304]{1,0:T(8,128)(2,1)}, bf16[2304,1152]{1,0:T(8,128)(2,1)}) custom-call(bf16[1792,1152]{1,0:T(8,128)(2,1)} %get-tuple-element.73.second_ref, bf16[1792,1152]{1,0:T(8,128)(2,1)} %fusion.dmlp_ref, bf16[1152,2304]{1,0:T(8,128)(2,1)} %refs_1_.1, ...), custom_call_target="tpu_custom_call" | custom-call | flops 60000002048 | bytes 60000000 | tf_op jit(solution)/shard_map/pallas_call | solution.py:580
  213.2 0.0 reduce-scatter.3.cloned.1.call-update
  213.2 0.0 reduce-scatter.5.cloned.1.call-start
  213.3 79.9 %shard_map.216 = (f32[1792,1152]{1,0:T(8,128)}, f32[1792,1152]{1,0:T(8,128)}, bf16[1152,4608]{1,0:T(8,128)(2,1)}) custom-call(bf16[1792,1152]{1,0:T(8,128)(2,1)} %get-tuple-element.73.second_ref, bf16[1792,1152]{1,0:T(8,128)(2,1)} %fusion.dmlp_ref, bf16[1152,2304]{1,0:T(8,128)(2,1)} %get-tuple-element.75.up_ref, ...), custom_call_target="tpu_custom_call" | custom-call | flops 10000000 | bytes 100000 | tf_op jit(solution)/shard_map/pallas_call | solution.py:580
  293.2 0.0 copy-start.5
  293.2 0.0 reduce-scatter.5.cloned.1.call-update
  293.3 0.6 copy-done.5
  294.0 100.6 %shard_map.217 = (bf16[1024,1152]{1,0:T(8,128)(2,1)}, bf16[716,1152]{1,0:T(8,128)(2,1)}, bf16[1024,1152]{1,0:T(8,128)(2,1)}, f32[4,8,1152]{2,1,0:T(8,128)}, bf16...) custom-call(bf16[1728,1152]{1,0:T(8,128)(2,1)} %bitcast.103, ...), custom_call_target="tpu_custom_call" | custom-call | flops 10000000 | bytes 100000 | tf_op jit(solution)/shard_map/pallas_call | solution.py:738
  394.6 3.8 reshape.89
  398.4 2.9 slice_bitcast_fusion.15
  401.3 0.0 copy-start.7
  401.3 1.1 add_convert_fusion
  402.4 0.1 slice.108
  402.5 0.1 slice.110
  402.9 0.6 pad.121.pack_own_ref
  403.5 0.6 pad.123.pack_other_ref
  404.1 101.3 %shard_map.218 = (bf16[4,144,576]{2,1,0:T(8,128)(2,1)}, f32[3,72,1152]{2,1,0:T(8,128)}, f32[16,1152]{1,0:T(8,128)}, f32[16,1152]{1,0:T(8,128)}) custom-call(bf16[1024,1152]{1,0:T(8,128)(2,1)} %get-tuple-element.65.refs_0_.first_ref, bf16[2048,1152]{1,0:T(8,128)(2,1)} %get-tuple-element.84.dattn_hbm, bf16[3456,1024]{1,0:T(8,128)(2,1)} %get-tuple-element.87.dqkv_ref, ...), custom_call_target="tpu_custom_call" | custom-call | flops 10000000 | bytes 100000 | tf_op jit(solution)/shard_map/pallas_call | solution.py:1200
  505.5 0.9 slice.112
  506.3 1.5 slice.117
  507.8 1.0 convert_bitcast_fusion
  508.8 0.2 copy.80
  509.0 0.5 reshape.95
  509.6 0.3 reshape.93
  509.8 0.8 copy.81
  510.7 1.0 copy.99
  511.7 0.6 reshape.92
  512.3 0.4 collective-permute-start.5
  512.7 0.8 slice_bitcast_fusion.16
  513.5 1.4 fusion.23
  514.9 14.5 %collective-permute-done.5 = bf16[72,4608]{1,0:T(8,128)(2,1)S(1)} collective-permute-done((bf16[72,4608]{1,0:T(8,128)(2,1)}, bf16[72,4608]{1,0:T(8,128)(2,1)S(1)}, u32[]{:S(2)}, u32[]{:S(2)}) %collective-permute-start.5) | collective-permute-done | bytes 663584 | tf_op jit(solution)/shard_map/ppermute | solution.py:1253
  529.4 1.3 convert_add_fusion
  530.6 0.9 reshape.94
  531.5 3.9 slice_reduce_fusion
  535.4 1.0 copy.101
  536.4 1.0 copy.100
  (33 shorter events, 0.4 us)
Async XLA Ops:
  7.2 25.6 %copy-start = (s32[8,179]{1,0:T(8,128)S(1)}, s32[8,179]{1,0:T(8,128)}, u32[]{:S(2)}) copy-start(s32[8,179]{1,0:T(8,128)} %param.15) | copy-start | bytes 17188
  8.4 11.4 %copy-start.8 = (f32[8,961]{1,0:T(8,128)S(1)}, f32[8,961]{1,0:T(8,128)}, u32[]{:S(2)}) copy-start(f32[8,961]{1,0:T(8,128)} %param.22) | copy-start | bytes 92260
  8.4 19.6 %collective-permute-start.1 = (bf16[288,1152]{1,0:T(8,128)(2,1)S(1)}, bf16[288,1152]{1,0:T(8,128)(2,1)}, u32[]{:S(2)}, u32[]{:S(2)}) collective-permute-start(bf16[288,1152]{1,0:T(8,128)(2,1)S(1)} %constant_dynamic-slice_fusion.3), channel_id=1, source_target_pairs={{0,1},{1,0},{2,3},{3,2},{4,5},{5,4},{6,7},{7,6},{8,9},{9,8},{10,11... | collective-permute-start | bytes 1990664 | tf_op jit(solution)/shard_map/ppermute | solution.py:1253
  15.8 18.2 %copy-start.6 = (f32[16,16,31,1]{2,1,0,3:T(8,128)S(1)}, f32[16,16,31,1]{2,1,0,3:T(8,128)}, u32[]{:S(2)}) copy-start(f32[16,16,31,1]{2,1,0,3:T(8,128)} %constant.135) | copy-start | bytes 95236
  16.4 10.8 %all-to-all-start = ((bf16[2,4,3456]{2,1,0:T(4,128)(2,1)}), bf16[2,4,3456]{2,1,0:T(4,128)(2,1)S(1)}, u32[]{:S(2)}, u32[]{:S(2)}) async-start(bf16[2,4,3456]{2,1,0:T(4,128)(2,1)} %all_to_all.10), calls=%async_computation | async-start | bytes 110592 | tf_op jit(solution)/shard_map/all_to_all | solution.py:1327
  19.7 384.4 %reduce-scatter.3.cloned.1.call-start = ((), (), s32[]{:S(2)}) async-start(), calls=%async_computation.3 | async-start | bytes 11280384 | tf_op jit(solution)/shard_map/reduce_scatter | solution.py:1307
  19.8 8.2 %collective-permute-start = (f32[8,961]{1,0:T(8,128)S(1)}, f32[8,961]{1,0:T(8,128)S(1)}, u32[]{:S(2)}, u32[]{:S(2)}) collective-permute-start(f32[8,961]{1,0:T(8,128)S(1)} %copy-done.8), channel_id=1, source_target_pairs={{0,1},{1,0},{2,3},{3,2},{4,5},{5,4},{6,7},{7,6},{8,9},{9,8},{10,11... | collective-permute-start | bytes 92264 | tf_op jit(solution)/shard_map/ppermute | solution.py:1253
  31.0 44.6 %collective-permute-start.2 = (bf16[864,1152]{1,0:T(8,128)(2,1)}, bf16[864,1152]{1,0:T(8,128)(2,1)}, u32[]{:S(2)}, u32[]{:S(2)}) collective-permute-start(bf16[864,1152]{1,0:T(8,128)(2,1)} %constant_dynamic-slice_fusion.2), channel_id=1, source_target_pairs={{0,1},{1,0},{2,3},{3,2},{4,5},{5,4},{6,7},{7,6},{8,9},{9,8},{10,11... | collective-permute-start | bytes 5971976 | tf_op jit(solution)/shard_map/ppermute | solution.py:1253
  54.1 22.0 %copy-start.3 = (bf16[716,1152]{1,0:T(8,128)(2,1)S(1)}, bf16[716,1152]{1,0:T(8,128)(2,1)}, u32[]{:S(2)}) copy-start(bf16[716,1152]{1,0:T(8,128)(2,1)} %param.23) | copy-start | bytes 4948996
  75.6 7.0 %collective-permute-start.3 = (bf16[864,1152]{1,0:T(8,128)(2,1)}, bf16[864,1152]{1,0:T(8,128)(2,1)}, u32[]{:S(2)}, u32[]{:S(2)}) collective-permute-start(bf16[864,1152]{1,0:T(8,128)(2,1)} %collective-permute-done.2.refs_8_.refs_1_), channel_id=1, source_target_pairs={{0,2},{2,0},{4,6},{6,4},{8,10},{10,8},{12,14},{14,12},{16,18},{18,... | collective-permute-start | bytes 5971976 | tf_op jit(solution)/shard_map/ppermute | solution.py:1285
  75.6 7.0 %collective-permute-start.4 = (bf16[288,1152]{1,0:T(8,128)(2,1)}, bf16[288,1152]{1,0:T(8,128)(2,1)}, u32[]{:S(2)}, u32[]{:S(2)}) collective-permute-start(bf16[288,1152]{1,0:T(8,128)(2,1)} %collective-permute-done.1.refs_11_.refs_4_), channel_id=1, source_target_pairs={{0,2},{2,0},{4,6},{6,4},{8,10},{10,8},{12,14},{14,12},{16,18},{18,... | collective-permute-start | bytes 1990664 | tf_op jit(solution)/shard_map/ppermute | solution.py:1285
  78.4 4.2 copy-start.2
  213.2 299.1 %reduce-scatter.5.cloned.1.call-start = ((), (), s32[]{:S(2)}) async-start(), calls=%async_computation.4 | async-start | bytes 11280384 | tf_op jit(solution)/shard_map/reduce_scatter | solution.py:1307
  293.2 0.7 copy-start.5
  401.3 1.4 copy-start.7
  505.5 5.2 copy-start.4
  512.3 17.0 %collective-permute-start.5 = (bf16[72,4608]{1,0:T(8,128)(2,1)}, bf16[72,4608]{1,0:T(8,128)(2,1)S(1)}, u32[]{:S(2)}, u32[]{:S(2)}) collective-permute-start(bf16[72,4608]{1,0:T(8,128)(2,1)} %reduce-scatter.5.cloned.1.call-done), channel_id=1, source_target_pairs={{0,1},{1,0},{2,3},{3,2},{4,5},{5,4},{6,7},{7,6},{8,9},{9,8},{10,11... | collective-permute-start | bytes 1990664 | tf_op jit(solution)/shard_map/ppermute | solution.py:1253
  529.4 8.0 %copy-start.1 = (s32[8,179]{1,0:T(8,128)S(1)}, s32[8,179]{1,0:T(8,128)}, u32[]{:S(2)}) copy-start(s32[8,179]{1,0:T(8,128)} %param.15) | copy-start | bytes 17188
Sparse Core Ops, SparseCore 0:
  213.4 120.5 reduce-scatter.2
  338.0 128.0 reduce-scatter.4

commit v9 on v7

--- a/solution.py
+++ b/solution.py
@@ -3,6 +3,7 @@
 
 import jax
 import jax.numpy as jnp
+import numpy as np
 from jax import lax
 from jax.experimental import pallas as pl
 from jax.experimental.pallas import tpu as pltpu
@@ -76,10 +77,13 @@
 
 def bias_whole(table):
     heads = table.shape[0]
-    grid_table = table.reshape(heads, SPAN, SPAN) * LOG2E
-    strip = jnp.stack(
-        [grid_table[:, :, GRID - 1 - c : 2 * GRID - 1 - c] for c in range(GRID)], axis=1
-    ).reshape(heads, GRID, SPAN * GRID)
+    grid_table = table.reshape(heads * SPAN, SPAN) * LOG2E
+    place = np.arange(GRID)
+    gap = place[None, :] - place[:, None] + GRID - 1
+    chooser = (np.arange(SPAN)[:, None, None] == gap[None]).astype(np.float32)
+    strip = jnp.dot(grid_table, chooser.reshape(SPAN, GRID * GRID), precision=PRECISE)
+    strip = strip.reshape(heads, SPAN, GRID, GRID).transpose(0, 2, 1, 3)
+    strip = strip.reshape(heads, GRID, SPAN * GRID)
     strip = jnp.pad(strip, ((0, 0), (0, 0), (0, 512 - SPAN * GRID)))
     return pl.pallas_call(
         bias_kernel,
@@ -599,18 +603,27 @@
     out_parts = refs[len(weight_layout) : count]
     weight_ref, out_w_ref, sems = refs[-3:]
 
+    weight_copies = part_copies(weight_layout, weight_parts, weight_ref, sems.at[0])
+
     @pl.when(pl.program_id(0) == 0)
     def _():
-        run_copies(
-            part_copies(weight_layout, weight_parts, weight_ref, sems.at[0])
-            + part_copies(out_layout, out_parts, out_w_ref, sems.at[1])
-        )
-
-    backward_body(per_block, weight_ref, out_w_ref, *refs[count:-3])
+        out_copies = part_copies(out_layout, out_parts, out_w_ref, sems.at[1])
+        for copy in out_copies + weight_copies:
+            copy.start()
+        for copy in out_copies:
+            copy.wait()
+
+    def wait_weight():
+        @pl.when(pl.program_id(0) == 0)
+        def _():
+            for copy in weight_copies:
+                copy.wait()
+
+    backward_body(per_block, wait_weight, weight_ref, out_w_ref, *refs[count:-3])
 
 
 def backward_body(
-    per_block, weight_ref, out_w_ref, tok_ref, mod_ref, pick_ref, bias_ref,
+    per_block, wait_weight, weight_ref, out_w_ref, tok_ref, mod_ref, pick_ref, bias_ref,
     qkv_ref, lse_ref, middle_ref, branch_ref, mlp_ref, dsecond_ref, grad_ref,
     out_full_ref, out_kept_ref, dtok_ref, dmod_ref, dattn_ref, dqkv_ref, strips_ref,
     qkv_s, datt_s, dattk_s, dscores_s,
@@ -690,6 +703,7 @@
     lax.fori_loop(0, heads, one_head, 0, unroll=4)
     dqkv = qkv_s[...].astype(BF)
     dqkv_ref[...] = dqkv
+    wait_weight()
     dfirst = tn(dqkv, weight_ref[...])
     normed, inverse = normalize(tok_ref[...].astype(F32))
     dmod_ref[0, 0:1, :] = jnp.sum(dfirst, axis=0, keepdims=True)
@@ -1059,16 +1073,21 @@
 
 
 def attn_grads_kernel(
-    images, pieces, table_rows, first_ref, dattn_ref, dqkv_ref, att_ref, pack_own_ref,
+    images, pieces, table_rows, first_ref, dattn_hbm, dqkv_ref, att_hbm, pack_own_ref,
     pack_other_ref, ada_ref, sums_ref, ada_grad_ref, small_ref, silu_ref, first_t,
     dattn_t, own, other, land0, land1, land2, land3, land_other, land_cross,
     sends, recvs, packs, pack_sends, pack_recvs, ada_s, part_s, silu_own, silu_got, small_sems,
+    dattn_ref, att_ref, load_sems,
 ):
     width = first_t.shape[0]
     tiles, _, columns = own.shape
     share = width // SUM_PLACES
     group = GroupSum(own, other, (land0, land1, land2, land3), land_other, land_cross, sends, recvs)
     ring = PackGather(pack_own_ref, pack_other_ref, packs, pack_sends, pack_recvs)
+    load_dattn = pltpu.make_async_copy(dattn_hbm, dattn_ref, load_sems.at[0])
+    load_att = pltpu.make_async_copy(att_hbm, att_ref, load_sems.at[1])
+    load_dattn.start()
+    load_att.start()
     barrier = pltpu.get_barrier_semaphore()
     small = SmallGrads(
         images, pieces, table_rows, ring, ada_ref, ada_s, part_s, silu_own, silu_got, small_sems
@@ -1110,7 +1129,9 @@
         @pl.when(s == 0)
         def _():
             small.piece(0).start()
+            load_dattn.wait()
             turn(dattn_ref, dattn_t)
+            load_att.wait()
 
         for stage in range(ring.stages):
 
@@ -1181,7 +1202,7 @@
     vmem = pl.BlockSpec(memory_space=pltpu.VMEM)
     sums, ada_grad, small, silu = pl.pallas_call(
         functools.partial(attn_grads_kernel, images, pieces, table_rows),
-        in_specs=[vmem] * 6 + [ANYWHERE],
+        in_specs=[vmem, ANYWHERE, vmem, ANYWHERE, vmem, vmem, ANYWHERE],
         out_specs=[vmem] * 4,
         out_shape=[
             jax.ShapeDtypeStruct((tiles, 2 * share, tile), BF),
@@ -1210,6 +1231,9 @@
             pltpu.VMEM((2, 16, width), BF),
             pltpu.VMEM((16, width), BF),
             pltpu.SemaphoreType.DMA((3,)),
+            pltpu.VMEM(dattn.shape, BF),
+            pltpu.VMEM(att.shape, BF),
+            pltpu.SemaphoreType.DMA((2,)),
         ],
         compiler_params=pltpu.CompilerParams(
             vmem_limit_bytes=VMEM_LIMIT, collective_id=1, has_side_effects=True
@@ -1303,13 +1327,14 @@
     silu_cond = jax.nn.silu(conditioning.astype(F32)).astype(BF)
     columns = (jnp.dot(silu_cond, ada_weight, preferred_element_type=F32) + ada_bias).astype(BF)
     near_o = near_halves(attn_out)
-    columns, near_o = lax.optimization_barrier((columns, near_o))
     mod = lax.all_to_all(columns, "mp", split_axis=0, concat_axis=1, tiled=True)
     mod = jnp.pad(mod.astype(F32).reshape(images, 6, width), ((0, 0), (0, 2), (0, 0)))
 
     weight_own = jnp.transpose(attn_qkv.reshape(width, -1))
     tables = [rel_table] + [shift_mp(rel_table, s) for s in range(1, ways)]
-    mod, tables, weight_sent = lax.optimization_barrier((mod, tables, weight_own))
+    mod, tables, near_o, weight_sent = lax.optimization_barrier(
+        (mod, tables, near_o, weight_own)
+    )
     near_w = near_halves(weight_sent)
     fetch = ways == 2 and lax.axis_size("dp") % 4 == 0 and mlp_up.shape[0] % 32 == 0
     fetch = fetch and mlp_down.shape[0] % 64 == 0

time: 560 us -> 544 us (0.971)
  local copies, waits for them, and re-layouts: 55.1 us -> 39.5 us
    another operation x17 -> x0, local copies, waits for them, and re-layouts: 19.9 us -> none  [bias_whole(): jnp.stack([grid_table[:, :, GRID - 1 - c:2 * GRID - 1 - c] for c in range...]
    ppermute x4, waiting for transfers between devices: 22.9 us -> 13.9 us  [shift_mp(): lax.ppermute(value, 'mp', [(i, (i - steps) % ways) for i in range(ways)])]
    pallas_call x1, Pallas kernels: 111 us -> 116 us  [attn_grads(): pl.pallas_call(functools.partial(attn_grads_kernel, images, pieces, table...]
  transfers between devices with their start and end apart: 9 -> 9, of which waited for: 3 -> 3; matrix products, arithmetic and copies ran while one was open for 10% -> 8% of each run, Pallas kernels for 55% -> 58%
where the time goes in v9:
time: 544 us; the launch traced here: 538 us
  Pallas kernels  435 us (80%)
  local copies, waits for them, and re-layouts  39.5 us (7%)
  waiting for transfers between devices  19.5 us (4%)
  between operations  14.7 us (3%)
  starting transfers between devices  12.1 us (2%)
  other arithmetic  11.3 us (2%)
  matrix products  6.21 us (1%)
    pallas_call x2, Pallas kernels, mlp(): pl.pallas_call(functools.partial(mlp_kernel, chunk, fresh, fetch is not N...  163 us
    pallas_call x1, Pallas kernels, attn_grads(): pl.pallas_call(functools.partial(attn_grads_kernel, images, pieces, table...  116 us
    pallas_call x1, Pallas kernels, backward(): pl.pallas_call(functools.partial(backward_kernel, per_block, weight_layou...  85 us
    pallas_call x1, Pallas kernels, forward(): pl.pallas_call(functools.partial(forward_kernel, per_block, weight_layout...  41.2 us
    pallas_call x1, Pallas kernels, own_heads(): pl.pallas_call(functools.partial(own_heads_kernel, per_block), grid=(imag...  19.8 us
    ppermute x4, waiting for transfers between devices, shift_mp(): lax.ppermute(value, 'mp', [(i, (i - steps) % ways) for i in range(ways)])  13.9 us
  transfers between devices with their start and end apart: 9, of which 3 were waited for; matrix products, arithmetic and copies ran while one was open for 8% of the time, Pallas kernels for 58%

profile of v9, /device:TPU:0, one launch (start us, length us, event | category | flops | bytes accessed | tf_op | source)
XLA Modules:
  0.0 538.1 jit_solution(17515103335789633210)
XLA Ops:
  7.2 0.0 copy-start
  7.2 1.1 constant_dynamic-slice_fusion.3
  8.4 3.0 collective-permute-start.1
  11.4 4.4 fusion.2
  15.8 0.7 all_to_all.10
  16.4 3.3 all-to-all-start
  19.7 0.0 reduce-scatter.3.cloned.1.call-start
  19.8 2.0 collective-permute-start
  21.7 5.5 %all-to-all-done = bf16[2,4,3456]{2,1,0:T(4,128)(2,1)S(1)} async-done(((bf16[2,4,3456]{2,1,0:T(4,128)(2,1)}), bf16[2,4,3456]{2,1,0:T(4,128)(2,1)S(1)}, u32[]{:S(2)}, u32[]{:S(2)}) %all-to-all-start) | async-done | bytes 55328 | tf_op jit(solution)/shard_map/all_to_all | solution.py:1330
  27.3 0.7 pad_convert_fusion.mod_ref.refs_5_.refs_7_
  28.0 3.0 constant_dynamic-slice_fusion.2
  31.0 1.7 collective-permute-start.2
  32.8 0.9 fusion.4.pick_ref.refs_6_.refs_8_
  33.7 0.2 concatenate.19
  33.8 0.2 concatenate.20
  34.0 1.8 convolution_bitcast_fusion
  35.8 3.5 copy.63
  39.3 4.4 reshape.91
  43.7 0.8 pad.102.strip_ref
  44.6 9.5 %shard_map.212.bias_ref.refs_7_.refs_9_ = f32[16,256,256]{2,1,0:T(8,128)} custom-call(f32[16,16,512]{2,1,0:T(8,128)} %pad.102.strip_ref), custom_call_target="tpu_custom_call" | custom-call | flops 1000000 | bytes 100000 | tf_op jit(solution)/shard_map/pallas_call | solution.py:88
  54.1 19.8 %shard_map.213 = (bf16[1024,1152]{1,0:T(8,128)(2,1)}, bf16[1728,1024]{1,0:T(8,128)(2,1)}, bf16[576,2048]{1,0:T(8,128)(2,1)}, f32[4,16,256]{2,1,0:T(8,128)}) custom-call(bf16[1024,1152]{1,0:T(8,128)(2,1)} %refs_6_.1, f32[4,8,1152]{2,1,0:T(8,128)} %pad_convert_fusion.mod_ref.refs_5_.refs_7_, bf16[4,192,256]{2,1,0:T(8,128)(2,1)} %fusion.4.pick_ref.refs_6_.refs_8_, ...), custom_call_target="tpu_custom_call" | custom-call | flops 10000000 | bytes 100000 | tf_op jit(solution)/shard_map/pallas_call | solution.py:233
  73.9 1.7 collective-permute-done.2.refs_8_.refs_1_
  75.6 0.5 collective-permute-start.4
  76.1 0.4 reshape.93
  76.6 1.8 fusion.3
  78.4 1.1 slice.92
  79.5 3.0 fusion.dmlp_ref
  82.6 41.2 %shard_map.214 = (bf16[3456,1024]{1,0:T(8,128)(2,1)}, bf16[1152,2048]{1,0:T(8,128)(2,1)}, f32[4,32,256]{2,1,0:T(8,128)}, f32[1792,1152]{1,0:T(8,128)}, bf16[1792...) custom-call(bf16[1024,1152]{1,0:T(8,128)(2,1)} %get-tuple-element.65.refs_0_.first_ref, ...), custom_call_target="tpu_custom_call" | custom-call | flops 8000000000 | bytes 32000000 | tf_op jit(solution)/shard_map/pallas_call | solution.py:358
  123.8 83.1 %shard_map.215 = (f32[1792,1152]{1,0:T(8,128)}, f32[1792,1152]{1,0:T(8,128)}, bf16[1152,4608]{1,0:T(8,128)(2,1)}, bf16[1152,2304]{1,0:T(8,128)(2,1)}, bf16[2304,1152]{1,0:T(8,128)(2,1)}) custom-call(bf16[1792,1152]{1,0:T(8,128)(2,1)} %get-tuple-element.73.second_ref, bf16[1792,1152]{1,0:T(8,128)(2,1)} %fusion.dmlp_ref, bf16[1152,2304]{1,0:T(8,128)(2,1)} %refs_1_.1, ...), custom_call_target="tpu_custom_call" | custom-call | flops 60000002048 | bytes 60000000 | tf_op jit(solution)/shard_map/pallas_call | solution.py:580
  206.9 0.0 reduce-scatter.3.cloned.1.call-update
  206.9 0.0 reduce-scatter.5.cloned.1.call-start
  206.9 79.9 %shard_map.216 = (f32[1792,1152]{1,0:T(8,128)}, f32[1792,1152]{1,0:T(8,128)}, bf16[1152,4608]{1,0:T(8,128)(2,1)}) custom-call(bf16[1792,1152]{1,0:T(8,128)(2,1)} %get-tuple-element.73.second_ref, bf16[1792,1152]{1,0:T(8,128)(2,1)} %fusion.dmlp_ref, bf16[1152,2304]{1,0:T(8,128)(2,1)} %get-tuple-element.75.up_ref, ...), custom_call_target="tpu_custom_call" | custom-call | flops 10000000 | bytes 100000 | tf_op jit(solution)/shard_map/pallas_call | solution.py:580
  286.8 0.0 copy-start.6
  286.8 0.0 reduce-scatter.5.cloned.1.call-update
  286.9 0.6 copy-done.6
  287.6 85.0 %shard_map.217 = (bf16[1024,1152]{1,0:T(8,128)(2,1)}, bf16[768,1152]{1,0:T(8,128)(2,1)}, bf16[1024,1152]{1,0:T(8,128)(2,1)}, f32[4,8,1152]{2,1,0:T(8,128)}, bf16...) custom-call(bf16[1728,1152]{1,0:T(8,128)(2,1)} %bitcast.104, ...), custom_call_target="tpu_custom_call" | custom-call | flops 10000000 | bytes 100000 | tf_op jit(solution)/shard_map/pallas_call | solution.py:741
  372.6 3.8 reshape.97
  376.5 2.9 slice_bitcast_fusion.15
  379.4 1.1 add_convert_fusion
  380.5 0.1 slice.112
  380.6 0.1 slice.114
  380.9 0.6 pad.121.pack_own_ref
  381.6 0.6 pad.123.pack_other_ref
  382.2 0.1 slice.122
  382.3 1.6 reshape.95
  384.0 116.3 %shard_map.218 = (bf16[4,144,576]{2,1,0:T(8,128)(2,1)}, f32[3,72,1152]{2,1,0:T(8,128)}, f32[16,1152]{1,0:T(8,128)}, f32[16,1152]{1,0:T(8,128)}) custom-call(bf16[1024,1152]{1,0:T(8,128)(2,1)} %get-tuple-element.65.refs_0_.first_ref, bf16[2048,1152]{1,0:T(8,128)(2,1)} %get-tuple-element.84.dattn_hbm, bf16[3456,1024]{1,0:T(8,128)(2,1)} %get-tuple-element.87.dqkv_ref, ...), custom_call_target="tpu_custom_call" | custom-call | flops 10000000 | bytes 100000 | tf_op jit(solution)/shard_map/pallas_call | solution.py:1203
  500.3 0.9 slice.116
  501.2 1.5 slice.121
  502.6 1.0 convert_bitcast_fusion
  503.7 0.2 copy.80
  503.9 0.5 reshape.103
  504.4 0.3 reshape.101
  504.7 0.8 copy.81
  505.5 1.0 copy.99
  506.5 0.6 reshape.100
  507.1 1.5 collective-permute-start.5
  508.6 0.8 slice_bitcast_fusion.16
  509.4 1.4 fusion.23
  510.8 12.3 %collective-permute-done.5 = bf16[72,4608]{1,0:T(8,128)(2,1)S(1)} collective-permute-done((bf16[72,4608]{1,0:T(8,128)(2,1)}, bf16[72,4608]{1,0:T(8,128)(2,1)S(1)}, u32[]{:S(2)}, u32[]{:S(2)}) %collective-permute-start.5) | collective-permute-done | bytes 663584 | tf_op jit(solution)/shard_map/ppermute | solution.py:1256
  523.1 1.3 convert_add_fusion
  524.4 0.9 reshape.102
  525.2 3.9 slice_reduce_fusion
  529.1 1.0 copy.101
  530.1 1.0 copy.100
  (37 shorter events, 0.4 us)
Async XLA Ops:
  7.2 25.6 %copy-start = (s32[8,179]{1,0:T(8,128)S(1)}, s32[8,179]{1,0:T(8,128)}, u32[]{:S(2)}) copy-start(s32[8,179]{1,0:T(8,128)} %param.15) | copy-start | bytes 17188
  8.4 11.4 %copy-start.9 = (f32[8,961]{1,0:T(8,128)S(1)}, f32[8,961]{1,0:T(8,128)}, u32[]{:S(2)}) copy-start(f32[8,961]{1,0:T(8,128)} %param.22) | copy-start | bytes 92260
  8.4 19.6 %collective-permute-start.1 = (bf16[288,1152]{1,0:T(8,128)(2,1)S(1)}, bf16[288,1152]{1,0:T(8,128)(2,1)}, u32[]{:S(2)}, u32[]{:S(2)}) collective-permute-start(bf16[288,1152]{1,0:T(8,128)(2,1)S(1)} %constant_dynamic-slice_fusion.3), channel_id=1, source_target_pairs={{0,1},{1,0},{2,3},{3,2},{4,5},{5,4},{6,7},{7,6},{8,9},{9,8},{10,11... | collective-permute-start | bytes 1990664 | tf_op jit(solution)/shard_map/ppermute | solution.py:1256
  15.8 18.2 %copy-start.7 = (f32[16,16,31,1]{2,1,0,3:T(8,128)S(1)}, f32[16,16,31,1]{2,1,0,3:T(8,128)}, u32[]{:S(2)}) copy-start(f32[16,16,31,1]{2,1,0,3:T(8,128)} %constant.135) | copy-start | bytes 95236
  16.4 10.8 %all-to-all-start = ((bf16[2,4,3456]{2,1,0:T(4,128)(2,1)}), bf16[2,4,3456]{2,1,0:T(4,128)(2,1)S(1)}, u32[]{:S(2)}, u32[]{:S(2)}) async-start(bf16[2,4,3456]{2,1,0:T(4,128)(2,1)} %all_to_all.10), calls=%async_computation | async-start | bytes 110592 | tf_op jit(solution)/shard_map/all_to_all | solution.py:1330
  19.7 364.2 %reduce-scatter.3.cloned.1.call-start = ((), (), s32[]{:S(2)}) async-start(), calls=%async_computation.3 | async-start | bytes 11280384 | tf_op jit(solution)/shard_map/reduce_scatter | solution.py:1310
  19.8 8.2 %collective-permute-start = (f32[8,961]{1,0:T(8,128)S(1)}, f32[8,961]{1,0:T(8,128)S(1)}, u32[]{:S(2)}, u32[]{:S(2)}) collective-permute-start(f32[8,961]{1,0:T(8,128)S(1)} %copy-done.9), channel_id=1, source_target_pairs={{0,1},{1,0},{2,3},{3,2},{4,5},{5,4},{6,7},{7,6},{8,9},{9,8},{10,11... | collective-permute-start | bytes 92264 | tf_op jit(solution)/shard_map/ppermute | solution.py:1256
  31.0 44.6 %collective-permute-start.2 = (bf16[864,1152]{1,0:T(8,128)(2,1)}, bf16[864,1152]{1,0:T(8,128)(2,1)}, u32[]{:S(2)}, u32[]{:S(2)}) collective-permute-start(bf16[864,1152]{1,0:T(8,128)(2,1)} %constant_dynamic-slice_fusion.2), channel_id=1, source_target_pairs={{0,1},{1,0},{2,3},{3,2},{4,5},{5,4},{6,7},{7,6},{8,9},{9,8},{10,11... | collective-permute-start | bytes 5971976 | tf_op jit(solution)/shard_map/ppermute | solution.py:1256
  54.1 22.0 %copy-start.3 = (bf16[716,1152]{1,0:T(8,128)(2,1)S(1)}, bf16[716,1152]{1,0:T(8,128)(2,1)}, u32[]{:S(2)}) copy-start(bf16[716,1152]{1,0:T(8,128)(2,1)} %param.23) | copy-start | bytes 4948996
  75.6 7.0 %collective-permute-start.3 = (bf16[864,1152]{1,0:T(8,128)(2,1)}, bf16[864,1152]{1,0:T(8,128)(2,1)}, u32[]{:S(2)}, u32[]{:S(2)}) collective-permute-start(bf16[864,1152]{1,0:T(8,128)(2,1)} %collective-permute-done.2.refs_8_.refs_1_), channel_id=1, source_target_pairs={{0,2},{2,0},{4,6},{6,4},{8,10},{10,8},{12,14},{14,12},{16,18},{18,... | collective-permute-start | bytes 5971976 | tf_op jit(solution)/shard_map/ppermute | solution.py:1288
  75.6 7.0 %collective-permute-start.4 = (bf16[288,1152]{1,0:T(8,128)(2,1)}, bf16[288,1152]{1,0:T(8,128)(2,1)}, u32[]{:S(2)}, u32[]{:S(2)}) collective-permute-start(bf16[288,1152]{1,0:T(8,128)(2,1)} %collective-permute-done.1.refs_11_.refs_4_), channel_id=1, source_target_pairs={{0,2},{2,0},{4,6},{6,4},{8,10},{10,8},{12,14},{14,12},{16,18},{18,... | collective-permute-start | bytes 1990664 | tf_op jit(solution)/shard_map/ppermute | solution.py:1288
  78.4 4.2 copy-start.2
  206.9 300.2 %reduce-scatter.5.cloned.1.call-start = ((), (), s32[]{:S(2)}) async-start(), calls=%async_computation.4 | async-start | bytes 11280384 | tf_op jit(solution)/shard_map/reduce_scatter | solution.py:1310
  286.8 0.7 copy-start.6
  379.4 1.4 copy-start.8
  379.4 2.8 copy-start.4
  500.3 5.2 copy-start.5
  507.1 16.0 %collective-permute-start.5 = (bf16[72,4608]{1,0:T(8,128)(2,1)}, bf16[72,4608]{1,0:T(8,128)(2,1)S(1)}, u32[]{:S(2)}, u32[]{:S(2)}) collective-permute-start(bf16[72,4608]{1,0:T(8,128)(2,1)} %reduce-scatter.5.cloned.1.call-done), channel_id=1, source_target_pairs={{0,1},{1,0},{2,3},{3,2},{4,5},{5,4},{6,7},{7,6},{8,9},{9,8},{10,11... | collective-permute-start | bytes 1990664 | tf_op jit(solution)/shard_map/ppermute | solution.py:1256
  523.1 8.0 %copy-start.1 = (s32[8,179]{1,0:T(8,128)S(1)}, s32[8,179]{1,0:T(8,128)}, u32[]{:S(2)}) copy-start(s32[8,179]{1,0:T(8,128)} %param.15) | copy-start | bytes 17188
Sparse Core Ops, SparseCore 0:
  207.0 120.5 reduce-scatter.2
  331.7 156.3 reduce-scatter.4

commit v10 on v9

--- a/solution.py
+++ b/solution.py
@@ -1241,14 +1241,57 @@
         cost_estimate=cost(1e7, 1e5),
     )(first, dattn, dqkv, att, pack_own, pack_other, ada_weight)
     here = place_bit(lax.axis_index("dp"), FINAL) * share
-    mine = lax.dynamic_slice_in_dim(sums, here, share, 1)
+    mine = lax.dynamic_slice_in_dim(sums, here, share, 1).astype(F32)
     return (
-        jnp.transpose(mine, (1, 0, 2)).reshape(share, -1),
+        jnp.transpose(mine[:3], (1, 0, 2)),
+        jnp.transpose(mine[3]),
         jnp.transpose(ada_grad, (1, 0, 2)).reshape(share, -1),
         small[:pieces].reshape(-1),
         small[pieces : pieces + table_rows, :BUCKETS],
         silu[:images],
     )
+
+
+def home_kernel(tile, own_ref, send_ref, up_ref, down_ref, sent, land, sems):
+    rows = own_ref.shape[0]
+    sent[:rows, :] = send_ref[...]
+    sent[rows:, :] = jnp.zeros((sent.shape[0] - rows, sent.shape[1]), BF)
+    greet_peers(())
+    copy = pltpu.make_async_remote_copy(
+        src_ref=sent,
+        dst_ref=land,
+        send_sem=sems.at[0],
+        recv_sem=sems.at[1],
+        device_id={"mp": 1 - lax.axis_index("mp")},
+        device_id_type=pl.DeviceIdType.MESH,
+    )
+    copy.start()
+    copy.wait()
+    for t in range(up_ref.shape[1] // tile):
+        for k, out_ref in enumerate((up_ref, down_ref)):
+            at = slice((2 * t + k) * tile, (2 * t + k + 1) * tile)
+            total = own_ref[:, at].astype(F32) + land[:rows, at].astype(F32)
+            out_ref[:, t * tile : (t + 1) * tile] = total
+
+
+def mlp_home(own, send, tile):
+    rows, columns = own.shape
+    padded = -(-rows // 16) * 16
+    vmem = pl.BlockSpec(memory_space=pltpu.VMEM)
+    half = jax.ShapeDtypeStruct((rows, columns // 2), F32)
+    return pl.pallas_call(
+        functools.partial(home_kernel, tile),
+        in_specs=[vmem] * 2,
+        out_specs=[vmem] * 2,
+        out_shape=[half, half],
+        scratch_shapes=[
+            pltpu.VMEM((padded, columns), BF),
+            pltpu.VMEM((padded, columns), BF),
+            pltpu.SemaphoreType.DMA((2,)),
+        ],
+        compiler_params=pltpu.CompilerParams(collective_id=4, has_side_effects=True),
+        cost_estimate=cost(1e7, 1e5),
+    )(own, send)
 
 
 def shift_mp(value, steps):
@@ -1408,7 +1451,7 @@
                 axis=0,
             )
             packs.append(jnp.pad(pack, ((0, 32 - used), (0, 0))))
-        attn_total, grad_ada_weight, grad_ada_bias, dtable, grad_silu = attn_grads(
+        grad_qkv, grad_out, grad_ada_weight, grad_ada_bias, dtable, grad_silu = attn_grads(
             first, dattn, dqkv, att, *packs, ada_weight, images, per_block
         )
     else:
@@ -1451,11 +1494,12 @@
                 for j in range(ways)
             ]
         )
-    mlp_grads = home(reduced)
-    attn_total = attn_total.astype(F32)
-    grad_up, grad_down_t = split_mlp_grads(mlp_grads, tile_own)
-    grad_qkv = attn_total[:, :proj_block].reshape(-1, 3, proj_block // 3)
-    grad_out = jnp.transpose(attn_total[:, proj_block:])
+        grad_qkv = attn_total[:, :proj_block].reshape(-1, 3, proj_block // 3)
+        grad_out = jnp.transpose(attn_total[:, proj_block:])
+    if here and tile_own % 128 == 0:
+        grad_up, grad_down_t = mlp_home(*reduced, tile_own)
+    else:
+        grad_up, grad_down_t = split_mlp_grads(home(reduced), tile_own)
 
     own_cond = lax.dynamic_slice_in_dim(conditioning, place * images, images, 0).astype(F32)
     grad_cond = jax.vjp(jax.nn.silu, own_cond)[1](grad_silu)[0].astype(BF)

time: 544 us -> 544 us (level)
  Pallas kernels: 435 us -> 454 us
  waiting for transfers between devices: 19.5 us -> 7.15 us
    pallas_call x0 -> x1, Pallas kernels: none -> 20.1 us  [mlp_home(): pl.pallas_call(functools.partial(home_kernel, tile), in_specs=[vmem] * 2,...]
    ppermute x4 -> x3, waiting for transfers between devices: 13.9 us -> 1.61 us  [shift_mp(): lax.ppermute(value, 'mp', [(i, (i - steps) % ways) for i in range(ways)])]
  transfers between devices with their start and end apart: 9 -> 8, of which waited for: 3 -> 2; matrix products, arithmetic and copies ran while one was open for 8% -> 7% of each run, Pallas kernels for 58% -> 58%
where the time goes in v10:
time: 544 us; the launch traced here: 538 us
  Pallas kernels  454 us (83%)
  local copies, waits for them, and re-layouts  35.7 us (7%)
  between operations  14.6 us (3%)
  starting transfers between devices  10.6 us (2%)
  other arithmetic  10 us (2%)
  waiting for transfers between devices  7.15 us (1%)
  matrix products  6.21 us (1%)
    pallas_call x2, Pallas kernels, mlp(): pl.pallas_call(functools.partial(mlp_kernel, chunk, fresh, fetch is not N...  163 us
    pallas_call x1, Pallas kernels, attn_grads(): pl.pallas_call(functools.partial(attn_grads_kernel, images, pieces, table...  115 us
    pallas_call x1, Pallas kernels, backward(): pl.pallas_call(functools.partial(backward_kernel, per_block, weight_layou...  85.1 us
    pallas_call x1, Pallas kernels, forward(): pl.pallas_call(functools.partial(forward_kernel, per_block, weight_layout...  41.2 us
    pallas_call x1, Pallas kernels, mlp_home(): pl.pallas_call(functools.partial(home_kernel, tile), in_specs=[vmem] * 2,...  20.1 us
    pallas_call x1, Pallas kernels, own_heads(): pl.pallas_call(functools.partial(own_heads_kernel, per_block), grid=(imag...  19.8 us
  transfers between devices with their start and end apart: 8, of which 2 were waited for; matrix products, arithmetic and copies ran while one was open for 7% of the time, Pallas kernels for 58%

profile of v10, /device:TPU:0, one launch (start us, length us, event | category | flops | bytes accessed | tf_op | source)
XLA Modules:
  0.0 538.2 jit_solution(15311999837287539381)
XLA Ops:
  7.2 0.0 copy-start
  7.2 1.1 constant_dynamic-slice_fusion.3
  8.4 0.0 copy-start.9
  8.4 3.0 collective-permute-start.1
  11.4 4.4 fusion.2
  15.8 0.7 all_to_all.10
  16.4 3.3 all-to-all-start
  19.7 0.0 reduce-scatter.3.cloned.1.call-start
  19.8 2.0 collective-permute-start
  21.7 5.5 %all-to-all-done = bf16[2,4,3456]{2,1,0:T(4,128)(2,1)S(1)} async-done(((bf16[2,4,3456]{2,1,0:T(4,128)(2,1)}), bf16[2,4,3456]{2,1,0:T(4,128)(2,1)S(1)}, u32[]{:S(2)}, u32[]{:S(2)}) %all-to-all-start) | async-done | bytes 55328 | tf_op jit(solution)/shard_map/all_to_all | solution.py:1373
  27.3 0.7 pad_convert_fusion.mod_ref.refs_5_.refs_7_
  28.0 0.0 collective-permute-done
  28.0 0.0 collective-permute-done.1.refs_11_.refs_4_
  28.0 3.0 constant_dynamic-slice_fusion.2
  31.0 1.7 collective-permute-start.2
  32.8 0.9 fusion.4.pick_ref.refs_6_.refs_8_
  33.7 0.2 concatenate.19
  33.8 0.2 concatenate.20
  34.0 1.8 convolution_bitcast_fusion
  35.8 3.4 copy.61
  39.3 4.4 reshape.82
  43.7 0.8 pad.102.strip_ref
  44.6 9.6 %shard_map.212.bias_ref.refs_7_.refs_9_ = f32[16,256,256]{2,1,0:T(8,128)} custom-call(f32[16,16,512]{2,1,0:T(8,128)} %pad.102.strip_ref), custom_call_target="tpu_custom_call" | custom-call | flops 1000000 | bytes 100000 | tf_op jit(solution)/shard_map/pallas_call | solution.py:88
  54.1 19.8 %shard_map.213 = (bf16[1024,1152]{1,0:T(8,128)(2,1)}, bf16[1728,1024]{1,0:T(8,128)(2,1)}, bf16[576,2048]{1,0:T(8,128)(2,1)}, f32[4,16,256]{2,1,0:T(8,128)}) custom-call(bf16[1024,1152]{1,0:T(8,128)(2,1)} %refs_6_.1, f32[4,8,1152]{2,1,0:T(8,128)} %pad_convert_fusion.mod_ref.refs_5_.refs_7_, bf16[4,192,256]{2,1,0:T(8,128)(2,1)} %fusion.4.pick_ref.refs_6_.refs_8_, ...), custom_call_target="tpu_custom_call" | custom-call | flops 10000000 | bytes 100000 | tf_op jit(solution)/shard_map/pallas_call | solution.py:233
  74.0 1.6 collective-permute-done.2.refs_8_.refs_1_
  75.6 0.0 collective-permute-start.3
  75.6 0.5 collective-permute-start.4
  76.1 0.4 reshape.84
  76.6 1.8 fusion.3
  78.4 1.1 slice.86
  79.5 3.0 fusion.dmlp_ref
  82.6 0.0 collective-permute-done.4.refs_12_.refs_5_
  82.6 0.0 collective-permute-done.3.refs_9_.refs_2_
  82.6 41.2 %shard_map.214 = (bf16[3456,1024]{1,0:T(8,128)(2,1)}, bf16[1152,2048]{1,0:T(8,128)(2,1)}, f32[4,32,256]{2,1,0:T(8,128)}, f32[1792,1152]{1,0:T(8,128)}, bf16[1792...) custom-call(bf16[1024,1152]{1,0:T(8,128)(2,1)} %get-tuple-element.67.refs_0_.first_ref, ...), custom_call_target="tpu_custom_call" | custom-call | flops 8000000000 | bytes 32000000 | tf_op jit(solution)/shard_map/pallas_call | solution.py:358
  123.8 83.0 %shard_map.215 = (f32[1792,1152]{1,0:T(8,128)}, f32[1792,1152]{1,0:T(8,128)}, bf16[1152,4608]{1,0:T(8,128)(2,1)}, bf16[1152,2304]{1,0:T(8,128)(2,1)}, bf16[2304,1152]{1,0:T(8,128)(2,1)}) custom-call(bf16[1792,1152]{1,0:T(8,128)(2,1)} %get-tuple-element.75.second_ref, bf16[1792,1152]{1,0:T(8,128)(2,1)} %fusion.dmlp_ref, bf16[1152,2304]{1,0:T(8,128)(2,1)} %refs_1_.1, ...), custom_call_target="tpu_custom_call" | custom-call | flops 60000002048 | bytes 60000000 | tf_op jit(solution)/shard_map/pallas_call | solution.py:580
  206.8 0.0 reduce-scatter.3.cloned.1.call-update
  206.8 0.0 reduce-scatter.5.cloned.1.call-start
  206.8 79.9 %shard_map.216 = (f32[1792,1152]{1,0:T(8,128)}, f32[1792,1152]{1,0:T(8,128)}, bf16[1152,4608]{1,0:T(8,128)(2,1)}) custom-call(bf16[1792,1152]{1,0:T(8,128)(2,1)} %get-tuple-element.75.second_ref, bf16[1792,1152]{1,0:T(8,128)(2,1)} %fusion.dmlp_ref, bf16[1152,2304]{1,0:T(8,128)(2,1)} %get-tuple-element.77.up_ref, ...), custom_call_target="tpu_custom_call" | custom-call | flops 10000000 | bytes 100000 | tf_op jit(solution)/shard_map/pallas_call | solution.py:580
  286.7 0.0 copy-start.6
  286.7 0.0 reduce-scatter.5.cloned.1.call-update
  286.8 0.6 copy-done.6
  287.5 85.1 %shard_map.217 = (bf16[1024,1152]{1,0:T(8,128)(2,1)}, bf16[768,1152]{1,0:T(8,128)(2,1)}, bf16[1024,1152]{1,0:T(8,128)(2,1)}, f32[4,8,1152]{2,1,0:T(8,128)}, bf16...) custom-call(bf16[1728,1152]{1,0:T(8,128)(2,1)} %bitcast.101, ...), custom_call_target="tpu_custom_call" | custom-call | flops 10000000 | bytes 100000 | tf_op jit(solution)/shard_map/pallas_call | solution.py:741
  372.5 3.8 reshape.88
  376.4 2.9 slice_bitcast_fusion.16
  379.3 0.0 copy-start.8
  379.3 1.1 add_convert_fusion
  380.4 0.1 slice.106
  380.5 0.1 slice.108
  380.8 0.6 pad.121.pack_own_ref
  381.5 0.6 pad.123.pack_other_ref
  382.1 0.1 slice.114
  382.3 1.6 reshape.86
  383.9 115.4 %shard_map.218 = (bf16[4,144,576]{2,1,0:T(8,128)(2,1)}, f32[3,72,1152]{2,1,0:T(8,128)}, f32[16,1152]{1,0:T(8,128)}, f32[16,1152]{1,0:T(8,128)}) custom-call(bf16[1024,1152]{1,0:T(8,128)(2,1)} %get-tuple-element.67.refs_0_.first_ref, bf16[2048,1152]{1,0:T(8,128)(2,1)} %get-tuple-element.86.dattn_hbm, bf16[3456,1024]{1,0:T(8,128)(2,1)} %get-tuple-element.89.dqkv_ref, ...), custom_call_target="tpu_custom_call" | custom-call | flops 10000000 | bytes 100000 | tf_op jit(solution)/shard_map/pallas_call | solution.py:1203
  499.2 0.9 slice.110
  500.1 1.5 slice.113
  501.6 1.1 dynamic-slice_convert_fusion
  502.6 0.7 slice_bitcast_fusion.17
  503.3 0.8 slice_bitcast_fusion
  504.1 20.1 %shard_map.219 = (f32[72,2304]{1,0:T(8,128)}, f32[72,2304]{1,0:T(8,128)}) custom-call(bf16[72,4608]{1,0:T(8,128)(2,1)} %reduce-scatter.3.cloned.1.call-done.own_ref, bf16[72,4608]{1,0:T(8,128)(2,1)} %reduce-scatter.5.cloned.1.call-done.send_ref), custom_call_target="tpu_custom_call" | custom-call | flops 10000000 | bytes 100000 | tf_op jit(solution)/shard_map/pallas_call | solution.py:1282
  524.2 1.0 copy.95
  525.2 0.6 reshape.91
  525.9 1.4 fusion.23
  527.2 2.0 copy.100
  529.2 2.0 copy.101
  (29 shorter events, 0.3 us)
Async XLA Ops:
  7.2 25.6 %copy-start = (s32[8,179]{1,0:T(8,128)S(1)}, s32[8,179]{1,0:T(8,128)}, u32[]{:S(2)}) copy-start(s32[8,179]{1,0:T(8,128)} %param.15) | copy-start | bytes 17188
  8.4 11.4 %copy-start.9 = (f32[8,961]{1,0:T(8,128)S(1)}, f32[8,961]{1,0:T(8,128)}, u32[]{:S(2)}) copy-start(f32[8,961]{1,0:T(8,128)} %param.22) | copy-start | bytes 92260
  8.4 19.6 %collective-permute-start.1 = (bf16[288,1152]{1,0:T(8,128)(2,1)S(1)}, bf16[288,1152]{1,0:T(8,128)(2,1)}, u32[]{:S(2)}, u32[]{:S(2)}) collective-permute-start(bf16[288,1152]{1,0:T(8,128)(2,1)S(1)} %constant_dynamic-slice_fusion.3), channel_id=1, source_target_pairs={{0,1},{1,0},{2,3},{3,2},{4,5},{5,4},{6,7},{7,6},{8,9},{9,8},{10,11... | collective-permute-start | bytes 1990664 | tf_op jit(solution)/shard_map/ppermute | solution.py:1299
  15.8 18.2 %copy-start.7 = (f32[16,16,31,1]{2,1,0,3:T(8,128)S(1)}, f32[16,16,31,1]{2,1,0,3:T(8,128)}, u32[]{:S(2)}) copy-start(f32[16,16,31,1]{2,1,0,3:T(8,128)} %constant.135) | copy-start | bytes 95236
  16.4 10.8 %all-to-all-start = ((bf16[2,4,3456]{2,1,0:T(4,128)(2,1)}), bf16[2,4,3456]{2,1,0:T(4,128)(2,1)S(1)}, u32[]{:S(2)}, u32[]{:S(2)}) async-start(bf16[2,4,3456]{2,1,0:T(4,128)(2,1)} %all_to_all.10), calls=%async_computation | async-start | bytes 110592 | tf_op jit(solution)/shard_map/all_to_all | solution.py:1373
  19.7 364.1 %reduce-scatter.3.cloned.1.call-start = ((), (), s32[]{:S(2)}) async-start(), calls=%async_computation.3 | async-start | bytes 11280384 | tf_op jit(solution)/shard_map/reduce_scatter | solution.py:1353
  19.8 8.2 %collective-permute-start = (f32[8,961]{1,0:T(8,128)S(1)}, f32[8,961]{1,0:T(8,128)S(1)}, u32[]{:S(2)}, u32[]{:S(2)}) collective-permute-start(f32[8,961]{1,0:T(8,128)S(1)} %copy-done.9), channel_id=1, source_target_pairs={{0,1},{1,0},{2,3},{3,2},{4,5},{5,4},{6,7},{7,6},{8,9},{9,8},{10,11... | collective-permute-start | bytes 92264 | tf_op jit(solution)/shard_map/ppermute | solution.py:1299
  31.0 44.6 %collective-permute-start.2 = (bf16[864,1152]{1,0:T(8,128)(2,1)}, bf16[864,1152]{1,0:T(8,128)(2,1)}, u32[]{:S(2)}, u32[]{:S(2)}) collective-permute-start(bf16[864,1152]{1,0:T(8,128)(2,1)} %constant_dynamic-slice_fusion.2), channel_id=1, source_target_pairs={{0,1},{1,0},{2,3},{3,2},{4,5},{5,4},{6,7},{7,6},{8,9},{9,8},{10,11... | collective-permute-start | bytes 5971976 | tf_op jit(solution)/shard_map/ppermute | solution.py:1299
  54.1 22.0 %copy-start.3 = (bf16[716,1152]{1,0:T(8,128)(2,1)S(1)}, bf16[716,1152]{1,0:T(8,128)(2,1)}, u32[]{:S(2)}) copy-start(bf16[716,1152]{1,0:T(8,128)(2,1)} %param.23) | copy-start | bytes 4948996
  75.6 7.0 %collective-permute-start.3 = (bf16[864,1152]{1,0:T(8,128)(2,1)}, bf16[864,1152]{1,0:T(8,128)(2,1)}, u32[]{:S(2)}, u32[]{:S(2)}) collective-permute-start(bf16[864,1152]{1,0:T(8,128)(2,1)} %collective-permute-done.2.refs_8_.refs_1_), channel_id=1, source_target_pairs={{0,2},{2,0},{4,6},{6,4},{8,10},{10,8},{12,14},{14,12},{16,18},{18,... | collective-permute-start | bytes 5971976 | tf_op jit(solution)/shard_map/ppermute | solution.py:1331
  75.6 7.0 %collective-permute-start.4 = (bf16[288,1152]{1,0:T(8,128)(2,1)}, bf16[288,1152]{1,0:T(8,128)(2,1)}, u32[]{:S(2)}, u32[]{:S(2)}) collective-permute-start(bf16[288,1152]{1,0:T(8,128)(2,1)} %collective-permute-done.1.refs_11_.refs_4_), channel_id=1, source_target_pairs={{0,2},{2,0},{4,6},{6,4},{8,10},{10,8},{12,14},{14,12},{16,18},{18,... | collective-permute-start | bytes 1990664 | tf_op jit(solution)/shard_map/ppermute | solution.py:1331
  78.4 4.2 copy-start.2
  206.8 297.4 %reduce-scatter.5.cloned.1.call-start = ((), (), s32[]{:S(2)}) async-start(), calls=%async_computation.4 | async-start | bytes 11280384 | tf_op jit(solution)/shard_map/reduce_scatter | solution.py:1353
  286.7 0.7 copy-start.6
  379.3 1.4 copy-start.8
  379.3 2.8 copy-start.4
  499.2 25.0 %copy-start.5 = (f32[3,72,1152]{2,1,0:T(8,128)S(1)}, f32[3,72,1152]{2,1,0:T(8,128)}, u32[]{:S(2)}) copy-start(f32[3,72,1152]{2,1,0:T(8,128)} %get-tuple-element.94) | copy-start | bytes 2985988
  501.6 29.6 %copy-start.1 = (s32[8,179]{1,0:T(8,128)S(1)}, s32[8,179]{1,0:T(8,128)}, u32[]{:S(2)}) copy-start(s32[8,179]{1,0:T(8,128)} %param.15) | copy-start | bytes 17188
Sparse Core Ops, SparseCore 0:
  206.9 120.5 reduce-scatter.2
  331.5 156.3 reduce-scatter.4

commit v11 on v9

--- a/solution.py
+++ b/solution.py
@@ -1256,10 +1256,13 @@
     return lax.ppermute(value, "mp", [(i, (i - steps) % ways) for i in range(ways)])
 
 
-def near_halves(block):
+def core_half(block):
     half = block.shape[0] // 2
-    core = lax.axis_index("dp") % 2
-    mine = lax.dynamic_slice_in_dim(block, core * half, half, 0)
+    return lax.dynamic_slice_in_dim(block, (lax.axis_index("dp") % 2) * half, half, 0)
+
+
+def near_halves(block, mine=None):
+    mine = core_half(block) if mine is None else mine
     return [shift_mp(mine, steps) for steps in range(1, lax.axis_size("mp"))]
 
 
@@ -1333,9 +1336,9 @@
     weight_own = jnp.transpose(attn_qkv.reshape(width, -1))
     tables = [rel_table] + [shift_mp(rel_table, s) for s in range(1, ways)]
     mod, tables, near_o, weight_sent = lax.optimization_barrier(
-        (mod, tables, near_o, weight_own)
-    )
-    near_w = near_halves(weight_sent)
+        (mod, tables, near_o, core_half(weight_own))
+    )
+    near_w = near_halves(weight_own, weight_sent)
     fetch = ways == 2 and lax.axis_size("dp") % 4 == 0 and mlp_up.shape[0] % 32 == 0
     fetch = fetch and mlp_down.shape[0] % 64 == 0
     bias = bias_whole(jnp.concatenate(tables, axis=0))
@@ -1361,7 +1364,7 @@
     weight_others = gathered_parts(near_w)
     weight = after_own(weight_others, weight_own)
     out_weight = gathered_parts(near_o, attn_out)
-    cut = (mlp_up.shape[0] * 5 // 18) // 16 * 16
+    cut = (mlp_up.shape[0] * 4 // 18) // 16 * 16
     qkv, att, lse, middle, second, branch, *near_up = forward(
         own, tokens, mod, pick, bias, weight_others, out_weight, per_block,
         mlp_up if fetch else None, cut,

time: 544 us -> 538 us (0.989)
    pallas_call x1, Pallas kernels: 41.2 us -> 34.9 us  [forward(): pl.pallas_call(functools.partial(forward_kernel, per_block, weight_layout...]
  transfers between devices with their start and end apart: 9 -> 9, of which waited for: 3 -> 3; matrix products, arithmetic and copies ran while one was open for 8% -> 9% of each run, Pallas kernels for 58% -> 58%
where the time goes in v11:
time: 538 us; the launch traced here: 532 us
  Pallas kernels  431 us (80%)
  local copies, waits for them, and re-layouts  39.5 us (7%)
  waiting for transfers between devices  15.6 us (3%)
  between operations  14.7 us (3%)
  starting transfers between devices  12.7 us (2%)
  other arithmetic  11.3 us (2%)
  matrix products  6.2 us (1%)
    pallas_call x2, Pallas kernels, mlp(): pl.pallas_call(functools.partial(mlp_kernel, chunk, fresh, fetch is not N...  167 us
    pallas_call x1, Pallas kernels, attn_grads(): pl.pallas_call(functools.partial(attn_grads_kernel, images, pieces, table...  116 us
    pallas_call x1, Pallas kernels, backward(): pl.pallas_call(functools.partial(backward_kernel, per_block, weight_layou...  85.1 us
    pallas_call x1, Pallas kernels, forward(): pl.pallas_call(functools.partial(forward_kernel, per_block, weight_layout...  34.9 us
    pallas_call x1, Pallas kernels, own_heads(): pl.pallas_call(functools.partial(own_heads_kernel, per_block), grid=(imag...  19.8 us
    ppermute x4, waiting for transfers between devices, shift_mp(): lax.ppermute(value, 'mp', [(i, (i - steps) % ways) for i in range(ways)])  13.1 us
  transfers between devices with their start and end apart: 9, of which 3 were waited for; matrix products, arithmetic and copies ran while one was open for 9% of the time, Pallas kernels for 58%

profile of v11, /device:TPU:0, one launch (start us, length us, event | category | flops | bytes accessed | tf_op | source)
XLA Modules:
  0.0 531.5 jit_solution(8635175793479673618)
XLA Ops:
  7.2 0.0 copy-start
  7.2 1.1 constant_dynamic-slice_fusion.2
  8.4 0.0 copy-start.9
  8.4 3.0 collective-permute-start.1
  11.4 4.4 fusion.2
  15.8 0.7 all_to_all.10
  16.4 3.3 all-to-all-start
  19.7 0.0 reduce-scatter.3.cloned.1.call-start
  19.8 2.0 collective-permute-start
  21.7 3.0 dynamic-slice_bitcast_fusion
  24.7 2.5 all-to-all-done
  27.3 0.7 pad_convert_fusion.mod_ref.refs_5_.refs_7_
  28.0 1.7 collective-permute-start.2
  29.8 0.9 fusion.4.pick_ref.refs_6_.refs_8_
  30.7 0.2 concatenate.19
  30.8 0.2 concatenate.20
  31.0 1.8 convolution_bitcast_fusion
  32.8 3.5 copy.63
  36.3 4.4 reshape.91
  40.8 0.8 pad.102.strip_ref
  41.6 9.5 %shard_map.212.bias_ref.refs_7_.refs_9_ = f32[16,256,256]{2,1,0:T(8,128)} custom-call(f32[16,16,512]{2,1,0:T(8,128)} %pad.102.strip_ref), custom_call_target="tpu_custom_call" | custom-call | flops 1000000 | bytes 100000 | tf_op jit(solution)/shard_map/pallas_call | solution.py:88
  51.1 19.8 %shard_map.213 = (bf16[1024,1152]{1,0:T(8,128)(2,1)}, bf16[1728,1024]{1,0:T(8,128)(2,1)}, bf16[576,2048]{1,0:T(8,128)(2,1)}, f32[4,16,256]{2,1,0:T(8,128)}) custom-call(bf16[1024,1152]{1,0:T(8,128)(2,1)} %refs_6_.1, f32[4,8,1152]{2,1,0:T(8,128)} %pad_convert_fusion.mod_ref.refs_5_.refs_7_, bf16[4,192,256]{2,1,0:T(8,128)(2,1)} %fusion.4.pick_ref.refs_6_.refs_8_, ...), custom_call_target="tpu_custom_call" | custom-call | flops 10000000 | bytes 100000 | tf_op jit(solution)/shard_map/pallas_call | solution.py:233
  70.9 1.7 collective-permute-done.2.refs_8_.refs_1_
  72.6 0.5 collective-permute-start.4
  73.1 0.4 reshape.93
  73.6 1.8 fusion.3
  75.4 1.1 slice.92
  76.5 3.0 fusion.dmlp_ref
  79.6 34.9 %shard_map.214 = (bf16[3456,1024]{1,0:T(8,128)(2,1)}, bf16[1152,2048]{1,0:T(8,128)(2,1)}, f32[4,32,256]{2,1,0:T(8,128)}, f32[1792,1152]{1,0:T(8,128)}, bf16[1792...) custom-call(bf16[1024,1152]{1,0:T(8,128)(2,1)} %get-tuple-element.65.refs_0_.first_ref, ...), custom_call_target="tpu_custom_call" | custom-call | flops 8000000000 | bytes 32000000 | tf_op jit(solution)/shard_map/pallas_call | solution.py:358
  114.5 86.7 %shard_map.215 = (f32[1792,1152]{1,0:T(8,128)}, f32[1792,1152]{1,0:T(8,128)}, bf16[1152,4608]{1,0:T(8,128)(2,1)}, bf16[1152,2304]{1,0:T(8,128)(2,1)}, bf16[2304,1152]{1,0:T(8,128)(2,1)}) custom-call(bf16[1792,1152]{1,0:T(8,128)(2,1)} %get-tuple-element.73.second_ref, bf16[1792,1152]{1,0:T(8,128)(2,1)} %fusion.dmlp_ref, bf16[1152,2304]{1,0:T(8,128)(2,1)} %refs_1_.1, ...), custom_call_target="tpu_custom_call" | custom-call | flops 60000002048 | bytes 60000000 | tf_op jit(solution)/shard_map/pallas_call | solution.py:580
  201.2 0.0 reduce-scatter.3.cloned.1.call-update
  201.2 0.0 reduce-scatter.5.cloned.1.call-start
  201.2 79.9 %shard_map.216 = (f32[1792,1152]{1,0:T(8,128)}, f32[1792,1152]{1,0:T(8,128)}, bf16[1152,4608]{1,0:T(8,128)(2,1)}) custom-call(bf16[1792,1152]{1,0:T(8,128)(2,1)} %get-tuple-element.73.second_ref, bf16[1792,1152]{1,0:T(8,128)(2,1)} %fusion.dmlp_ref, bf16[1152,2304]{1,0:T(8,128)(2,1)} %get-tuple-element.75.up_ref, ...), custom_call_target="tpu_custom_call" | custom-call | flops 10000000 | bytes 100000 | tf_op jit(solution)/shard_map/pallas_call | solution.py:580
  281.1 0.0 reduce-scatter.5.cloned.1.call-update
  281.2 0.6 copy-done.6
  281.9 85.1 %shard_map.217 = (bf16[1024,1152]{1,0:T(8,128)(2,1)}, bf16[768,1152]{1,0:T(8,128)(2,1)}, bf16[1024,1152]{1,0:T(8,128)(2,1)}, f32[4,8,1152]{2,1,0:T(8,128)}, bf16...) custom-call(bf16[1728,1152]{1,0:T(8,128)(2,1)} %bitcast.106, ...), custom_call_target="tpu_custom_call" | custom-call | flops 10000000 | bytes 100000 | tf_op jit(solution)/shard_map/pallas_call | solution.py:741
  367.0 3.8 reshape.97
  370.8 2.9 slice_bitcast_fusion.15
  373.7 1.1 add_convert_fusion
  374.8 0.1 slice.112
  374.9 0.1 slice.114
  375.3 0.6 pad.121.pack_own_ref
  375.9 0.6 pad.123.pack_other_ref
  376.5 0.1 slice.122
  376.7 1.6 reshape.95
  378.3 115.6 %shard_map.218 = (bf16[4,144,576]{2,1,0:T(8,128)(2,1)}, f32[3,72,1152]{2,1,0:T(8,128)}, f32[16,1152]{1,0:T(8,128)}, f32[16,1152]{1,0:T(8,128)}) custom-call(bf16[1024,1152]{1,0:T(8,128)(2,1)} %get-tuple-element.65.refs_0_.first_ref, bf16[2048,1152]{1,0:T(8,128)(2,1)} %get-tuple-element.84.dattn_hbm, bf16[3456,1024]{1,0:T(8,128)(2,1)} %get-tuple-element.87.dqkv_ref, ...), custom_call_target="tpu_custom_call" | custom-call | flops 10000000 | bytes 100000 | tf_op jit(solution)/shard_map/pallas_call | solution.py:1203
  493.9 0.9 slice.116
  494.8 1.5 slice.121
  496.2 1.0 convert_bitcast_fusion
  497.3 0.2 copy.80
  497.4 0.5 reshape.103
  498.0 0.3 reshape.101
  498.2 0.8 copy.81
  499.1 1.0 copy.99
  500.1 0.6 reshape.100
  500.7 2.1 collective-permute-start.5
  502.8 0.8 slice_bitcast_fusion.16
  503.6 1.4 fusion.23
  505.0 11.4 %collective-permute-done.5 = bf16[72,4608]{1,0:T(8,128)(2,1)S(1)} collective-permute-done((bf16[72,4608]{1,0:T(8,128)(2,1)}, bf16[72,4608]{1,0:T(8,128)(2,1)S(1)}, u32[]{:S(2)}, u32[]{:S(2)}) %collective-permute-start.5) | collective-permute-done | bytes 663584 | tf_op jit(solution)/shard_map/ppermute | solution.py:1256
  516.5 1.3 convert_add_fusion
  517.7 0.9 reshape.102
  518.6 3.9 slice_reduce_fusion
  522.5 1.0 copy.101
  523.5 1.0 copy.100
  (37 shorter events, 0.4 us)
Async XLA Ops:
  7.2 22.6 %copy-start = (s32[8,179]{1,0:T(8,128)S(1)}, s32[8,179]{1,0:T(8,128)}, u32[]{:S(2)}) copy-start(s32[8,179]{1,0:T(8,128)} %param.15) | copy-start | bytes 17188
  8.4 11.4 %copy-start.9 = (f32[8,961]{1,0:T(8,128)S(1)}, f32[8,961]{1,0:T(8,128)}, u32[]{:S(2)}) copy-start(f32[8,961]{1,0:T(8,128)} %param.22) | copy-start | bytes 92260
  8.4 19.6 %collective-permute-start.1 = (bf16[288,1152]{1,0:T(8,128)(2,1)S(1)}, bf16[288,1152]{1,0:T(8,128)(2,1)}, u32[]{:S(2)}, u32[]{:S(2)}) collective-permute-start(bf16[288,1152]{1,0:T(8,128)(2,1)S(1)} %constant_dynamic-slice_fusion.2), channel_id=1, source_target_pairs={{0,1},{1,0},{2,3},{3,2},{4,5},{5,4},{6,7},{7,6},{8,9},{9,8},{10,11... | collective-permute-start | bytes 1990664 | tf_op jit(solution)/shard_map/ppermute | solution.py:1256
  15.8 15.2 %copy-start.7 = (f32[16,16,31,1]{2,1,0,3:T(8,128)S(1)}, f32[16,16,31,1]{2,1,0,3:T(8,128)}, u32[]{:S(2)}) copy-start(f32[16,16,31,1]{2,1,0,3:T(8,128)} %constant.135) | copy-start | bytes 95236
  16.4 10.8 %all-to-all-start = ((bf16[2,4,3456]{2,1,0:T(4,128)(2,1)}), bf16[2,4,3456]{2,1,0:T(4,128)(2,1)S(1)}, u32[]{:S(2)}, u32[]{:S(2)}) async-start(bf16[2,4,3456]{2,1,0:T(4,128)(2,1)} %all_to_all.10), calls=%async_computation | async-start | bytes 110592 | tf_op jit(solution)/shard_map/all_to_all | solution.py:1333
  19.7 358.6 %reduce-scatter.3.cloned.1.call-start = ((), (), s32[]{:S(2)}) async-start(), calls=%async_computation.3 | async-start | bytes 11280384 | tf_op jit(solution)/shard_map/reduce_scatter | solution.py:1313
  19.8 8.2 %collective-permute-start = (f32[8,961]{1,0:T(8,128)S(1)}, f32[8,961]{1,0:T(8,128)S(1)}, u32[]{:S(2)}, u32[]{:S(2)}) collective-permute-start(f32[8,961]{1,0:T(8,128)S(1)} %copy-done.9), channel_id=1, source_target_pairs={{0,1},{1,0},{2,3},{3,2},{4,5},{5,4},{6,7},{7,6},{8,9},{9,8},{10,11... | collective-permute-start | bytes 92264 | tf_op jit(solution)/shard_map/ppermute | solution.py:1256
  28.0 44.6 %collective-permute-start.2 = (bf16[864,1152]{1,0:T(8,128)(2,1)}, bf16[864,1152]{1,0:T(8,128)(2,1)}, u32[]{:S(2)}, u32[]{:S(2)}) collective-permute-start(bf16[864,1152]{1,0:T(8,128)(2,1)} %dynamic-slice_bitcast_fusion), channel_id=1, source_target_pairs={{0,1},{1,0},{2,3},{3,2},{4,5},{5,4},{6,7},{7,6},{8,9},{9,8},{10,11... | collective-permute-start | bytes 5971976 | tf_op jit(solution)/shard_map/ppermute | solution.py:1256
  51.1 22.0 %copy-start.3 = (bf16[716,1152]{1,0:T(8,128)(2,1)S(1)}, bf16[716,1152]{1,0:T(8,128)(2,1)}, u32[]{:S(2)}) copy-start(bf16[716,1152]{1,0:T(8,128)(2,1)} %param.23) | copy-start | bytes 4948996
  72.6 7.0 %collective-permute-start.3 = (bf16[864,1152]{1,0:T(8,128)(2,1)}, bf16[864,1152]{1,0:T(8,128)(2,1)}, u32[]{:S(2)}, u32[]{:S(2)}) collective-permute-start(bf16[864,1152]{1,0:T(8,128)(2,1)} %collective-permute-done.2.refs_8_.refs_1_), channel_id=1, source_target_pairs={{0,2},{2,0},{4,6},{6,4},{8,10},{10,8},{12,14},{14,12},{16,18},{18,... | collective-permute-start | bytes 5971976 | tf_op jit(solution)/shard_map/ppermute | solution.py:1291
  72.6 7.0 %collective-permute-start.4 = (bf16[288,1152]{1,0:T(8,128)(2,1)}, bf16[288,1152]{1,0:T(8,128)(2,1)}, u32[]{:S(2)}, u32[]{:S(2)}) collective-permute-start(bf16[288,1152]{1,0:T(8,128)(2,1)} %collective-permute-done.1.refs_11_.refs_4_), channel_id=1, source_target_pairs={{0,2},{2,0},{4,6},{6,4},{8,10},{10,8},{12,14},{14,12},{16,18},{18,... | collective-permute-start | bytes 1990664 | tf_op jit(solution)/shard_map/ppermute | solution.py:1291
  75.4 4.2 copy-start.2
  201.2 299.5 %reduce-scatter.5.cloned.1.call-start = ((), (), s32[]{:S(2)}) async-start(), calls=%async_computation.4 | async-start | bytes 11280384 | tf_op jit(solution)/shard_map/reduce_scatter | solution.py:1313
  281.1 0.7 copy-start.6
  373.7 1.4 copy-start.8
  373.7 2.8 copy-start.4
  493.9 5.2 copy-start.5
  500.7 15.7 %collective-permute-start.5 = (bf16[72,4608]{1,0:T(8,128)(2,1)}, bf16[72,4608]{1,0:T(8,128)(2,1)S(1)}, u32[]{:S(2)}, u32[]{:S(2)}) collective-permute-start(bf16[72,4608]{1,0:T(8,128)(2,1)} %reduce-scatter.5.cloned.1.call-done), channel_id=1, source_target_pairs={{0,1},{1,0},{2,3},{3,2},{4,5},{5,4},{6,7},{7,6},{8,9},{9,8},{10,11... | collective-permute-start | bytes 1990664 | tf_op jit(solution)/shard_map/ppermute | solution.py:1256
  516.5 8.0 %copy-start.1 = (s32[8,179]{1,0:T(8,128)S(1)}, s32[8,179]{1,0:T(8,128)}, u32[]{:S(2)}) copy-start(s32[8,179]{1,0:T(8,128)} %param.15) | copy-start | bytes 17188
Sparse Core Ops, SparseCore 0:
  201.3 120.5 reduce-scatter.2
  326.0 155.8 reduce-scatter.4
